TPU v7x, 32 devices: a whole 2x2x4 slice. The times are simulated.
32 devices in a mesh: dp: 4 (over z), expert: 4 (over y, core), hidden: 2 (over x).
Axes of the slice: x: 2, y: 2, z: 4, core: 2. Of those that a mesh axis runs over, the one named last changes fastest.
Arguments:
- layer_input: bfloat16 [4, 256, 3072], P('dp', 'expert'), may hold values from -6 to 6
- grad_out: bfloat16 [4, 256, 3072], P('dp', 'expert'), may hold values from -6 to 6
- picks: int32 [4, 4, 4, 8], P('dp', 'expert'), may hold values from 0 to 63, as said below
- gates: float32 [4, 4, 4, 8], P('dp', 'expert'), may hold values from 0.1 to 1
- w_up: bfloat16 [4, 3072, 2048], P('expert', None, 'hidden'), may hold values from -0.109375 to 0.109375
- w_down: bfloat16 [4, 3072, 2048], P('expert', None, 'hidden'), may hold values from -0.125 to 0.125
Outputs:
- grad_in: bfloat16 [4, 256, 3072], P('dp', 'expert', 'hidden')
- grad_up: float32 [4, 3072, 2048], P('expert', 'dp', 'hidden')
- grad_down: float32 [4, 3072, 2048], P('expert', 'dp', 'hidden')
Inputs may be any that keep to these rules, and one draw needn't show every extreme that they name: `picks`: for every group, block and expert, the 8 positions are distinct, so each expert takes exactly 8 tokens from every block of 64 tokens.
All inputs are finite; a program needn't handle non-finite values.
Results may differ from a plain program's by a relative error of at most 0.015.
Values may be sent and summed in bfloat16 or wider, within the bound.
No kernel may reach another device: no remote copies, remote signals or barrier semaphores. Data moves between devices by JAX's collectives and lax.ppermute only.
A program may use at most 64 MiB of HBM per device.

v0:
```python
import jax
import jax.numpy as jnp
from jax import lax
from jax.sharding import PartitionSpec as P

ROOT_TERM = 0.7978845608028654
CUBIC_TERM = 0.044715


def gelu_value(pre):
    inner = jnp.tanh(ROOT_TERM * (pre + CUBIC_TERM * pre * pre * pre))
    return 0.5 * pre * (1.0 + inner)


def gelu_slope(pre):
    inner = jnp.tanh(ROOT_TERM * (pre + CUBIC_TERM * pre * pre * pre))
    return 0.5 * (1.0 + inner) + 0.5 * pre * (1.0 - inner * inner) * ROOT_TERM * (
        1.0 + 3.0 * CUBIC_TERM * pre * pre
    )


def local(layer_input, grad_out, picks, gates, w_up, w_down):
    tokens = layer_input[0]
    upstream = grad_out[0]
    chosen = picks[0, 0]
    tok_dev, width = tokens.shape
    n_exp, n_pick = chosen.shape
    slots = n_exp * n_pick
    upper = w_up[0]
    lower = w_down[0]
    units = upper.shape[1]
    flat = chosen.reshape(slots)
    selector = (flat[:, None] == jnp.arange(tok_dev, dtype=jnp.int32)[None, :]).astype(jnp.bfloat16)
    send_in = jnp.dot(selector, tokens, preferred_element_type=jnp.float32).astype(jnp.bfloat16)
    send_out = jnp.dot(selector, upstream, preferred_element_type=jnp.float32).astype(jnp.bfloat16)
    rows_in, rows_out = (
        lax.all_to_all(send_in, "expert", split_axis=0, concat_axis=0, tiled=True),
        lax.all_to_all(send_out, "expert", split_axis=0, concat_axis=0, tiled=True),
    )
    scaled = (gates[0, 0].reshape(slots, 1) * rows_out.astype(jnp.float32)).astype(jnp.bfloat16)
    pre = jnp.dot(rows_in, upper, preferred_element_type=jnp.float32)
    act = gelu_value(pre).astype(jnp.bfloat16)
    grad_pre = (
        jnp.dot(scaled, lower, preferred_element_type=jnp.float32) * gelu_slope(pre)
    ).astype(jnp.bfloat16)
    contract = (((0,), (0,)), ((), ()))
    term_up = lax.dot_general(rows_in, grad_pre, contract, preferred_element_type=jnp.float32)
    term_down = lax.dot_general(scaled, act, contract, preferred_element_type=jnp.float32)
    summed = lax.psum_scatter(
        jnp.concatenate([term_up, term_down], axis=1).astype(jnp.bfloat16),
        "dp",
        scatter_dimension=0,
        tiled=True,
    ).astype(jnp.float32)
    grad_upper = summed[:, :units][None]
    grad_lower = summed[:, units:][None]
    column_sums = lax.psum_scatter(
        lax.dot_general(
            upper, grad_pre, (((1,), (1,)), ((), ())), preferred_element_type=jnp.float32
        ).astype(jnp.bfloat16),
        "hidden",
        scatter_dimension=0,
        tiled=True,
    )
    returned = lax.all_to_all(column_sums, "expert", split_axis=1, concat_axis=1, tiled=True)
    grad_rows = lax.dot_general(
        selector, returned, (((0,), (1,)), ((), ())), preferred_element_type=jnp.float32
    )
    return (grad_rows.astype(jnp.bfloat16)[None], grad_upper, grad_lower)


def solution(mesh):
    placed = (
        P("dp", "expert", None),
        P("dp", "expert", None),
        P("dp", "expert", None, None),
        P("dp", "expert", None, None),
        P("expert", None, "hidden"),
        P("expert", None, "hidden"),
    )
    return jax.shard_map(
        local,
        mesh=mesh,
        in_specs=placed,
        out_specs=(
            P("dp", "expert", "hidden"),
            P("expert", "dp", "hidden"),
            P("expert", "dp", "hidden"),
        ),
        check_vma=False,
    )
```

profile of v0, /device:TPU:0, one launch (start us, length us, event | category | flops | bytes accessed | tf_op | source)
XLA Modules:
  0.0 280.3 jit_solution(724129514038333231)
XLA Ops:
  7.2 0.0 copy-start
  7.2 0.0 copy-start.1
  7.2 0.8 eq.15
  8.0 0.2 copy-done
  8.2 0.9 fusion.10
  9.1 4.2 %all-to-all-start.1 = ((bf16[4,8,3072]{2,1,0:T(8,128)(2,1)}), bf16[4,8,3072]{2,1,0:T(8,128)(2,1)S(1)}, u32[]{:S(2)}, u32[]{:S(2)}) async-start(bf16[4,8,3072]{2,1,0:T(8,128)(2,1)} %fusion.10), calls=%async_computation.1 | async-start | bytes 393216 | tf_op jit(solution)/shard_map/all_to_all | solution.py:37
  13.4 0.8 mul.84
  14.1 1.9 fusion.9
  16.0 2.6 all-to-all-done.1
  18.7 3.4 %all-to-all-start = ((bf16[4,8,3072]{2,1,0:T(8,128)(2,1)}), bf16[4,8,3072]{2,1,0:T(8,128)(2,1)S(1)}, u32[]{:S(2)}, u32[]{:S(2)}) async-start(bf16[4,8,3072]{2,1,0:T(8,128)(2,1)} %fusion.9), calls=%async_computation | async-start | bytes 393216 | tf_op jit(solution)/shard_map/all_to_all | solution.py:38
  22.1 0.0 reduce-scatter.3.cloned.1.call-start
  22.1 4.0 %fusion.2 = f32[32,1024]{1,0:T(8,128)S(1)} fusion(bf16[1,3072,1024]{2,1,0:T(8,128)(2,1)} %param.10, bf16[4,8,3072]{2,1,0:T(8,128)(2,1)S(1)} %all-to-all-done.1), kind=kOutput, calls=%fused_computation.3 | convolution fusion | flops 201326592 | bytes 6619136 | tf_op jit(solution)/shard_map/dot_general | solution.py:41
  26.1 1.3 all-to-all-done
  27.4 0.0 copy-done.1
  27.4 4.0 %fusion.18 = bf16[32,1024]{1,0:T(8,128)(2,1)S(1)} fusion(bf16[1,3072,1024]{2,1,0:T(8,128)(2,1)} %param.11, bf16[4,8,3072]{2,1,0:T(8,128)(2,1)S(1)} %all-to-all-done, f32[4,8]{1,0:T(4,128)S(1)} %bitcast.57, f32[32,1024]{1,0:T(8,128)S(1)} %fusion.2), kind=kOutput, calls=%fused_computation.20 | convolution fusion | flops 202244096 | bytes 6684800 | tf_op jit(solution)/shard_map/dot_general | solution.py:44
  31.4 5.4 %fusion.11 = bf16[3072,32]{0,1:T(8,128)(2,1)} fusion(bf16[32,1024]{1,0:T(8,128)(2,1)S(1)} %fusion.18, bf16[1,3072,1024]{2,1,0:T(8,128)(2,1)} %param.10), kind=kOutput, calls=%fused_computation.14 | convolution fusion | flops 201424896 | bytes 6553600 | tf_op jit(solution)/shard_map/dot_general | solution.py:58
  36.8 0.0 reduce-scatter.3.cloned.1.call-update
  36.8 0.0 reduce-scatter.5.cloned.1.call-start
  36.9 1.8 convolution_convert_fusion.1
  38.7 1.9 convolution_convert_fusion
  40.6 5.9 %pad_maximum_fusion = bf16[3072,2048]{0,1:T(8,128)(2,1)} fusion(bf16[3072,1024]{0,1:T(8,128)(2,1)S(1)} %convolution_convert_fusion, bf16[3072,1024]{0,1:T(8,128)(2,1)S(1)} %convolution_convert_fusion.1), kind=kLoop, calls=%fused_computation | loop fusion | flops 25165824 | bytes 25165824 | tf_op jit(solution)/shard_map/concatenate | solution.py:50
  46.5 0.0 reduce-scatter.5.cloned.1.call-update
  46.5 2.4 reduce-scatter.3.cloned.1.call-done
  48.9 7.6 %all_to_all.33 = bf16[1536,4,8]{0,2,1:T(8,128)(2,1)S(1)} all-to-all(bf16[1536,4,8]{0,2,1:T(8,128)(2,1)} %bitcast.56), channel_id=1, replica_groups=mesh['dp'=4,'expert'=4,'hidden'=2] {'expert'}, dimensions={1} | all-to-all | bytes 196608 | tf_op jit(solution)/shard_map/all_to_all | solution.py:65
  56.5 1.0 fusion.14
  57.5 205.7 %reduce-scatter.5.cloned.1.call-done = bf16[768,2048]{0,1:T(8,128)(2,1)} async-done(((bf16[3072,2048]{0,1:T(8,128)(2,1)}), bf16[768,2048]{0,1:T(8,128)(2,1)}) %reduce-scatter.5.cloned.1.call-update) | async-done | bytes 3145744 | tf_op jit(solution)/shard_map/reduce_scatter | solution.py:49
  263.1 2.4 convert_element_type.56
  265.5 2.1 slice_bitcast_fusion
  267.6 3.5 %copy.10 = f32[1,768,1024]{2,1,0:T(8,128)} copy(f32[1,768,1024]{1,2,0:T(8,128)} %get-tuple-element.6) | data formatting | bytes 6291456
  271.1 2.4 copy.9
Async XLA Ops:
  7.2 1.0 copy-start
  7.2 20.2 %copy-start.1 = (f32[1,1,4,8]{3,2,1,0:T(4,128)S(1)}, f32[1,1,4,8]{3,2,1,0:T(4,128)}, u32[]{:S(2)}) copy-start(f32[1,1,4,8]{3,2,1,0:T(4,128)} %param.9) | copy-start | bytes 388
  9.1 9.6 %all-to-all-start.1 = ((bf16[4,8,3072]{2,1,0:T(8,128)(2,1)}), bf16[4,8,3072]{2,1,0:T(8,128)(2,1)S(1)}, u32[]{:S(2)}, u32[]{:S(2)}) async-start(bf16[4,8,3072]{2,1,0:T(8,128)(2,1)} %fusion.10), calls=%async_computation.1 | async-start | bytes 393216 | tf_op jit(solution)/shard_map/all_to_all | solution.py:37
  18.7 8.7 %all-to-all-start = ((bf16[4,8,3072]{2,1,0:T(8,128)(2,1)}), bf16[4,8,3072]{2,1,0:T(8,128)(2,1)S(1)}, u32[]{:S(2)}, u32[]{:S(2)}) async-start(bf16[4,8,3072]{2,1,0:T(8,128)(2,1)} %fusion.9), calls=%async_computation | async-start | bytes 393216 | tf_op jit(solution)/shard_map/all_to_all | solution.py:38
  22.1 26.9 %reduce-scatter.3.cloned.1.call-start = ((), (), s32[]{:S(2)}) async-start(), calls=%async_computation.5 | async-start | bytes 294912 | tf_op jit(solution)/shard_map/reduce_scatter | solution.py:57
  36.8 226.3 %reduce-scatter.5.cloned.1.call-start = ((), (), s32[]{:S(2)}) async-start(), calls=%async_computation.6 | async-start | bytes 15728640 | tf_op jit(solution)/shard_map/reduce_scatter | solution.py:49
Sparse Core Ops, SparseCore 0:
  37.0 11.9 reduce-scatter.2
  51.3 211.8 reduce-scatter.4
where the time goes:
time: 281 us; the launch traced here: 280 us
  waiting for transfers between devices  212 us (75%)
  matrix products  21 us (7%)
  between operations  14.1 us (5%)
  local copies, waits for them, and re-layouts  9.73 us (3%)
  other arithmetic  8.27 us (3%)
  starting transfers between devices  7.69 us (3%)
  blocking collectives  7.57 us (3%)
    reduce_scatter x1, waiting for transfers between devices, local(): lax.psum_scatter(jnp.concatenate([term_up, term_down], axis=1).astype(jnp...  206 us
    all_to_all x1, blocking collectives, local(): lax.all_to_all(column_sums, 'expert', split_axis=1, concat_axis=1, tiled=...  7.57 us
    unnamed x6, local copies, waits for them, and re-layouts  6.09 us
    concatenate x1, other arithmetic, local(): jnp.concatenate([term_up, term_down], axis=1).astype(jnp.bfloat16)  5.9 us
  transfers between devices with their start and end apart: 4, of which 4 were waited for; matrix products, arithmetic and copies ran while one was open for 6% of the time, Pallas kernels for 0%

commit v1 on v0

v1 whole, which is shorter than its diff:
```python
import functools

import jax
import jax.numpy as jnp
from jax import lax
from jax.experimental import pallas as pl
from jax.experimental.pallas import tpu as pltpu
from jax.sharding import PartitionSpec as P

ROOT_TERM = 0.7978845608028654
CUBIC_TERM = 0.044715


def gelu_pair(pre):
    square = pre * pre
    inner = jnp.tanh(ROOT_TERM * (pre + CUBIC_TERM * square * pre))
    value = 0.5 * pre * (1.0 + inner)
    slope = 0.5 * (1.0 + inner) + 0.5 * pre * (1.0 - inner * inner) * ROOT_TERM * (
        1.0 + 3.0 * CUBIC_TERM * square
    )
    return value, slope


def hop(x, axis, step):
    n = lax.axis_size(axis)
    if step % n == 0:
        return x
    return lax.ppermute(x, axis, [(i, (i + step) % n) for i in range(n)])


def column(ref, order):
    n = ref.shape[-1]
    down = lax.broadcasted_iota(jnp.int32, (n, n), 0)
    along = lax.broadcasted_iota(jnp.int32, (n, n), 1)
    out = []
    for at in order:
        row = ref[0, 0, pl.ds(at, 1), :].astype(jnp.float32)
        out.append(jnp.sum(jnp.where(down == along, row, 0.0), axis=1, keepdims=True))
    return jnp.concatenate(out, axis=0)


def pick_kernel(n_dp, picks_hbm, tokens_hbm, upstream_hbm, rows_ref, *refs):
    *side_refs, picks_ref, tokens_ref, upstream_ref, sems = refs
    n_exp, n_pick = picks_ref.shape[2:]
    tok_dev, width = tokens_ref.shape[1:]
    cols = width // n_dp
    copies = [
        pltpu.make_async_copy(picks_hbm, picks_ref, sems.at[0]),
        pltpu.make_async_copy(tokens_hbm, tokens_ref, sems.at[1]),
        pltpu.make_async_copy(upstream_hbm, upstream_ref, sems.at[2]),
    ]
    for copy in copies:
        copy.start()
    me = lax.axis_index("expert")
    my_dp = lax.axis_index("dp")
    copies[0].wait()
    wanted = column(picks_ref, [(me + s) % n_exp for s in range(n_exp)])
    spots = lax.broadcasted_iota(jnp.int32, (n_exp * n_pick, tok_dev), 1)
    selector = jnp.where(wanted.astype(jnp.int32) == spots, 1.0, 0.0).astype(jnp.bfloat16)
    for at, copy, source in ((0, copies[1], tokens_ref), (width, copies[2], upstream_ref)):
        copy.wait()
        rows_ref[:, at : at + width] = jnp.dot(
            selector, source[0], preferred_element_type=jnp.float32
        ).astype(jnp.bfloat16)
    for s in range(1, n_dp):
        start = ((my_dp + s) % n_dp) * cols
        for half in range(2):
            side_refs[s - 1][:, half * cols : (half + 1) * cols] = rows_ref[
                :, pl.ds(pl.multiple_of(half * width + start, 128), cols)
            ]


def load_kernel(after_ref, gates_hbm, upper_hbm, lower_hbm, gates_ref, upper_ref, lower_ref, sems):
    copies = [
        pltpu.make_async_copy(source, target, sems.at[k])
        for k, (source, target) in enumerate(
            ((gates_hbm, gates_ref), (upper_hbm, upper_ref), (lower_hbm, lower_ref))
        )
    ]
    for copy in copies:
        copy.start()
    for copy in copies:
        copy.wait()


def factor_kernel(gates_ref, rows_ref, upper_ref, lower_ref, out_ref):
    n_exp = gates_ref.shape[2]
    width, units = upper_ref.shape[1:]
    me = lax.axis_index("expert")
    gate = column(gates_ref, [(me + n_exp - s) % n_exp for s in range(n_exp)])
    pre = jnp.dot(rows_ref[:, :width], upper_ref[0], preferred_element_type=jnp.float32)
    back = jnp.dot(rows_ref[:, width:], lower_ref[0], preferred_element_type=jnp.float32)
    value, slope = gelu_pair(pre)
    out_ref[:, :units] = (back * gate * slope).astype(jnp.bfloat16)
    out_ref[:, units:] = (value * gate).astype(jnp.bfloat16)


def piece_kernel(n_hid, factor_ref, upper_ref, out_ref):
    n_pick, part = out_ref.shape[1:]
    width, units = upper_ref.shape[1:]
    n_exp = out_ref.shape[0] // n_hid
    me = lax.axis_index("expert")
    piece = lax.dot_general(
        factor_ref[:, :units], upper_ref[0], (((1,), (1,)), ((), ())), preferred_element_type=jnp.float32
    )
    for s in range(n_exp):
        owner = ((me + n_exp - s) % n_exp) * n_hid
        for h in range(n_hid):
            out_ref[owner + h] = piece[
                s * n_pick : (s + 1) * n_pick, h * part : (h + 1) * part
            ].astype(jnp.bfloat16)


def weight_kernel(chunks, side_ref, factor_ref, up_ref, down_ref, held, sems):
    units = factor_ref.shape[1] // 2
    cols = side_ref.shape[1] // 2
    step = units // chunks
    copies = []
    for which, out in ((0, up_ref), (1, down_ref)):
        for c in range(chunks):
            spot = pl.ds(c * step, step)
            held[which, :, spot] = lax.dot_general(
                side_ref[:, which * cols : (which + 1) * cols],
                factor_ref[:, pl.ds(which * units + c * step, step)],
                (((0,), (0,)), ((), ())),
                preferred_element_type=jnp.float32,
            )
            copy = pltpu.make_async_copy(
                held.at[which, :, spot], out.at[0, :, spot], sems.at[which, c]
            )
            copy.start()
            copies.append(copy)
    for copy in copies:
        copy.wait()


VMEM = pl.BlockSpec(memory_space=pltpu.VMEM)
HBM = pl.BlockSpec(memory_space=pltpu.HBM)
ROOM = pltpu.CompilerParams(vmem_limit_bytes=16 << 20)


def local(layer_input, grad_out, picks, gates, w_up, w_down):
    tok_dev, width = layer_input.shape[1:]
    n_exp, n_pick = picks.shape[2:]
    slots = n_exp * n_pick
    units = w_up.shape[2]
    n_dp = lax.axis_size("dp")
    n_hid = lax.axis_size("hidden")
    cols = width // n_dp
    part = width // n_hid
    bf16 = jnp.bfloat16
    layer_input, grad_out, w_up, w_down = (
        pltpu.with_memory_space_constraint(x, pltpu.HBM)
        for x in (layer_input, grad_out, w_up, w_down)
    )

    send, *side = pl.pallas_call(
        functools.partial(pick_kernel, n_dp),
        out_shape=[jax.ShapeDtypeStruct((slots, 2 * width), bf16)]
        + [jax.ShapeDtypeStruct((slots, 2 * cols), bf16)] * (n_dp - 1),
        in_specs=[HBM] * 3,
        out_specs=[VMEM] * n_dp,
        scratch_shapes=[
            pltpu.VMEM(picks.shape, jnp.int32),
            pltpu.VMEM(layer_input.shape, bf16),
            pltpu.VMEM(grad_out.shape, bf16),
            pltpu.SemaphoreType.DMA((3,)),
        ],
        compiler_params=ROOM,
        name="pick",
    )(picks, layer_input, grad_out)

    rows = jnp.concatenate(
        [hop(send[s * n_pick : (s + 1) * n_pick], "expert", s) for s in range(n_exp)], axis=0
    )
    side = [hop(x, "dp", s + 1).reshape(n_exp, n_pick, 2 * cols) for s, x in enumerate(side)]
    side = jnp.stack(side)
    side = [hop(side[:, s], "expert", s) for s in range(n_exp)]
    side = jnp.stack(side, axis=1).reshape((n_dp - 1) * slots, 2 * cols)
    at = lax.axis_index("dp") * cols
    own = jnp.concatenate(
        [
            lax.dynamic_slice_in_dim(rows, at, cols, 1),
            lax.dynamic_slice_in_dim(rows, width + at, cols, 1),
        ],
        axis=1,
    )
    side = jnp.concatenate([own, side], axis=0)

    gate_held, upper, lower = pl.pallas_call(
        load_kernel,
        out_shape=[jax.ShapeDtypeStruct(x.shape, x.dtype) for x in (gates, w_up, w_down)],
        in_specs=[HBM] * 4,
        out_specs=[VMEM] * 3,
        scratch_shapes=[pltpu.SemaphoreType.DMA((3,))],
        cost_estimate=pl.CostEstimate(
            flops=0, bytes_accessed=4 * w_up.size + 4 * w_down.size, transcendentals=0
        ),
        compiler_params=ROOM,
        name="load",
    )(send, gates, w_up, w_down)
    factors = pl.pallas_call(
        factor_kernel,
        out_shape=jax.ShapeDtypeStruct((slots, 2 * units), bf16),
        in_specs=[VMEM] * 4,
        out_specs=VMEM,
        compiler_params=ROOM,
        name="factor",
    )(gate_held, rows, upper, lower)

    gathered = jnp.concatenate([hop(factors, "dp", s) for s in range(n_dp)], axis=0)

    piece = pl.pallas_call(
        functools.partial(piece_kernel, n_hid),
        out_shape=jax.ShapeDtypeStruct((n_exp * n_hid, n_pick, part), bf16),
        in_specs=[VMEM, VMEM],
        out_specs=VMEM,
        compiler_params=ROOM,
        name="piece",
    )(factors, upper)
    returned = lax.all_to_all(piece, ("expert", "hidden"), 0, 0)
    twice = jnp.broadcast_to(picks[0, 0][:, None, :], (n_exp, n_hid, n_pick)).reshape(slots * n_hid)
    spread = (jnp.arange(tok_dev, dtype=jnp.int32)[:, None] == twice[None, :]).astype(bf16)
    grad_rows = jnp.dot(
        spread, returned.reshape(slots * n_hid, part), preferred_element_type=jnp.float32
    )

    chunks = max(1, units // 256)
    grads = pl.pallas_call(
        functools.partial(weight_kernel, chunks),
        out_shape=[jax.ShapeDtypeStruct((1, cols, units), jnp.float32)] * 2,
        in_specs=[VMEM, VMEM],
        out_specs=[HBM] * 2,
        scratch_shapes=[
            pltpu.VMEM((2, cols, units), jnp.float32),
            pltpu.SemaphoreType.DMA((2, chunks)),
        ],
        compiler_params=ROOM,
        name="weight",
    )(side, gathered)
    return (grad_rows.astype(bf16)[None], *grads)


def solution(mesh):
    placed = (
        P("dp", "expert", None),
        P("dp", "expert", None),
        P("dp", "expert", None, None),
        P("dp", "expert", None, None),
        P("expert", None, "hidden"),
        P("expert", None, "hidden"),
    )
    return jax.shard_map(
        local,
        mesh=mesh,
        in_specs=placed,
        out_specs=(
            P("dp", "expert", "hidden"),
            P("expert", "dp", "hidden"),
            P("expert", "dp", "hidden"),
        ),
        check_vma=False,
    )
```

time: 281 us -> 45 us (0.16)
  waiting for transfers between devices: 212 us -> 7.6 us
  matrix products: 21 us -> 0.87 us
  Pallas kernels: 0 us -> 14.1 us
  between operations: 14.1 us -> 0.81 us
  starting transfers between devices: 7.69 us -> 19 us
  other arithmetic: 8.27 us -> 0.16 us
  blocking collectives: 7.57 us -> 0 us
  local copies, waits for them, and re-layouts: 9.73 us -> 2.19 us
    reduce_scatter x2 -> x0, waiting for transfers between devices: 208 us -> none  [the longest x1 206 us: local(): lax.psum_scatter(jnp.concatenate([term_up, term_down], axis=1).astype(jnp...]
    dot_general x8 -> x1, matrix products: 21 us -> 0.87 us  [local(): jnp.dot(spread, returned.reshape(slots * n_hid, part), preferred_element_...]
    ppermute x0 -> x12, starting transfers between devices: none -> 15.2 us  [hop(): return lax.ppermute(x, axis, [(i, (i + step) % n) for i in range(n)])]
    pallas_call x0 -> x5, Pallas kernels: none -> 14.1 us  [the longest x1 4.63 us: local(): pl.pallas_call(load_kernel, out_shape=[jax.ShapeDtypeStruct(x.shape, x.dt...]
    ppermute x0 -> x12, waiting for transfers between devices: none -> 7.6 us  [hop(): return lax.ppermute(x, axis, [(i, (i + step) % n) for i in range(n)])]
    all_to_all x1 -> x0, blocking collectives: 7.57 us -> none  [local(): lax.all_to_all(column_sums, 'expert', split_axis=1, concat_axis=1, tiled=...]
    concatenate x1 -> x3, other arithmetic: 5.9 us -> 0.09 us  [the longest x1 0.03 us: local(): jnp.concatenate([hop(factors, 'dp', s) for s in range(n_dp)], axis=0)]
    unnamed x6 -> x4, local copies, waits for them, and re-layouts: 6.09 us -> 1.36 us
  transfers between devices with their start and end apart: 4 -> 13, of which waited for: 4 -> 1; matrix products, arithmetic and copies ran while one was open for 6% -> 2% of each run, Pallas kernels for 0% -> 28%
where the time goes in v1:
time: 45 us; the launch traced here: 44.7 us
  starting transfers between devices  19 us (42%)
  Pallas kernels  14.1 us (31%)
  waiting for transfers between devices  7.6 us (17%)
  local copies, waits for them, and re-layouts  2.19 us (5%)
  matrix products  0.87 us (2%)
  between operations  0.81 us (2%)
    ppermute x12, starting transfers between devices, hop(): return lax.ppermute(x, axis, [(i, (i + step) % n) for i in range(n)])  15.2 us
    ppermute x12, waiting for transfers between devices, hop(): return lax.ppermute(x, axis, [(i, (i + step) % n) for i in range(n)])  7.6 us
    pallas_call x1, Pallas kernels, local(): pl.pallas_call(load_kernel, out_shape=[jax.ShapeDtypeStruct(x.shape, x.dt...  4.63 us
    all_to_all x1, starting transfers between devices, local(): returned = lax.all_to_all(piece, ('expert', 'hidden'), 0, 0)  3.72 us
    pallas_call x1, Pallas kernels, local(): pl.pallas_call(functools.partial(weight_kernel, chunks), out_shape=[jax.S...  3.14 us
    pallas_call x1, Pallas kernels, local(): pl.pallas_call(functools.partial(piece_kernel, n_hid), out_shape=jax.Shap...  2.63 us
    pallas_call x1, Pallas kernels, local(): pl.pallas_call(factor_kernel, out_shape=jax.ShapeDtypeStruct((slots, 2 *...  2.27 us
    pallas_call x1, Pallas kernels, local(): pl.pallas_call(functools.partial(pick_kernel, n_dp), out_shape=[jax.Shape...  1.43 us
  transfers between devices with their start and end apart: 13, of which 1 were waited for; matrix products, arithmetic and copies ran while one was open for 2% of the time, Pallas kernels for 28%

profile of v1, /device:TPU:0, one launch (start us, length us, event | category | flops | bytes accessed | tf_op | source)
XLA Modules:
  0.0 44.7 jit_solution(13627291310438698242)
XLA Ops:
  0.6 0.0 copy-start
  0.6 0.7 %copy-done = s32[1,1,4,8]{3,2,1,0:T(4,128)S(1)} copy-done((s32[1,1,4,8]{3,2,1,0:T(4,128)S(1)}, s32[1,1,4,8]{3,2,1,0:T(4,128)}, u32[]{:S(2)}) %copy-start) | copy-done | bytes 152
  1.3 1.4 %pick.1 = (bf16[32,6144]{1,0:T(8,128)(2,1)S(1)}, bf16[32,1536]{1,0:T(8,128)(2,1)S(1)}, bf16[32,1536]{1,0:T(8,128)(2,1)S(1)}, bf16[32,1536]{1,0:T(8,128)(2,1)S(1)}) custom-call(s32[1,1,4,8]{3,2,1,0:T(4,128)S(1)} %copy-done, bf16[1,64,3072]{2,1,0:T(8,128)(2,1)} %tokens_hbm.1, bf16[1,64,3072]{2,1,0:T(8,128)(2,1)} %upstream_hbm.1), custom_call_target="tpu_custom_call" | custom-call | tf_op jit(solution)/shard_map/pick/pallas_call | solution.py:157
  2.8 0.5 %collective-permute-start = (bf16[8,6144]{1,0:T(8,128)(2,1)S(1)}, bf16[8,6144]{1,0:T(8,128)(2,1)S(1)}, u32[]{:S(2)}, u32[]{:S(2)}) collective-permute-start(bf16[8,6144]{1,0:T(8,128)(2,1)S(1)} %get-tuple-element.26), channel_id=1, source_target_pairs={{0,2},{2,4},{4,6},{6,0},{1,3},{3,5},{5,7},{7,1},{8,10},{10,12},{12... | collective-permute-start | bytes 294920 | tf_op jit(solution)/shard_map/ppermute | solution.py:28
  3.3 2.6 %collective-permute-start.1 = (bf16[8,6144]{1,0:T(8,128)(2,1)S(1)}, bf16[8,6144]{1,0:T(8,128)(2,1)S(1)}, u32[]{:S(2)}, u32[]{:S(2)}) collective-permute-start(bf16[8,6144]{1,0:T(8,128)(2,1)S(1)} %get-tuple-element.25), channel_id=1, source_target_pairs={{0,4},{2,6},{4,0},{6,2},{1,5},{3,7},{5,1},{7,3},{8,12},{10,14},{12... | collective-permute-start | bytes 294920 | tf_op jit(solution)/shard_map/ppermute | solution.py:28
  5.9 1.4 %collective-permute-start.2 = (bf16[8,6144]{1,0:T(8,128)(2,1)S(1)}, bf16[8,6144]{1,0:T(8,128)(2,1)S(1)}, u32[]{:S(2)}, u32[]{:S(2)}) collective-permute-start(bf16[8,6144]{1,0:T(8,128)(2,1)S(1)} %get-tuple-element.24), channel_id=1, source_target_pairs={{0,6},{2,0},{4,2},{6,4},{1,7},{3,1},{5,3},{7,5},{8,14},{10,8},{12,... | collective-permute-start | bytes 294920 | tf_op jit(solution)/shard_map/ppermute | solution.py:28
  7.3 1.6 %collective-permute-start.3 = (bf16[32,1536]{1,0:T(8,128)(2,1)S(1)}, bf16[32,1536]{1,0:T(8,128)(2,1)S(1)}, u32[]{:S(2)}, u32[]{:S(2)}) collective-permute-start(bf16[32,1536]{1,0:T(8,128)(2,1)S(1)} %get-tuple-element.16), channel_id=1, source_target_pairs={{0,8},{8,16},{16,24},{24,0},{1,9},{9,17},{17,25},{25,1},{2,10},{10... | collective-permute-start | bytes 294920 | tf_op jit(solution)/shard_map/ppermute | solution.py:28
  8.9 2.6 %collective-permute-start.4 = (bf16[32,1536]{1,0:T(8,128)(2,1)S(1)}, bf16[32,1536]{1,0:T(8,128)(2,1)S(1)}, u32[]{:S(2)}, u32[]{:S(2)}) collective-permute-start(bf16[32,1536]{1,0:T(8,128)(2,1)S(1)} %get-tuple-element.17), channel_id=1, source_target_pairs={{0,16},{8,24},{16,0},{24,8},{1,17},{9,25},{17,1},{25,9},{2,18},{10... | collective-permute-start | bytes 294920 | tf_op jit(solution)/shard_map/ppermute | solution.py:28
  11.4 0.7 %broadcast_in_dim.12 = s32[4,2,8]{2,1,0:T(2,128)S(1)} broadcast(s32[4,8]{1,0:T(4,128)} %bitcast.31), dimensions={0,2} | broadcast | bytes 384 | tf_op jit(solution)/shard_map/broadcast_in_dim | solution.py:222
  12.1 0.1 eq.16
  12.2 0.7 %copy-done.1 = f32[1,1,4,8]{3,2,1,0:T(4,128)S(1)} copy-done((f32[1,1,4,8]{3,2,1,0:T(4,128)S(1)}, f32[1,1,4,8]{3,2,1,0:T(4,128)}, u32[]{:S(2)}) %copy-start.1) | copy-done | bytes 152
  12.9 4.6 %load.1 = (f32[1,1,4,8]{3,2,1,0:T(4,128)S(1)}, bf16[1,3072,1024]{2,1,0:T(8,128)(2,1)S(1)}, bf16[1,3072,1024]{2,1,0:T(8,128)(2,1)S(1)}) custom-call(bf16[32,6144]{1,0:T(8,128)(2,1)S(1)} %get-tuple-element.12.after_ref, f32[1,1,4,8]{3,2,1,0:T(4,128)S(1)} %copy-done.1, bf16[1,3072,1024]{2,1,0:T(8,128)(2,1)} %upper_hbm.1, bf16[1,3072,1024]{2,1,0:T(8,128)(2,1)} %lower_hbm.1), custom_call_target="tpu_custom_call" | custom-call | bytes 25165824 | tf_op jit(solution)/shard_map/load/pallas_call | solution.py:190
  17.5 0.0 collective-permute-done
  17.5 1.4 %collective-permute-start.5 = (bf16[32,1536]{1,0:T(8,128)(2,1)S(1)}, bf16[32,1536]{1,0:T(8,128)(2,1)S(1)}, u32[]{:S(2)}, u32[]{:S(2)}) collective-permute-start(bf16[32,1536]{1,0:T(8,128)(2,1)S(1)} %get-tuple-element.18), channel_id=1, source_target_pairs={{0,24},{8,0},{16,8},{24,16},{1,25},{9,1},{17,9},{25,17},{2,26},{10... | collective-permute-start | bytes 294920 | tf_op jit(solution)/shard_map/ppermute | solution.py:28
  18.9 0.0 collective-permute-done.1
  19.0 2.3 %factor.1.factor_ref = bf16[32,2048]{1,0:T(8,128)(2,1)S(1)} custom-call(f32[1,1,4,8]{3,2,1,0:T(4,128)S(1)} %get-tuple-element.13.gates_ref, bf16[32,6144]{1,0:T(8,128)(2,1)S(1)} %pad_maximum_fusion.1.rows_ref, bf16[1,3072,1024]{2,1,0:T(8,128)(2,1)S(1)} %get-tuple-element.14.upper_ref, bf16[1,3072,1024]{2,1,0:T(8,128)(2,1)S(1)} %get-tuple-element.15.lower_ref), custom_call_target="tpu_custom_call" | custom-call | tf_op jit(solution)/shard_map/factor/pallas_call | solution.py:202
  21.3 0.4 collective-permute-start.10
  21.7 2.7 %collective-permute-start.11 = (bf16[32,2048]{1,0:T(8,128)(2,1)S(1)}, bf16[32,2048]{1,0:T(8,128)(2,1)S(1)}, u32[]{:S(2)}, u32[]{:S(2)}) collective-permute-start(bf16[32,2048]{1,0:T(8,128)(2,1)S(1)} %factor.1.factor_ref), channel_id=1, source_target_pairs={{0,24},{8,0},{16,8},{24,16},{1,25},{9,1},{17,9},{25,17},{2,26},{10... | collective-permute-start | bytes 393224 | tf_op jit(solution)/shard_map/ppermute | solution.py:28
  24.4 2.6 %piece.1 = bf16[8,8,1536]{2,1,0:T(8,128)(2,1)} custom-call(bf16[32,2048]{1,0:T(8,128)(2,1)S(1)} %factor.1.factor_ref, bf16[1,3072,1024]{2,1,0:T(8,128)(2,1)S(1)} %get-tuple-element.14.upper_ref), custom_call_target="tpu_custom_call" | custom-call | tf_op jit(solution)/shard_map/piece/pallas_call | solution.py:213
  27.0 0.0 collective-permute-done.3
  27.0 0.0 collective-permute-done.4
  27.0 0.0 collective-permute-done.5
  27.1 0.1 collective-permute-start.6
  27.1 0.6 %collective-permute-start.7 = (bf16[3,8,1536]{2,1,0:T(8,128)(2,1)S(1)}, bf16[3,8,1536]{2,1,0:T(8,128)(2,1)S(1)}, u32[]{:S(2)}, u32[]{:S(2)}) collective-permute-start(bf16[3,8,1536]{2,1,0:T(8,128)(2,1)S(1)} %get-tuple-element.29), channel_id=1, source_target_pairs={{0,4},{2,6},{4,0},{6,2},{1,5},{3,7},{5,1},{7,3},{8,12},{10,14},{12... | collective-permute-start | bytes 221192 | tf_op jit(solution)/shard_map/ppermute | solution.py:28
  27.7 1.4 %collective-permute-start.8 = (bf16[3,8,1536]{2,1,0:T(8,128)(2,1)S(1)}, bf16[3,8,1536]{2,1,0:T(8,128)(2,1)S(1)}, u32[]{:S(2)}, u32[]{:S(2)}) collective-permute-start(bf16[3,8,1536]{2,1,0:T(8,128)(2,1)S(1)} %get-tuple-element.28), channel_id=1, source_target_pairs={{0,6},{2,0},{4,2},{6,4},{1,7},{3,1},{5,3},{7,5},{8,14},{10,8},{12,... | collective-permute-start | bytes 221192 | tf_op jit(solution)/shard_map/ppermute | solution.py:28
  29.1 3.7 %all-to-all-start = ((bf16[8,8,1536]{2,1,0:T(8,128)(2,1)}), bf16[8,8,1536]{2,1,0:T(8,128)(2,1)S(1)}, u32[]{:S(2)}, u32[]{:S(2)}) async-start(bf16[8,8,1536]{2,1,0:T(8,128)(2,1)} %piece.1), calls=%async_computation | async-start | bytes 393216 | tf_op jit(solution)/shard_map/all_to_all | solution.py:221
  32.9 0.1 collective-permute-start.9
  32.9 0.0 collective-permute-done.8
  33.0 7.6 %collective-permute-done.9 = bf16[32,2048]{1,0:T(8,128)(2,1)S(1)} collective-permute-done((bf16[32,2048]{1,0:T(8,128)(2,1)S(1)}, bf16[32,2048]{1,0:T(8,128)(2,1)S(1)}, u32[]{:S(2)}, u32[]{:S(2)}) %collective-permute-start.9) | collective-permute-done | bytes 131104 | tf_op jit(solution)/shard_map/ppermute | solution.py:28
  40.6 3.1 %weight.1 = (f32[1,768,1024]{2,1,0:T(8,128)}, f32[1,768,1024]{2,1,0:T(8,128)}) custom-call(bf16[128,1536]{1,0:T(8,128)(2,1)S(1)} %pad_maximum_fusion.2.side_ref, bf16[128,2048]{1,0:T(8,128)(2,1)S(1)} %pad_maximum_fusion.factor_ref), custom_call_target="tpu_custom_call" | custom-call | tf_op jit(solution)/shard_map/weight/pallas_call | solution.py:229
  43.8 0.0 all-to-all-done
  43.8 0.9 %fusion = bf16[1,64,1536]{2,1,0:T(8,128)(2,1)} fusion(bf16[8,8,1536]{2,1,0:T(8,128)(2,1)S(1)} %all-to-all-done, s32[64]{0:T(128)S(1)} %eq.16), kind=kOutput, calls=%fused_computation.1 | convolution fusion | flops 12685312 | bytes 393472 | tf_op jit(solution)/shard_map/dot_general | solution.py:224
  (14 shorter events, 0.2 us)
Async XLA Ops:
  0.6 0.7 %copy-start = (s32[1,1,4,8]{3,2,1,0:T(4,128)S(1)}, s32[1,1,4,8]{3,2,1,0:T(4,128)}, u32[]{:S(2)}) copy-start(s32[1,1,4,8]{3,2,1,0:T(4,128)} %picks_hbm.1) | copy-start | bytes 388
  2.8 14.8 %collective-permute-start = (bf16[8,6144]{1,0:T(8,128)(2,1)S(1)}, bf16[8,6144]{1,0:T(8,128)(2,1)S(1)}, u32[]{:S(2)}, u32[]{:S(2)}) collective-permute-start(bf16[8,6144]{1,0:T(8,128)(2,1)S(1)} %get-tuple-element.26), channel_id=1, source_target_pairs={{0,2},{2,4},{4,6},{6,0},{1,3},{3,5},{5,7},{7,1},{8,10},{10,12},{12... | collective-permute-start | bytes 294920 | tf_op jit(solution)/shard_map/ppermute | solution.py:28
  3.3 15.7 %collective-permute-start.1 = (bf16[8,6144]{1,0:T(8,128)(2,1)S(1)}, bf16[8,6144]{1,0:T(8,128)(2,1)S(1)}, u32[]{:S(2)}, u32[]{:S(2)}) collective-permute-start(bf16[8,6144]{1,0:T(8,128)(2,1)S(1)} %get-tuple-element.25), channel_id=1, source_target_pairs={{0,4},{2,6},{4,0},{6,2},{1,5},{3,7},{5,1},{7,3},{8,12},{10,14},{12... | collective-permute-start | bytes 294920 | tf_op jit(solution)/shard_map/ppermute | solution.py:28
  5.9 13.1 %collective-permute-start.2 = (bf16[8,6144]{1,0:T(8,128)(2,1)S(1)}, bf16[8,6144]{1,0:T(8,128)(2,1)S(1)}, u32[]{:S(2)}, u32[]{:S(2)}) collective-permute-start(bf16[8,6144]{1,0:T(8,128)(2,1)S(1)} %get-tuple-element.24), channel_id=1, source_target_pairs={{0,6},{2,0},{4,2},{6,4},{1,7},{3,1},{5,3},{7,5},{8,14},{10,8},{12,... | collective-permute-start | bytes 294920 | tf_op jit(solution)/shard_map/ppermute | solution.py:28
  7.3 19.7 %collective-permute-start.3 = (bf16[32,1536]{1,0:T(8,128)(2,1)S(1)}, bf16[32,1536]{1,0:T(8,128)(2,1)S(1)}, u32[]{:S(2)}, u32[]{:S(2)}) collective-permute-start(bf16[32,1536]{1,0:T(8,128)(2,1)S(1)} %get-tuple-element.16), channel_id=1, source_target_pairs={{0,8},{8,16},{16,24},{24,0},{1,9},{9,17},{17,25},{25,1},{2,10},{10... | collective-permute-start | bytes 294920 | tf_op jit(solution)/shard_map/ppermute | solution.py:28
  8.9 18.2 %collective-permute-start.4 = (bf16[32,1536]{1,0:T(8,128)(2,1)S(1)}, bf16[32,1536]{1,0:T(8,128)(2,1)S(1)}, u32[]{:S(2)}, u32[]{:S(2)}) collective-permute-start(bf16[32,1536]{1,0:T(8,128)(2,1)S(1)} %get-tuple-element.17), channel_id=1, source_target_pairs={{0,16},{8,24},{16,0},{24,8},{1,17},{9,25},{17,1},{25,9},{2,18},{10... | collective-permute-start | bytes 294920 | tf_op jit(solution)/shard_map/ppermute | solution.py:28
  12.2 0.7 %copy-start.1 = (f32[1,1,4,8]{3,2,1,0:T(4,128)S(1)}, f32[1,1,4,8]{3,2,1,0:T(4,128)}, u32[]{:S(2)}) copy-start(f32[1,1,4,8]{3,2,1,0:T(4,128)} %gates_hbm.1) | copy-start | bytes 388
  17.5 9.5 %collective-permute-start.5 = (bf16[32,1536]{1,0:T(8,128)(2,1)S(1)}, bf16[32,1536]{1,0:T(8,128)(2,1)S(1)}, u32[]{:S(2)}, u32[]{:S(2)}) collective-permute-start(bf16[32,1536]{1,0:T(8,128)(2,1)S(1)} %get-tuple-element.18), channel_id=1, source_target_pairs={{0,24},{8,0},{16,8},{24,16},{1,25},{9,1},{17,9},{25,17},{2,26},{10... | collective-permute-start | bytes 294920 | tf_op jit(solution)/shard_map/ppermute | solution.py:28
  21.3 11.8 %collective-permute-start.10 = (bf16[32,2048]{1,0:T(8,128)(2,1)S(1)}, bf16[32,2048]{1,0:T(8,128)(2,1)S(1)}, u32[]{:S(2)}, u32[]{:S(2)}) collective-permute-start(bf16[32,2048]{1,0:T(8,128)(2,1)S(1)} %factor.1.factor_ref), channel_id=1, source_target_pairs={{0,16},{8,24},{16,0},{24,8},{1,17},{9,25},{17,1},{25,9},{2,18},{10... | collective-permute-start | bytes 393224 | tf_op jit(solution)/shard_map/ppermute | solution.py:28
  21.7 11.4 %collective-permute-start.11 = (bf16[32,2048]{1,0:T(8,128)(2,1)S(1)}, bf16[32,2048]{1,0:T(8,128)(2,1)S(1)}, u32[]{:S(2)}, u32[]{:S(2)}) collective-permute-start(bf16[32,2048]{1,0:T(8,128)(2,1)S(1)} %factor.1.factor_ref), channel_id=1, source_target_pairs={{0,24},{8,0},{16,8},{24,16},{1,25},{9,1},{17,9},{25,17},{2,26},{10... | collective-permute-start | bytes 393224 | tf_op jit(solution)/shard_map/ppermute | solution.py:28
  27.1 5.8 %collective-permute-start.6 = (bf16[3,8,1536]{2,1,0:T(8,128)(2,1)S(1)}, bf16[3,8,1536]{2,1,0:T(8,128)(2,1)S(1)}, u32[]{:S(2)}, u32[]{:S(2)}) collective-permute-start(bf16[3,8,1536]{2,1,0:T(8,128)(2,1)S(1)} %get-tuple-element.30), channel_id=1, source_target_pairs={{0,2},{2,4},{4,6},{6,0},{1,3},{3,5},{5,7},{7,1},{8,10},{10,12},{12... | collective-permute-start | bytes 221192 | tf_op jit(solution)/shard_map/ppermute | solution.py:28
  27.1 5.8 %collective-permute-start.7 = (bf16[3,8,1536]{2,1,0:T(8,128)(2,1)S(1)}, bf16[3,8,1536]{2,1,0:T(8,128)(2,1)S(1)}, u32[]{:S(2)}, u32[]{:S(2)}) collective-permute-start(bf16[3,8,1536]{2,1,0:T(8,128)(2,1)S(1)} %get-tuple-element.29), channel_id=1, source_target_pairs={{0,4},{2,6},{4,0},{6,2},{1,5},{3,7},{5,1},{7,3},{8,12},{10,14},{12... | collective-permute-start | bytes 221192 | tf_op jit(solution)/shard_map/ppermute | solution.py:28
  27.7 5.2 %collective-permute-start.8 = (bf16[3,8,1536]{2,1,0:T(8,128)(2,1)S(1)}, bf16[3,8,1536]{2,1,0:T(8,128)(2,1)S(1)}, u32[]{:S(2)}, u32[]{:S(2)}) collective-permute-start(bf16[3,8,1536]{2,1,0:T(8,128)(2,1)S(1)} %get-tuple-element.28), channel_id=1, source_target_pairs={{0,6},{2,0},{4,2},{6,4},{1,7},{3,1},{5,3},{7,5},{8,14},{10,8},{12,... | collective-permute-start | bytes 221192 | tf_op jit(solution)/shard_map/ppermute | solution.py:28
  29.1 14.7 %all-to-all-start = ((bf16[8,8,1536]{2,1,0:T(8,128)(2,1)}), bf16[8,8,1536]{2,1,0:T(8,128)(2,1)S(1)}, u32[]{:S(2)}, u32[]{:S(2)}) async-start(bf16[8,8,1536]{2,1,0:T(8,128)(2,1)} %piece.1), calls=%async_computation | async-start | bytes 393216 | tf_op jit(solution)/shard_map/all_to_all | solution.py:221
  32.9 7.8 %collective-permute-start.9 = (bf16[32,2048]{1,0:T(8,128)(2,1)S(1)}, bf16[32,2048]{1,0:T(8,128)(2,1)S(1)}, u32[]{:S(2)}, u32[]{:S(2)}) collective-permute-start(bf16[32,2048]{1,0:T(8,128)(2,1)S(1)} %factor.1.factor_ref), channel_id=1, source_target_pairs={{0,8},{8,16},{16,24},{24,0},{1,9},{9,17},{17,25},{25,1},{2,10},{10... | collective-permute-start | bytes 393224 | tf_op jit(solution)/shard_map/ppermute | solution.py:28

commit v2 on v1

v2 whole, which is shorter than its diff:
```python
import functools

import jax
import jax.numpy as jnp
from jax import lax
from jax.experimental import pallas as pl
from jax.experimental.pallas import tpu as pltpu
from jax.sharding import PartitionSpec as P

ROOT_TERM = 0.7978845608028654
CUBIC_TERM = 0.044715


def gelu_pair(pre):
    square = pre * pre
    inner = jnp.tanh(ROOT_TERM * (pre + CUBIC_TERM * square * pre))
    value = 0.5 * pre * (1.0 + inner)
    slope = 0.5 * (1.0 + inner) + 0.5 * pre * (1.0 - inner * inner) * ROOT_TERM * (
        1.0 + 3.0 * CUBIC_TERM * square
    )
    return value, slope


def hop(x, axis, step):
    n = lax.axis_size(axis)
    if step % n == 0:
        return x
    return lax.ppermute(x, axis, [(i, (i + step) % n) for i in range(n)])


def column(ref, order):
    n = ref.shape[-1]
    down = lax.broadcasted_iota(jnp.int32, (n, n), 0)
    along = lax.broadcasted_iota(jnp.int32, (n, n), 1)
    out = []
    for at in order:
        row = ref[0, 0, pl.ds(at, 1), :].astype(jnp.float32)
        out.append(jnp.sum(jnp.where(down == along, row, 0.0), axis=1, keepdims=True))
    return jnp.concatenate(out, axis=0)


def pick_kernel(n_hid, n_share, picks_hbm, tokens_hbm, upstream_hbm, rows_ref, side_ref, spread_ref, *refs):
    picks_ref, tokens_ref, upstream_ref, sems = refs
    n_exp = picks_ref.shape[2]
    tok_dev, width = tokens_ref.shape[1:]
    copies = [
        pltpu.make_async_copy(picks_hbm, picks_ref, sems.at[0]),
        pltpu.make_async_copy(tokens_hbm, tokens_ref, sems.at[1]),
        pltpu.make_async_copy(upstream_hbm, upstream_ref, sems.at[2]),
    ]
    for copy in copies:
        copy.start()
    me = lax.axis_index("expert")
    copies[0].wait()

    def one_hot(order):
        wanted = column(picks_ref, order).astype(jnp.int32)
        spots = lax.broadcasted_iota(jnp.int32, (wanted.shape[0], tok_dev), 1)
        return jnp.where(wanted == spots, 1.0, 0.0).astype(jnp.bfloat16)

    selector = one_hot([(me + s) % n_exp for s in range(n_exp)])
    spread_ref[...] = one_hot([e for e in range(n_exp) for _ in range(n_hid)])
    for at, copy, source in ((0, copies[1], tokens_ref), (width, copies[2], upstream_ref)):
        copy.wait()
        rows_ref[:, at : at + width] = jnp.dot(
            selector, source[0], preferred_element_type=jnp.float32
        ).astype(jnp.bfloat16)
    blocks, n_pick, span = side_ref.shape
    n_dp = blocks // n_exp
    cols = width // n_dp
    if n_share == 1:
        starts = [0, width]
    else:
        per_half = n_share // 2
        share = lax.axis_index("hidden")
        starts = [(share // per_half) * width + (share % per_half) * span]
    for p in range(n_dp):
        for k, start in enumerate(starts):
            wide = span // len(starts)
            cut = rows_ref[:, pl.ds(pl.multiple_of(start + p * cols, 128), wide)].astype(jnp.float32)
            for s in range(n_exp):
                side_ref[p * n_exp + (me + s) % n_exp, :, k * wide : (k + 1) * wide] = cut[
                    s * n_pick : (s + 1) * n_pick
                ].astype(jnp.bfloat16)


def load_kernel(after_ref, source, target, sem):
    copy = pltpu.make_async_copy(source, target, sem)
    copy.start()
    copy.wait()


def factor_kernel(chunks, gates_hbm, rows_ref, upper_ref, lower_hbm, out_ref, gates_ref, lower_ref, gate_sem, sems):
    n_exp = gates_ref.shape[2]
    width, units = upper_ref.shape[1:]
    step = width // chunks
    gate_copy = pltpu.make_async_copy(gates_hbm, gates_ref, gate_sem)
    gate_copy.start()
    copies = []
    for c in range(chunks):
        spot = pl.ds(c * step, step)
        copies.append(pltpu.make_async_copy(lower_hbm.at[0, spot, :], lower_ref.at[spot, :], sems.at[c]))
        copies[-1].start()
    me = lax.axis_index("expert")
    pre = jnp.dot(rows_ref[:, :width], upper_ref[0], preferred_element_type=jnp.float32)
    value, slope = gelu_pair(pre)
    gate_copy.wait()
    gate = column(gates_ref, [(me + n_exp - s) % n_exp for s in range(n_exp)])
    out_ref[:, units:] = (value * gate).astype(jnp.bfloat16)
    slope = slope * gate
    back = jnp.zeros_like(pre)
    for c in range(chunks):
        copies[c].wait()
        back += jnp.dot(
            rows_ref[:, width + c * step : width + (c + 1) * step],
            lower_ref[c * step : (c + 1) * step, :],
            preferred_element_type=jnp.float32,
        )
    out_ref[:, :units] = (back * slope).astype(jnp.bfloat16)


def piece_kernel(n_hid, factor_ref, upper_ref, out_ref):
    n_pick, part = out_ref.shape[1:]
    width, units = upper_ref.shape[1:]
    n_exp = out_ref.shape[0] // n_hid
    me = lax.axis_index("expert")
    piece = lax.dot_general(
        factor_ref[:, :units], upper_ref[0], (((1,), (1,)), ((), ())), preferred_element_type=jnp.float32
    )
    for s in range(n_exp):
        owner = ((me + n_exp - s) % n_exp) * n_hid
        for h in range(n_hid):
            out_ref[owner + h] = piece[
                s * n_pick : (s + 1) * n_pick, h * part : (h + 1) * part
            ].astype(jnp.bfloat16)


def weight_kernel(chunks, n_dp, after_ref, *refs):
    *part_refs, factor_ref, up_ref, down_ref, side_ref, held, sems = refs
    n_share = len(part_refs)
    units = factor_ref.shape[1] // 2
    cols = side_ref.shape[1] // 2
    n_exp = part_refs[0].shape[0] // n_dp
    slots = side_ref.shape[0] // n_dp
    span = part_refs[0].shape[2]
    me = lax.axis_index("expert")
    my_dp = lax.axis_index("dp")
    my_hid = lax.axis_index("hidden")
    for t, part in enumerate(part_refs):
        at = 0 if n_share == 1 else pl.multiple_of(((my_hid + n_share - t) % n_share) * span, 128)
        for s in range(n_dp):
            first = ((my_dp + n_dp - s) % n_dp) * n_exp
            blocks = [part[first + (me + n_exp - b) % n_exp].astype(jnp.float32) for b in range(n_exp)]
            side_ref[s * slots : (s + 1) * slots, pl.ds(at, span)] = jnp.concatenate(blocks, axis=0).astype(
                jnp.bfloat16
            )
    step = units // chunks
    copies = []
    for which, out in ((0, up_ref), (1, down_ref)):
        for c in range(chunks):
            spot = pl.ds(c * step, step)
            held[which, :, spot] = lax.dot_general(
                side_ref[:, which * cols : (which + 1) * cols],
                factor_ref[:, pl.ds(which * units + c * step, step)],
                (((0,), (0,)), ((), ())),
                preferred_element_type=jnp.float32,
            )
            copy = pltpu.make_async_copy(
                held.at[which, :, spot], out.at[0, :, spot], sems.at[which, c]
            )
            copy.start()
            copies.append(copy)
    for copy in copies:
        copy.wait()


VMEM = pl.BlockSpec(memory_space=pltpu.VMEM)
HBM = pl.BlockSpec(memory_space=pltpu.HBM)
ROOM = pltpu.CompilerParams(vmem_limit_bytes=16 << 20)


def local(layer_input, grad_out, picks, gates, w_up, w_down):
    tok_dev, width = layer_input.shape[1:]
    n_exp, n_pick = picks.shape[2:]
    slots = n_exp * n_pick
    units = w_up.shape[2]
    n_dp = lax.axis_size("dp")
    n_hid = lax.axis_size("hidden")
    cols = width // n_dp
    part = width // n_hid
    bf16 = jnp.bfloat16
    layer_input, grad_out, picks, gates, w_up, w_down = (
        pltpu.with_memory_space_constraint(x, pltpu.HBM)
        for x in (layer_input, grad_out, picks, gates, w_up, w_down)
    )

    n_share = n_hid if n_hid % 2 == 0 and 2 * cols % (n_hid * 128) == 0 else 1
    span = 2 * cols // n_share
    send, side, spread = pl.pallas_call(
        functools.partial(pick_kernel, n_hid, n_share),
        out_shape=[
            jax.ShapeDtypeStruct((slots, 2 * width), bf16),
            jax.ShapeDtypeStruct((n_dp * n_exp, n_pick, span), bf16),
            jax.ShapeDtypeStruct((slots * n_hid, tok_dev), bf16),
        ],
        in_specs=[HBM] * 3,
        out_specs=[VMEM] * 3,
        scratch_shapes=[
            pltpu.VMEM(picks.shape, jnp.int32),
            pltpu.VMEM(layer_input.shape, bf16),
            pltpu.VMEM(grad_out.shape, bf16),
            pltpu.SemaphoreType.DMA((3,)),
        ],
        compiler_params=ROOM,
        name="pick",
    )(picks, layer_input, grad_out)

    rows = jnp.concatenate(
        [hop(send[s * n_pick : (s + 1) * n_pick], "expert", s) for s in range(n_exp)], axis=0
    )
    side = lax.all_to_all(side, ("dp", "expert"), 0, 0)
    parts = [hop(side, "hidden", t) for t in range(n_share)]

    upper = pl.pallas_call(
        load_kernel,
        out_shape=jax.ShapeDtypeStruct(w_up.shape, w_up.dtype),
        in_specs=[HBM] * 2,
        out_specs=VMEM,
        scratch_shapes=[pltpu.SemaphoreType.DMA],
        compiler_params=ROOM,
        cost_estimate=pl.CostEstimate(flops=0, bytes_accessed=4 * w_up.size, transcendentals=0),
        name="load",
    )(send, w_up)
    chunks = max(1, width // 768)
    factors = pl.pallas_call(
        functools.partial(factor_kernel, chunks),
        out_shape=jax.ShapeDtypeStruct((slots, 2 * units), bf16),
        in_specs=[HBM, VMEM, VMEM, HBM],
        out_specs=VMEM,
        scratch_shapes=[
            pltpu.VMEM(gates.shape, jnp.float32),
            pltpu.VMEM(w_down.shape[1:], bf16),
            pltpu.SemaphoreType.DMA,
            pltpu.SemaphoreType.DMA((chunks,)),
        ],
        compiler_params=ROOM,
        cost_estimate=pl.CostEstimate(
            flops=4 * slots * w_up.size, bytes_accessed=4 * w_up.size, transcendentals=slots * units
        ),
        name="factor",
    )(gates, rows, upper, w_down)

    gathered = jnp.concatenate([hop(factors, "dp", s) for s in range(n_dp)], axis=0)

    piece = pl.pallas_call(
        functools.partial(piece_kernel, n_hid),
        out_shape=jax.ShapeDtypeStruct((n_exp * n_hid, n_pick, part), bf16),
        in_specs=[VMEM, VMEM],
        out_specs=VMEM,
        compiler_params=ROOM,
        cost_estimate=pl.CostEstimate(
            flops=2 * slots * w_up.size, bytes_accessed=2 * w_up.size, transcendentals=0
        ),
        name="piece",
    )(factors, upper)
    returned = lax.all_to_all(piece, ("expert", "hidden"), 0, 0)
    grad_rows = lax.dot_general(
        spread,
        returned.reshape(slots * n_hid, part),
        (((0,), (0,)), ((), ())),
        preferred_element_type=jnp.float32,
    ).astype(bf16)

    chunks = max(1, units // 256)
    grads = pl.pallas_call(
        functools.partial(weight_kernel, chunks, n_dp),
        out_shape=[jax.ShapeDtypeStruct((1, cols, units), jnp.float32)] * 2,
        in_specs=[pl.BlockSpec(memory_space=pl.ANY)] + [VMEM] * (n_share + 1),
        out_specs=[HBM] * 2,
        scratch_shapes=[
            pltpu.VMEM((n_dp * slots, 2 * cols), bf16),
            pltpu.VMEM((2, cols, units), jnp.float32),
            pltpu.SemaphoreType.DMA((2, chunks)),
        ],
        compiler_params=ROOM,
        name="weight",
    )(grad_rows, *parts, gathered)
    return (grad_rows[None], *grads)


def solution(mesh):
    placed = (
        P("dp", "expert", None),
        P("dp", "expert", None),
        P("dp", "expert", None, None),
        P("dp", "expert", None, None),
        P("expert", None, "hidden"),
        P("expert", None, "hidden"),
    )
    return jax.shard_map(
        local,
        mesh=mesh,
        in_specs=placed,
        out_specs=(
            P("dp", "expert", "hidden"),
            P("expert", "dp", "hidden"),
            P("expert", "dp", "hidden"),
        ),
        check_vma=False,
    )
```

time: 45 us -> 44.8 us (level)
  local copies, waits for them, and re-layouts: 2.19 us -> 0.03 us
  waiting for transfers between devices: 7.6 us -> 8.93 us
  Pallas kernels: 14.1 us -> 15.1 us
  matrix products: 0.87 us -> 0.22 us
    all_to_all x0 -> x1, starting transfers between devices: none -> 6 us  [local(): side = lax.all_to_all(side, ('dp', 'expert'), 0, 0)]
    ppermute x12 -> x7, starting transfers between devices: 15.2 us -> 9.74 us  [hop(): return lax.ppermute(x, axis, [(i, (i + step) % n) for i in range(n)])]
    unnamed x4 -> x2, local copies, waits for them, and re-layouts: 1.36 us -> 0.01 us
    ppermute x12 -> x7, waiting for transfers between devices: 7.6 us -> 8.93 us  [hop(): return lax.ppermute(x, axis, [(i, (i + step) % n) for i in range(n)])]
    pallas_call x4, Pallas kernels: 11.5 us -> 12.4 us  [the longest x1 4.32 us: local(): pl.pallas_call(functools.partial(factor_kernel, chunks), out_shape=jax.Sh...]
    broadcast_in_dim x1 -> x0, local copies, waits for them, and re-layouts: 0.68 us -> none  [local(): jnp.broadcast_to(picks[0, 0][:, None, :], (n_exp, n_hid, n_pick))]
    dot_general x1, matrix products: 0.87 us -> 0.22 us  [local(): lax.dot_general(spread, returned.reshape(slots * n_hid, part), (((0,), (0...]
  transfers between devices with their start and end apart: 13 -> 9, of which waited for: 1 -> 2; matrix products, arithmetic and copies ran while one was open for 2% -> 1% of each run, Pallas kernels for 28% -> 22%
where the time goes in v2:
time: 44.8 us; the launch traced here: 44.5 us
  starting transfers between devices  19.4 us (43%)
  Pallas kernels  15.1 us (34%)
  waiting for transfers between devices  8.93 us (20%)
  between operations  0.74 us (2%)
    ppermute x7, starting transfers between devices, hop(): return lax.ppermute(x, axis, [(i, (i + step) % n) for i in range(n)])  9.74 us
    ppermute x7, waiting for transfers between devices, hop(): return lax.ppermute(x, axis, [(i, (i + step) % n) for i in range(n)])  8.93 us
    all_to_all x1, starting transfers between devices, local(): side = lax.all_to_all(side, ('dp', 'expert'), 0, 0)  6 us
    pallas_call x1, Pallas kernels, local(): pl.pallas_call(functools.partial(factor_kernel, chunks), out_shape=jax.Sh...  4.32 us
    all_to_all x1, starting transfers between devices, local(): returned = lax.all_to_all(piece, ('expert', 'hidden'), 0, 0)  3.69 us
    pallas_call x1, Pallas kernels, local(): pl.pallas_call(functools.partial(weight_kernel, chunks, n_dp), out_shape=...  3.2 us
    pallas_call x1, Pallas kernels, local(): pl.pallas_call(load_kernel, out_shape=jax.ShapeDtypeStruct(w_up.shape, w_...  2.8 us
    pallas_call x1, Pallas kernels, local(): pl.pallas_call(functools.partial(piece_kernel, n_hid), out_shape=jax.Shap...  2.63 us
  transfers between devices with their start and end apart: 9, of which 2 were waited for; matrix products, arithmetic and copies ran while one was open for 1% of the time, Pallas kernels for 22%

profile of v2, /device:TPU:0, one launch (start us, length us, event | category | flops | bytes accessed | tf_op | source)
XLA Modules:
  0.0 44.5 jit_solution(17351731262234180491)
XLA Ops:
  0.6 2.1 %pick.1 = (bf16[32,6144]{1,0:T(8,128)(2,1)S(1)}, bf16[16,8,768]{2,1,0:T(8,128)(2,1)}, bf16[64,64]{1,0:T(8,128)(2,1)S(1)}) custom-call(s32[1,1,4,8]{3,2,1,0:T(4,128)} %picks_hbm.1, bf16[1,64,3072]{2,1,0:T(8,128)(2,1)} %tokens_hbm.1, bf16[1,64,3072]{2,1,0:T(8,128)(2,1)} %upstream_hbm.1), custom_call_target="tpu_custom_call" | custom-call | tf_op jit(solution)/shard_map/pick/pallas_call | solution.py:199
  2.8 2.5 %collective-permute-start.2 = (bf16[8,6144]{1,0:T(8,128)(2,1)S(1)}, bf16[8,6144]{1,0:T(8,128)(2,1)S(1)}, u32[]{:S(2)}, u32[]{:S(2)}) collective-permute-start(bf16[8,6144]{1,0:T(8,128)(2,1)S(1)} %get-tuple-element.14), channel_id=1, source_target_pairs={{0,6},{2,0},{4,2},{6,4},{1,7},{3,1},{5,3},{7,5},{8,14},{10,8},{12,... | collective-permute-start | bytes 294920 | tf_op jit(solution)/shard_map/ppermute | solution.py:28
  5.3 0.6 %collective-permute-start.1 = (bf16[8,6144]{1,0:T(8,128)(2,1)S(1)}, bf16[8,6144]{1,0:T(8,128)(2,1)S(1)}, u32[]{:S(2)}, u32[]{:S(2)}) collective-permute-start(bf16[8,6144]{1,0:T(8,128)(2,1)S(1)} %get-tuple-element.15), channel_id=1, source_target_pairs={{0,4},{2,6},{4,0},{6,2},{1,5},{3,7},{5,1},{7,3},{8,12},{10,14},{12... | collective-permute-start | bytes 294920 | tf_op jit(solution)/shard_map/ppermute | solution.py:28
  5.9 0.2 collective-permute-start
  6.1 6.0 %all-to-all-start.1 = ((bf16[16,8,768]{2,1,0:T(8,128)(2,1)}), bf16[16,8,768]{2,1,0:T(8,128)(2,1)S(1)}, u32[]{:S(2)}, u32[]{:S(2)}) async-start(bf16[16,8,768]{2,1,0:T(8,128)(2,1)} %get-tuple-element.10), calls=%async_computation.1 | async-start | bytes 393216 | tf_op jit(solution)/shard_map/all_to_all | solution.py:221
  12.1 2.8 %load.1.upper_ref = bf16[1,3072,1024]{2,1,0:T(8,128)(2,1)S(1)} custom-call(bf16[32,6144]{1,0:T(8,128)(2,1)S(1)} %get-tuple-element.9.after_ref, bf16[1,3072,1024]{2,1,0:T(8,128)(2,1)} %source.1), custom_call_target="tpu_custom_call" | custom-call | bytes 12582912 | tf_op jit(solution)/shard_map/load/pallas_call | solution.py:224
  14.9 0.0 collective-permute-done.2
  14.9 0.0 collective-permute-done.1
  14.9 0.0 collective-permute-done
  14.9 4.3 %factor.1.factor_ref = bf16[32,2048]{1,0:T(8,128)(2,1)S(1)} custom-call(f32[1,1,4,8]{3,2,1,0:T(4,128)} %gates_hbm.1, bf16[32,6144]{1,0:T(8,128)(2,1)S(1)} %pad_maximum_fusion.1.rows_ref, bf16[1,3072,1024]{2,1,0:T(8,128)(2,1)S(1)} %load.1.upper_ref, bf16[1,3072,1024]{2,1,0:T(8,128)(2,1)} %lower_hbm.1), custom_call_target="tpu_custom_call" | custom-call | flops 402653184 | bytes 12582912 | tf_op jit(solution)/shard_map/factor/pallas_call | solution.py:235
  19.3 3.8 %collective-permute-start.6 = (bf16[32,2048]{1,0:T(8,128)(2,1)S(1)}, bf16[32,2048]{1,0:T(8,128)(2,1)S(1)}, u32[]{:S(2)}, u32[]{:S(2)}) collective-permute-start(bf16[32,2048]{1,0:T(8,128)(2,1)S(1)} %factor.1.factor_ref), channel_id=1, source_target_pairs={{0,24},{8,0},{16,8},{24,16},{1,25},{9,1},{17,9},{25,17},{2,26},{10... | collective-permute-start | bytes 393224 | tf_op jit(solution)/shard_map/ppermute | solution.py:28
  23.1 0.0 collective-permute-start.5
  23.1 1.1 %collective-permute-start.4 = (bf16[32,2048]{1,0:T(8,128)(2,1)S(1)}, bf16[32,2048]{1,0:T(8,128)(2,1)S(1)}, u32[]{:S(2)}, u32[]{:S(2)}) collective-permute-start(bf16[32,2048]{1,0:T(8,128)(2,1)S(1)} %factor.1.factor_ref), channel_id=1, source_target_pairs={{0,8},{8,16},{16,24},{24,0},{1,9},{9,17},{17,25},{25,1},{2,10},{10... | collective-permute-start | bytes 393224 | tf_op jit(solution)/shard_map/ppermute | solution.py:28
  24.2 2.6 %piece.1 = bf16[8,8,1536]{2,1,0:T(8,128)(2,1)} custom-call(bf16[32,2048]{1,0:T(8,128)(2,1)S(1)} %factor.1.factor_ref, bf16[1,3072,1024]{2,1,0:T(8,128)(2,1)S(1)} %load.1.upper_ref), custom_call_target="tpu_custom_call" | custom-call | flops 201326592 | bytes 6291456 | tf_op jit(solution)/shard_map/piece/pallas_call | solution.py:255
  26.8 0.0 all-to-all-done.1.refs_0_
  26.8 3.7 %all-to-all-start = ((bf16[8,8,1536]{2,1,0:T(8,128)(2,1)}), bf16[8,8,1536]{2,1,0:T(8,128)(2,1)S(1)}, u32[]{:S(2)}, u32[]{:S(2)}) async-start(bf16[8,8,1536]{2,1,0:T(8,128)(2,1)} %piece.1), calls=%async_computation | async-start | bytes 393216 | tf_op jit(solution)/shard_map/all_to_all | solution.py:266
  30.5 0.0 collective-permute-done.6
  30.5 4.3 %collective-permute-done.5 = bf16[32,2048]{1,0:T(8,128)(2,1)S(1)} collective-permute-done((bf16[32,2048]{1,0:T(8,128)(2,1)S(1)}, bf16[32,2048]{1,0:T(8,128)(2,1)S(1)}, u32[]{:S(2)}, u32[]{:S(2)}) %collective-permute-start.5) | collective-permute-done | bytes 131104 | tf_op jit(solution)/shard_map/ppermute | solution.py:28
  34.8 0.0 collective-permute-done.4
  34.9 1.6 %collective-permute-start.3 = (bf16[16,8,768]{2,1,0:T(8,128)(2,1)S(1)}, bf16[16,8,768]{2,1,0:T(8,128)(2,1)S(1)}, u32[]{:S(2)}, u32[]{:S(2)}) collective-permute-start(bf16[16,8,768]{2,1,0:T(8,128)(2,1)S(1)} %all-to-all-done.1.refs_0_), channel_id=1, source_target_pairs={{0,1},{1,0},{2,3},{3,2},{4,5},{5,4},{6,7},{7,6},{8,9},{9,8},{10,11... | collective-permute-start | bytes 589832 | tf_op jit(solution)/shard_map/ppermute | solution.py:28
  36.4 0.0 all-to-all-done
  36.4 0.2 convolution_convert_fusion.after_ref
  36.7 0.0 copy-start
  36.7 4.6 %collective-permute-done.3.refs_1_ = bf16[16,8,768]{2,1,0:T(8,128)(2,1)S(1)} collective-permute-done((bf16[16,8,768]{2,1,0:T(8,128)(2,1)S(1)}, bf16[16,8,768]{2,1,0:T(8,128)(2,1)S(1)}, u32[]{:S(2)}, u32[]{:S(2)}) %collective-permute-start.3) | collective-permute-done | bytes 196640 | tf_op jit(solution)/shard_map/ppermute | solution.py:28
  41.3 3.2 %weight.1 = (f32[1,768,1024]{2,1,0:T(8,128)}, f32[1,768,1024]{2,1,0:T(8,128)}) custom-call(bf16[64,1536]{1,0:T(8,128)(2,1)S(1)} %convolution_convert_fusion.after_ref, bf16[16,8,768]{2,1,0:T(8,128)(2,1)S(1)} %all-to-all-done.1.refs_0_, bf16[16,8,768]{2,1,0:T(8,128)(2,1)S(1)} %collective-permute-done.3.refs_1_, bf16[128,2048]{1,0:T(8,128)(2,1)S(1)} %pad_maximum_fusion.refs_2_), custom_call_target="tpu_custom_call" | custom-call | tf_op jit(solution)/shard_map/weight/pallas_call | solution.py:275
  44.5 0.0 copy-done
  (3 shorter events, 0.1 us)
Async XLA Ops:
  2.8 12.1 %collective-permute-start.2 = (bf16[8,6144]{1,0:T(8,128)(2,1)S(1)}, bf16[8,6144]{1,0:T(8,128)(2,1)S(1)}, u32[]{:S(2)}, u32[]{:S(2)}) collective-permute-start(bf16[8,6144]{1,0:T(8,128)(2,1)S(1)} %get-tuple-element.14), channel_id=1, source_target_pairs={{0,6},{2,0},{4,2},{6,4},{1,7},{3,1},{5,3},{7,5},{8,14},{10,8},{12,... | collective-permute-start | bytes 294920 | tf_op jit(solution)/shard_map/ppermute | solution.py:28
  5.3 9.6 %collective-permute-start.1 = (bf16[8,6144]{1,0:T(8,128)(2,1)S(1)}, bf16[8,6144]{1,0:T(8,128)(2,1)S(1)}, u32[]{:S(2)}, u32[]{:S(2)}) collective-permute-start(bf16[8,6144]{1,0:T(8,128)(2,1)S(1)} %get-tuple-element.15), channel_id=1, source_target_pairs={{0,4},{2,6},{4,0},{6,2},{1,5},{3,7},{5,1},{7,3},{8,12},{10,14},{12... | collective-permute-start | bytes 294920 | tf_op jit(solution)/shard_map/ppermute | solution.py:28
  5.9 9.0 %collective-permute-start = (bf16[8,6144]{1,0:T(8,128)(2,1)S(1)}, bf16[8,6144]{1,0:T(8,128)(2,1)S(1)}, u32[]{:S(2)}, u32[]{:S(2)}) collective-permute-start(bf16[8,6144]{1,0:T(8,128)(2,1)S(1)} %get-tuple-element.16), channel_id=1, source_target_pairs={{0,2},{2,4},{4,6},{6,0},{1,3},{3,5},{5,7},{7,1},{8,10},{10,12},{12... | collective-permute-start | bytes 294920 | tf_op jit(solution)/shard_map/ppermute | solution.py:28
  6.1 20.7 %all-to-all-start.1 = ((bf16[16,8,768]{2,1,0:T(8,128)(2,1)}), bf16[16,8,768]{2,1,0:T(8,128)(2,1)S(1)}, u32[]{:S(2)}, u32[]{:S(2)}) async-start(bf16[16,8,768]{2,1,0:T(8,128)(2,1)} %get-tuple-element.10), calls=%async_computation.1 | async-start | bytes 393216 | tf_op jit(solution)/shard_map/all_to_all | solution.py:221
  19.3 11.2 %collective-permute-start.6 = (bf16[32,2048]{1,0:T(8,128)(2,1)S(1)}, bf16[32,2048]{1,0:T(8,128)(2,1)S(1)}, u32[]{:S(2)}, u32[]{:S(2)}) collective-permute-start(bf16[32,2048]{1,0:T(8,128)(2,1)S(1)} %factor.1.factor_ref), channel_id=1, source_target_pairs={{0,24},{8,0},{16,8},{24,16},{1,25},{9,1},{17,9},{25,17},{2,26},{10... | collective-permute-start | bytes 393224 | tf_op jit(solution)/shard_map/ppermute | solution.py:28
  23.1 11.8 %collective-permute-start.5 = (bf16[32,2048]{1,0:T(8,128)(2,1)S(1)}, bf16[32,2048]{1,0:T(8,128)(2,1)S(1)}, u32[]{:S(2)}, u32[]{:S(2)}) collective-permute-start(bf16[32,2048]{1,0:T(8,128)(2,1)S(1)} %factor.1.factor_ref), channel_id=1, source_target_pairs={{0,16},{8,24},{16,0},{24,8},{1,17},{9,25},{17,1},{25,9},{2,18},{10... | collective-permute-start | bytes 393224 | tf_op jit(solution)/shard_map/ppermute | solution.py:28
  23.1 11.8 %collective-permute-start.4 = (bf16[32,2048]{1,0:T(8,128)(2,1)S(1)}, bf16[32,2048]{1,0:T(8,128)(2,1)S(1)}, u32[]{:S(2)}, u32[]{:S(2)}) collective-permute-start(bf16[32,2048]{1,0:T(8,128)(2,1)S(1)} %factor.1.factor_ref), channel_id=1, source_target_pairs={{0,8},{8,16},{16,24},{24,0},{1,9},{9,17},{17,25},{25,1},{2,10},{10... | collective-permute-start | bytes 393224 | tf_op jit(solution)/shard_map/ppermute | solution.py:28
  26.8 9.6 %all-to-all-start = ((bf16[8,8,1536]{2,1,0:T(8,128)(2,1)}), bf16[8,8,1536]{2,1,0:T(8,128)(2,1)S(1)}, u32[]{:S(2)}, u32[]{:S(2)}) async-start(bf16[8,8,1536]{2,1,0:T(8,128)(2,1)} %piece.1), calls=%async_computation | async-start | bytes 393216 | tf_op jit(solution)/shard_map/all_to_all | solution.py:266
  34.9 6.4 %collective-permute-start.3 = (bf16[16,8,768]{2,1,0:T(8,128)(2,1)S(1)}, bf16[16,8,768]{2,1,0:T(8,128)(2,1)S(1)}, u32[]{:S(2)}, u32[]{:S(2)}) collective-permute-start(bf16[16,8,768]{2,1,0:T(8,128)(2,1)S(1)} %all-to-all-done.1.refs_0_), channel_id=1, source_target_pairs={{0,1},{1,0},{2,3},{3,2},{4,5},{5,4},{6,7},{7,6},{8,9},{9,8},{10,11... | collective-permute-start | bytes 589832 | tf_op jit(solution)/shard_map/ppermute | solution.py:28
  36.7 7.8 %copy-start = (bf16[64,1536]{1,0:T(8,128)(2,1)}, bf16[64,1536]{1,0:T(8,128)(2,1)S(1)}, u32[]{:S(2)}) copy-start(bf16[64,1536]{1,0:T(8,128)(2,1)S(1)} %convolution_convert_fusion.after_ref) | copy-start | bytes 589828

commit v3 on v1

--- a/solution.py
+++ b/solution.py
@@ -39,11 +39,10 @@
     return jnp.concatenate(out, axis=0)
 
 
-def pick_kernel(n_dp, picks_hbm, tokens_hbm, upstream_hbm, rows_ref, *refs):
-    *side_refs, picks_ref, tokens_ref, upstream_ref, sems = refs
-    n_exp, n_pick = picks_ref.shape[2:]
+def pick_kernel(n_hid, picks_hbm, tokens_hbm, upstream_hbm, rows_ref, spread_ref, *refs):
+    picks_ref, tokens_ref, upstream_ref, sems = refs
+    n_exp = picks_ref.shape[2]
     tok_dev, width = tokens_ref.shape[1:]
-    cols = width // n_dp
     copies = [
         pltpu.make_async_copy(picks_hbm, picks_ref, sems.at[0]),
         pltpu.make_async_copy(tokens_hbm, tokens_ref, sems.at[1]),
@@ -52,21 +51,34 @@
     for copy in copies:
         copy.start()
     me = lax.axis_index("expert")
-    my_dp = lax.axis_index("dp")
     copies[0].wait()
-    wanted = column(picks_ref, [(me + s) % n_exp for s in range(n_exp)])
-    spots = lax.broadcasted_iota(jnp.int32, (n_exp * n_pick, tok_dev), 1)
-    selector = jnp.where(wanted.astype(jnp.int32) == spots, 1.0, 0.0).astype(jnp.bfloat16)
+
+    def one_hot(order):
+        wanted = column(picks_ref, order).astype(jnp.int32)
+        spots = lax.broadcasted_iota(jnp.int32, (wanted.shape[0], tok_dev), 1)
+        return jnp.where(wanted == spots, 1.0, 0.0).astype(jnp.bfloat16)
+
+    selector = one_hot([(me + s) % n_exp for s in range(n_exp)])
+    spread_ref[...] = one_hot([e for e in range(n_exp) for _ in range(n_hid)])
     for at, copy, source in ((0, copies[1], tokens_ref), (width, copies[2], upstream_ref)):
         copy.wait()
         rows_ref[:, at : at + width] = jnp.dot(
             selector, source[0], preferred_element_type=jnp.float32
         ).astype(jnp.bfloat16)
-    for s in range(1, n_dp):
-        start = ((my_dp + s) % n_dp) * cols
+
+
+def cut_kernel(after_ref, rows_ref, *out_refs):
+    n_dp = len(out_refs) + 1
+    share, wide = out_refs[0].shape
+    cols = wide // 2
+    width = rows_ref.shape[1] // 2
+    my_dp = lax.axis_index("dp")
+    spot = pl.ds(pl.multiple_of(lax.axis_index("hidden") * share, 16), share)
+    for s, out_ref in enumerate(out_refs):
+        at = ((my_dp + s + 1) % n_dp) * cols
         for half in range(2):
-            side_refs[s - 1][:, half * cols : (half + 1) * cols] = rows_ref[
-                :, pl.ds(pl.multiple_of(half * width + start, 128), cols)
+            out_ref[:, half * cols : (half + 1) * cols] = rows_ref[
+                spot, pl.ds(pl.multiple_of(half * width + at, 128), cols)
             ]
 
 
@@ -83,7 +95,7 @@
         copy.wait()
 
 
-def factor_kernel(gates_ref, rows_ref, upper_ref, lower_ref, out_ref):
+def factor_kernel(after_ref, gates_ref, rows_ref, upper_ref, lower_ref, out_ref):
     n_exp = gates_ref.shape[2]
     width, units = upper_ref.shape[1:]
     me = lax.axis_index("expert")
@@ -111,9 +123,25 @@
             ].astype(jnp.bfloat16)
 
 
-def weight_kernel(chunks, side_ref, factor_ref, up_ref, down_ref, held, sems):
+def weight_kernel(chunks, shape, own_ref, *refs):
+    n_dp, n_hid = shape
+    part_refs, refs = refs[:n_hid], refs[n_hid:]
+    factor_ref, up_ref, down_ref, side_ref, held, sems = refs
     units = factor_ref.shape[1] // 2
     cols = side_ref.shape[1] // 2
+    width = own_ref.shape[1] // 2
+    slots = own_ref.shape[0]
+    rows = slots // n_hid
+    my_hid = lax.axis_index("hidden")
+    start = lax.axis_index("dp") * cols
+    for half in range(2):
+        side_ref[:slots, half * cols : (half + 1) * cols] = own_ref[
+            :, pl.ds(pl.multiple_of(half * width + start, 128), cols)
+        ]
+    for t, part in enumerate(part_refs):
+        spot = ((my_hid + n_hid - t) % n_hid) * rows
+        for s in range(1, n_dp):
+            side_ref[pl.ds(pl.multiple_of(s * slots + spot, 16), rows), :] = part[s - 1]
     step = units // chunks
     copies = []
     for which, out in ((0, up_ref), (1, down_ref)):
@@ -135,6 +163,7 @@
 
 
 VMEM = pl.BlockSpec(memory_space=pltpu.VMEM)
+ANY = pl.BlockSpec(memory_space=pl.ANY)
 HBM = pl.BlockSpec(memory_space=pltpu.HBM)
 ROOM = pltpu.CompilerParams(vmem_limit_bytes=16 << 20)
 
@@ -149,17 +178,19 @@
     cols = width // n_dp
     part = width // n_hid
     bf16 = jnp.bfloat16
-    layer_input, grad_out, w_up, w_down = (
+    layer_input, grad_out, picks, gates, w_up, w_down = (
         pltpu.with_memory_space_constraint(x, pltpu.HBM)
-        for x in (layer_input, grad_out, w_up, w_down)
-    )
-
-    send, *side = pl.pallas_call(
-        functools.partial(pick_kernel, n_dp),
-        out_shape=[jax.ShapeDtypeStruct((slots, 2 * width), bf16)]
-        + [jax.ShapeDtypeStruct((slots, 2 * cols), bf16)] * (n_dp - 1),
+        for x in (layer_input, grad_out, picks, gates, w_up, w_down)
+    )
+
+    send, spread = pl.pallas_call(
+        functools.partial(pick_kernel, n_hid),
+        out_shape=[
+            jax.ShapeDtypeStruct((slots, 2 * width), bf16),
+            jax.ShapeDtypeStruct((slots * n_hid, tok_dev), bf16),
+        ],
         in_specs=[HBM] * 3,
-        out_specs=[VMEM] * n_dp,
+        out_specs=[VMEM] * 2,
         scratch_shapes=[
             pltpu.VMEM(picks.shape, jnp.int32),
             pltpu.VMEM(layer_input.shape, bf16),
@@ -173,20 +204,6 @@
     rows = jnp.concatenate(
         [hop(send[s * n_pick : (s + 1) * n_pick], "expert", s) for s in range(n_exp)], axis=0
     )
-    side = [hop(x, "dp", s + 1).reshape(n_exp, n_pick, 2 * cols) for s, x in enumerate(side)]
-    side = jnp.stack(side)
-    side = [hop(side[:, s], "expert", s) for s in range(n_exp)]
-    side = jnp.stack(side, axis=1).reshape((n_dp - 1) * slots, 2 * cols)
-    at = lax.axis_index("dp") * cols
-    own = jnp.concatenate(
-        [
-            lax.dynamic_slice_in_dim(rows, at, cols, 1),
-            lax.dynamic_slice_in_dim(rows, width + at, cols, 1),
-        ],
-        axis=1,
-    )
-    side = jnp.concatenate([own, side], axis=0)
-
     gate_held, upper, lower = pl.pallas_call(
         load_kernel,
         out_shape=[jax.ShapeDtypeStruct(x.shape, x.dtype) for x in (gates, w_up, w_down)],
@@ -199,14 +216,30 @@
         compiler_params=ROOM,
         name="load",
     )(send, gates, w_up, w_down)
+    share = slots // n_hid
+    parts = pl.pallas_call(
+        cut_kernel,
+        out_shape=[jax.ShapeDtypeStruct((share, 2 * cols), bf16)] * (n_dp - 1),
+        in_specs=[ANY, VMEM],
+        out_specs=[VMEM] * (n_dp - 1),
+        compiler_params=ROOM,
+        name="cut",
+    )(gate_held, rows)
+    parts = [hop(x, "dp", s + 1) for s, x in enumerate(parts)]
+
     factors = pl.pallas_call(
         factor_kernel,
         out_shape=jax.ShapeDtypeStruct((slots, 2 * units), bf16),
-        in_specs=[VMEM] * 4,
+        in_specs=[ANY] + [VMEM] * 4,
         out_specs=VMEM,
         compiler_params=ROOM,
+        cost_estimate=pl.CostEstimate(
+            flops=4 * slots * w_up.size, bytes_accessed=4 * w_up.size, transcendentals=slots * units
+        ),
         name="factor",
-    )(gate_held, rows, upper, lower)
+    )(parts[0], gate_held, rows, upper, lower)
+    parts = jnp.stack(parts)
+    parts = [hop(parts, "hidden", t) for t in range(n_hid)]
 
     gathered = jnp.concatenate([hop(factors, "dp", s) for s in range(n_dp)], axis=0)
 
@@ -216,29 +249,37 @@
         in_specs=[VMEM, VMEM],
         out_specs=VMEM,
         compiler_params=ROOM,
+        cost_estimate=pl.CostEstimate(
+            flops=2 * slots * w_up.size, bytes_accessed=2 * w_up.size, transcendentals=0
+        ),
         name="piece",
     )(factors, upper)
     returned = lax.all_to_all(piece, ("expert", "hidden"), 0, 0)
-    twice = jnp.broadcast_to(picks[0, 0][:, None, :], (n_exp, n_hid, n_pick)).reshape(slots * n_hid)
-    spread = (jnp.arange(tok_dev, dtype=jnp.int32)[:, None] == twice[None, :]).astype(bf16)
-    grad_rows = jnp.dot(
-        spread, returned.reshape(slots * n_hid, part), preferred_element_type=jnp.float32
-    )
+    grad_rows = lax.dot_general(
+        spread,
+        returned.reshape(slots * n_hid, part),
+        (((0,), (0,)), ((), ())),
+        preferred_element_type=jnp.float32,
+    ).astype(bf16)
 
     chunks = max(1, units // 256)
     grads = pl.pallas_call(
-        functools.partial(weight_kernel, chunks),
+        functools.partial(weight_kernel, chunks, (n_dp, n_hid)),
         out_shape=[jax.ShapeDtypeStruct((1, cols, units), jnp.float32)] * 2,
-        in_specs=[VMEM, VMEM],
+        in_specs=[VMEM] * (n_hid + 2),
         out_specs=[HBM] * 2,
         scratch_shapes=[
+            pltpu.VMEM((n_dp * slots, 2 * cols), bf16),
             pltpu.VMEM((2, cols, units), jnp.float32),
             pltpu.SemaphoreType.DMA((2, chunks)),
         ],
         compiler_params=ROOM,
+        cost_estimate=pl.CostEstimate(
+            flops=4 * n_dp * slots * cols * units, bytes_accessed=64 * cols * units, transcendentals=0
+        ),
         name="weight",
-    )(side, gathered)
-    return (grad_rows.astype(bf16)[None], *grads)
+    )(rows, *parts, gathered)
+    return (grad_rows[None], *grads)
 
 
 def solution(mesh):

time: 45 us -> 41.5 us (0.922)
  local copies, waits for them, and re-layouts: 2.19 us -> 0.03 us
  starting transfers between devices: 19 us -> 17.8 us
    ppermute x12 -> x10, starting transfers between devices: 15.2 us -> 13.8 us  [hop(): return lax.ppermute(x, axis, [(i, (i + step) % n) for i in range(n)])]
    unnamed x4 -> x0, local copies, waits for them, and re-layouts: 1.36 us -> none
    broadcast_in_dim x1 -> x0, local copies, waits for them, and re-layouts: 0.68 us -> none  [local(): jnp.broadcast_to(picks[0, 0][:, None, :], (n_exp, n_hid, n_pick))]
    pallas_call x2 -> x3, Pallas kernels: 4.57 us -> 4.61 us  [the longest x1 3.16 us: local(): pl.pallas_call(functools.partial(weight_kernel, chunks, (n_dp, n_hid)), o...]
    ppermute x12 -> x10, waiting for transfers between devices: 7.6 us -> 7.59 us  [hop(): return lax.ppermute(x, axis, [(i, (i + step) % n) for i in range(n)])]
  transfers between devices with their start and end apart: 13 -> 11, of which waited for: 1 -> 4; matrix products, arithmetic and copies ran while one was open for 2% -> 0% of each run, Pallas kernels for 28% -> 31%
where the time goes in v3:
time: 41.5 us; the launch traced here: 41.3 us
  starting transfers between devices  17.8 us (43%)
  Pallas kernels  14.2 us (34%)
  waiting for transfers between devices  7.59 us (18%)
  matrix products  0.91 us (2%)
  between operations  0.73 us (2%)
    ppermute x10, starting transfers between devices, hop(): return lax.ppermute(x, axis, [(i, (i + step) % n) for i in range(n)])  13.8 us
    ppermute x10, waiting for transfers between devices, hop(): return lax.ppermute(x, axis, [(i, (i + step) % n) for i in range(n)])  7.59 us
    pallas_call x1, Pallas kernels, local(): pl.pallas_call(load_kernel, out_shape=[jax.ShapeDtypeStruct(x.shape, x.dt...  4.64 us
    all_to_all x1, starting transfers between devices, local(): returned = lax.all_to_all(piece, ('expert', 'hidden'), 0, 0)  3.94 us
    pallas_call x1, Pallas kernels, local(): pl.pallas_call(functools.partial(weight_kernel, chunks, (n_dp, n_hid)), o...  3.16 us
    pallas_call x1, Pallas kernels, local(): pl.pallas_call(functools.partial(piece_kernel, n_hid), out_shape=jax.Shap...  2.63 us
    pallas_call x1, Pallas kernels, local(): pl.pallas_call(factor_kernel, out_shape=jax.ShapeDtypeStruct((slots, 2 *...  2.29 us
    pallas_call x1, Pallas kernels, local(): pl.pallas_call(functools.partial(pick_kernel, n_hid), out_shape=[jax.Shap...  1.42 us
  transfers between devices with their start and end apart: 11, of which 4 were waited for; matrix products, arithmetic and copies ran while one was open for 0% of the time, Pallas kernels for 31%

profile of v3, /device:TPU:0, one launch (start us, length us, event | category | flops | bytes accessed | tf_op | source)
XLA Modules:
  0.0 41.3 jit_solution(4405396627521758833)
XLA Ops:
  0.6 1.4 %pick.1 = (bf16[32,6144]{1,0:T(8,128)(2,1)S(1)}, bf16[64,64]{1,0:T(8,128)(2,1)S(1)}) custom-call(s32[1,1,4,8]{3,2,1,0:T(4,128)} %picks_hbm.1, bf16[1,64,3072]{2,1,0:T(8,128)(2,1)} %tokens_hbm.1, bf16[1,64,3072]{2,1,0:T(8,128)(2,1)} %upstream_hbm.1), custom_call_target="tpu_custom_call" | custom-call | tf_op jit(solution)/shard_map/pick/pallas_call | solution.py:186
  2.1 2.5 %collective-permute-start.2 = (bf16[8,6144]{1,0:T(8,128)(2,1)S(1)}, bf16[8,6144]{1,0:T(8,128)(2,1)S(1)}, u32[]{:S(2)}, u32[]{:S(2)}) collective-permute-start(bf16[8,6144]{1,0:T(8,128)(2,1)S(1)} %get-tuple-element.24), channel_id=1, source_target_pairs={{0,6},{2,0},{4,2},{6,4},{1,7},{3,1},{5,3},{7,5},{8,14},{10,8},{12,... | collective-permute-start | bytes 294920 | tf_op jit(solution)/shard_map/ppermute | solution.py:28
  4.6 0.6 %collective-permute-start.1 = (bf16[8,6144]{1,0:T(8,128)(2,1)S(1)}, bf16[8,6144]{1,0:T(8,128)(2,1)S(1)}, u32[]{:S(2)}, u32[]{:S(2)}) collective-permute-start(bf16[8,6144]{1,0:T(8,128)(2,1)S(1)} %get-tuple-element.25), channel_id=1, source_target_pairs={{0,4},{2,6},{4,0},{6,2},{1,5},{3,7},{5,1},{7,3},{8,12},{10,14},{12... | collective-permute-start | bytes 294920 | tf_op jit(solution)/shard_map/ppermute | solution.py:28
  5.2 0.2 collective-permute-start
  5.4 4.6 %load.1 = (f32[1,1,4,8]{3,2,1,0:T(4,128)S(1)}, bf16[1,3072,1024]{2,1,0:T(8,128)(2,1)S(1)}, bf16[1,3072,1024]{2,1,0:T(8,128)(2,1)S(1)}) custom-call(bf16[32,6144]{1,0:T(8,128)(2,1)S(1)} %get-tuple-element.14.after_ref, f32[1,1,4,8]{3,2,1,0:T(4,128)} %gates_hbm.1, bf16[1,3072,1024]{2,1,0:T(8,128)(2,1)} %upper_hbm.1, bf16[1,3072,1024]{2,1,0:T(8,128)(2,1)} %lower_hbm.1), custom_call_target="tpu_custom_call" | custom-call | bytes 25165824 | tf_op jit(solution)/shard_map/load/pallas_call | solution.py:207
  10.0 0.0 collective-permute-done.2
  10.0 0.7 %collective-permute-done.1 = bf16[8,6144]{1,0:T(8,128)(2,1)S(1)} collective-permute-done((bf16[8,6144]{1,0:T(8,128)(2,1)S(1)}, bf16[8,6144]{1,0:T(8,128)(2,1)S(1)}, u32[]{:S(2)}, u32[]{:S(2)}) %collective-permute-start.1) | collective-permute-done | bytes 98336 | tf_op jit(solution)/shard_map/ppermute | solution.py:28
  10.7 0.0 collective-permute-done
  10.8 1.8 %collective-permute-start.3 = (bf16[16,1536]{1,0:T(8,128)(2,1)S(1)}, bf16[16,1536]{1,0:T(8,128)(2,1)S(1)}, u32[]{:S(2)}, u32[]{:S(2)}) collective-permute-start(bf16[16,1536]{1,0:T(8,128)(2,1)S(1)} %get-tuple-element.16), channel_id=1, source_target_pairs={{0,8},{8,16},{16,24},{24,0},{1,9},{9,17},{17,25},{25,1},{2,10},{10... | collective-permute-start | bytes 147464 | tf_op jit(solution)/shard_map/ppermute | solution.py:28
  12.6 2.6 %collective-permute-start.4 = (bf16[16,1536]{1,0:T(8,128)(2,1)S(1)}, bf16[16,1536]{1,0:T(8,128)(2,1)S(1)}, u32[]{:S(2)}, u32[]{:S(2)}) collective-permute-start(bf16[16,1536]{1,0:T(8,128)(2,1)S(1)} %get-tuple-element.19), channel_id=1, source_target_pairs={{0,16},{8,24},{16,0},{24,8},{1,17},{9,25},{17,1},{25,9},{2,18},{10... | collective-permute-start | bytes 147464 | tf_op jit(solution)/shard_map/ppermute | solution.py:28
  15.2 1.3 %collective-permute-start.5 = (bf16[16,1536]{1,0:T(8,128)(2,1)S(1)}, bf16[16,1536]{1,0:T(8,128)(2,1)S(1)}, u32[]{:S(2)}, u32[]{:S(2)}) collective-permute-start(bf16[16,1536]{1,0:T(8,128)(2,1)S(1)} %get-tuple-element.20), channel_id=1, source_target_pairs={{0,24},{8,0},{16,8},{24,16},{1,25},{9,1},{17,9},{25,17},{2,26},{10... | collective-permute-start | bytes 147464 | tf_op jit(solution)/shard_map/ppermute | solution.py:28
  16.5 0.6 %collective-permute-done.3.after_ref = bf16[16,1536]{1,0:T(8,128)(2,1)S(1)} collective-permute-done((bf16[16,1536]{1,0:T(8,128)(2,1)S(1)}, bf16[16,1536]{1,0:T(8,128)(2,1)S(1)}, u32[]{:S(2)}, u32[]{:S(2)}) %collective-permute-start.3) | collective-permute-done | bytes 49184 | tf_op jit(solution)/shard_map/ppermute | solution.py:28
  17.1 2.3 %factor.1.factor_ref = bf16[32,2048]{1,0:T(8,128)(2,1)S(1)} custom-call(bf16[16,1536]{1,0:T(8,128)(2,1)S(1)} %collective-permute-done.3.after_ref, f32[1,1,4,8]{3,2,1,0:T(4,128)S(1)} %get-tuple-element.15.after_ref.gates_ref, bf16[32,6144]{1,0:T(8,128)(2,1)S(1)} %pad_maximum_fusion.1.rows_ref.own_ref, ...), custom_call_target="tpu_custom_call" | custom-call | flops 402653184 | bytes 12582912 | tf_op jit(solution)/shard_map/factor/pallas_call | solution.py:230
  19.4 1.7 %collective-permute-start.9 = (bf16[32,2048]{1,0:T(8,128)(2,1)S(1)}, bf16[32,2048]{1,0:T(8,128)(2,1)S(1)}, u32[]{:S(2)}, u32[]{:S(2)}) collective-permute-start(bf16[32,2048]{1,0:T(8,128)(2,1)S(1)} %factor.1.factor_ref), channel_id=1, source_target_pairs={{0,24},{8,0},{16,8},{24,16},{1,25},{9,1},{17,9},{25,17},{2,26},{10... | collective-permute-start | bytes 393224 | tf_op jit(solution)/shard_map/ppermute | solution.py:28
  21.1 0.0 collective-permute-start.8
  21.1 1.0 %collective-permute-start.7 = (bf16[32,2048]{1,0:T(8,128)(2,1)S(1)}, bf16[32,2048]{1,0:T(8,128)(2,1)S(1)}, u32[]{:S(2)}, u32[]{:S(2)}) collective-permute-start(bf16[32,2048]{1,0:T(8,128)(2,1)S(1)} %factor.1.factor_ref), channel_id=1, source_target_pairs={{0,8},{8,16},{16,24},{24,0},{1,9},{9,17},{17,25},{25,1},{2,10},{10... | collective-permute-start | bytes 393224 | tf_op jit(solution)/shard_map/ppermute | solution.py:28
  22.1 2.6 %piece.1 = bf16[8,8,1536]{2,1,0:T(8,128)(2,1)} custom-call(bf16[32,2048]{1,0:T(8,128)(2,1)S(1)} %factor.1.factor_ref, bf16[1,3072,1024]{2,1,0:T(8,128)(2,1)S(1)} %get-tuple-element.17.upper_ref), custom_call_target="tpu_custom_call" | custom-call | flops 201326592 | bytes 6291456 | tf_op jit(solution)/shard_map/piece/pallas_call | solution.py:246
  24.7 3.9 %all-to-all-start = ((bf16[8,8,1536]{2,1,0:T(8,128)(2,1)}), bf16[8,8,1536]{2,1,0:T(8,128)(2,1)S(1)}, u32[]{:S(2)}, u32[]{:S(2)}) async-start(bf16[8,8,1536]{2,1,0:T(8,128)(2,1)} %piece.1), calls=%async_computation | async-start | bytes 393216 | tf_op jit(solution)/shard_map/all_to_all | solution.py:257
  28.7 0.0 collective-permute-done.4
  28.7 0.0 collective-permute-done.5
  28.7 2.1 %collective-permute-start.6 = (bf16[3,16,1536]{2,1,0:T(8,128)(2,1)S(1)}, bf16[3,16,1536]{2,1,0:T(8,128)(2,1)S(1)}, u32[]{:S(2)}, u32[]{:S(2)}) collective-permute-start(bf16[3,16,1536]{2,1,0:T(8,128)(2,1)S(1)} %pad_maximum_fusion.2.refs_0_), channel_id=1, source_target_pairs={{0,1},{1,0},{2,3},{3,2},{4,5},{5,4},{6,7},{7,6},{8,9},{9,8},{10,11... | collective-permute-start | bytes 442376 | tf_op jit(solution)/shard_map/ppermute | solution.py:28
  30.8 0.0 collective-permute-done.9
  30.8 1.7 %collective-permute-done.8 = bf16[32,2048]{1,0:T(8,128)(2,1)S(1)} collective-permute-done((bf16[32,2048]{1,0:T(8,128)(2,1)S(1)}, bf16[32,2048]{1,0:T(8,128)(2,1)S(1)}, u32[]{:S(2)}, u32[]{:S(2)}) %collective-permute-start.8) | collective-permute-done | bytes 131104 | tf_op jit(solution)/shard_map/ppermute | solution.py:28
  32.5 0.0 collective-permute-done.7
  32.5 4.7 %collective-permute-done.6.refs_1_ = bf16[3,16,1536]{2,1,0:T(8,128)(2,1)S(1)} collective-permute-done((bf16[3,16,1536]{2,1,0:T(8,128)(2,1)S(1)}, bf16[3,16,1536]{2,1,0:T(8,128)(2,1)S(1)}, u32[]{:S(2)}, u32[]{:S(2)}) %collective-permute-start.6) | collective-permute-done | bytes 147488 | tf_op jit(solution)/shard_map/ppermute | solution.py:28
  37.2 3.2 %weight.1 = (f32[1,768,1024]{2,1,0:T(8,128)}, f32[1,768,1024]{2,1,0:T(8,128)}) custom-call(bf16[32,6144]{1,0:T(8,128)(2,1)S(1)} %pad_maximum_fusion.1.rows_ref.own_ref, bf16[3,16,1536]{2,1,0:T(8,128)(2,1)S(1)} %pad_maximum_fusion.2.refs_0_, bf16[3,16,1536]{2,1,0:T(8,128)(2,1)S(1)} %collective-permute-done.6.refs_1_, ...), custom_call_target="tpu_custom_call" | custom-call | flops 402653184 | bytes 50331648 | tf_op jit(solution)/shard_map/weight/pallas_call | solution.py:266
  40.3 0.0 all-to-all-done
  40.4 0.9 %fusion = bf16[1,64,1536]{2,1,0:T(8,128)(2,1)} fusion(bf16[64,64]{1,0:T(8,128)(2,1)S(1)} %get-tuple-element.13, bf16[8,8,1536]{2,1,0:T(8,128)(2,1)S(1)} %all-to-all-done), kind=kOutput, calls=%fused_computation.1 | convolution fusion | flops 12681216 | bytes 401408 | tf_op jit(solution)/shard_map/dot_general | solution.py:258
  (5 shorter events, 0.1 us)
Async XLA Ops:
  2.1 7.9 %collective-permute-start.2 = (bf16[8,6144]{1,0:T(8,128)(2,1)S(1)}, bf16[8,6144]{1,0:T(8,128)(2,1)S(1)}, u32[]{:S(2)}, u32[]{:S(2)}) collective-permute-start(bf16[8,6144]{1,0:T(8,128)(2,1)S(1)} %get-tuple-element.24), channel_id=1, source_target_pairs={{0,6},{2,0},{4,2},{6,4},{1,7},{3,1},{5,3},{7,5},{8,14},{10,8},{12,... | collective-permute-start | bytes 294920 | tf_op jit(solution)/shard_map/ppermute | solution.py:28
  4.6 6.1 %collective-permute-start.1 = (bf16[8,6144]{1,0:T(8,128)(2,1)S(1)}, bf16[8,6144]{1,0:T(8,128)(2,1)S(1)}, u32[]{:S(2)}, u32[]{:S(2)}) collective-permute-start(bf16[8,6144]{1,0:T(8,128)(2,1)S(1)} %get-tuple-element.25), channel_id=1, source_target_pairs={{0,4},{2,6},{4,0},{6,2},{1,5},{3,7},{5,1},{7,3},{8,12},{10,14},{12... | collective-permute-start | bytes 294920 | tf_op jit(solution)/shard_map/ppermute | solution.py:28
  5.2 5.5 %collective-permute-start = (bf16[8,6144]{1,0:T(8,128)(2,1)S(1)}, bf16[8,6144]{1,0:T(8,128)(2,1)S(1)}, u32[]{:S(2)}, u32[]{:S(2)}) collective-permute-start(bf16[8,6144]{1,0:T(8,128)(2,1)S(1)} %get-tuple-element.26), channel_id=1, source_target_pairs={{0,2},{2,4},{4,6},{6,0},{1,3},{3,5},{5,7},{7,1},{8,10},{10,12},{12... | collective-permute-start | bytes 294920 | tf_op jit(solution)/shard_map/ppermute | solution.py:28
  10.8 6.3 %collective-permute-start.3 = (bf16[16,1536]{1,0:T(8,128)(2,1)S(1)}, bf16[16,1536]{1,0:T(8,128)(2,1)S(1)}, u32[]{:S(2)}, u32[]{:S(2)}) collective-permute-start(bf16[16,1536]{1,0:T(8,128)(2,1)S(1)} %get-tuple-element.16), channel_id=1, source_target_pairs={{0,8},{8,16},{16,24},{24,0},{1,9},{9,17},{17,25},{25,1},{2,10},{10... | collective-permute-start | bytes 147464 | tf_op jit(solution)/shard_map/ppermute | solution.py:28
  12.6 16.1 %collective-permute-start.4 = (bf16[16,1536]{1,0:T(8,128)(2,1)S(1)}, bf16[16,1536]{1,0:T(8,128)(2,1)S(1)}, u32[]{:S(2)}, u32[]{:S(2)}) collective-permute-start(bf16[16,1536]{1,0:T(8,128)(2,1)S(1)} %get-tuple-element.19), channel_id=1, source_target_pairs={{0,16},{8,24},{16,0},{24,8},{1,17},{9,25},{17,1},{25,9},{2,18},{10... | collective-permute-start | bytes 147464 | tf_op jit(solution)/shard_map/ppermute | solution.py:28
  15.2 13.5 %collective-permute-start.5 = (bf16[16,1536]{1,0:T(8,128)(2,1)S(1)}, bf16[16,1536]{1,0:T(8,128)(2,1)S(1)}, u32[]{:S(2)}, u32[]{:S(2)}) collective-permute-start(bf16[16,1536]{1,0:T(8,128)(2,1)S(1)} %get-tuple-element.20), channel_id=1, source_target_pairs={{0,24},{8,0},{16,8},{24,16},{1,25},{9,1},{17,9},{25,17},{2,26},{10... | collective-permute-start | bytes 147464 | tf_op jit(solution)/shard_map/ppermute | solution.py:28
  19.4 11.4 %collective-permute-start.9 = (bf16[32,2048]{1,0:T(8,128)(2,1)S(1)}, bf16[32,2048]{1,0:T(8,128)(2,1)S(1)}, u32[]{:S(2)}, u32[]{:S(2)}) collective-permute-start(bf16[32,2048]{1,0:T(8,128)(2,1)S(1)} %factor.1.factor_ref), channel_id=1, source_target_pairs={{0,24},{8,0},{16,8},{24,16},{1,25},{9,1},{17,9},{25,17},{2,26},{10... | collective-permute-start | bytes 393224 | tf_op jit(solution)/shard_map/ppermute | solution.py:28
  21.1 11.4 %collective-permute-start.8 = (bf16[32,2048]{1,0:T(8,128)(2,1)S(1)}, bf16[32,2048]{1,0:T(8,128)(2,1)S(1)}, u32[]{:S(2)}, u32[]{:S(2)}) collective-permute-start(bf16[32,2048]{1,0:T(8,128)(2,1)S(1)} %factor.1.factor_ref), channel_id=1, source_target_pairs={{0,16},{8,24},{16,0},{24,8},{1,17},{9,25},{17,1},{25,9},{2,18},{10... | collective-permute-start | bytes 393224 | tf_op jit(solution)/shard_map/ppermute | solution.py:28
  21.1 11.4 %collective-permute-start.7 = (bf16[32,2048]{1,0:T(8,128)(2,1)S(1)}, bf16[32,2048]{1,0:T(8,128)(2,1)S(1)}, u32[]{:S(2)}, u32[]{:S(2)}) collective-permute-start(bf16[32,2048]{1,0:T(8,128)(2,1)S(1)} %factor.1.factor_ref), channel_id=1, source_target_pairs={{0,8},{8,16},{16,24},{24,0},{1,9},{9,17},{17,25},{25,1},{2,10},{10... | collective-permute-start | bytes 393224 | tf_op jit(solution)/shard_map/ppermute | solution.py:28
  24.7 15.6 %all-to-all-start = ((bf16[8,8,1536]{2,1,0:T(8,128)(2,1)}), bf16[8,8,1536]{2,1,0:T(8,128)(2,1)S(1)}, u32[]{:S(2)}, u32[]{:S(2)}) async-start(bf16[8,8,1536]{2,1,0:T(8,128)(2,1)} %piece.1), calls=%async_computation | async-start | bytes 393216 | tf_op jit(solution)/shard_map/all_to_all | solution.py:257
  28.7 8.4 %collective-permute-start.6 = (bf16[3,16,1536]{2,1,0:T(8,128)(2,1)S(1)}, bf16[3,16,1536]{2,1,0:T(8,128)(2,1)S(1)}, u32[]{:S(2)}, u32[]{:S(2)}) collective-permute-start(bf16[3,16,1536]{2,1,0:T(8,128)(2,1)S(1)} %pad_maximum_fusion.2.refs_0_), channel_id=1, source_target_pairs={{0,1},{1,0},{2,3},{3,2},{4,5},{5,4},{6,7},{7,6},{8,9},{9,8},{10,11... | collective-permute-start | bytes 442376 | tf_op jit(solution)/shard_map/ppermute | solution.py:28

commit v4 on v3

--- a/solution.py
+++ b/solution.py
@@ -69,16 +69,14 @@
 
 def cut_kernel(after_ref, rows_ref, *out_refs):
     n_dp = len(out_refs) + 1
-    share, wide = out_refs[0].shape
-    cols = wide // 2
+    cols = out_refs[0].shape[1] // 2
     width = rows_ref.shape[1] // 2
     my_dp = lax.axis_index("dp")
-    spot = pl.ds(pl.multiple_of(lax.axis_index("hidden") * share, 16), share)
     for s, out_ref in enumerate(out_refs):
         at = ((my_dp + s + 1) % n_dp) * cols
         for half in range(2):
             out_ref[:, half * cols : (half + 1) * cols] = rows_ref[
-                spot, pl.ds(pl.multiple_of(half * width + at, 128), cols)
+                :, pl.ds(pl.multiple_of(half * width + at, 128), cols)
             ]
 
 
@@ -107,7 +105,8 @@
     out_ref[:, units:] = (value * gate).astype(jnp.bfloat16)
 
 
-def piece_kernel(n_hid, factor_ref, upper_ref, out_ref):
+def piece_kernel(n_hid, factor_ref, upper_ref, *refs):
+    out_ref = refs[-1]
     n_pick, part = out_ref.shape[1:]
     width, units = upper_ref.shape[1:]
     n_exp = out_ref.shape[0] // n_hid
@@ -123,25 +122,20 @@
             ].astype(jnp.bfloat16)
 
 
-def weight_kernel(chunks, shape, own_ref, *refs):
-    n_dp, n_hid = shape
-    part_refs, refs = refs[:n_hid], refs[n_hid:]
+def weight_kernel(chunks, n_dp, own_ref, *refs):
+    part_refs, refs = refs[: n_dp - 1], refs[n_dp - 1 :]
     factor_ref, up_ref, down_ref, side_ref, held, sems = refs
     units = factor_ref.shape[1] // 2
     cols = side_ref.shape[1] // 2
     width = own_ref.shape[1] // 2
     slots = own_ref.shape[0]
-    rows = slots // n_hid
-    my_hid = lax.axis_index("hidden")
     start = lax.axis_index("dp") * cols
     for half in range(2):
         side_ref[:slots, half * cols : (half + 1) * cols] = own_ref[
             :, pl.ds(pl.multiple_of(half * width + start, 128), cols)
         ]
-    for t, part in enumerate(part_refs):
-        spot = ((my_hid + n_hid - t) % n_hid) * rows
-        for s in range(1, n_dp):
-            side_ref[pl.ds(pl.multiple_of(s * slots + spot, 16), rows), :] = part[s - 1]
+    for s, part in enumerate(part_refs):
+        side_ref[(s + 1) * slots : (s + 2) * slots, :] = part[...]
     step = units // chunks
     copies = []
     for which, out in ((0, up_ref), (1, down_ref)):
@@ -216,10 +210,9 @@
         compiler_params=ROOM,
         name="load",
     )(send, gates, w_up, w_down)
-    share = slots // n_hid
     parts = pl.pallas_call(
         cut_kernel,
-        out_shape=[jax.ShapeDtypeStruct((share, 2 * cols), bf16)] * (n_dp - 1),
+        out_shape=[jax.ShapeDtypeStruct((slots, 2 * cols), bf16)] * (n_dp - 1),
         in_specs=[ANY, VMEM],
         out_specs=[VMEM] * (n_dp - 1),
         compiler_params=ROOM,
@@ -238,47 +231,44 @@
         ),
         name="factor",
     )(parts[0], gate_held, rows, upper, lower)
-    parts = jnp.stack(parts)
-    parts = [hop(parts, "hidden", t) for t in range(n_hid)]
 
     gathered = jnp.concatenate([hop(factors, "dp", s) for s in range(n_dp)], axis=0)
 
     piece = pl.pallas_call(
         functools.partial(piece_kernel, n_hid),
         out_shape=jax.ShapeDtypeStruct((n_exp * n_hid, n_pick, part), bf16),
-        in_specs=[VMEM, VMEM],
+        in_specs=[VMEM, VMEM] + [ANY] * (n_dp - 2),
         out_specs=VMEM,
         compiler_params=ROOM,
         cost_estimate=pl.CostEstimate(
             flops=2 * slots * w_up.size, bytes_accessed=2 * w_up.size, transcendentals=0
         ),
         name="piece",
-    )(factors, upper)
+    )(factors, upper, *parts[1:])
     returned = lax.all_to_all(piece, ("expert", "hidden"), 0, 0)
+    chunks = max(1, units // 256)
+    grads = pl.pallas_call(
+        functools.partial(weight_kernel, chunks, n_dp),
+        out_shape=[jax.ShapeDtypeStruct((1, cols, units), jnp.float32)] * 2,
+        in_specs=[VMEM] * (n_dp + 1),
+        out_specs=[HBM] * 2,
+        scratch_shapes=[
+            pltpu.VMEM((n_dp * slots, 2 * cols), bf16),
+            pltpu.VMEM((2, cols, units), jnp.float32),
+            pltpu.SemaphoreType.DMA((2, chunks)),
+        ],
+        compiler_params=ROOM,
+        cost_estimate=pl.CostEstimate(
+            flops=4 * n_dp * slots * cols * units, bytes_accessed=64 * cols * units, transcendentals=0
+        ),
+        name="weight",
+    )(rows, *parts, gathered)
     grad_rows = lax.dot_general(
         spread,
         returned.reshape(slots * n_hid, part),
         (((0,), (0,)), ((), ())),
         preferred_element_type=jnp.float32,
     ).astype(bf16)
-
-    chunks = max(1, units // 256)
-    grads = pl.pallas_call(
-        functools.partial(weight_kernel, chunks, (n_dp, n_hid)),
-        out_shape=[jax.ShapeDtypeStruct((1, cols, units), jnp.float32)] * 2,
-        in_specs=[VMEM] * (n_hid + 2),
-        out_specs=[HBM] * 2,
-        scratch_shapes=[
-            pltpu.VMEM((n_dp * slots, 2 * cols), bf16),
-            pltpu.VMEM((2, cols, units), jnp.float32),
-            pltpu.SemaphoreType.DMA((2, chunks)),
-        ],
-        compiler_params=ROOM,
-        cost_estimate=pl.CostEstimate(
-            flops=4 * n_dp * slots * cols * units, bytes_accessed=64 * cols * units, transcendentals=0
-        ),
-        name="weight",
-    )(rows, *parts, gathered)
     return (grad_rows[None], *grads)
 
 

time: 41.5 us -> 51.4 us (1.24)
  waiting for transfers between devices: 7.59 us -> 19.2 us
  starting transfers between devices: 17.8 us -> 16.1 us
    ppermute x10 -> x9, waiting for transfers between devices: 7.59 us -> 16.7 us  [hop(): return lax.ppermute(x, axis, [(i, (i + step) % n) for i in range(n)])]
    all_to_all x1, waiting for transfers between devices: 0.01 us -> 2.45 us  [local(): returned = lax.all_to_all(piece, ('expert', 'hidden'), 0, 0)]
    ppermute x10 -> x9, starting transfers between devices: 13.8 us -> 12.7 us  [hop(): return lax.ppermute(x, axis, [(i, (i + step) % n) for i in range(n)])]
    all_to_all x1, starting transfers between devices: 3.94 us -> 3.39 us  [local(): returned = lax.all_to_all(piece, ('expert', 'hidden'), 0, 0)]
  transfers between devices with their start and end apart: 11 -> 10, of which waited for: 4 -> 4; matrix products, arithmetic and copies ran while one was open for 0% -> 0% of each run, Pallas kernels for 31% -> 20%
where the time goes in v4:
time: 51.4 us; the launch traced here: 51.2 us
  waiting for transfers between devices  19.2 us (37%)
  starting transfers between devices  16.1 us (31%)
  Pallas kernels  14.2 us (28%)
  matrix products  0.91 us (2%)
  between operations  0.74 us (1%)
    ppermute x9, waiting for transfers between devices, hop(): return lax.ppermute(x, axis, [(i, (i + step) % n) for i in range(n)])  16.7 us
    ppermute x9, starting transfers between devices, hop(): return lax.ppermute(x, axis, [(i, (i + step) % n) for i in range(n)])  12.7 us
    pallas_call x1, Pallas kernels, local(): pl.pallas_call(load_kernel, out_shape=[jax.ShapeDtypeStruct(x.shape, x.dt...  4.64 us
    all_to_all x1, starting transfers between devices, local(): returned = lax.all_to_all(piece, ('expert', 'hidden'), 0, 0)  3.39 us
    pallas_call x1, Pallas kernels, local(): pl.pallas_call(functools.partial(weight_kernel, chunks, n_dp), out_shape=...  3.14 us
    pallas_call x1, Pallas kernels, local(): pl.pallas_call(functools.partial(piece_kernel, n_hid), out_shape=jax.Shap...  2.63 us
    all_to_all x1, waiting for transfers between devices, local(): returned = lax.all_to_all(piece, ('expert', 'hidden'), 0, 0)  2.45 us
    pallas_call x1, Pallas kernels, local(): pl.pallas_call(factor_kernel, out_shape=jax.ShapeDtypeStruct((slots, 2 *...  2.29 us
  transfers between devices with their start and end apart: 10, of which 4 were waited for; matrix products, arithmetic and copies ran while one was open for 0% of the time, Pallas kernels for 20%

profile of v4, /device:TPU:0, one launch (start us, length us, event | category | flops | bytes accessed | tf_op | source)
XLA Modules:
  0.0 51.2 jit_solution(3767702861325788895)
XLA Ops:
  0.6 1.4 %pick.1 = (bf16[32,6144]{1,0:T(8,128)(2,1)S(1)}, bf16[64,64]{1,0:T(8,128)(2,1)S(1)}) custom-call(s32[1,1,4,8]{3,2,1,0:T(4,128)} %picks_hbm.1, bf16[1,64,3072]{2,1,0:T(8,128)(2,1)} %tokens_hbm.1, bf16[1,64,3072]{2,1,0:T(8,128)(2,1)} %upstream_hbm.1), custom_call_target="tpu_custom_call" | custom-call | tf_op jit(solution)/shard_map/pick/pallas_call | solution.py:180
  2.1 2.5 %collective-permute-start.2 = (bf16[8,6144]{1,0:T(8,128)(2,1)S(1)}, bf16[8,6144]{1,0:T(8,128)(2,1)S(1)}, u32[]{:S(2)}, u32[]{:S(2)}) collective-permute-start(bf16[8,6144]{1,0:T(8,128)(2,1)S(1)} %get-tuple-element.24), channel_id=1, source_target_pairs={{0,6},{2,0},{4,2},{6,4},{1,7},{3,1},{5,3},{7,5},{8,14},{10,8},{12,... | collective-permute-start | bytes 294920 | tf_op jit(solution)/shard_map/ppermute | solution.py:28
  4.6 0.6 %collective-permute-start.1 = (bf16[8,6144]{1,0:T(8,128)(2,1)S(1)}, bf16[8,6144]{1,0:T(8,128)(2,1)S(1)}, u32[]{:S(2)}, u32[]{:S(2)}) collective-permute-start(bf16[8,6144]{1,0:T(8,128)(2,1)S(1)} %get-tuple-element.25), channel_id=1, source_target_pairs={{0,4},{2,6},{4,0},{6,2},{1,5},{3,7},{5,1},{7,3},{8,12},{10,14},{12... | collective-permute-start | bytes 294920 | tf_op jit(solution)/shard_map/ppermute | solution.py:28
  5.2 0.2 collective-permute-start
  5.4 4.6 %load.1 = (f32[1,1,4,8]{3,2,1,0:T(4,128)S(1)}, bf16[1,3072,1024]{2,1,0:T(8,128)(2,1)S(1)}, bf16[1,3072,1024]{2,1,0:T(8,128)(2,1)S(1)}) custom-call(bf16[32,6144]{1,0:T(8,128)(2,1)S(1)} %get-tuple-element.14.after_ref, f32[1,1,4,8]{3,2,1,0:T(4,128)} %gates_hbm.1, bf16[1,3072,1024]{2,1,0:T(8,128)(2,1)} %upper_hbm.1, bf16[1,3072,1024]{2,1,0:T(8,128)(2,1)} %lower_hbm.1), custom_call_target="tpu_custom_call" | custom-call | bytes 25165824 | tf_op jit(solution)/shard_map/load/pallas_call | solution.py:201
  10.0 0.0 collective-permute-done.2
  10.0 0.7 %collective-permute-done.1 = bf16[8,6144]{1,0:T(8,128)(2,1)S(1)} collective-permute-done((bf16[8,6144]{1,0:T(8,128)(2,1)S(1)}, bf16[8,6144]{1,0:T(8,128)(2,1)S(1)}, u32[]{:S(2)}, u32[]{:S(2)}) %collective-permute-start.1) | collective-permute-done | bytes 98336 | tf_op jit(solution)/shard_map/ppermute | solution.py:28
  10.7 0.0 collective-permute-done
  10.8 1.8 %collective-permute-start.3 = (bf16[32,1536]{1,0:T(8,128)(2,1)S(1)}, bf16[32,1536]{1,0:T(8,128)(2,1)S(1)}, u32[]{:S(2)}, u32[]{:S(2)}) collective-permute-start(bf16[32,1536]{1,0:T(8,128)(2,1)S(1)} %get-tuple-element.16), channel_id=1, source_target_pairs={{0,8},{8,16},{16,24},{24,0},{1,9},{9,17},{17,25},{25,1},{2,10},{10... | collective-permute-start | bytes 294920 | tf_op jit(solution)/shard_map/ppermute | solution.py:28
  12.6 5.5 %collective-permute-done.3.after_ref.refs_0_ = bf16[32,1536]{1,0:T(8,128)(2,1)S(1)} collective-permute-done((bf16[32,1536]{1,0:T(8,128)(2,1)S(1)}, bf16[32,1536]{1,0:T(8,128)(2,1)S(1)}, u32[]{:S(2)}, u32[]{:S(2)}) %collective-permute-start.3) | collective-permute-done | bytes 98336 | tf_op jit(solution)/shard_map/ppermute | solution.py:28
  18.1 2.3 %factor.1.factor_ref = bf16[32,2048]{1,0:T(8,128)(2,1)S(1)} custom-call(bf16[32,1536]{1,0:T(8,128)(2,1)S(1)} %collective-permute-done.3.after_ref.refs_0_, f32[1,1,4,8]{3,2,1,0:T(4,128)S(1)} %get-tuple-element.15.after_ref.gates_ref, bf16[32,6144]{1,0:T(8,128)(2,1)S(1)} %pad_maximum_fusion.1.rows_ref.own_ref, ...), custom_call_target="tpu_custom_call" | custom-call | flops 402653184 | bytes 12582912 | tf_op jit(solution)/shard_map/factor/pallas_call | solution.py:223
  20.4 1.8 %collective-permute-start.8 = (bf16[32,2048]{1,0:T(8,128)(2,1)S(1)}, bf16[32,2048]{1,0:T(8,128)(2,1)S(1)}, u32[]{:S(2)}, u32[]{:S(2)}) collective-permute-start(bf16[32,2048]{1,0:T(8,128)(2,1)S(1)} %factor.1.factor_ref), channel_id=1, source_target_pairs={{0,24},{8,0},{16,8},{24,16},{1,25},{9,1},{17,9},{25,17},{2,26},{10... | collective-permute-start | bytes 393224 | tf_op jit(solution)/shard_map/ppermute | solution.py:28
  22.2 0.0 collective-permute-start.7
  22.2 1.0 %collective-permute-start.6 = (bf16[32,2048]{1,0:T(8,128)(2,1)S(1)}, bf16[32,2048]{1,0:T(8,128)(2,1)S(1)}, u32[]{:S(2)}, u32[]{:S(2)}) collective-permute-start(bf16[32,2048]{1,0:T(8,128)(2,1)S(1)} %factor.1.factor_ref), channel_id=1, source_target_pairs={{0,8},{8,16},{16,24},{24,0},{1,9},{9,17},{17,25},{25,1},{2,10},{10... | collective-permute-start | bytes 393224 | tf_op jit(solution)/shard_map/ppermute | solution.py:28
  23.2 2.2 %collective-permute-start.4 = (bf16[32,1536]{1,0:T(8,128)(2,1)S(1)}, bf16[32,1536]{1,0:T(8,128)(2,1)S(1)}, u32[]{:S(2)}, u32[]{:S(2)}) collective-permute-start(bf16[32,1536]{1,0:T(8,128)(2,1)S(1)} %get-tuple-element.19), channel_id=1, source_target_pairs={{0,16},{8,24},{16,0},{24,8},{1,17},{9,25},{17,1},{25,9},{2,18},{10... | collective-permute-start | bytes 294920 | tf_op jit(solution)/shard_map/ppermute | solution.py:28
  25.4 2.6 %collective-permute-start.5 = (bf16[32,1536]{1,0:T(8,128)(2,1)S(1)}, bf16[32,1536]{1,0:T(8,128)(2,1)S(1)}, u32[]{:S(2)}, u32[]{:S(2)}) collective-permute-start(bf16[32,1536]{1,0:T(8,128)(2,1)S(1)} %get-tuple-element.20), channel_id=1, source_target_pairs={{0,24},{8,0},{16,8},{24,16},{1,25},{9,1},{17,9},{25,17},{2,26},{10... | collective-permute-start | bytes 294920 | tf_op jit(solution)/shard_map/ppermute | solution.py:28
  28.0 10.5 %collective-permute-done.4.refs_0_.refs_1_ = bf16[32,1536]{1,0:T(8,128)(2,1)S(1)} collective-permute-done((bf16[32,1536]{1,0:T(8,128)(2,1)S(1)}, bf16[32,1536]{1,0:T(8,128)(2,1)S(1)}, u32[]{:S(2)}, u32[]{:S(2)}) %collective-permute-start.4) | collective-permute-done | bytes 98336 | tf_op jit(solution)/shard_map/ppermute | solution.py:28
  38.6 0.0 collective-permute-done.5.refs_1_.refs_2_
  38.6 2.6 %piece.1 = bf16[8,8,1536]{2,1,0:T(8,128)(2,1)} custom-call(bf16[32,2048]{1,0:T(8,128)(2,1)S(1)} %factor.1.factor_ref, bf16[1,3072,1024]{2,1,0:T(8,128)(2,1)S(1)} %get-tuple-element.17.upper_ref, bf16[32,1536]{1,0:T(8,128)(2,1)S(1)} %collective-permute-done.4.refs_0_.refs_1_, bf16[32,1536]{1,0:T(8,128)(2,1)S(1)} %collective-permute-done.5.refs_1_.refs_2_), custom_call_target="tpu_custom_call" | custom-call | flops 201326592 | bytes 6291456 | tf_op jit(solution)/shard_map/piece/pallas_call | solution.py:237
  41.2 3.4 %all-to-all-start = ((bf16[8,8,1536]{2,1,0:T(8,128)(2,1)}), bf16[8,8,1536]{2,1,0:T(8,128)(2,1)S(1)}, u32[]{:S(2)}, u32[]{:S(2)}) async-start(bf16[8,8,1536]{2,1,0:T(8,128)(2,1)} %piece.1), calls=%async_computation | async-start | bytes 393216 | tf_op jit(solution)/shard_map/all_to_all | solution.py:248
  44.6 0.0 collective-permute-done.8
  44.6 0.0 collective-permute-done.7
  44.6 0.0 collective-permute-done.6
  44.7 3.1 %weight.1 = (f32[1,768,1024]{2,1,0:T(8,128)}, f32[1,768,1024]{2,1,0:T(8,128)}) custom-call(bf16[32,6144]{1,0:T(8,128)(2,1)S(1)} %pad_maximum_fusion.1.rows_ref.own_ref, bf16[32,1536]{1,0:T(8,128)(2,1)S(1)} %collective-permute-done.3.after_ref.refs_0_, bf16[32,1536]{1,0:T(8,128)(2,1)S(1)} %collective-permute-done.4.refs_0_.refs_1_, ...), custom_call_target="tpu_custom_call" | custom-call | flops 402653184 | bytes 50331648 | tf_op jit(solution)/shard_map/weight/pallas_call | solution.py:250
  47.8 2.4 %all-to-all-done = bf16[8,8,1536]{2,1,0:T(8,128)(2,1)S(1)} async-done(((bf16[8,8,1536]{2,1,0:T(8,128)(2,1)}), bf16[8,8,1536]{2,1,0:T(8,128)(2,1)S(1)}, u32[]{:S(2)}, u32[]{:S(2)}) %all-to-all-start) | async-done | bytes 196640 | tf_op jit(solution)/shard_map/all_to_all | solution.py:248
  50.3 0.9 %fusion = bf16[1,64,1536]{2,1,0:T(8,128)(2,1)} fusion(bf16[64,64]{1,0:T(8,128)(2,1)S(1)} %get-tuple-element.13, bf16[8,8,1536]{2,1,0:T(8,128)(2,1)S(1)} %all-to-all-done), kind=kOutput, calls=%fused_computation.1 | convolution fusion | flops 12681216 | bytes 401408 | tf_op jit(solution)/shard_map/dot_general | solution.py:266
  (4 shorter events, 0.1 us)
Async XLA Ops:
  2.1 7.9 %collective-permute-start.2 = (bf16[8,6144]{1,0:T(8,128)(2,1)S(1)}, bf16[8,6144]{1,0:T(8,128)(2,1)S(1)}, u32[]{:S(2)}, u32[]{:S(2)}) collective-permute-start(bf16[8,6144]{1,0:T(8,128)(2,1)S(1)} %get-tuple-element.24), channel_id=1, source_target_pairs={{0,6},{2,0},{4,2},{6,4},{1,7},{3,1},{5,3},{7,5},{8,14},{10,8},{12,... | collective-permute-start | bytes 294920 | tf_op jit(solution)/shard_map/ppermute | solution.py:28
  4.6 6.1 %collective-permute-start.1 = (bf16[8,6144]{1,0:T(8,128)(2,1)S(1)}, bf16[8,6144]{1,0:T(8,128)(2,1)S(1)}, u32[]{:S(2)}, u32[]{:S(2)}) collective-permute-start(bf16[8,6144]{1,0:T(8,128)(2,1)S(1)} %get-tuple-element.25), channel_id=1, source_target_pairs={{0,4},{2,6},{4,0},{6,2},{1,5},{3,7},{5,1},{7,3},{8,12},{10,14},{12... | collective-permute-start | bytes 294920 | tf_op jit(solution)/shard_map/ppermute | solution.py:28
  5.2 5.5 %collective-permute-start = (bf16[8,6144]{1,0:T(8,128)(2,1)S(1)}, bf16[8,6144]{1,0:T(8,128)(2,1)S(1)}, u32[]{:S(2)}, u32[]{:S(2)}) collective-permute-start(bf16[8,6144]{1,0:T(8,128)(2,1)S(1)} %get-tuple-element.26), channel_id=1, source_target_pairs={{0,2},{2,4},{4,6},{6,0},{1,3},{3,5},{5,7},{7,1},{8,10},{10,12},{12... | collective-permute-start | bytes 294920 | tf_op jit(solution)/shard_map/ppermute | solution.py:28
  10.8 7.3 %collective-permute-start.3 = (bf16[32,1536]{1,0:T(8,128)(2,1)S(1)}, bf16[32,1536]{1,0:T(8,128)(2,1)S(1)}, u32[]{:S(2)}, u32[]{:S(2)}) collective-permute-start(bf16[32,1536]{1,0:T(8,128)(2,1)S(1)} %get-tuple-element.16), channel_id=1, source_target_pairs={{0,8},{8,16},{16,24},{24,0},{1,9},{9,17},{17,25},{25,1},{2,10},{10... | collective-permute-start | bytes 294920 | tf_op jit(solution)/shard_map/ppermute | solution.py:28
  20.4 24.2 %collective-permute-start.8 = (bf16[32,2048]{1,0:T(8,128)(2,1)S(1)}, bf16[32,2048]{1,0:T(8,128)(2,1)S(1)}, u32[]{:S(2)}, u32[]{:S(2)}) collective-permute-start(bf16[32,2048]{1,0:T(8,128)(2,1)S(1)} %factor.1.factor_ref), channel_id=1, source_target_pairs={{0,24},{8,0},{16,8},{24,16},{1,25},{9,1},{17,9},{25,17},{2,26},{10... | collective-permute-start | bytes 393224 | tf_op jit(solution)/shard_map/ppermute | solution.py:28
  22.2 22.4 %collective-permute-start.7 = (bf16[32,2048]{1,0:T(8,128)(2,1)S(1)}, bf16[32,2048]{1,0:T(8,128)(2,1)S(1)}, u32[]{:S(2)}, u32[]{:S(2)}) collective-permute-start(bf16[32,2048]{1,0:T(8,128)(2,1)S(1)} %factor.1.factor_ref), channel_id=1, source_target_pairs={{0,16},{8,24},{16,0},{24,8},{1,17},{9,25},{17,1},{25,9},{2,18},{10... | collective-permute-start | bytes 393224 | tf_op jit(solution)/shard_map/ppermute | solution.py:28
  22.2 22.5 %collective-permute-start.6 = (bf16[32,2048]{1,0:T(8,128)(2,1)S(1)}, bf16[32,2048]{1,0:T(8,128)(2,1)S(1)}, u32[]{:S(2)}, u32[]{:S(2)}) collective-permute-start(bf16[32,2048]{1,0:T(8,128)(2,1)S(1)} %factor.1.factor_ref), channel_id=1, source_target_pairs={{0,8},{8,16},{16,24},{24,0},{1,9},{9,17},{17,25},{25,1},{2,10},{10... | collective-permute-start | bytes 393224 | tf_op jit(solution)/shard_map/ppermute | solution.py:28
  23.2 15.4 %collective-permute-start.4 = (bf16[32,1536]{1,0:T(8,128)(2,1)S(1)}, bf16[32,1536]{1,0:T(8,128)(2,1)S(1)}, u32[]{:S(2)}, u32[]{:S(2)}) collective-permute-start(bf16[32,1536]{1,0:T(8,128)(2,1)S(1)} %get-tuple-element.19), channel_id=1, source_target_pairs={{0,16},{8,24},{16,0},{24,8},{1,17},{9,25},{17,1},{25,9},{2,18},{10... | collective-permute-start | bytes 294920 | tf_op jit(solution)/shard_map/ppermute | solution.py:28
  25.4 13.2 %collective-permute-start.5 = (bf16[32,1536]{1,0:T(8,128)(2,1)S(1)}, bf16[32,1536]{1,0:T(8,128)(2,1)S(1)}, u32[]{:S(2)}, u32[]{:S(2)}) collective-permute-start(bf16[32,1536]{1,0:T(8,128)(2,1)S(1)} %get-tuple-element.20), channel_id=1, source_target_pairs={{0,24},{8,0},{16,8},{24,16},{1,25},{9,1},{17,9},{25,17},{2,26},{10... | collective-permute-start | bytes 294920 | tf_op jit(solution)/shard_map/ppermute | solution.py:28
  41.2 9.1 %all-to-all-start = ((bf16[8,8,1536]{2,1,0:T(8,128)(2,1)}), bf16[8,8,1536]{2,1,0:T(8,128)(2,1)S(1)}, u32[]{:S(2)}, u32[]{:S(2)}) async-start(bf16[8,8,1536]{2,1,0:T(8,128)(2,1)} %piece.1), calls=%async_computation | async-start | bytes 393216 | tf_op jit(solution)/shard_map/all_to_all | solution.py:248

commit v5 on v3

--- a/solution.py
+++ b/solution.py
@@ -107,7 +107,8 @@
     out_ref[:, units:] = (value * gate).astype(jnp.bfloat16)
 
 
-def piece_kernel(n_hid, factor_ref, upper_ref, out_ref):
+def piece_kernel(n_hid, factor_ref, upper_ref, *refs):
+    out_ref = refs[-1]
     n_pick, part = out_ref.shape[1:]
     width, units = upper_ref.shape[1:]
     n_exp = out_ref.shape[0] // n_hid
@@ -246,14 +247,14 @@
     piece = pl.pallas_call(
         functools.partial(piece_kernel, n_hid),
         out_shape=jax.ShapeDtypeStruct((n_exp * n_hid, n_pick, part), bf16),
-        in_specs=[VMEM, VMEM],
+        in_specs=[VMEM, VMEM] + [ANY] * n_hid,
         out_specs=VMEM,
         compiler_params=ROOM,
         cost_estimate=pl.CostEstimate(
             flops=2 * slots * w_up.size, bytes_accessed=2 * w_up.size, transcendentals=0
         ),
         name="piece",
-    )(factors, upper)
+    )(factors, upper, *parts)
     returned = lax.all_to_all(piece, ("expert", "hidden"), 0, 0)
     grad_rows = lax.dot_general(
         spread,

time: 41.5 us -> 42.1 us (1.014)
  waiting for transfers between devices: 7.59 us -> 8.37 us
    ppermute x10, waiting for transfers between devices: 7.59 us -> 8.37 us  [hop(): return lax.ppermute(x, axis, [(i, (i + step) % n) for i in range(n)])]
    all_to_all x1, starting transfers between devices: 3.94 us -> 3.39 us  [local(): returned = lax.all_to_all(piece, ('expert', 'hidden'), 0, 0)]
  transfers between devices with their start and end apart: 11 -> 11, of which waited for: 4 -> 5; matrix products, arithmetic and copies ran while one was open for 0% -> 0% of each run, Pallas kernels for 31% -> 30%
where the time goes in v5:
time: 42.1 us; the launch traced here: 41.8 us
  starting transfers between devices  17.5 us (42%)
  Pallas kernels  14.2 us (34%)
  waiting for transfers between devices  8.37 us (20%)
  matrix products  0.91 us (2%)
  between operations  0.74 us (2%)
    ppermute x10, starting transfers between devices, hop(): return lax.ppermute(x, axis, [(i, (i + step) % n) for i in range(n)])  14.1 us
    ppermute x10, waiting for transfers between devices, hop(): return lax.ppermute(x, axis, [(i, (i + step) % n) for i in range(n)])  8.37 us
    pallas_call x1, Pallas kernels, local(): pl.pallas_call(load_kernel, out_shape=[jax.ShapeDtypeStruct(x.shape, x.dt...  4.64 us
    all_to_all x1, starting transfers between devices, local(): returned = lax.all_to_all(piece, ('expert', 'hidden'), 0, 0)  3.39 us
    pallas_call x1, Pallas kernels, local(): pl.pallas_call(functools.partial(weight_kernel, chunks, (n_dp, n_hid)), o...  3.15 us
    pallas_call x1, Pallas kernels, local(): pl.pallas_call(functools.partial(piece_kernel, n_hid), out_shape=jax.Shap...  2.63 us
    pallas_call x1, Pallas kernels, local(): pl.pallas_call(factor_kernel, out_shape=jax.ShapeDtypeStruct((slots, 2 *...  2.29 us
    pallas_call x1, Pallas kernels, local(): pl.pallas_call(functools.partial(pick_kernel, n_hid), out_shape=[jax.Shap...  1.42 us
  transfers between devices with their start and end apart: 11, of which 5 were waited for; matrix products, arithmetic and copies ran while one was open for 0% of the time, Pallas kernels for 30%

profile of v5, /device:TPU:0, one launch (start us, length us, event | category | flops | bytes accessed | tf_op | source)
XLA Modules:
  0.0 41.8 jit_solution(3805737897159993279)
XLA Ops:
  0.6 1.4 %pick.1 = (bf16[32,6144]{1,0:T(8,128)(2,1)S(1)}, bf16[64,64]{1,0:T(8,128)(2,1)S(1)}) custom-call(s32[1,1,4,8]{3,2,1,0:T(4,128)} %picks_hbm.1, bf16[1,64,3072]{2,1,0:T(8,128)(2,1)} %tokens_hbm.1, bf16[1,64,3072]{2,1,0:T(8,128)(2,1)} %upstream_hbm.1), custom_call_target="tpu_custom_call" | custom-call | tf_op jit(solution)/shard_map/pick/pallas_call | solution.py:187
  2.1 2.5 %collective-permute-start.2 = (bf16[8,6144]{1,0:T(8,128)(2,1)S(1)}, bf16[8,6144]{1,0:T(8,128)(2,1)S(1)}, u32[]{:S(2)}, u32[]{:S(2)}) collective-permute-start(bf16[8,6144]{1,0:T(8,128)(2,1)S(1)} %get-tuple-element.24), channel_id=1, source_target_pairs={{0,6},{2,0},{4,2},{6,4},{1,7},{3,1},{5,3},{7,5},{8,14},{10,8},{12,... | collective-permute-start | bytes 294920 | tf_op jit(solution)/shard_map/ppermute | solution.py:28
  4.6 0.6 %collective-permute-start.1 = (bf16[8,6144]{1,0:T(8,128)(2,1)S(1)}, bf16[8,6144]{1,0:T(8,128)(2,1)S(1)}, u32[]{:S(2)}, u32[]{:S(2)}) collective-permute-start(bf16[8,6144]{1,0:T(8,128)(2,1)S(1)} %get-tuple-element.25), channel_id=1, source_target_pairs={{0,4},{2,6},{4,0},{6,2},{1,5},{3,7},{5,1},{7,3},{8,12},{10,14},{12... | collective-permute-start | bytes 294920 | tf_op jit(solution)/shard_map/ppermute | solution.py:28
  5.2 0.2 collective-permute-start
  5.4 4.6 %load.1 = (f32[1,1,4,8]{3,2,1,0:T(4,128)S(1)}, bf16[1,3072,1024]{2,1,0:T(8,128)(2,1)S(1)}, bf16[1,3072,1024]{2,1,0:T(8,128)(2,1)S(1)}) custom-call(bf16[32,6144]{1,0:T(8,128)(2,1)S(1)} %get-tuple-element.14.after_ref, f32[1,1,4,8]{3,2,1,0:T(4,128)} %gates_hbm.1, bf16[1,3072,1024]{2,1,0:T(8,128)(2,1)} %upper_hbm.1, bf16[1,3072,1024]{2,1,0:T(8,128)(2,1)} %lower_hbm.1), custom_call_target="tpu_custom_call" | custom-call | bytes 25165824 | tf_op jit(solution)/shard_map/load/pallas_call | solution.py:208
  10.0 0.0 collective-permute-done.2
  10.0 0.7 %collective-permute-done.1 = bf16[8,6144]{1,0:T(8,128)(2,1)S(1)} collective-permute-done((bf16[8,6144]{1,0:T(8,128)(2,1)S(1)}, bf16[8,6144]{1,0:T(8,128)(2,1)S(1)}, u32[]{:S(2)}, u32[]{:S(2)}) %collective-permute-start.1) | collective-permute-done | bytes 98336 | tf_op jit(solution)/shard_map/ppermute | solution.py:28
  10.7 0.0 collective-permute-done
  10.8 1.8 %collective-permute-start.3 = (bf16[16,1536]{1,0:T(8,128)(2,1)S(1)}, bf16[16,1536]{1,0:T(8,128)(2,1)S(1)}, u32[]{:S(2)}, u32[]{:S(2)}) collective-permute-start(bf16[16,1536]{1,0:T(8,128)(2,1)S(1)} %get-tuple-element.16), channel_id=1, source_target_pairs={{0,8},{8,16},{16,24},{24,0},{1,9},{9,17},{17,25},{25,1},{2,10},{10... | collective-permute-start | bytes 147464 | tf_op jit(solution)/shard_map/ppermute | solution.py:28
  12.6 2.6 %collective-permute-start.4 = (bf16[16,1536]{1,0:T(8,128)(2,1)S(1)}, bf16[16,1536]{1,0:T(8,128)(2,1)S(1)}, u32[]{:S(2)}, u32[]{:S(2)}) collective-permute-start(bf16[16,1536]{1,0:T(8,128)(2,1)S(1)} %get-tuple-element.19), channel_id=1, source_target_pairs={{0,16},{8,24},{16,0},{24,8},{1,17},{9,25},{17,1},{25,9},{2,18},{10... | collective-permute-start | bytes 147464 | tf_op jit(solution)/shard_map/ppermute | solution.py:28
  15.2 1.3 %collective-permute-start.5 = (bf16[16,1536]{1,0:T(8,128)(2,1)S(1)}, bf16[16,1536]{1,0:T(8,128)(2,1)S(1)}, u32[]{:S(2)}, u32[]{:S(2)}) collective-permute-start(bf16[16,1536]{1,0:T(8,128)(2,1)S(1)} %get-tuple-element.20), channel_id=1, source_target_pairs={{0,24},{8,0},{16,8},{24,16},{1,25},{9,1},{17,9},{25,17},{2,26},{10... | collective-permute-start | bytes 147464 | tf_op jit(solution)/shard_map/ppermute | solution.py:28
  16.5 0.6 %collective-permute-done.3.after_ref = bf16[16,1536]{1,0:T(8,128)(2,1)S(1)} collective-permute-done((bf16[16,1536]{1,0:T(8,128)(2,1)S(1)}, bf16[16,1536]{1,0:T(8,128)(2,1)S(1)}, u32[]{:S(2)}, u32[]{:S(2)}) %collective-permute-start.3) | collective-permute-done | bytes 49184 | tf_op jit(solution)/shard_map/ppermute | solution.py:28
  17.1 2.1 %collective-permute-done.4 = bf16[16,1536]{1,0:T(8,128)(2,1)S(1)} collective-permute-done((bf16[16,1536]{1,0:T(8,128)(2,1)S(1)}, bf16[16,1536]{1,0:T(8,128)(2,1)S(1)}, u32[]{:S(2)}, u32[]{:S(2)}) %collective-permute-start.4) | collective-permute-done | bytes 49184 | tf_op jit(solution)/shard_map/ppermute | solution.py:28
  19.2 0.3 collective-permute-done.5
  19.5 1.6 %collective-permute-start.6 = (bf16[3,16,1536]{2,1,0:T(8,128)(2,1)S(1)}, bf16[3,16,1536]{2,1,0:T(8,128)(2,1)S(1)}, u32[]{:S(2)}, u32[]{:S(2)}) collective-permute-start(bf16[3,16,1536]{2,1,0:T(8,128)(2,1)S(1)} %pad_maximum_fusion.2.refs_0_), channel_id=1, source_target_pairs={{0,1},{1,0},{2,3},{3,2},{4,5},{5,4},{6,7},{7,6},{8,9},{9,8},{10,11... | collective-permute-start | bytes 442376 | tf_op jit(solution)/shard_map/ppermute | solution.py:28
  21.1 2.3 %factor.1.factor_ref = bf16[32,2048]{1,0:T(8,128)(2,1)S(1)} custom-call(bf16[16,1536]{1,0:T(8,128)(2,1)S(1)} %collective-permute-done.3.after_ref, f32[1,1,4,8]{3,2,1,0:T(4,128)S(1)} %get-tuple-element.15.after_ref.gates_ref, bf16[32,6144]{1,0:T(8,128)(2,1)S(1)} %pad_maximum_fusion.1.rows_ref.own_ref, ...), custom_call_target="tpu_custom_call" | custom-call | flops 402653184 | bytes 12582912 | tf_op jit(solution)/shard_map/factor/pallas_call | solution.py:231
  23.4 2.9 %collective-permute-start.9 = (bf16[32,2048]{1,0:T(8,128)(2,1)S(1)}, bf16[32,2048]{1,0:T(8,128)(2,1)S(1)}, u32[]{:S(2)}, u32[]{:S(2)}) collective-permute-start(bf16[32,2048]{1,0:T(8,128)(2,1)S(1)} %factor.1.factor_ref), channel_id=1, source_target_pairs={{0,24},{8,0},{16,8},{24,16},{1,25},{9,1},{17,9},{25,17},{2,26},{10... | collective-permute-start | bytes 393224 | tf_op jit(solution)/shard_map/ppermute | solution.py:28
  26.3 0.0 collective-permute-start.8
  26.3 0.6 %collective-permute-start.7 = (bf16[32,2048]{1,0:T(8,128)(2,1)S(1)}, bf16[32,2048]{1,0:T(8,128)(2,1)S(1)}, u32[]{:S(2)}, u32[]{:S(2)}) collective-permute-start(bf16[32,2048]{1,0:T(8,128)(2,1)S(1)} %factor.1.factor_ref), channel_id=1, source_target_pairs={{0,8},{8,16},{16,24},{24,0},{1,9},{9,17},{17,25},{25,1},{2,10},{10... | collective-permute-start | bytes 393224 | tf_op jit(solution)/shard_map/ppermute | solution.py:28
  27.0 0.0 collective-permute-done.6.refs_1_
  27.0 2.6 %piece.1 = bf16[8,8,1536]{2,1,0:T(8,128)(2,1)} custom-call(bf16[32,2048]{1,0:T(8,128)(2,1)S(1)} %factor.1.factor_ref, bf16[1,3072,1024]{2,1,0:T(8,128)(2,1)S(1)} %get-tuple-element.17.upper_ref, bf16[3,16,1536]{2,1,0:T(8,128)(2,1)S(1)} %pad_maximum_fusion.2.refs_0_, bf16[3,16,1536]{2,1,0:T(8,128)(2,1)S(1)} %collective-permute-done.6.refs_1_), custom_call_target="tpu_custom_call" | custom-call | flops 201326592 | bytes 6291456 | tf_op jit(solution)/shard_map/piece/pallas_call | solution.py:247
  29.6 3.4 %all-to-all-start = ((bf16[8,8,1536]{2,1,0:T(8,128)(2,1)}), bf16[8,8,1536]{2,1,0:T(8,128)(2,1)S(1)}, u32[]{:S(2)}, u32[]{:S(2)}) async-start(bf16[8,8,1536]{2,1,0:T(8,128)(2,1)} %piece.1), calls=%async_computation | async-start | bytes 393216 | tf_op jit(solution)/shard_map/all_to_all | solution.py:258
  33.0 0.0 collective-permute-done.9
  33.0 4.7 %collective-permute-done.8 = bf16[32,2048]{1,0:T(8,128)(2,1)S(1)} collective-permute-done((bf16[32,2048]{1,0:T(8,128)(2,1)S(1)}, bf16[32,2048]{1,0:T(8,128)(2,1)S(1)}, u32[]{:S(2)}, u32[]{:S(2)}) %collective-permute-start.8) | collective-permute-done | bytes 131104 | tf_op jit(solution)/shard_map/ppermute | solution.py:28
  37.7 0.0 collective-permute-done.7
  37.8 3.2 %weight.1 = (f32[1,768,1024]{2,1,0:T(8,128)}, f32[1,768,1024]{2,1,0:T(8,128)}) custom-call(bf16[32,6144]{1,0:T(8,128)(2,1)S(1)} %pad_maximum_fusion.1.rows_ref.own_ref, bf16[3,16,1536]{2,1,0:T(8,128)(2,1)S(1)} %pad_maximum_fusion.2.refs_0_, bf16[3,16,1536]{2,1,0:T(8,128)(2,1)S(1)} %collective-permute-done.6.refs_1_, ...), custom_call_target="tpu_custom_call" | custom-call | flops 402653184 | bytes 50331648 | tf_op jit(solution)/shard_map/weight/pallas_call | solution.py:267
  40.9 0.0 all-to-all-done
  40.9 0.9 %fusion = bf16[1,64,1536]{2,1,0:T(8,128)(2,1)} fusion(bf16[64,64]{1,0:T(8,128)(2,1)S(1)} %get-tuple-element.13, bf16[8,8,1536]{2,1,0:T(8,128)(2,1)S(1)} %all-to-all-done), kind=kOutput, calls=%fused_computation.1 | convolution fusion | flops 12681216 | bytes 401408 | tf_op jit(solution)/shard_map/dot_general | solution.py:259
  (5 shorter events, 0.1 us)
Async XLA Ops:
  2.1 7.9 %collective-permute-start.2 = (bf16[8,6144]{1,0:T(8,128)(2,1)S(1)}, bf16[8,6144]{1,0:T(8,128)(2,1)S(1)}, u32[]{:S(2)}, u32[]{:S(2)}) collective-permute-start(bf16[8,6144]{1,0:T(8,128)(2,1)S(1)} %get-tuple-element.24), channel_id=1, source_target_pairs={{0,6},{2,0},{4,2},{6,4},{1,7},{3,1},{5,3},{7,5},{8,14},{10,8},{12,... | collective-permute-start | bytes 294920 | tf_op jit(solution)/shard_map/ppermute | solution.py:28
  4.6 6.1 %collective-permute-start.1 = (bf16[8,6144]{1,0:T(8,128)(2,1)S(1)}, bf16[8,6144]{1,0:T(8,128)(2,1)S(1)}, u32[]{:S(2)}, u32[]{:S(2)}) collective-permute-start(bf16[8,6144]{1,0:T(8,128)(2,1)S(1)} %get-tuple-element.25), channel_id=1, source_target_pairs={{0,4},{2,6},{4,0},{6,2},{1,5},{3,7},{5,1},{7,3},{8,12},{10,14},{12... | collective-permute-start | bytes 294920 | tf_op jit(solution)/shard_map/ppermute | solution.py:28
  5.2 5.5 %collective-permute-start = (bf16[8,6144]{1,0:T(8,128)(2,1)S(1)}, bf16[8,6144]{1,0:T(8,128)(2,1)S(1)}, u32[]{:S(2)}, u32[]{:S(2)}) collective-permute-start(bf16[8,6144]{1,0:T(8,128)(2,1)S(1)} %get-tuple-element.26), channel_id=1, source_target_pairs={{0,2},{2,4},{4,6},{6,0},{1,3},{3,5},{5,7},{7,1},{8,10},{10,12},{12... | collective-permute-start | bytes 294920 | tf_op jit(solution)/shard_map/ppermute | solution.py:28
  10.8 6.3 %collective-permute-start.3 = (bf16[16,1536]{1,0:T(8,128)(2,1)S(1)}, bf16[16,1536]{1,0:T(8,128)(2,1)S(1)}, u32[]{:S(2)}, u32[]{:S(2)}) collective-permute-start(bf16[16,1536]{1,0:T(8,128)(2,1)S(1)} %get-tuple-element.16), channel_id=1, source_target_pairs={{0,8},{8,16},{16,24},{24,0},{1,9},{9,17},{17,25},{25,1},{2,10},{10... | collective-permute-start | bytes 147464 | tf_op jit(solution)/shard_map/ppermute | solution.py:28
  12.6 6.6 %collective-permute-start.4 = (bf16[16,1536]{1,0:T(8,128)(2,1)S(1)}, bf16[16,1536]{1,0:T(8,128)(2,1)S(1)}, u32[]{:S(2)}, u32[]{:S(2)}) collective-permute-start(bf16[16,1536]{1,0:T(8,128)(2,1)S(1)} %get-tuple-element.19), channel_id=1, source_target_pairs={{0,16},{8,24},{16,0},{24,8},{1,17},{9,25},{17,1},{25,9},{2,18},{10... | collective-permute-start | bytes 147464 | tf_op jit(solution)/shard_map/ppermute | solution.py:28
  15.2 4.4 %collective-permute-start.5 = (bf16[16,1536]{1,0:T(8,128)(2,1)S(1)}, bf16[16,1536]{1,0:T(8,128)(2,1)S(1)}, u32[]{:S(2)}, u32[]{:S(2)}) collective-permute-start(bf16[16,1536]{1,0:T(8,128)(2,1)S(1)} %get-tuple-element.20), channel_id=1, source_target_pairs={{0,24},{8,0},{16,8},{24,16},{1,25},{9,1},{17,9},{25,17},{2,26},{10... | collective-permute-start | bytes 147464 | tf_op jit(solution)/shard_map/ppermute | solution.py:28
  19.5 7.4 %collective-permute-start.6 = (bf16[3,16,1536]{2,1,0:T(8,128)(2,1)S(1)}, bf16[3,16,1536]{2,1,0:T(8,128)(2,1)S(1)}, u32[]{:S(2)}, u32[]{:S(2)}) collective-permute-start(bf16[3,16,1536]{2,1,0:T(8,128)(2,1)S(1)} %pad_maximum_fusion.2.refs_0_), channel_id=1, source_target_pairs={{0,1},{1,0},{2,3},{3,2},{4,5},{5,4},{6,7},{7,6},{8,9},{9,8},{10,11... | collective-permute-start | bytes 442376 | tf_op jit(solution)/shard_map/ppermute | solution.py:28
  23.4 9.6 %collective-permute-start.9 = (bf16[32,2048]{1,0:T(8,128)(2,1)S(1)}, bf16[32,2048]{1,0:T(8,128)(2,1)S(1)}, u32[]{:S(2)}, u32[]{:S(2)}) collective-permute-start(bf16[32,2048]{1,0:T(8,128)(2,1)S(1)} %factor.1.factor_ref), channel_id=1, source_target_pairs={{0,24},{8,0},{16,8},{24,16},{1,25},{9,1},{17,9},{25,17},{2,26},{10... | collective-permute-start | bytes 393224 | tf_op jit(solution)/shard_map/ppermute | solution.py:28
  26.3 11.4 %collective-permute-start.8 = (bf16[32,2048]{1,0:T(8,128)(2,1)S(1)}, bf16[32,2048]{1,0:T(8,128)(2,1)S(1)}, u32[]{:S(2)}, u32[]{:S(2)}) collective-permute-start(bf16[32,2048]{1,0:T(8,128)(2,1)S(1)} %factor.1.factor_ref), channel_id=1, source_target_pairs={{0,16},{8,24},{16,0},{24,8},{1,17},{9,25},{17,1},{25,9},{2,18},{10... | collective-permute-start | bytes 393224 | tf_op jit(solution)/shard_map/ppermute | solution.py:28
  26.3 11.4 %collective-permute-start.7 = (bf16[32,2048]{1,0:T(8,128)(2,1)S(1)}, bf16[32,2048]{1,0:T(8,128)(2,1)S(1)}, u32[]{:S(2)}, u32[]{:S(2)}) collective-permute-start(bf16[32,2048]{1,0:T(8,128)(2,1)S(1)} %factor.1.factor_ref), channel_id=1, source_target_pairs={{0,8},{8,16},{16,24},{24,0},{1,9},{9,17},{17,25},{25,1},{2,10},{10... | collective-permute-start | bytes 393224 | tf_op jit(solution)/shard_map/ppermute | solution.py:28
  29.6 11.3 %all-to-all-start = ((bf16[8,8,1536]{2,1,0:T(8,128)(2,1)}), bf16[8,8,1536]{2,1,0:T(8,128)(2,1)S(1)}, u32[]{:S(2)}, u32[]{:S(2)}) async-start(bf16[8,8,1536]{2,1,0:T(8,128)(2,1)} %piece.1), calls=%async_computation | async-start | bytes 393216 | tf_op jit(solution)/shard_map/all_to_all | solution.py:258

commit v6 on v5

--- a/solution.py
+++ b/solution.py
@@ -39,8 +39,8 @@
     return jnp.concatenate(out, axis=0)
 
 
-def pick_kernel(n_hid, picks_hbm, tokens_hbm, upstream_hbm, rows_ref, spread_ref, *refs):
-    picks_ref, tokens_ref, upstream_ref, sems = refs
+def pick_kernel(n_hid, n_share, picks_hbm, tokens_hbm, upstream_hbm, rows_ref, spread_ref, *refs):
+    *side_refs, picks_ref, tokens_ref, upstream_ref, sems = refs
     n_exp = picks_ref.shape[2]
     tok_dev, width = tokens_ref.shape[1:]
     copies = [
@@ -65,37 +65,44 @@
         rows_ref[:, at : at + width] = jnp.dot(
             selector, source[0], preferred_element_type=jnp.float32
         ).astype(jnp.bfloat16)
-
-
-def cut_kernel(after_ref, rows_ref, *out_refs):
-    n_dp = len(out_refs) + 1
-    share, wide = out_refs[0].shape
-    cols = wide // 2
-    width = rows_ref.shape[1] // 2
+    n_dp = len(side_refs) + 1
+    cols = width // n_dp
+    span = side_refs[0].shape[1]
     my_dp = lax.axis_index("dp")
-    spot = pl.ds(pl.multiple_of(lax.axis_index("hidden") * share, 16), share)
-    for s, out_ref in enumerate(out_refs):
-        at = ((my_dp + s + 1) % n_dp) * cols
-        for half in range(2):
-            out_ref[:, half * cols : (half + 1) * cols] = rows_ref[
-                spot, pl.ds(pl.multiple_of(half * width + at, 128), cols)
+    if n_share == 1:
+        starts = [0, width]
+    else:
+        per_half = n_share // 2
+        share = lax.axis_index("hidden")
+        starts = [(share // per_half) * width + (share % per_half) * span]
+    wide = span // len(starts)
+    for s in range(1, n_dp):
+        at = ((my_dp + s) % n_dp) * cols
+        for k, start in enumerate(starts):
+            side_refs[s - 1][:, k * wide : (k + 1) * wide] = rows_ref[
+                :, pl.ds(pl.multiple_of(start + at, 128), wide)
             ]
 
 
-def load_kernel(after_ref, gates_hbm, upper_hbm, lower_hbm, gates_ref, upper_ref, lower_ref, sems):
-    copies = [
-        pltpu.make_async_copy(source, target, sems.at[k])
-        for k, (source, target) in enumerate(
-            ((gates_hbm, gates_ref), (upper_hbm, upper_ref), (lower_hbm, lower_ref))
-        )
-    ]
+def load_kernel(chunks, after_ref, gates_hbm, upper_hbm, lower_hbm, gates_ref, upper_ref, lower_ref, sems):
+    step = upper_ref.shape[1] // chunks
+    copies = [pltpu.make_async_copy(gates_hbm, gates_ref, sems.at[2 * chunks])]
+    for k, (source, target) in enumerate(((upper_hbm, upper_ref), (lower_hbm, lower_ref))):
+        for c in range(chunks):
+            spot = pl.ds(c * step, step)
+            copies.append(
+                pltpu.make_async_copy(
+                    source.at[:, spot, :], target.at[:, spot, :], sems.at[k * chunks + c]
+                )
+            )
     for copy in copies:
         copy.start()
     for copy in copies:
         copy.wait()
 
 
-def factor_kernel(after_ref, gates_ref, rows_ref, upper_ref, lower_ref, out_ref):
+def factor_kernel(gates_ref, rows_ref, upper_ref, lower_ref, *refs):
+    out_ref = refs[-1]
     n_exp = gates_ref.shape[2]
     width, units = upper_ref.shape[1:]
     me = lax.axis_index("expert")
@@ -108,41 +115,59 @@
 
 
 def piece_kernel(n_hid, factor_ref, upper_ref, *refs):
-    out_ref = refs[-1]
-    n_pick, part = out_ref.shape[1:]
+    *side_refs, out_ref = refs
+    n_pick = out_ref.shape[1]
     width, units = upper_ref.shape[1:]
+    part = width // n_hid
+    span = side_refs[0].shape[1]
     n_exp = out_ref.shape[0] // n_hid
     me = lax.axis_index("expert")
+    for k, side in enumerate(side_refs):
+        rows = side[...].astype(jnp.float32)
+        for s in range(n_exp):
+            block = rows[s * n_pick : (s + 1) * n_pick].astype(jnp.bfloat16)
+            owner = ((me + s) % n_exp) * n_hid
+            for h in range(n_hid):
+                out_ref[owner + h, :, part + k * span : part + (k + 1) * span] = block
     piece = lax.dot_general(
         factor_ref[:, :units], upper_ref[0], (((1,), (1,)), ((), ())), preferred_element_type=jnp.float32
     )
     for s in range(n_exp):
         owner = ((me + n_exp - s) % n_exp) * n_hid
         for h in range(n_hid):
-            out_ref[owner + h] = piece[
+            out_ref[owner + h, :, :part] = piece[
                 s * n_pick : (s + 1) * n_pick, h * part : (h + 1) * part
             ].astype(jnp.bfloat16)
 
 
-def weight_kernel(chunks, shape, own_ref, *refs):
-    n_dp, n_hid = shape
-    part_refs, refs = refs[:n_hid], refs[n_hid:]
-    factor_ref, up_ref, down_ref, side_ref, held, sems = refs
+def weight_kernel(chunks, n_dp, n_share, after_ref, own_ref, came_ref, factor_ref, *refs):
+    up_ref, down_ref, side_ref, held, sems = refs
+    slots = own_ref.shape[0]
+    width = own_ref.shape[1] // 2
     units = factor_ref.shape[1] // 2
     cols = side_ref.shape[1] // 2
-    width = own_ref.shape[1] // 2
-    slots = own_ref.shape[0]
-    rows = slots // n_hid
-    my_hid = lax.axis_index("hidden")
+    span = 2 * cols // n_share
+    n_pick = came_ref.shape[1]
+    n_exp = slots // n_pick
+    n_hid = came_ref.shape[0] // n_exp
+    part = width // n_hid
+    me = lax.axis_index("expert")
     start = lax.axis_index("dp") * cols
     for half in range(2):
         side_ref[:slots, half * cols : (half + 1) * cols] = own_ref[
             :, pl.ds(pl.multiple_of(half * width + start, 128), cols)
         ]
-    for t, part in enumerate(part_refs):
-        spot = ((my_hid + n_hid - t) % n_hid) * rows
+    for t in range(n_share):
+        sender = lax.axis_index("hidden") if n_share == 1 else t
         for s in range(1, n_dp):
-            side_ref[pl.ds(pl.multiple_of(s * slots + spot, 16), rows), :] = part[s - 1]
+            spot = part + (s - 1) * span
+            blocks = [
+                came_ref[((me + n_exp - b) % n_exp) * n_hid + sender, :, spot : spot + span].astype(jnp.float32)
+                for b in range(n_exp)
+            ]
+            side_ref[s * slots : (s + 1) * slots, t * span : (t + 1) * span] = jnp.concatenate(
+                blocks, axis=0
+            ).astype(jnp.bfloat16)
     step = units // chunks
     copies = []
     for which, out in ((0, up_ref), (1, down_ref)):
@@ -184,14 +209,17 @@
         for x in (layer_input, grad_out, picks, gates, w_up, w_down)
     )
 
-    send, spread = pl.pallas_call(
-        functools.partial(pick_kernel, n_hid),
+    n_share = n_hid if n_hid % 2 == 0 and 2 * cols % (n_hid * 128) == 0 else 1
+    span = 2 * cols // n_share
+    send, spread, *side = pl.pallas_call(
+        functools.partial(pick_kernel, n_hid, n_share),
         out_shape=[
             jax.ShapeDtypeStruct((slots, 2 * width), bf16),
             jax.ShapeDtypeStruct((slots * n_hid, tok_dev), bf16),
-        ],
+        ]
+        + [jax.ShapeDtypeStruct((slots, span), bf16)] * (n_dp - 1),
         in_specs=[HBM] * 3,
-        out_specs=[VMEM] * 2,
+        out_specs=[VMEM] * (n_dp + 1),
         scratch_shapes=[
             pltpu.VMEM(picks.shape, jnp.int32),
             pltpu.VMEM(layer_input.shape, bf16),
@@ -205,69 +233,61 @@
     rows = jnp.concatenate(
         [hop(send[s * n_pick : (s + 1) * n_pick], "expert", s) for s in range(n_exp)], axis=0
     )
+    side = [hop(x, "dp", s + 1) for s, x in enumerate(side)]
+
+    splits = 4
     gate_held, upper, lower = pl.pallas_call(
-        load_kernel,
+        functools.partial(load_kernel, splits),
         out_shape=[jax.ShapeDtypeStruct(x.shape, x.dtype) for x in (gates, w_up, w_down)],
         in_specs=[HBM] * 4,
         out_specs=[VMEM] * 3,
-        scratch_shapes=[pltpu.SemaphoreType.DMA((3,))],
+        scratch_shapes=[pltpu.SemaphoreType.DMA((2 * splits + 1,))],
+        compiler_params=ROOM,
         cost_estimate=pl.CostEstimate(
             flops=0, bytes_accessed=4 * w_up.size + 4 * w_down.size, transcendentals=0
         ),
-        compiler_params=ROOM,
         name="load",
     )(send, gates, w_up, w_down)
-    share = slots // n_hid
-    parts = pl.pallas_call(
-        cut_kernel,
-        out_shape=[jax.ShapeDtypeStruct((share, 2 * cols), bf16)] * (n_dp - 1),
-        in_specs=[ANY, VMEM],
-        out_specs=[VMEM] * (n_dp - 1),
-        compiler_params=ROOM,
-        name="cut",
-    )(gate_held, rows)
-    parts = [hop(x, "dp", s + 1) for s, x in enumerate(parts)]
-
     factors = pl.pallas_call(
         factor_kernel,
         out_shape=jax.ShapeDtypeStruct((slots, 2 * units), bf16),
-        in_specs=[ANY] + [VMEM] * 4,
+        in_specs=[VMEM] * 4 + [ANY] * (n_dp - 2),
         out_specs=VMEM,
         compiler_params=ROOM,
         cost_estimate=pl.CostEstimate(
             flops=4 * slots * w_up.size, bytes_accessed=4 * w_up.size, transcendentals=slots * units
         ),
         name="factor",
-    )(parts[0], gate_held, rows, upper, lower)
-    parts = jnp.stack(parts)
-    parts = [hop(parts, "hidden", t) for t in range(n_hid)]
+    )(gate_held, rows, upper, lower, *side[:-1])
 
     gathered = jnp.concatenate([hop(factors, "dp", s) for s in range(n_dp)], axis=0)
 
     piece = pl.pallas_call(
         functools.partial(piece_kernel, n_hid),
-        out_shape=jax.ShapeDtypeStruct((n_exp * n_hid, n_pick, part), bf16),
-        in_specs=[VMEM, VMEM] + [ANY] * n_hid,
+        out_shape=jax.ShapeDtypeStruct((n_exp * n_hid, n_pick, part + (n_dp - 1) * span), bf16),
+        in_specs=[VMEM] * (n_dp + 1),
         out_specs=VMEM,
         compiler_params=ROOM,
         cost_estimate=pl.CostEstimate(
             flops=2 * slots * w_up.size, bytes_accessed=2 * w_up.size, transcendentals=0
         ),
         name="piece",
-    )(factors, upper, *parts)
-    returned = lax.all_to_all(piece, ("expert", "hidden"), 0, 0)
+    )(factors, upper, *side)
+    returned = lax.all_to_all(
+        piece.transpose(1, 0, 2), ("expert", "hidden"), split_axis=1, concat_axis=1, tiled=True
+    ).transpose(1, 0, 2)
     grad_rows = lax.dot_general(
         spread,
-        returned.reshape(slots * n_hid, part),
+        returned[:, :, :part].reshape(slots * n_hid, part),
         (((0,), (0,)), ((), ())),
         preferred_element_type=jnp.float32,
     ).astype(bf16)
 
     chunks = max(1, units // 256)
     grads = pl.pallas_call(
-        functools.partial(weight_kernel, chunks, (n_dp, n_hid)),
+        functools.partial(weight_kernel, chunks, n_dp, n_share),
         out_shape=[jax.ShapeDtypeStruct((1, cols, units), jnp.float32)] * 2,
-        in_specs=[VMEM] * (n_hid + 2),
+        in_specs=[ANY] + [VMEM] * 3,
         out_specs=[HBM] * 2,
         scratch_shapes=[
             pltpu.VMEM((n_dp * slots, 2 * cols), bf16),
@@ -275,11 +295,8 @@
             pltpu.SemaphoreType.DMA((2, chunks)),
         ],
         compiler_params=ROOM,
-        cost_estimate=pl.CostEstimate(
-            flops=4 * n_dp * slots * cols * units, bytes_accessed=64 * cols * units, transcendentals=0
-        ),
         name="weight",
-    )(rows, *parts, gathered)
+    )(grad_rows, rows, returned, gathered)
     return (grad_rows[None], *grads)
 
 

time: 42.1 us -> 43.9 us (1.043)
  waiting for transfers between devices: 8.37 us -> 12.1 us
  starting transfers between devices: 17.5 us -> 16.2 us
  matrix products: 0.91 us -> 0.22 us
    ppermute x10 -> x9, waiting for transfers between devices: 8.37 us -> 12.1 us  [hop(): return lax.ppermute(x, axis, [(i, (i + step) % n) for i in range(n)])]
    ppermute x10 -> x9, starting transfers between devices: 14.1 us -> 12.7 us  [hop(): return lax.ppermute(x, axis, [(i, (i + step) % n) for i in range(n)])]
    dot_general x1, matrix products: 0.91 us -> 0.22 us  [local(): lax.dot_general(spread, returned[:, :, :part].reshape(slots * n_hid, part...]
    pallas_call x4 -> x3, Pallas kernels: 9.25 us -> 9.31 us  [the longest x1 4.72 us: local(): pl.pallas_call(functools.partial(load_kernel, splits), out_shape=[jax.Sha...]
  transfers between devices with their start and end apart: 11 -> 10, of which waited for: 5 -> 3; matrix products, arithmetic and copies ran while one was open for 0% -> 0% of each run, Pallas kernels for 30% -> 16%
where the time goes in v6:
time: 43.9 us; the launch traced here: 43.6 us
  starting transfers between devices  16.2 us (37%)
  Pallas kernels  14.3 us (33%)
  waiting for transfers between devices  12.1 us (28%)
  between operations  0.74 us (2%)
    ppermute x9, starting transfers between devices, hop(): return lax.ppermute(x, axis, [(i, (i + step) % n) for i in range(n)])  12.7 us
    ppermute x9, waiting for transfers between devices, hop(): return lax.ppermute(x, axis, [(i, (i + step) % n) for i in range(n)])  12.1 us
    pallas_call x1, Pallas kernels, local(): pl.pallas_call(functools.partial(load_kernel, splits), out_shape=[jax.Sha...  4.72 us
    all_to_all x1, starting transfers between devices, local(): lax.all_to_all(piece.transpose(1, 0, 2), ('expert', 'hidden'), split_axis...  3.48 us
    pallas_call x1, Pallas kernels, local(): pl.pallas_call(functools.partial(weight_kernel, chunks, n_dp, n_share), o...  3.16 us
    pallas_call x1, Pallas kernels, local(): pl.pallas_call(functools.partial(piece_kernel, n_hid), out_shape=jax.Shap...  2.73 us
    pallas_call x1, Pallas kernels, local(): pl.pallas_call(factor_kernel, out_shape=jax.ShapeDtypeStruct((slots, 2 *...  2.29 us
    pallas_call x1, Pallas kernels, local(): pl.pallas_call(functools.partial(pick_kernel, n_hid, n_share), out_shape=...  1.44 us
  transfers between devices with their start and end apart: 10, of which 3 were waited for; matrix products, arithmetic and copies ran while one was open for 0% of the time, Pallas kernels for 16%

profile of v6, /device:TPU:0, one launch (start us, length us, event | category | flops | bytes accessed | tf_op | source)
XLA Modules:
  0.0 43.6 jit_solution(2663151041396607172)
XLA Ops:
  0.6 1.4 %pick.1 = (bf16[32,6144]{1,0:T(8,128)(2,1)S(1)}, bf16[64,64]{1,0:T(8,128)(2,1)S(1)}, bf16[32,768]{1,0:T(8,128)(2,1)S(1)}, bf16[32,768]{1,0:T(8,128)(2,1)S(1)}, bf16[32,768]{1,0:T(8,128)(2,1)S(1)}) custom-call(s32[1,1,4,8]{3,2,1,0:T(4,128)} %picks_hbm.1, bf16[1,64,3072]{2,1,0:T(8,128)(2,1)} %tokens_hbm.1, bf16[1,64,3072]{2,1,0:T(8,128)(2,1)} %upstream_hbm.1), custom_call_target="tpu_custom_call" | custom-call | tf_op jit(solution)/shard_map/pick/pallas_call | solution.py:214
  2.1 2.5 %collective-permute-start.2 = (bf16[8,6144]{1,0:T(8,128)(2,1)S(1)}, bf16[8,6144]{1,0:T(8,128)(2,1)S(1)}, u32[]{:S(2)}, u32[]{:S(2)}) collective-permute-start(bf16[8,6144]{1,0:T(8,128)(2,1)S(1)} %get-tuple-element.24), channel_id=1, source_target_pairs={{0,6},{2,0},{4,2},{6,4},{1,7},{3,1},{5,3},{7,5},{8,14},{10,8},{12,... | collective-permute-start | bytes 294920 | tf_op jit(solution)/shard_map/ppermute | solution.py:28
  4.6 0.6 %collective-permute-start.1 = (bf16[8,6144]{1,0:T(8,128)(2,1)S(1)}, bf16[8,6144]{1,0:T(8,128)(2,1)S(1)}, u32[]{:S(2)}, u32[]{:S(2)}) collective-permute-start(bf16[8,6144]{1,0:T(8,128)(2,1)S(1)} %get-tuple-element.25), channel_id=1, source_target_pairs={{0,4},{2,6},{4,0},{6,2},{1,5},{3,7},{5,1},{7,3},{8,12},{10,14},{12... | collective-permute-start | bytes 294920 | tf_op jit(solution)/shard_map/ppermute | solution.py:28
  5.2 0.2 collective-permute-start
  5.4 1.6 %collective-permute-start.3 = (bf16[32,768]{1,0:T(8,128)(2,1)S(1)}, bf16[32,768]{1,0:T(8,128)(2,1)S(1)}, u32[]{:S(2)}, u32[]{:S(2)}) collective-permute-start(bf16[32,768]{1,0:T(8,128)(2,1)S(1)} %get-tuple-element.18), channel_id=1, source_target_pairs={{0,8},{8,16},{16,24},{24,0},{1,9},{9,17},{17,25},{25,1},{2,10},{10... | collective-permute-start | bytes 147464 | tf_op jit(solution)/shard_map/ppermute | solution.py:28
  7.0 2.6 %collective-permute-start.4 = (bf16[32,768]{1,0:T(8,128)(2,1)S(1)}, bf16[32,768]{1,0:T(8,128)(2,1)S(1)}, u32[]{:S(2)}, u32[]{:S(2)}) collective-permute-start(bf16[32,768]{1,0:T(8,128)(2,1)S(1)} %get-tuple-element.19), channel_id=1, source_target_pairs={{0,16},{8,24},{16,0},{24,8},{1,17},{9,25},{17,1},{25,9},{2,18},{10... | collective-permute-start | bytes 147464 | tf_op jit(solution)/shard_map/ppermute | solution.py:28
  9.5 4.7 %load.1 = (f32[1,1,4,8]{3,2,1,0:T(4,128)S(1)}, bf16[1,3072,1024]{2,1,0:T(8,128)(2,1)S(1)}, bf16[1,3072,1024]{2,1,0:T(8,128)(2,1)S(1)}) custom-call(bf16[32,6144]{1,0:T(8,128)(2,1)S(1)} %get-tuple-element.14.after_ref, f32[1,1,4,8]{3,2,1,0:T(4,128)} %gates_hbm.1, bf16[1,3072,1024]{2,1,0:T(8,128)(2,1)} %upper_hbm.1, bf16[1,3072,1024]{2,1,0:T(8,128)(2,1)} %lower_hbm.1), custom_call_target="tpu_custom_call" | custom-call | bytes 25165824 | tf_op jit(solution)/shard_map/load/pallas_call | solution.py:239
  14.3 0.0 collective-permute-done.2
  14.3 1.4 %collective-permute-start.5 = (bf16[32,768]{1,0:T(8,128)(2,1)S(1)}, bf16[32,768]{1,0:T(8,128)(2,1)S(1)}, u32[]{:S(2)}, u32[]{:S(2)}) collective-permute-start(bf16[32,768]{1,0:T(8,128)(2,1)S(1)} %get-tuple-element.20), channel_id=1, source_target_pairs={{0,24},{8,0},{16,8},{24,16},{1,25},{9,1},{17,9},{25,17},{2,26},{10... | collective-permute-start | bytes 147464 | tf_op jit(solution)/shard_map/ppermute | solution.py:28
  15.7 0.0 collective-permute-done.1
  15.7 0.0 collective-permute-done
  15.7 0.0 collective-permute-done.3.refs_0_
  15.7 0.0 collective-permute-done.4.refs_1_
  15.7 2.3 %factor.1.factor_ref = bf16[32,2048]{1,0:T(8,128)(2,1)S(1)} custom-call(f32[1,1,4,8]{3,2,1,0:T(4,128)S(1)} %get-tuple-element.15.gates_ref, bf16[32,6144]{1,0:T(8,128)(2,1)S(1)} %pad_maximum_fusion.1.rows_ref.own_ref, bf16[1,3072,1024]{2,1,0:T(8,128)(2,1)S(1)} %get-tuple-element.16.upper_ref, bf16[1,3072,1024]{2,1,0:T(8,128)(2,1)S(1)} %get-tuple-element.17.lower_ref, ...), custom_call_target="tpu_custom_call" | custom-call | flops 402653184 | bytes 12582912 | tf_op jit(solution)/shard_map/factor/pallas_call | solution.py:251
  18.0 0.7 %collective-permute-done.5.refs_2_ = bf16[32,768]{1,0:T(8,128)(2,1)S(1)} collective-permute-done((bf16[32,768]{1,0:T(8,128)(2,1)S(1)}, bf16[32,768]{1,0:T(8,128)(2,1)S(1)}, u32[]{:S(2)}, u32[]{:S(2)}) %collective-permute-start.5) | collective-permute-done | bytes 49184 | tf_op jit(solution)/shard_map/ppermute | solution.py:28
  18.8 2.7 %piece.1 = bf16[8,8,3840]{2,1,0:T(8,128)(2,1)} custom-call(bf16[32,2048]{1,0:T(8,128)(2,1)S(1)} %factor.1.factor_ref, bf16[1,3072,1024]{2,1,0:T(8,128)(2,1)S(1)} %get-tuple-element.16.upper_ref, bf16[32,768]{1,0:T(8,128)(2,1)S(1)} %collective-permute-done.3.refs_0_, bf16[32,768]{1,0:T(8,128)(2,1)S(1)} %collective-permute-done.4.refs_1_, ...), custom_call_target="tpu_custom_call" | custom-call | flops 201326592 | bytes 6291456 | tf_op jit(solution)/shard_map/piece/pallas_call | solution.py:265
  21.5 3.5 %all-to-all-start = ((bf16[8,8,3840]{2,0,1:T(8,128)(2,1)}), bf16[8,8,3840]{2,0,1:T(8,128)(2,1)S(1)}, u32[]{:S(2)}, u32[]{:S(2)}) async-start(bf16[8,8,3840]{2,0,1:T(8,128)(2,1)} %bitcast), calls=%async_computation | async-start | bytes 983040 | tf_op jit(solution)/shard_map/all_to_all | solution.py:276
  25.0 3.2 %collective-permute-start.8 = (bf16[32,2048]{1,0:T(8,128)(2,1)S(1)}, bf16[32,2048]{1,0:T(8,128)(2,1)S(1)}, u32[]{:S(2)}, u32[]{:S(2)}) collective-permute-start(bf16[32,2048]{1,0:T(8,128)(2,1)S(1)} %factor.1.factor_ref), channel_id=1, source_target_pairs={{0,24},{8,0},{16,8},{24,16},{1,25},{9,1},{17,9},{25,17},{2,26},{10... | collective-permute-start | bytes 393224 | tf_op jit(solution)/shard_map/ppermute | solution.py:28
  28.2 0.0 collective-permute-start.7
  28.2 0.6 %collective-permute-start.6 = (bf16[32,2048]{1,0:T(8,128)(2,1)S(1)}, bf16[32,2048]{1,0:T(8,128)(2,1)S(1)}, u32[]{:S(2)}, u32[]{:S(2)}) collective-permute-start(bf16[32,2048]{1,0:T(8,128)(2,1)S(1)} %factor.1.factor_ref), channel_id=1, source_target_pairs={{0,8},{8,16},{16,24},{24,0},{1,9},{9,17},{17,25},{25,1},{2,10},{10... | collective-permute-start | bytes 393224 | tf_op jit(solution)/shard_map/ppermute | solution.py:28
  28.8 3.3 %collective-permute-done.8 = bf16[32,2048]{1,0:T(8,128)(2,1)S(1)} collective-permute-done((bf16[32,2048]{1,0:T(8,128)(2,1)S(1)}, bf16[32,2048]{1,0:T(8,128)(2,1)S(1)}, u32[]{:S(2)}, u32[]{:S(2)}) %collective-permute-start.8) | collective-permute-done | bytes 131104 | tf_op jit(solution)/shard_map/ppermute | solution.py:28
  32.1 8.1 %collective-permute-done.7 = bf16[32,2048]{1,0:T(8,128)(2,1)S(1)} collective-permute-done((bf16[32,2048]{1,0:T(8,128)(2,1)S(1)}, bf16[32,2048]{1,0:T(8,128)(2,1)S(1)}, u32[]{:S(2)}, u32[]{:S(2)}) %collective-permute-start.7) | collective-permute-done | bytes 131104 | tf_op jit(solution)/shard_map/ppermute | solution.py:28
  40.2 0.0 collective-permute-done.6
  40.2 0.0 all-to-all-done
  40.2 0.2 convolution_convert_fusion.after_ref
  40.5 0.0 copy-start
  40.5 3.2 %weight.1 = (f32[1,768,1024]{2,1,0:T(8,128)}, f32[1,768,1024]{2,1,0:T(8,128)}) custom-call(bf16[64,1536]{1,0:T(8,128)(2,1)S(1)} %convolution_convert_fusion.after_ref, bf16[32,6144]{1,0:T(8,128)(2,1)S(1)} %pad_maximum_fusion.1.rows_ref.own_ref, bf16[8,8,3840]{2,1,0:T(8,128)(2,1)S(1)} %bitcast.8, bf16[128,2048]{1,0:T(8,128)(2,1)S(1)} %pad_maximum_fusion.factor_ref), custom_call_target="tpu_custom_call" | custom-call | tf_op jit(solution)/shard_map/weight/pallas_call | solution.py:287
  43.6 0.0 copy-done
  (3 shorter events, 0.1 us)
Async XLA Ops:
  2.1 12.2 %collective-permute-start.2 = (bf16[8,6144]{1,0:T(8,128)(2,1)S(1)}, bf16[8,6144]{1,0:T(8,128)(2,1)S(1)}, u32[]{:S(2)}, u32[]{:S(2)}) collective-permute-start(bf16[8,6144]{1,0:T(8,128)(2,1)S(1)} %get-tuple-element.24), channel_id=1, source_target_pairs={{0,6},{2,0},{4,2},{6,4},{1,7},{3,1},{5,3},{7,5},{8,14},{10,8},{12,... | collective-permute-start | bytes 294920 | tf_op jit(solution)/shard_map/ppermute | solution.py:28
  4.6 11.1 %collective-permute-start.1 = (bf16[8,6144]{1,0:T(8,128)(2,1)S(1)}, bf16[8,6144]{1,0:T(8,128)(2,1)S(1)}, u32[]{:S(2)}, u32[]{:S(2)}) collective-permute-start(bf16[8,6144]{1,0:T(8,128)(2,1)S(1)} %get-tuple-element.25), channel_id=1, source_target_pairs={{0,4},{2,6},{4,0},{6,2},{1,5},{3,7},{5,1},{7,3},{8,12},{10,14},{12... | collective-permute-start | bytes 294920 | tf_op jit(solution)/shard_map/ppermute | solution.py:28
  5.2 10.5 %collective-permute-start = (bf16[8,6144]{1,0:T(8,128)(2,1)S(1)}, bf16[8,6144]{1,0:T(8,128)(2,1)S(1)}, u32[]{:S(2)}, u32[]{:S(2)}) collective-permute-start(bf16[8,6144]{1,0:T(8,128)(2,1)S(1)} %get-tuple-element.26), channel_id=1, source_target_pairs={{0,2},{2,4},{4,6},{6,0},{1,3},{3,5},{5,7},{7,1},{8,10},{10,12},{12... | collective-permute-start | bytes 294920 | tf_op jit(solution)/shard_map/ppermute | solution.py:28
  5.4 10.4 %collective-permute-start.3 = (bf16[32,768]{1,0:T(8,128)(2,1)S(1)}, bf16[32,768]{1,0:T(8,128)(2,1)S(1)}, u32[]{:S(2)}, u32[]{:S(2)}) collective-permute-start(bf16[32,768]{1,0:T(8,128)(2,1)S(1)} %get-tuple-element.18), channel_id=1, source_target_pairs={{0,8},{8,16},{16,24},{24,0},{1,9},{9,17},{17,25},{25,1},{2,10},{10... | collective-permute-start | bytes 147464 | tf_op jit(solution)/shard_map/ppermute | solution.py:28
  7.0 8.8 %collective-permute-start.4 = (bf16[32,768]{1,0:T(8,128)(2,1)S(1)}, bf16[32,768]{1,0:T(8,128)(2,1)S(1)}, u32[]{:S(2)}, u32[]{:S(2)}) collective-permute-start(bf16[32,768]{1,0:T(8,128)(2,1)S(1)} %get-tuple-element.19), channel_id=1, source_target_pairs={{0,16},{8,24},{16,0},{24,8},{1,17},{9,25},{17,1},{25,9},{2,18},{10... | collective-permute-start | bytes 147464 | tf_op jit(solution)/shard_map/ppermute | solution.py:28
  14.3 4.5 %collective-permute-start.5 = (bf16[32,768]{1,0:T(8,128)(2,1)S(1)}, bf16[32,768]{1,0:T(8,128)(2,1)S(1)}, u32[]{:S(2)}, u32[]{:S(2)}) collective-permute-start(bf16[32,768]{1,0:T(8,128)(2,1)S(1)} %get-tuple-element.20), channel_id=1, source_target_pairs={{0,24},{8,0},{16,8},{24,16},{1,25},{9,1},{17,9},{25,17},{2,26},{10... | collective-permute-start | bytes 147464 | tf_op jit(solution)/shard_map/ppermute | solution.py:28
  21.5 18.7 %all-to-all-start = ((bf16[8,8,3840]{2,0,1:T(8,128)(2,1)}), bf16[8,8,3840]{2,0,1:T(8,128)(2,1)S(1)}, u32[]{:S(2)}, u32[]{:S(2)}) async-start(bf16[8,8,3840]{2,0,1:T(8,128)(2,1)} %bitcast), calls=%async_computation | async-start | bytes 983040 | tf_op jit(solution)/shard_map/all_to_all | solution.py:276
  25.0 7.1 %collective-permute-start.8 = (bf16[32,2048]{1,0:T(8,128)(2,1)S(1)}, bf16[32,2048]{1,0:T(8,128)(2,1)S(1)}, u32[]{:S(2)}, u32[]{:S(2)}) collective-permute-start(bf16[32,2048]{1,0:T(8,128)(2,1)S(1)} %factor.1.factor_ref), channel_id=1, source_target_pairs={{0,24},{8,0},{16,8},{24,16},{1,25},{9,1},{17,9},{25,17},{2,26},{10... | collective-permute-start | bytes 393224 | tf_op jit(solution)/shard_map/ppermute | solution.py:28
  28.2 12.0 %collective-permute-start.7 = (bf16[32,2048]{1,0:T(8,128)(2,1)S(1)}, bf16[32,2048]{1,0:T(8,128)(2,1)S(1)}, u32[]{:S(2)}, u32[]{:S(2)}) collective-permute-start(bf16[32,2048]{1,0:T(8,128)(2,1)S(1)} %factor.1.factor_ref), channel_id=1, source_target_pairs={{0,16},{8,24},{16,0},{24,8},{1,17},{9,25},{17,1},{25,9},{2,18},{10... | collective-permute-start | bytes 393224 | tf_op jit(solution)/shard_map/ppermute | solution.py:28
  28.2 12.0 %collective-permute-start.6 = (bf16[32,2048]{1,0:T(8,128)(2,1)S(1)}, bf16[32,2048]{1,0:T(8,128)(2,1)S(1)}, u32[]{:S(2)}, u32[]{:S(2)}) collective-permute-start(bf16[32,2048]{1,0:T(8,128)(2,1)S(1)} %factor.1.factor_ref), channel_id=1, source_target_pairs={{0,8},{8,16},{16,24},{24,0},{1,9},{9,17},{17,25},{25,1},{2,10},{10... | collective-permute-start | bytes 393224 | tf_op jit(solution)/shard_map/ppermute | solution.py:28
  40.5 3.2 %copy-start = (bf16[64,1536]{1,0:T(8,128)(2,1)}, bf16[64,1536]{1,0:T(8,128)(2,1)S(1)}, u32[]{:S(2)}) copy-start(bf16[64,1536]{1,0:T(8,128)(2,1)S(1)} %convolution_convert_fusion.after_ref) | copy-start | bytes 589828

commit v7 on v6

--- a/solution.py
+++ b/solution.py
@@ -273,9 +273,12 @@
         ),
         name="piece",
     )(factors, upper, *side)
-    returned = lax.all_to_all(
-        piece.transpose(1, 0, 2), ("expert", "hidden"), split_axis=1, concat_axis=1, tiled=True
-    ).transpose(1, 0, 2)
+    returned = lax.cond(
+        lax.axis_index("dp") >= 0,
+        lambda x: lax.all_to_all(x, ("expert", "hidden"), 0, 0),
+        lambda x: x,
+        piece,
+    )
     grad_rows = lax.dot_general(
         spread,
         returned[:, :, :part].reshape(slots * n_hid, part),

time: 43.9 us -> 40.3 us (0.918)
  waiting for transfers between devices: 12.1 us -> 0.02 us
  blocking collectives: 0 us -> 11.5 us
  starting transfers between devices: 16.2 us -> 13.9 us
  Pallas kernels: 14.3 us -> 13.6 us
    ppermute x9, waiting for transfers between devices: 12.1 us -> 0.02 us  [hop(): return lax.ppermute(x, axis, [(i, (i + step) % n) for i in range(n)])]
    all_to_all x0 -> x1, blocking collectives: none -> 11.5 us  [local(): lax.all_to_all(x, ('expert', 'hidden'), 0, 0)]
    all_to_all x1 -> x0, starting transfers between devices: 3.48 us -> none  [local(): lax.all_to_all(piece.transpose(1, 0, 2), ('expert', 'hidden'), split_axis...]
    ppermute x9, starting transfers between devices: 12.7 us -> 13.9 us  [hop(): return lax.ppermute(x, axis, [(i, (i + step) % n) for i in range(n)])]
    pallas_call x1, Pallas kernels: 2.73 us -> 1.95 us  [local(): pl.pallas_call(functools.partial(piece_kernel, n_hid), out_shape=jax.Shap...]
  transfers between devices with their start and end apart: 10 -> 9, of which waited for: 3 -> 0; matrix products, arithmetic and copies ran while one was open for 0% -> 1% of each run, Pallas kernels for 16% -> 22%
where the time goes in v7:
time: 40.3 us; the launch traced here: 40.1 us
  starting transfers between devices  13.9 us (34%)
  Pallas kernels  13.6 us (34%)
  blocking collectives  11.5 us (29%)
  between operations  0.76 us (2%)
    ppermute x9, starting transfers between devices, hop(): return lax.ppermute(x, axis, [(i, (i + step) % n) for i in range(n)])  13.9 us
    all_to_all x1, blocking collectives, local(): lax.all_to_all(x, ('expert', 'hidden'), 0, 0)  11.5 us
    pallas_call x1, Pallas kernels, local(): pl.pallas_call(functools.partial(load_kernel, splits), out_shape=[jax.Sha...  4.72 us
    pallas_call x1, Pallas kernels, local(): pl.pallas_call(functools.partial(weight_kernel, chunks, n_dp, n_share), o...  3.15 us
    pallas_call x1, Pallas kernels, local(): pl.pallas_call(factor_kernel, out_shape=jax.ShapeDtypeStruct((slots, 2 *...  2.29 us
    pallas_call x1, Pallas kernels, local(): pl.pallas_call(functools.partial(piece_kernel, n_hid), out_shape=jax.Shap...  1.95 us
    pallas_call x1, Pallas kernels, local(): pl.pallas_call(functools.partial(pick_kernel, n_hid, n_share), out_shape=...  1.44 us
  transfers between devices with their start and end apart: 9, of which 0 were waited for; matrix products, arithmetic and copies ran while one was open for 1% of the time, Pallas kernels for 22%

profile of v7, /device:TPU:0, one launch (start us, length us, event | category | flops | bytes accessed | tf_op | source)
XLA Modules:
  0.0 40.1 jit_solution(15720215628235559232)
XLA Ops:
  0.6 1.4 %pick.1 = (bf16[32,6144]{1,0:T(8,128)(2,1)S(1)}, bf16[64,64]{1,0:T(8,128)(2,1)S(1)}, bf16[32,768]{1,0:T(8,128)(2,1)S(1)}, bf16[32,768]{1,0:T(8,128)(2,1)S(1)}, bf16[32,768]{1,0:T(8,128)(2,1)S(1)}) custom-call(s32[1,1,4,8]{3,2,1,0:T(4,128)} %picks_hbm.1, bf16[1,64,3072]{2,1,0:T(8,128)(2,1)} %tokens_hbm.1, bf16[1,64,3072]{2,1,0:T(8,128)(2,1)} %upstream_hbm.1), custom_call_target="tpu_custom_call" | custom-call | tf_op jit(solution)/shard_map/pick/pallas_call | solution.py:214
  2.1 0.5 %collective-permute-start = (bf16[8,6144]{1,0:T(8,128)(2,1)S(1)}, bf16[8,6144]{1,0:T(8,128)(2,1)S(1)}, u32[]{:S(2)}, u32[]{:S(2)}) collective-permute-start(bf16[8,6144]{1,0:T(8,128)(2,1)S(1)} %get-tuple-element.37), channel_id=1, source_target_pairs={{0,2},{2,4},{4,6},{6,0},{1,3},{3,5},{5,7},{7,1},{8,10},{10,12},{12... | collective-permute-start | bytes 294920 | tf_op jit(solution)/shard_map/ppermute | solution.py:28
  2.6 2.6 %collective-permute-start.1 = (bf16[8,6144]{1,0:T(8,128)(2,1)S(1)}, bf16[8,6144]{1,0:T(8,128)(2,1)S(1)}, u32[]{:S(2)}, u32[]{:S(2)}) collective-permute-start(bf16[8,6144]{1,0:T(8,128)(2,1)S(1)} %get-tuple-element.36), channel_id=1, source_target_pairs={{0,4},{2,6},{4,0},{6,2},{1,5},{3,7},{5,1},{7,3},{8,12},{10,14},{12... | collective-permute-start | bytes 294920 | tf_op jit(solution)/shard_map/ppermute | solution.py:28
  5.2 1.4 %collective-permute-start.2 = (bf16[8,6144]{1,0:T(8,128)(2,1)S(1)}, bf16[8,6144]{1,0:T(8,128)(2,1)S(1)}, u32[]{:S(2)}, u32[]{:S(2)}) collective-permute-start(bf16[8,6144]{1,0:T(8,128)(2,1)S(1)} %get-tuple-element.35), channel_id=1, source_target_pairs={{0,6},{2,0},{4,2},{6,4},{1,7},{3,1},{5,3},{7,5},{8,14},{10,8},{12,... | collective-permute-start | bytes 294920 | tf_op jit(solution)/shard_map/ppermute | solution.py:28
  6.6 1.6 %collective-permute-start.3 = (bf16[32,768]{1,0:T(8,128)(2,1)S(1)}, bf16[32,768]{1,0:T(8,128)(2,1)S(1)}, u32[]{:S(2)}, u32[]{:S(2)}) collective-permute-start(bf16[32,768]{1,0:T(8,128)(2,1)S(1)} %get-tuple-element.29), channel_id=1, source_target_pairs={{0,8},{8,16},{16,24},{24,0},{1,9},{9,17},{17,25},{25,1},{2,10},{10... | collective-permute-start | bytes 147464 | tf_op jit(solution)/shard_map/ppermute | solution.py:28
  8.2 2.6 %collective-permute-start.4 = (bf16[32,768]{1,0:T(8,128)(2,1)S(1)}, bf16[32,768]{1,0:T(8,128)(2,1)S(1)}, u32[]{:S(2)}, u32[]{:S(2)}) collective-permute-start(bf16[32,768]{1,0:T(8,128)(2,1)S(1)} %get-tuple-element.30), channel_id=1, source_target_pairs={{0,16},{8,24},{16,0},{24,8},{1,17},{9,25},{17,1},{25,9},{2,18},{10... | collective-permute-start | bytes 147464 | tf_op jit(solution)/shard_map/ppermute | solution.py:28
  10.8 4.7 %load.1 = (f32[1,1,4,8]{3,2,1,0:T(4,128)S(1)}, bf16[1,3072,1024]{2,1,0:T(8,128)(2,1)S(1)}, bf16[1,3072,1024]{2,1,0:T(8,128)(2,1)S(1)}) custom-call(bf16[32,6144]{1,0:T(8,128)(2,1)S(1)} %get-tuple-element.25.after_ref, f32[1,1,4,8]{3,2,1,0:T(4,128)} %gates_hbm.1, bf16[1,3072,1024]{2,1,0:T(8,128)(2,1)} %upper_hbm.1, bf16[1,3072,1024]{2,1,0:T(8,128)(2,1)} %lower_hbm.1), custom_call_target="tpu_custom_call" | custom-call | bytes 25165824 | tf_op jit(solution)/shard_map/load/pallas_call | solution.py:239
  15.5 0.0 collective-permute-done
  15.5 1.4 %collective-permute-start.5 = (bf16[32,768]{1,0:T(8,128)(2,1)S(1)}, bf16[32,768]{1,0:T(8,128)(2,1)S(1)}, u32[]{:S(2)}, u32[]{:S(2)}) collective-permute-start(bf16[32,768]{1,0:T(8,128)(2,1)S(1)} %get-tuple-element.31), channel_id=1, source_target_pairs={{0,24},{8,0},{16,8},{24,16},{1,25},{9,1},{17,9},{25,17},{2,26},{10... | collective-permute-start | bytes 147464 | tf_op jit(solution)/shard_map/ppermute | solution.py:28
  16.9 0.0 collective-permute-done.1
  16.9 0.0 collective-permute-done.2
  16.9 0.0 collective-permute-done.3.refs_0_
  17.0 0.0 collective-permute-done.4.refs_1_
  17.0 2.3 %factor.1.factor_ref = bf16[32,2048]{1,0:T(8,128)(2,1)S(1)} custom-call(f32[1,1,4,8]{3,2,1,0:T(4,128)S(1)} %get-tuple-element.26.gates_ref, bf16[32,6144]{1,0:T(8,128)(2,1)S(1)} %pad_maximum_fusion.1.rows_ref.own_ref, bf16[1,3072,1024]{2,1,0:T(8,128)(2,1)S(1)} %get-tuple-element.27.upper_ref, bf16[1,3072,1024]{2,1,0:T(8,128)(2,1)S(1)} %get-tuple-element.28.lower_ref, ...), custom_call_target="tpu_custom_call" | custom-call | flops 402653184 | bytes 12582912 | tf_op jit(solution)/shard_map/factor/pallas_call | solution.py:251
  19.3 0.7 %collective-permute-start.6 = (bf16[32,2048]{1,0:T(8,128)(2,1)S(1)}, bf16[32,2048]{1,0:T(8,128)(2,1)S(1)}, u32[]{:S(2)}, u32[]{:S(2)}) collective-permute-start(bf16[32,2048]{1,0:T(8,128)(2,1)S(1)} %factor.1.factor_ref), channel_id=1, source_target_pairs={{0,8},{8,16},{16,24},{24,0},{1,9},{9,17},{17,25},{25,1},{2,10},{10... | collective-permute-start | bytes 393224 | tf_op jit(solution)/shard_map/ppermute | solution.py:28
  20.0 0.3 collective-permute-start.7
  20.3 2.8 %collective-permute-start.8 = (bf16[32,2048]{1,0:T(8,128)(2,1)S(1)}, bf16[32,2048]{1,0:T(8,128)(2,1)S(1)}, u32[]{:S(2)}, u32[]{:S(2)}) collective-permute-start(bf16[32,2048]{1,0:T(8,128)(2,1)S(1)} %factor.1.factor_ref), channel_id=1, source_target_pairs={{0,24},{8,0},{16,8},{24,16},{1,25},{9,1},{17,9},{25,17},{2,26},{10... | collective-permute-start | bytes 393224 | tf_op jit(solution)/shard_map/ppermute | solution.py:28
  23.1 0.0 collective-permute-done.5.refs_2_
  23.1 2.0 %piece.1 = bf16[8,8,3840]{2,1,0:T(8,128)(2,1)S(1)} custom-call(bf16[32,2048]{1,0:T(8,128)(2,1)S(1)} %factor.1.factor_ref, bf16[1,3072,1024]{2,1,0:T(8,128)(2,1)S(1)} %get-tuple-element.27.upper_ref, bf16[32,768]{1,0:T(8,128)(2,1)S(1)} %collective-permute-done.3.refs_0_, bf16[32,768]{1,0:T(8,128)(2,1)S(1)} %collective-permute-done.4.refs_1_, ...), custom_call_target="tpu_custom_call" | custom-call | flops 201326592 | bytes 6291456 | tf_op jit(solution)/shard_map/piece/pallas_call | solution.py:265
  25.1 11.5 %conditional.1 = (bf16[8,8,3840]{2,1,0:T(8,128)(2,1)S(1)}) conditional(s32[]{:T(128)} %convert_element_type.6, bf16[8,8,3840]{2,1,0:T(8,128)(2,1)S(1)} %piece.1, bf16[8,8,3840]{2,1,0:T(8,128)(2,1)S(1)} %piece.1), branch_computations={%region_0.0_spmd, %region_1.0_spmd} | conditional | bytes 1966088 | solution.py:276
  25.2 11.5 %all_to_all.4 = bf16[8,8,3840]{2,1,0:T(8,128)(2,1)S(1)} all-to-all(bf16[8,8,3840]{2,1,0:T(8,128)(2,1)S(1)} %copy.11), channel_id=1, replica_groups=mesh['dp'=4,'expert'=4,'hidden'=2] {'expert','hidden'}, dimensions={0} | all-to-all | bytes 983040 | tf_op jit(solution)/shard_map/cond/branch_1_fun/all_to_all | solution.py:278
  36.6 0.2 convolution_convert_fusion.after_ref
  36.9 0.0 copy-start
  36.9 0.0 collective-permute-done.6
  36.9 0.0 collective-permute-done.7
  36.9 0.0 collective-permute-done.8
  37.0 3.2 %weight.1 = (f32[1,768,1024]{2,1,0:T(8,128)}, f32[1,768,1024]{2,1,0:T(8,128)}) custom-call(bf16[64,1536]{1,0:T(8,128)(2,1)S(1)} %convolution_convert_fusion.after_ref, bf16[32,6144]{1,0:T(8,128)(2,1)S(1)} %pad_maximum_fusion.1.rows_ref.own_ref, bf16[8,8,3840]{2,1,0:T(8,128)(2,1)S(1)} %get-tuple-element.38.came_ref, ...), custom_call_target="tpu_custom_call" | custom-call | tf_op jit(solution)/shard_map/weight/pallas_call | solution.py:290
  40.1 0.0 copy-done
  (4 shorter events, 0.1 us)
Async XLA Ops:
  2.1 13.4 %collective-permute-start = (bf16[8,6144]{1,0:T(8,128)(2,1)S(1)}, bf16[8,6144]{1,0:T(8,128)(2,1)S(1)}, u32[]{:S(2)}, u32[]{:S(2)}) collective-permute-start(bf16[8,6144]{1,0:T(8,128)(2,1)S(1)} %get-tuple-element.37), channel_id=1, source_target_pairs={{0,2},{2,4},{4,6},{6,0},{1,3},{3,5},{5,7},{7,1},{8,10},{10,12},{12... | collective-permute-start | bytes 294920 | tf_op jit(solution)/shard_map/ppermute | solution.py:28
  2.6 14.3 %collective-permute-start.1 = (bf16[8,6144]{1,0:T(8,128)(2,1)S(1)}, bf16[8,6144]{1,0:T(8,128)(2,1)S(1)}, u32[]{:S(2)}, u32[]{:S(2)}) collective-permute-start(bf16[8,6144]{1,0:T(8,128)(2,1)S(1)} %get-tuple-element.36), channel_id=1, source_target_pairs={{0,4},{2,6},{4,0},{6,2},{1,5},{3,7},{5,1},{7,3},{8,12},{10,14},{12... | collective-permute-start | bytes 294920 | tf_op jit(solution)/shard_map/ppermute | solution.py:28
  5.2 11.7 %collective-permute-start.2 = (bf16[8,6144]{1,0:T(8,128)(2,1)S(1)}, bf16[8,6144]{1,0:T(8,128)(2,1)S(1)}, u32[]{:S(2)}, u32[]{:S(2)}) collective-permute-start(bf16[8,6144]{1,0:T(8,128)(2,1)S(1)} %get-tuple-element.35), channel_id=1, source_target_pairs={{0,6},{2,0},{4,2},{6,4},{1,7},{3,1},{5,3},{7,5},{8,14},{10,8},{12,... | collective-permute-start | bytes 294920 | tf_op jit(solution)/shard_map/ppermute | solution.py:28
  6.6 10.3 %collective-permute-start.3 = (bf16[32,768]{1,0:T(8,128)(2,1)S(1)}, bf16[32,768]{1,0:T(8,128)(2,1)S(1)}, u32[]{:S(2)}, u32[]{:S(2)}) collective-permute-start(bf16[32,768]{1,0:T(8,128)(2,1)S(1)} %get-tuple-element.29), channel_id=1, source_target_pairs={{0,8},{8,16},{16,24},{24,0},{1,9},{9,17},{17,25},{25,1},{2,10},{10... | collective-permute-start | bytes 147464 | tf_op jit(solution)/shard_map/ppermute | solution.py:28
  8.2 8.8 %collective-permute-start.4 = (bf16[32,768]{1,0:T(8,128)(2,1)S(1)}, bf16[32,768]{1,0:T(8,128)(2,1)S(1)}, u32[]{:S(2)}, u32[]{:S(2)}) collective-permute-start(bf16[32,768]{1,0:T(8,128)(2,1)S(1)} %get-tuple-element.30), channel_id=1, source_target_pairs={{0,16},{8,24},{16,0},{24,8},{1,17},{9,25},{17,1},{25,9},{2,18},{10... | collective-permute-start | bytes 147464 | tf_op jit(solution)/shard_map/ppermute | solution.py:28
  15.5 7.6 %collective-permute-start.5 = (bf16[32,768]{1,0:T(8,128)(2,1)S(1)}, bf16[32,768]{1,0:T(8,128)(2,1)S(1)}, u32[]{:S(2)}, u32[]{:S(2)}) collective-permute-start(bf16[32,768]{1,0:T(8,128)(2,1)S(1)} %get-tuple-element.31), channel_id=1, source_target_pairs={{0,24},{8,0},{16,8},{24,16},{1,25},{9,1},{17,9},{25,17},{2,26},{10... | collective-permute-start | bytes 147464 | tf_op jit(solution)/shard_map/ppermute | solution.py:28
  19.3 17.6 %collective-permute-start.6 = (bf16[32,2048]{1,0:T(8,128)(2,1)S(1)}, bf16[32,2048]{1,0:T(8,128)(2,1)S(1)}, u32[]{:S(2)}, u32[]{:S(2)}) collective-permute-start(bf16[32,2048]{1,0:T(8,128)(2,1)S(1)} %factor.1.factor_ref), channel_id=1, source_target_pairs={{0,8},{8,16},{16,24},{24,0},{1,9},{9,17},{17,25},{25,1},{2,10},{10... | collective-permute-start | bytes 393224 | tf_op jit(solution)/shard_map/ppermute | solution.py:28
  20.0 16.9 %collective-permute-start.7 = (bf16[32,2048]{1,0:T(8,128)(2,1)S(1)}, bf16[32,2048]{1,0:T(8,128)(2,1)S(1)}, u32[]{:S(2)}, u32[]{:S(2)}) collective-permute-start(bf16[32,2048]{1,0:T(8,128)(2,1)S(1)} %factor.1.factor_ref), channel_id=1, source_target_pairs={{0,16},{8,24},{16,0},{24,8},{1,17},{9,25},{17,1},{25,9},{2,18},{10... | collective-permute-start | bytes 393224 | tf_op jit(solution)/shard_map/ppermute | solution.py:28
  20.3 16.6 %collective-permute-start.8 = (bf16[32,2048]{1,0:T(8,128)(2,1)S(1)}, bf16[32,2048]{1,0:T(8,128)(2,1)S(1)}, u32[]{:S(2)}, u32[]{:S(2)}) collective-permute-start(bf16[32,2048]{1,0:T(8,128)(2,1)S(1)} %factor.1.factor_ref), channel_id=1, source_target_pairs={{0,24},{8,0},{16,8},{24,16},{1,25},{9,1},{17,9},{25,17},{2,26},{10... | collective-permute-start | bytes 393224 | tf_op jit(solution)/shard_map/ppermute | solution.py:28
  36.9 3.3 %copy-start = (bf16[64,1536]{1,0:T(8,128)(2,1)}, bf16[64,1536]{1,0:T(8,128)(2,1)S(1)}, u32[]{:S(2)}) copy-start(bf16[64,1536]{1,0:T(8,128)(2,1)S(1)} %convolution_convert_fusion.after_ref) | copy-start | bytes 589828

commit v8 on v3

--- a/solution.py
+++ b/solution.py
@@ -82,7 +82,7 @@
             ]
 
 
-def load_kernel(after_ref, gates_hbm, upper_hbm, lower_hbm, gates_ref, upper_ref, lower_ref, sems):
+def load_kernel(after_ref, always_ref, gates_hbm, upper_hbm, lower_hbm, gates_ref, upper_ref, lower_ref, sems):
     copies = [
         pltpu.make_async_copy(source, target, sems.at[k])
         for k, (source, target) in enumerate(
@@ -126,7 +126,7 @@
 def weight_kernel(chunks, shape, own_ref, *refs):
     n_dp, n_hid = shape
     part_refs, refs = refs[:n_hid], refs[n_hid:]
-    factor_ref, up_ref, down_ref, side_ref, held, sems = refs
+    factor_ref, spread_ref, came_ref, up_ref, down_ref, in_ref, side_ref, held, in_held, sems, in_sem = refs
     units = factor_ref.shape[1] // 2
     cols = side_ref.shape[1] // 2
     width = own_ref.shape[1] // 2
@@ -158,6 +158,15 @@
             )
             copy.start()
             copies.append(copy)
+    came = jnp.concatenate([came_ref[k].astype(jnp.float32) for k in range(came_ref.shape[0])], axis=0)
+    in_held[...] = lax.dot_general(
+        spread_ref[...],
+        came.astype(jnp.bfloat16),
+        (((0,), (0,)), ((), ())),
+        preferred_element_type=jnp.float32,
+    ).astype(jnp.bfloat16)
+    copies.append(pltpu.make_async_copy(in_held, in_ref.at[0], in_sem))
+    copies[-1].start()
     for copy in copies:
         copy.wait()
 
@@ -204,10 +213,11 @@
     rows = jnp.concatenate(
         [hop(send[s * n_pick : (s + 1) * n_pick], "expert", s) for s in range(n_exp)], axis=0
     )
+    always = (lax.axis_index("dp") >= 0).astype(jnp.int32)
     gate_held, upper, lower = pl.pallas_call(
         load_kernel,
         out_shape=[jax.ShapeDtypeStruct(x.shape, x.dtype) for x in (gates, w_up, w_down)],
-        in_specs=[HBM] * 4,
+        in_specs=[HBM, pl.BlockSpec(memory_space=pltpu.SMEM)] + [HBM] * 3,
         out_specs=[VMEM] * 3,
         scratch_shapes=[pltpu.SemaphoreType.DMA((3,))],
         cost_estimate=pl.CostEstimate(
@@ -215,7 +225,7 @@
         ),
         compiler_params=ROOM,
         name="load",
-    )(send, gates, w_up, w_down)
+    )(send, lax.clamp(0, always, 1).reshape(1), gates, w_up, w_down)
     share = slots // n_hid
     parts = pl.pallas_call(
         cut_kernel,
@@ -254,32 +264,32 @@
         ),
         name="piece",
     )(factors, upper)
-    returned = lax.all_to_all(piece, ("expert", "hidden"), 0, 0)
-    grad_rows = lax.dot_general(
-        spread,
-        returned.reshape(slots * n_hid, part),
-        (((0,), (0,)), ((), ())),
-        preferred_element_type=jnp.float32,
-    ).astype(bf16)
+    returned = lax.switch(
+        always, [lambda x: x, lambda x: lax.all_to_all(x, ("expert", "hidden"), 0, 0)], piece
+    )
 
     chunks = max(1, units // 256)
     grads = pl.pallas_call(
         functools.partial(weight_kernel, chunks, (n_dp, n_hid)),
-        out_shape=[jax.ShapeDtypeStruct((1, cols, units), jnp.float32)] * 2,
-        in_specs=[VMEM] * (n_hid + 2),
-        out_specs=[HBM] * 2,
+        out_shape=[jax.ShapeDtypeStruct((1, cols, units), jnp.float32)] * 2
+        + [jax.ShapeDtypeStruct((1, tok_dev, part), bf16)],
+        in_specs=[VMEM] * (n_hid + 4),
+        out_specs=[HBM] * 3,
         scratch_shapes=[
             pltpu.VMEM((n_dp * slots, 2 * cols), bf16),
             pltpu.VMEM((2, cols, units), jnp.float32),
+            pltpu.VMEM((tok_dev, part), bf16),
             pltpu.SemaphoreType.DMA((2, chunks)),
+            pltpu.SemaphoreType.DMA,
         ],
         compiler_params=ROOM,
         cost_estimate=pl.CostEstimate(
             flops=4 * n_dp * slots * cols * units, bytes_accessed=64 * cols * units, transcendentals=0
         ),
         name="weight",
-    )(rows, *parts, gathered)
-    return (grad_rows[None], *grads)
+    )(rows, *parts, gathered, spread, returned)
+    grad_up, grad_down, grad_in = grads
+    return grad_in, grad_up, grad_down
 
 
 def solution(mesh):

time: 41.5 us -> 43 us (1.036)
  blocking collectives: 0 us -> 9.49 us
  starting transfers between devices: 17.8 us -> 12.8 us
  waiting for transfers between devices: 7.59 us -> 6.03 us
  matrix products: 0.91 us -> 0 us
  Pallas kernels: 14.2 us -> 13.5 us
    all_to_all x0 -> x1, blocking collectives: none -> 9.49 us  [local(): lax.all_to_all(x, ('expert', 'hidden'), 0, 0)]
    all_to_all x1 -> x0, starting transfers between devices: 3.94 us -> none  [local(): returned = lax.all_to_all(piece, ('expert', 'hidden'), 0, 0)]
    ppermute x10, waiting for transfers between devices: 7.59 us -> 6.03 us  [hop(): return lax.ppermute(x, axis, [(i, (i + step) % n) for i in range(n)])]
    ppermute x10, starting transfers between devices: 13.8 us -> 12.8 us  [hop(): return lax.ppermute(x, axis, [(i, (i + step) % n) for i in range(n)])]
    dot_general x1 -> x0, matrix products: 0.91 us -> none  [local(): lax.dot_general(spread, returned.reshape(slots * n_hid, part), (((0,), (0...]
    pallas_call x1, Pallas kernels: 2.63 us -> 1.95 us  [local(): pl.pallas_call(functools.partial(piece_kernel, n_hid), out_shape=jax.Shap...]
  transfers between devices with their start and end apart: 11 -> 10, of which waited for: 4 -> 3; matrix products, arithmetic and copies ran while one was open for 0% -> 0% of each run, Pallas kernels for 31% -> 21%
where the time goes in v8:
time: 43 us; the launch traced here: 42.8 us
  Pallas kernels  13.5 us (31%)
  starting transfers between devices  12.8 us (30%)
  blocking collectives  9.49 us (22%)
  waiting for transfers between devices  6.03 us (14%)
  between operations  0.72 us (2%)
    ppermute x10, starting transfers between devices, hop(): return lax.ppermute(x, axis, [(i, (i + step) % n) for i in range(n)])  12.8 us
    all_to_all x1, blocking collectives, local(): lax.all_to_all(x, ('expert', 'hidden'), 0, 0)  9.49 us
    ppermute x10, waiting for transfers between devices, hop(): return lax.ppermute(x, axis, [(i, (i + step) % n) for i in range(n)])  6.03 us
    pallas_call x1, Pallas kernels, local(): pl.pallas_call(load_kernel, out_shape=[jax.ShapeDtypeStruct(x.shape, x.dt...  4.64 us
    pallas_call x1, Pallas kernels, local(): pl.pallas_call(functools.partial(weight_kernel, chunks, (n_dp, n_hid)), o...  3.2 us
    pallas_call x1, Pallas kernels, local(): pl.pallas_call(factor_kernel, out_shape=jax.ShapeDtypeStruct((slots, 2 *...  2.29 us
    pallas_call x1, Pallas kernels, local(): pl.pallas_call(functools.partial(piece_kernel, n_hid), out_shape=jax.Shap...  1.95 us
    pallas_call x1, Pallas kernels, local(): pl.pallas_call(functools.partial(pick_kernel, n_hid), out_shape=[jax.Shap...  1.42 us
  transfers between devices with their start and end apart: 10, of which 3 were waited for; matrix products, arithmetic and copies ran while one was open for 0% of the time, Pallas kernels for 21%

profile of v8, /device:TPU:0, one launch (start us, length us, event | category | flops | bytes accessed | tf_op | source)
XLA Modules:
  0.0 42.8 jit_solution(2240250982197050767)
XLA Ops:
  0.6 1.4 %pick.1 = (bf16[32,6144]{1,0:T(8,128)(2,1)S(1)}, bf16[64,64]{1,0:T(8,128)(2,1)S(1)}) custom-call(s32[1,1,4,8]{3,2,1,0:T(4,128)} %picks_hbm.1, bf16[1,64,3072]{2,1,0:T(8,128)(2,1)} %tokens_hbm.1, bf16[1,64,3072]{2,1,0:T(8,128)(2,1)} %upstream_hbm.1), custom_call_target="tpu_custom_call" | custom-call | tf_op jit(solution)/shard_map/pick/pallas_call | solution.py:195
  2.1 2.5 %collective-permute-start.2 = (bf16[8,6144]{1,0:T(8,128)(2,1)S(1)}, bf16[8,6144]{1,0:T(8,128)(2,1)S(1)}, u32[]{:S(2)}, u32[]{:S(2)}) collective-permute-start(bf16[8,6144]{1,0:T(8,128)(2,1)S(1)} %get-tuple-element.31), channel_id=1, source_target_pairs={{0,6},{2,0},{4,2},{6,4},{1,7},{3,1},{5,3},{7,5},{8,14},{10,8},{12,... | collective-permute-start | bytes 294920 | tf_op jit(solution)/shard_map/ppermute | solution.py:28
  4.6 0.6 %collective-permute-start.1 = (bf16[8,6144]{1,0:T(8,128)(2,1)S(1)}, bf16[8,6144]{1,0:T(8,128)(2,1)S(1)}, u32[]{:S(2)}, u32[]{:S(2)}) collective-permute-start(bf16[8,6144]{1,0:T(8,128)(2,1)S(1)} %get-tuple-element.32), channel_id=1, source_target_pairs={{0,4},{2,6},{4,0},{6,2},{1,5},{3,7},{5,1},{7,3},{8,12},{10,14},{12... | collective-permute-start | bytes 294920 | tf_op jit(solution)/shard_map/ppermute | solution.py:28
  5.2 0.2 collective-permute-start
  5.4 4.6 %load.1 = (f32[1,1,4,8]{3,2,1,0:T(4,128)S(1)}, bf16[1,3072,1024]{2,1,0:T(8,128)(2,1)S(1)}, bf16[1,3072,1024]{2,1,0:T(8,128)(2,1)S(1)}) custom-call(bf16[32,6144]{1,0:T(8,128)(2,1)S(1)} %get-tuple-element.19.after_ref, s32[1]{0:T(128)} %bitcast.always_ref, f32[1,1,4,8]{3,2,1,0:T(4,128)} %gates_hbm.1, bf16[1,3072,1024]{2,1,0:T(8,128)(2,1)} %upper_hbm.1, ...), custom_call_target="tpu_custom_call" | custom-call | bytes 25165824 | tf_op jit(solution)/shard_map/load/pallas_call | solution.py:217
  10.0 0.0 collective-permute-done.2
  10.0 0.7 %collective-permute-done.1 = bf16[8,6144]{1,0:T(8,128)(2,1)S(1)} collective-permute-done((bf16[8,6144]{1,0:T(8,128)(2,1)S(1)}, bf16[8,6144]{1,0:T(8,128)(2,1)S(1)}, u32[]{:S(2)}, u32[]{:S(2)}) %collective-permute-start.1) | collective-permute-done | bytes 98336 | tf_op jit(solution)/shard_map/ppermute | solution.py:28
  10.7 0.0 collective-permute-done
  10.8 1.8 %collective-permute-start.3 = (bf16[16,1536]{1,0:T(8,128)(2,1)S(1)}, bf16[16,1536]{1,0:T(8,128)(2,1)S(1)}, u32[]{:S(2)}, u32[]{:S(2)}) collective-permute-start(bf16[16,1536]{1,0:T(8,128)(2,1)S(1)} %get-tuple-element.21), channel_id=1, source_target_pairs={{0,8},{8,16},{16,24},{24,0},{1,9},{9,17},{17,25},{25,1},{2,10},{10... | collective-permute-start | bytes 147464 | tf_op jit(solution)/shard_map/ppermute | solution.py:28
  12.6 2.6 %collective-permute-start.4 = (bf16[16,1536]{1,0:T(8,128)(2,1)S(1)}, bf16[16,1536]{1,0:T(8,128)(2,1)S(1)}, u32[]{:S(2)}, u32[]{:S(2)}) collective-permute-start(bf16[16,1536]{1,0:T(8,128)(2,1)S(1)} %get-tuple-element.22), channel_id=1, source_target_pairs={{0,16},{8,24},{16,0},{24,8},{1,17},{9,25},{17,1},{25,9},{2,18},{10... | collective-permute-start | bytes 147464 | tf_op jit(solution)/shard_map/ppermute | solution.py:28
  15.2 1.3 %collective-permute-start.5 = (bf16[16,1536]{1,0:T(8,128)(2,1)S(1)}, bf16[16,1536]{1,0:T(8,128)(2,1)S(1)}, u32[]{:S(2)}, u32[]{:S(2)}) collective-permute-start(bf16[16,1536]{1,0:T(8,128)(2,1)S(1)} %get-tuple-element.23), channel_id=1, source_target_pairs={{0,24},{8,0},{16,8},{24,16},{1,25},{9,1},{17,9},{25,17},{2,26},{10... | collective-permute-start | bytes 147464 | tf_op jit(solution)/shard_map/ppermute | solution.py:28
  16.5 0.6 %collective-permute-done.3.after_ref = bf16[16,1536]{1,0:T(8,128)(2,1)S(1)} collective-permute-done((bf16[16,1536]{1,0:T(8,128)(2,1)S(1)}, bf16[16,1536]{1,0:T(8,128)(2,1)S(1)}, u32[]{:S(2)}, u32[]{:S(2)}) %collective-permute-start.3) | collective-permute-done | bytes 49184 | tf_op jit(solution)/shard_map/ppermute | solution.py:28
  17.1 2.3 %factor.1.factor_ref = bf16[32,2048]{1,0:T(8,128)(2,1)S(1)} custom-call(bf16[16,1536]{1,0:T(8,128)(2,1)S(1)} %collective-permute-done.3.after_ref, f32[1,1,4,8]{3,2,1,0:T(4,128)S(1)} %get-tuple-element.20.after_ref.gates_ref, bf16[32,6144]{1,0:T(8,128)(2,1)S(1)} %pad_maximum_fusion.1.rows_ref.own_ref, ...), custom_call_target="tpu_custom_call" | custom-call | flops 402653184 | bytes 12582912 | tf_op jit(solution)/shard_map/factor/pallas_call | solution.py:240
  19.4 1.7 %collective-permute-start.9 = (bf16[32,2048]{1,0:T(8,128)(2,1)S(1)}, bf16[32,2048]{1,0:T(8,128)(2,1)S(1)}, u32[]{:S(2)}, u32[]{:S(2)}) collective-permute-start(bf16[32,2048]{1,0:T(8,128)(2,1)S(1)} %factor.1.factor_ref), channel_id=1, source_target_pairs={{0,24},{8,0},{16,8},{24,16},{1,25},{9,1},{17,9},{25,17},{2,26},{10... | collective-permute-start | bytes 393224 | tf_op jit(solution)/shard_map/ppermute | solution.py:28
  21.1 0.0 collective-permute-start.8
  21.1 1.0 %collective-permute-start.7 = (bf16[32,2048]{1,0:T(8,128)(2,1)S(1)}, bf16[32,2048]{1,0:T(8,128)(2,1)S(1)}, u32[]{:S(2)}, u32[]{:S(2)}) collective-permute-start(bf16[32,2048]{1,0:T(8,128)(2,1)S(1)} %factor.1.factor_ref), channel_id=1, source_target_pairs={{0,8},{8,16},{16,24},{24,0},{1,9},{9,17},{17,25},{25,1},{2,10},{10... | collective-permute-start | bytes 393224 | tf_op jit(solution)/shard_map/ppermute | solution.py:28
  22.1 1.9 %piece.1 = bf16[8,8,1536]{2,1,0:T(8,128)(2,1)S(1)} custom-call(bf16[32,2048]{1,0:T(8,128)(2,1)S(1)} %factor.1.factor_ref, bf16[1,3072,1024]{2,1,0:T(8,128)(2,1)S(1)} %get-tuple-element.24.upper_ref), custom_call_target="tpu_custom_call" | custom-call | flops 201326592 | bytes 6291456 | tf_op jit(solution)/shard_map/piece/pallas_call | solution.py:256
  24.1 9.5 %conditional.1 = (bf16[8,8,1536]{2,1,0:T(8,128)(2,1)S(1)}) conditional(s32[]{:T(128)} %clamp.4, bf16[8,8,1536]{2,1,0:T(8,128)(2,1)S(1)} %piece.1, bf16[8,8,1536]{2,1,0:T(8,128)(2,1)S(1)} %piece.1), branch_computations={%region_0.0_spmd, %region_1.0_spmd} | conditional | bytes 786440 | solution.py:267
  24.1 9.5 %all_to_all.4 = bf16[8,8,1536]{2,1,0:T(8,128)(2,1)S(1)} all-to-all(bf16[8,8,1536]{2,1,0:T(8,128)(2,1)S(1)} %copy.11), channel_id=1, replica_groups=mesh['dp'=4,'expert'=4,'hidden'=2] {'expert','hidden'}, dimensions={0} | all-to-all | bytes 393216 | tf_op jit(solution)/shard_map/cond/branch_1_fun/all_to_all | solution.py:268
  33.6 0.0 collective-permute-done.4
  33.6 0.0 collective-permute-done.5
  33.6 1.1 %collective-permute-start.6 = (bf16[3,16,1536]{2,1,0:T(8,128)(2,1)S(1)}, bf16[3,16,1536]{2,1,0:T(8,128)(2,1)S(1)}, u32[]{:S(2)}, u32[]{:S(2)}) collective-permute-start(bf16[3,16,1536]{2,1,0:T(8,128)(2,1)S(1)} %pad_maximum_fusion.2.refs_0_), channel_id=1, source_target_pairs={{0,1},{1,0},{2,3},{3,2},{4,5},{5,4},{6,7},{7,6},{8,9},{9,8},{10,11... | collective-permute-start | bytes 442376 | tf_op jit(solution)/shard_map/ppermute | solution.py:28
  34.7 0.0 collective-permute-done.9
  34.7 0.0 collective-permute-done.8
  34.7 0.0 collective-permute-done.7
  34.8 4.8 %collective-permute-done.6.refs_1_ = bf16[3,16,1536]{2,1,0:T(8,128)(2,1)S(1)} collective-permute-done((bf16[3,16,1536]{2,1,0:T(8,128)(2,1)S(1)}, bf16[3,16,1536]{2,1,0:T(8,128)(2,1)S(1)}, u32[]{:S(2)}, u32[]{:S(2)}) %collective-permute-start.6) | collective-permute-done | bytes 147488 | tf_op jit(solution)/shard_map/ppermute | solution.py:28
  39.6 3.2 %weight.1 = (f32[1,768,1024]{2,1,0:T(8,128)}, f32[1,768,1024]{2,1,0:T(8,128)}, bf16[1,64,1536]{2,1,0:T(8,128)(2,1)}) custom-call(bf16[32,6144]{1,0:T(8,128)(2,1)S(1)} %pad_maximum_fusion.1.rows_ref.own_ref, bf16[3,16,1536]{2,1,0:T(8,128)(2,1)S(1)} %pad_maximum_fusion.2.refs_0_, bf16[3,16,1536]{2,1,0:T(8,128)(2,1)S(1)} %collective-permute-done.6.refs_1_, ...), custom_call_target="tpu_custom_call" | custom-call | flops 402653184 | bytes 50331648 | tf_op jit(solution)/shard_map/weight/pallas_call | solution.py:272
  (6 shorter events, 0.2 us)
Async XLA Ops:
  2.1 7.9 %collective-permute-start.2 = (bf16[8,6144]{1,0:T(8,128)(2,1)S(1)}, bf16[8,6144]{1,0:T(8,128)(2,1)S(1)}, u32[]{:S(2)}, u32[]{:S(2)}) collective-permute-start(bf16[8,6144]{1,0:T(8,128)(2,1)S(1)} %get-tuple-element.31), channel_id=1, source_target_pairs={{0,6},{2,0},{4,2},{6,4},{1,7},{3,1},{5,3},{7,5},{8,14},{10,8},{12,... | collective-permute-start | bytes 294920 | tf_op jit(solution)/shard_map/ppermute | solution.py:28
  4.6 6.1 %collective-permute-start.1 = (bf16[8,6144]{1,0:T(8,128)(2,1)S(1)}, bf16[8,6144]{1,0:T(8,128)(2,1)S(1)}, u32[]{:S(2)}, u32[]{:S(2)}) collective-permute-start(bf16[8,6144]{1,0:T(8,128)(2,1)S(1)} %get-tuple-element.32), channel_id=1, source_target_pairs={{0,4},{2,6},{4,0},{6,2},{1,5},{3,7},{5,1},{7,3},{8,12},{10,14},{12... | collective-permute-start | bytes 294920 | tf_op jit(solution)/shard_map/ppermute | solution.py:28
  5.2 5.5 %collective-permute-start = (bf16[8,6144]{1,0:T(8,128)(2,1)S(1)}, bf16[8,6144]{1,0:T(8,128)(2,1)S(1)}, u32[]{:S(2)}, u32[]{:S(2)}) collective-permute-start(bf16[8,6144]{1,0:T(8,128)(2,1)S(1)} %get-tuple-element.33), channel_id=1, source_target_pairs={{0,2},{2,4},{4,6},{6,0},{1,3},{3,5},{5,7},{7,1},{8,10},{10,12},{12... | collective-permute-start | bytes 294920 | tf_op jit(solution)/shard_map/ppermute | solution.py:28
  10.8 6.3 %collective-permute-start.3 = (bf16[16,1536]{1,0:T(8,128)(2,1)S(1)}, bf16[16,1536]{1,0:T(8,128)(2,1)S(1)}, u32[]{:S(2)}, u32[]{:S(2)}) collective-permute-start(bf16[16,1536]{1,0:T(8,128)(2,1)S(1)} %get-tuple-element.21), channel_id=1, source_target_pairs={{0,8},{8,16},{16,24},{24,0},{1,9},{9,17},{17,25},{25,1},{2,10},{10... | collective-permute-start | bytes 147464 | tf_op jit(solution)/shard_map/ppermute | solution.py:28
  12.6 21.0 %collective-permute-start.4 = (bf16[16,1536]{1,0:T(8,128)(2,1)S(1)}, bf16[16,1536]{1,0:T(8,128)(2,1)S(1)}, u32[]{:S(2)}, u32[]{:S(2)}) collective-permute-start(bf16[16,1536]{1,0:T(8,128)(2,1)S(1)} %get-tuple-element.22), channel_id=1, source_target_pairs={{0,16},{8,24},{16,0},{24,8},{1,17},{9,25},{17,1},{25,9},{2,18},{10... | collective-permute-start | bytes 147464 | tf_op jit(solution)/shard_map/ppermute | solution.py:28
  15.2 18.4 %collective-permute-start.5 = (bf16[16,1536]{1,0:T(8,128)(2,1)S(1)}, bf16[16,1536]{1,0:T(8,128)(2,1)S(1)}, u32[]{:S(2)}, u32[]{:S(2)}) collective-permute-start(bf16[16,1536]{1,0:T(8,128)(2,1)S(1)} %get-tuple-element.23), channel_id=1, source_target_pairs={{0,24},{8,0},{16,8},{24,16},{1,25},{9,1},{17,9},{25,17},{2,26},{10... | collective-permute-start | bytes 147464 | tf_op jit(solution)/shard_map/ppermute | solution.py:28
  19.4 15.3 %collective-permute-start.9 = (bf16[32,2048]{1,0:T(8,128)(2,1)S(1)}, bf16[32,2048]{1,0:T(8,128)(2,1)S(1)}, u32[]{:S(2)}, u32[]{:S(2)}) collective-permute-start(bf16[32,2048]{1,0:T(8,128)(2,1)S(1)} %factor.1.factor_ref), channel_id=1, source_target_pairs={{0,24},{8,0},{16,8},{24,16},{1,25},{9,1},{17,9},{25,17},{2,26},{10... | collective-permute-start | bytes 393224 | tf_op jit(solution)/shard_map/ppermute | solution.py:28
  21.1 13.6 %collective-permute-start.8 = (bf16[32,2048]{1,0:T(8,128)(2,1)S(1)}, bf16[32,2048]{1,0:T(8,128)(2,1)S(1)}, u32[]{:S(2)}, u32[]{:S(2)}) collective-permute-start(bf16[32,2048]{1,0:T(8,128)(2,1)S(1)} %factor.1.factor_ref), channel_id=1, source_target_pairs={{0,16},{8,24},{16,0},{24,8},{1,17},{9,25},{17,1},{25,9},{2,18},{10... | collective-permute-start | bytes 393224 | tf_op jit(solution)/shard_map/ppermute | solution.py:28
  21.1 13.6 %collective-permute-start.7 = (bf16[32,2048]{1,0:T(8,128)(2,1)S(1)}, bf16[32,2048]{1,0:T(8,128)(2,1)S(1)}, u32[]{:S(2)}, u32[]{:S(2)}) collective-permute-start(bf16[32,2048]{1,0:T(8,128)(2,1)S(1)} %factor.1.factor_ref), channel_id=1, source_target_pairs={{0,8},{8,16},{16,24},{24,0},{1,9},{9,17},{17,25},{25,1},{2,10},{10... | collective-permute-start | bytes 393224 | tf_op jit(solution)/shard_map/ppermute | solution.py:28
  33.6 5.9 %collective-permute-start.6 = (bf16[3,16,1536]{2,1,0:T(8,128)(2,1)S(1)}, bf16[3,16,1536]{2,1,0:T(8,128)(2,1)S(1)}, u32[]{:S(2)}, u32[]{:S(2)}) collective-permute-start(bf16[3,16,1536]{2,1,0:T(8,128)(2,1)S(1)} %pad_maximum_fusion.2.refs_0_), channel_id=1, source_target_pairs={{0,1},{1,0},{2,3},{3,2},{4,5},{5,4},{6,7},{7,6},{8,9},{9,8},{10,11... | collective-permute-start | bytes 442376 | tf_op jit(solution)/shard_map/ppermute | solution.py:28

commit v9 on v3

--- a/solution.py
+++ b/solution.py
@@ -121,6 +121,16 @@
             out_ref[owner + h] = piece[
                 s * n_pick : (s + 1) * n_pick, h * part : (h + 1) * part
             ].astype(jnp.bfloat16)
+
+
+def stack_kernel(after_ref, *refs):
+    *part_refs, out_ref = refs
+    for s, part in enumerate(part_refs):
+        out_ref[s] = part[...]
+
+
+def tie_kernel(*refs):
+    pass
 
 
 def weight_kernel(chunks, shape, own_ref, *refs):
@@ -238,7 +248,14 @@
         ),
         name="factor",
     )(parts[0], gate_held, rows, upper, lower)
-    parts = jnp.stack(parts)
+    parts = pl.pallas_call(
+        stack_kernel,
+        out_shape=jax.ShapeDtypeStruct((n_dp - 1, share, 2 * cols), bf16),
+        in_specs=[ANY] + [VMEM] * (n_dp - 1),
+        out_specs=VMEM,
+        compiler_params=ROOM,
+        name="stack",
+    )(factors, *parts)
     parts = [hop(parts, "hidden", t) for t in range(n_hid)]
 
     gathered = jnp.concatenate([hop(factors, "dp", s) for s in range(n_dp)], axis=0)
@@ -254,6 +271,15 @@
         ),
         name="piece",
     )(factors, upper)
+    piece = pl.pallas_call(
+        tie_kernel,
+        out_shape=jax.ShapeDtypeStruct(piece.shape, piece.dtype),
+        in_specs=[ANY] * n_hid,
+        out_specs=ANY,
+        input_output_aliases={0: 0},
+        compiler_params=ROOM,
+        name="tie",
+    )(piece, *parts[1:])
     returned = lax.all_to_all(piece, ("expert", "hidden"), 0, 0)
     grad_rows = lax.dot_general(
         spread,

time: 41.5 us -> 39.7 us (0.957)
  waiting for transfers between devices: 7.59 us -> 6.14 us
    ppermute x10, waiting for transfers between devices: 7.59 us -> 6.13 us  [hop(): return lax.ppermute(x, axis, [(i, (i + step) % n) for i in range(n)])]
    all_to_all x1, starting transfers between devices: 3.94 us -> 3.39 us  [local(): returned = lax.all_to_all(piece, ('expert', 'hidden'), 0, 0)]
  transfers between devices with their start and end apart: 11 -> 11, of which waited for: 4 -> 4; matrix products, arithmetic and copies ran while one was open for 0% -> 0% of each run, Pallas kernels for 31% -> 32%
where the time goes in v9:
time: 39.7 us; the launch traced here: 39.5 us
  starting transfers between devices  17.4 us (44%)
  Pallas kernels  14.2 us (36%)
  waiting for transfers between devices  6.14 us (15%)
  matrix products  0.91 us (2%)
  between operations  0.74 us (2%)
    ppermute x10, starting transfers between devices, hop(): return lax.ppermute(x, axis, [(i, (i + step) % n) for i in range(n)])  14 us
    ppermute x10, waiting for transfers between devices, hop(): return lax.ppermute(x, axis, [(i, (i + step) % n) for i in range(n)])  6.13 us
    pallas_call x1, Pallas kernels, local(): pl.pallas_call(load_kernel, out_shape=[jax.ShapeDtypeStruct(x.shape, x.dt...  4.64 us
    all_to_all x1, starting transfers between devices, local(): returned = lax.all_to_all(piece, ('expert', 'hidden'), 0, 0)  3.39 us
    pallas_call x1, Pallas kernels, local(): pl.pallas_call(functools.partial(weight_kernel, chunks, (n_dp, n_hid)), o...  3.16 us
    pallas_call x1, Pallas kernels, local(): pl.pallas_call(functools.partial(piece_kernel, n_hid), out_shape=jax.Shap...  2.63 us
    pallas_call x1, Pallas kernels, local(): pl.pallas_call(factor_kernel, out_shape=jax.ShapeDtypeStruct((slots, 2 *...  2.29 us
    pallas_call x1, Pallas kernels, local(): pl.pallas_call(functools.partial(pick_kernel, n_hid), out_shape=[jax.Shap...  1.42 us
  transfers between devices with their start and end apart: 11, of which 4 were waited for; matrix products, arithmetic and copies ran while one was open for 0% of the time, Pallas kernels for 32%

profile of v9, /device:TPU:0, one launch (start us, length us, event | category | flops | bytes accessed | tf_op | source)
XLA Modules:
  0.0 39.5 jit_solution(15971545517208213319)
XLA Ops:
  0.6 1.4 %pick.1 = (bf16[32,6144]{1,0:T(8,128)(2,1)S(1)}, bf16[64,64]{1,0:T(8,128)(2,1)S(1)}) custom-call(s32[1,1,4,8]{3,2,1,0:T(4,128)} %picks_hbm.1, bf16[1,64,3072]{2,1,0:T(8,128)(2,1)} %tokens_hbm.1, bf16[1,64,3072]{2,1,0:T(8,128)(2,1)} %upstream_hbm.1), custom_call_target="tpu_custom_call" | custom-call | tf_op jit(solution)/shard_map/pick/pallas_call | solution.py:196
  2.1 2.5 %collective-permute-start.2 = (bf16[8,6144]{1,0:T(8,128)(2,1)S(1)}, bf16[8,6144]{1,0:T(8,128)(2,1)S(1)}, u32[]{:S(2)}, u32[]{:S(2)}) collective-permute-start(bf16[8,6144]{1,0:T(8,128)(2,1)S(1)} %get-tuple-element.24), channel_id=1, source_target_pairs={{0,6},{2,0},{4,2},{6,4},{1,7},{3,1},{5,3},{7,5},{8,14},{10,8},{12,... | collective-permute-start | bytes 294920 | tf_op jit(solution)/shard_map/ppermute | solution.py:28
  4.6 0.6 %collective-permute-start.1 = (bf16[8,6144]{1,0:T(8,128)(2,1)S(1)}, bf16[8,6144]{1,0:T(8,128)(2,1)S(1)}, u32[]{:S(2)}, u32[]{:S(2)}) collective-permute-start(bf16[8,6144]{1,0:T(8,128)(2,1)S(1)} %get-tuple-element.25), channel_id=1, source_target_pairs={{0,4},{2,6},{4,0},{6,2},{1,5},{3,7},{5,1},{7,3},{8,12},{10,14},{12... | collective-permute-start | bytes 294920 | tf_op jit(solution)/shard_map/ppermute | solution.py:28
  5.2 0.2 collective-permute-start
  5.4 4.6 %load.1 = (f32[1,1,4,8]{3,2,1,0:T(4,128)S(1)}, bf16[1,3072,1024]{2,1,0:T(8,128)(2,1)S(1)}, bf16[1,3072,1024]{2,1,0:T(8,128)(2,1)S(1)}) custom-call(bf16[32,6144]{1,0:T(8,128)(2,1)S(1)} %get-tuple-element.14.after_ref, f32[1,1,4,8]{3,2,1,0:T(4,128)} %gates_hbm.1, bf16[1,3072,1024]{2,1,0:T(8,128)(2,1)} %upper_hbm.1, bf16[1,3072,1024]{2,1,0:T(8,128)(2,1)} %lower_hbm.1), custom_call_target="tpu_custom_call" | custom-call | bytes 25165824 | tf_op jit(solution)/shard_map/load/pallas_call | solution.py:217
  10.0 0.0 collective-permute-done.2
  10.0 0.7 %collective-permute-done.1 = bf16[8,6144]{1,0:T(8,128)(2,1)S(1)} collective-permute-done((bf16[8,6144]{1,0:T(8,128)(2,1)S(1)}, bf16[8,6144]{1,0:T(8,128)(2,1)S(1)}, u32[]{:S(2)}, u32[]{:S(2)}) %collective-permute-start.1) | collective-permute-done | bytes 98336 | tf_op jit(solution)/shard_map/ppermute | solution.py:28
  10.7 0.0 collective-permute-done
  10.8 1.8 %collective-permute-start.3 = (bf16[16,1536]{1,0:T(8,128)(2,1)S(1)}, bf16[16,1536]{1,0:T(8,128)(2,1)S(1)}, u32[]{:S(2)}, u32[]{:S(2)}) collective-permute-start(bf16[16,1536]{1,0:T(8,128)(2,1)S(1)} %get-tuple-element.16), channel_id=1, source_target_pairs={{0,8},{8,16},{16,24},{24,0},{1,9},{9,17},{17,25},{25,1},{2,10},{10... | collective-permute-start | bytes 147464 | tf_op jit(solution)/shard_map/ppermute | solution.py:28
  12.6 2.6 %collective-permute-start.4 = (bf16[16,1536]{1,0:T(8,128)(2,1)S(1)}, bf16[16,1536]{1,0:T(8,128)(2,1)S(1)}, u32[]{:S(2)}, u32[]{:S(2)}) collective-permute-start(bf16[16,1536]{1,0:T(8,128)(2,1)S(1)} %get-tuple-element.19), channel_id=1, source_target_pairs={{0,16},{8,24},{16,0},{24,8},{1,17},{9,25},{17,1},{25,9},{2,18},{10... | collective-permute-start | bytes 147464 | tf_op jit(solution)/shard_map/ppermute | solution.py:28
  15.2 1.3 %collective-permute-start.5 = (bf16[16,1536]{1,0:T(8,128)(2,1)S(1)}, bf16[16,1536]{1,0:T(8,128)(2,1)S(1)}, u32[]{:S(2)}, u32[]{:S(2)}) collective-permute-start(bf16[16,1536]{1,0:T(8,128)(2,1)S(1)} %get-tuple-element.20), channel_id=1, source_target_pairs={{0,24},{8,0},{16,8},{24,16},{1,25},{9,1},{17,9},{25,17},{2,26},{10... | collective-permute-start | bytes 147464 | tf_op jit(solution)/shard_map/ppermute | solution.py:28
  16.5 0.6 %collective-permute-done.3.after_ref.refs_0_ = bf16[16,1536]{1,0:T(8,128)(2,1)S(1)} collective-permute-done((bf16[16,1536]{1,0:T(8,128)(2,1)S(1)}, bf16[16,1536]{1,0:T(8,128)(2,1)S(1)}, u32[]{:S(2)}, u32[]{:S(2)}) %collective-permute-start.3) | collective-permute-done | bytes 49184 | tf_op jit(solution)/shard_map/ppermute | solution.py:28
  17.1 2.3 %factor.1.factor_ref.after_ref = bf16[32,2048]{1,0:T(8,128)(2,1)S(1)} custom-call(bf16[16,1536]{1,0:T(8,128)(2,1)S(1)} %collective-permute-done.3.after_ref.refs_0_, f32[1,1,4,8]{3,2,1,0:T(4,128)S(1)} %get-tuple-element.15.after_ref.gates_ref, bf16[32,6144]{1,0:T(8,128)(2,1)S(1)} %pad_maximum_fusion.1.rows_ref.own_ref, ...), custom_call_target="tpu_custom_call" | custom-call | flops 402653184 | bytes 12582912 | tf_op jit(solution)/shard_map/factor/pallas_call | solution.py:240
  19.4 0.0 collective-permute-done.4.refs_1_
  19.4 0.1 collective-permute-done.5.refs_2_
  19.5 1.6 %collective-permute-start.6 = (bf16[3,16,1536]{2,1,0:T(8,128)(2,1)S(1)}, bf16[3,16,1536]{2,1,0:T(8,128)(2,1)S(1)}, u32[]{:S(2)}, u32[]{:S(2)}) collective-permute-start(bf16[3,16,1536]{2,1,0:T(8,128)(2,1)S(1)} %stack.1.refs_0_), channel_id=1, source_target_pairs={{0,1},{1,0},{2,3},{3,2},{4,5},{5,4},{6,7},{7,6},{8,9},{9,8},{10,11... | collective-permute-start | bytes 442376 | tf_op jit(solution)/shard_map/ppermute | solution.py:28
  21.1 2.9 %collective-permute-start.9 = (bf16[32,2048]{1,0:T(8,128)(2,1)S(1)}, bf16[32,2048]{1,0:T(8,128)(2,1)S(1)}, u32[]{:S(2)}, u32[]{:S(2)}) collective-permute-start(bf16[32,2048]{1,0:T(8,128)(2,1)S(1)} %factor.1.factor_ref.after_ref), channel_id=1, source_target_pairs={{0,24},{8,0},{16,8},{24,16},{1,25},{9,1},{17,9},{25,17},{2,26},{10... | collective-permute-start | bytes 393224 | tf_op jit(solution)/shard_map/ppermute | solution.py:28
  24.0 0.0 collective-permute-start.8
  24.0 0.6 %collective-permute-start.7 = (bf16[32,2048]{1,0:T(8,128)(2,1)S(1)}, bf16[32,2048]{1,0:T(8,128)(2,1)S(1)}, u32[]{:S(2)}, u32[]{:S(2)}) collective-permute-start(bf16[32,2048]{1,0:T(8,128)(2,1)S(1)} %factor.1.factor_ref.after_ref), channel_id=1, source_target_pairs={{0,8},{8,16},{16,24},{24,0},{1,9},{9,17},{17,25},{25,1},{2,10},{10... | collective-permute-start | bytes 393224 | tf_op jit(solution)/shard_map/ppermute | solution.py:28
  24.5 2.6 %piece.1.refs_0_ = bf16[8,8,1536]{2,1,0:T(8,128)(2,1)} custom-call(bf16[32,2048]{1,0:T(8,128)(2,1)S(1)} %factor.1.factor_ref.after_ref, bf16[1,3072,1024]{2,1,0:T(8,128)(2,1)S(1)} %get-tuple-element.17.upper_ref), custom_call_target="tpu_custom_call" | custom-call | flops 201326592 | bytes 6291456 | tf_op jit(solution)/shard_map/piece/pallas_call | solution.py:263
  27.2 0.0 collective-permute-done.6.refs_1_
  27.2 3.4 %all-to-all-start = ((bf16[8,8,1536]{2,1,0:T(8,128)(2,1)}), bf16[8,8,1536]{2,1,0:T(8,128)(2,1)S(1)}, u32[]{:S(2)}, u32[]{:S(2)}) async-start(bf16[8,8,1536]{2,1,0:T(8,128)(2,1)} %tie.1), calls=%async_computation | async-start | bytes 393216 | tf_op jit(solution)/shard_map/all_to_all | solution.py:283
  30.6 0.0 collective-permute-done.9
  30.6 4.8 %collective-permute-done.8 = bf16[32,2048]{1,0:T(8,128)(2,1)S(1)} collective-permute-done((bf16[32,2048]{1,0:T(8,128)(2,1)S(1)}, bf16[32,2048]{1,0:T(8,128)(2,1)S(1)}, u32[]{:S(2)}, u32[]{:S(2)}) %collective-permute-start.8) | collective-permute-done | bytes 131104 | tf_op jit(solution)/shard_map/ppermute | solution.py:28
  35.3 0.0 collective-permute-done.7
  35.4 3.2 %weight.1 = (f32[1,768,1024]{2,1,0:T(8,128)}, f32[1,768,1024]{2,1,0:T(8,128)}) custom-call(bf16[32,6144]{1,0:T(8,128)(2,1)S(1)} %pad_maximum_fusion.1.rows_ref.own_ref, bf16[3,16,1536]{2,1,0:T(8,128)(2,1)S(1)} %stack.1.refs_0_, bf16[3,16,1536]{2,1,0:T(8,128)(2,1)S(1)} %collective-permute-done.6.refs_1_, bf16[128,2048]{1,0:T(8,128)(2,1)S(1)} %pad_maximum_fusion.refs_2_), custom_call_target="tpu_custom_call" | custom-call | flops 402653184 | bytes 50331648 | tf_op jit(solution)/shard_map/weight/pallas_call | solution.py:292
  38.6 0.0 all-to-all-done
  38.6 0.9 %fusion = bf16[1,64,1536]{2,1,0:T(8,128)(2,1)} fusion(bf16[64,64]{1,0:T(8,128)(2,1)S(1)} %get-tuple-element.13, bf16[8,8,1536]{2,1,0:T(8,128)(2,1)S(1)} %all-to-all-done), kind=kOutput, calls=%fused_computation.1 | convolution fusion | flops 12681216 | bytes 401408 | tf_op jit(solution)/shard_map/dot_general | solution.py:284
  (6 shorter events, 0.1 us)
Async XLA Ops:
  2.1 7.9 %collective-permute-start.2 = (bf16[8,6144]{1,0:T(8,128)(2,1)S(1)}, bf16[8,6144]{1,0:T(8,128)(2,1)S(1)}, u32[]{:S(2)}, u32[]{:S(2)}) collective-permute-start(bf16[8,6144]{1,0:T(8,128)(2,1)S(1)} %get-tuple-element.24), channel_id=1, source_target_pairs={{0,6},{2,0},{4,2},{6,4},{1,7},{3,1},{5,3},{7,5},{8,14},{10,8},{12,... | collective-permute-start | bytes 294920 | tf_op jit(solution)/shard_map/ppermute | solution.py:28
  4.6 6.1 %collective-permute-start.1 = (bf16[8,6144]{1,0:T(8,128)(2,1)S(1)}, bf16[8,6144]{1,0:T(8,128)(2,1)S(1)}, u32[]{:S(2)}, u32[]{:S(2)}) collective-permute-start(bf16[8,6144]{1,0:T(8,128)(2,1)S(1)} %get-tuple-element.25), channel_id=1, source_target_pairs={{0,4},{2,6},{4,0},{6,2},{1,5},{3,7},{5,1},{7,3},{8,12},{10,14},{12... | collective-permute-start | bytes 294920 | tf_op jit(solution)/shard_map/ppermute | solution.py:28
  5.2 5.5 %collective-permute-start = (bf16[8,6144]{1,0:T(8,128)(2,1)S(1)}, bf16[8,6144]{1,0:T(8,128)(2,1)S(1)}, u32[]{:S(2)}, u32[]{:S(2)}) collective-permute-start(bf16[8,6144]{1,0:T(8,128)(2,1)S(1)} %get-tuple-element.26), channel_id=1, source_target_pairs={{0,2},{2,4},{4,6},{6,0},{1,3},{3,5},{5,7},{7,1},{8,10},{10,12},{12... | collective-permute-start | bytes 294920 | tf_op jit(solution)/shard_map/ppermute | solution.py:28
  10.8 6.3 %collective-permute-start.3 = (bf16[16,1536]{1,0:T(8,128)(2,1)S(1)}, bf16[16,1536]{1,0:T(8,128)(2,1)S(1)}, u32[]{:S(2)}, u32[]{:S(2)}) collective-permute-start(bf16[16,1536]{1,0:T(8,128)(2,1)S(1)} %get-tuple-element.16), channel_id=1, source_target_pairs={{0,8},{8,16},{16,24},{24,0},{1,9},{9,17},{17,25},{25,1},{2,10},{10... | collective-permute-start | bytes 147464 | tf_op jit(solution)/shard_map/ppermute | solution.py:28
  12.6 6.8 %collective-permute-start.4 = (bf16[16,1536]{1,0:T(8,128)(2,1)S(1)}, bf16[16,1536]{1,0:T(8,128)(2,1)S(1)}, u32[]{:S(2)}, u32[]{:S(2)}) collective-permute-start(bf16[16,1536]{1,0:T(8,128)(2,1)S(1)} %get-tuple-element.19), channel_id=1, source_target_pairs={{0,16},{8,24},{16,0},{24,8},{1,17},{9,25},{17,1},{25,9},{2,18},{10... | collective-permute-start | bytes 147464 | tf_op jit(solution)/shard_map/ppermute | solution.py:28
  15.2 4.4 %collective-permute-start.5 = (bf16[16,1536]{1,0:T(8,128)(2,1)S(1)}, bf16[16,1536]{1,0:T(8,128)(2,1)S(1)}, u32[]{:S(2)}, u32[]{:S(2)}) collective-permute-start(bf16[16,1536]{1,0:T(8,128)(2,1)S(1)} %get-tuple-element.20), channel_id=1, source_target_pairs={{0,24},{8,0},{16,8},{24,16},{1,25},{9,1},{17,9},{25,17},{2,26},{10... | collective-permute-start | bytes 147464 | tf_op jit(solution)/shard_map/ppermute | solution.py:28
  19.5 7.6 %collective-permute-start.6 = (bf16[3,16,1536]{2,1,0:T(8,128)(2,1)S(1)}, bf16[3,16,1536]{2,1,0:T(8,128)(2,1)S(1)}, u32[]{:S(2)}, u32[]{:S(2)}) collective-permute-start(bf16[3,16,1536]{2,1,0:T(8,128)(2,1)S(1)} %stack.1.refs_0_), channel_id=1, source_target_pairs={{0,1},{1,0},{2,3},{3,2},{4,5},{5,4},{6,7},{7,6},{8,9},{9,8},{10,11... | collective-permute-start | bytes 442376 | tf_op jit(solution)/shard_map/ppermute | solution.py:28
  21.1 9.5 %collective-permute-start.9 = (bf16[32,2048]{1,0:T(8,128)(2,1)S(1)}, bf16[32,2048]{1,0:T(8,128)(2,1)S(1)}, u32[]{:S(2)}, u32[]{:S(2)}) collective-permute-start(bf16[32,2048]{1,0:T(8,128)(2,1)S(1)} %factor.1.factor_ref.after_ref), channel_id=1, source_target_pairs={{0,24},{8,0},{16,8},{24,16},{1,25},{9,1},{17,9},{25,17},{2,26},{10... | collective-permute-start | bytes 393224 | tf_op jit(solution)/shard_map/ppermute | solution.py:28
  24.0 11.4 %collective-permute-start.8 = (bf16[32,2048]{1,0:T(8,128)(2,1)S(1)}, bf16[32,2048]{1,0:T(8,128)(2,1)S(1)}, u32[]{:S(2)}, u32[]{:S(2)}) collective-permute-start(bf16[32,2048]{1,0:T(8,128)(2,1)S(1)} %factor.1.factor_ref.after_ref), channel_id=1, source_target_pairs={{0,16},{8,24},{16,0},{24,8},{1,17},{9,25},{17,1},{25,9},{2,18},{10... | collective-permute-start | bytes 393224 | tf_op jit(solution)/shard_map/ppermute | solution.py:28
  24.0 11.4 %collective-permute-start.7 = (bf16[32,2048]{1,0:T(8,128)(2,1)S(1)}, bf16[32,2048]{1,0:T(8,128)(2,1)S(1)}, u32[]{:S(2)}, u32[]{:S(2)}) collective-permute-start(bf16[32,2048]{1,0:T(8,128)(2,1)S(1)} %factor.1.factor_ref.after_ref), channel_id=1, source_target_pairs={{0,8},{8,16},{16,24},{24,0},{1,9},{9,17},{17,25},{25,1},{2,10},{10... | collective-permute-start | bytes 393224 | tf_op jit(solution)/shard_map/ppermute | solution.py:28
  27.2 11.4 %all-to-all-start = ((bf16[8,8,1536]{2,1,0:T(8,128)(2,1)}), bf16[8,8,1536]{2,1,0:T(8,128)(2,1)S(1)}, u32[]{:S(2)}, u32[]{:S(2)}) async-start(bf16[8,8,1536]{2,1,0:T(8,128)(2,1)} %tie.1), calls=%async_computation | async-start | bytes 393216 | tf_op jit(solution)/shard_map/all_to_all | solution.py:283

commit v10 on v3

--- a/solution.py
+++ b/solution.py
@@ -69,16 +69,14 @@
 
 def cut_kernel(after_ref, rows_ref, *out_refs):
     n_dp = len(out_refs) + 1
-    share, wide = out_refs[0].shape
-    cols = wide // 2
+    cols = out_refs[0].shape[1] // 2
     width = rows_ref.shape[1] // 2
     my_dp = lax.axis_index("dp")
-    spot = pl.ds(pl.multiple_of(lax.axis_index("hidden") * share, 16), share)
     for s, out_ref in enumerate(out_refs):
         at = ((my_dp + s + 1) % n_dp) * cols
         for half in range(2):
             out_ref[:, half * cols : (half + 1) * cols] = rows_ref[
-                spot, pl.ds(pl.multiple_of(half * width + at, 128), cols)
+                :, pl.ds(pl.multiple_of(half * width + at, 128), cols)
             ]
 
 
@@ -95,7 +93,7 @@
         copy.wait()
 
 
-def factor_kernel(after_ref, gates_ref, rows_ref, upper_ref, lower_ref, out_ref):
+def factor_kernel(gates_ref, rows_ref, upper_ref, lower_ref, out_ref):
     n_exp = gates_ref.shape[2]
     width, units = upper_ref.shape[1:]
     me = lax.axis_index("expert")
@@ -123,25 +121,21 @@
             ].astype(jnp.bfloat16)
 
 
-def weight_kernel(chunks, shape, own_ref, *refs):
-    n_dp, n_hid = shape
-    part_refs, refs = refs[:n_hid], refs[n_hid:]
-    factor_ref, up_ref, down_ref, side_ref, held, sems = refs
+def tie_kernel(*refs):
+    pass
+
+
+def weight_kernel(chunks, own_ref, part_ref, factor_ref, up_ref, down_ref, side_ref, held, sems):
     units = factor_ref.shape[1] // 2
     cols = side_ref.shape[1] // 2
     width = own_ref.shape[1] // 2
     slots = own_ref.shape[0]
-    rows = slots // n_hid
-    my_hid = lax.axis_index("hidden")
     start = lax.axis_index("dp") * cols
     for half in range(2):
         side_ref[:slots, half * cols : (half + 1) * cols] = own_ref[
             :, pl.ds(pl.multiple_of(half * width + start, 128), cols)
         ]
-    for t, part in enumerate(part_refs):
-        spot = ((my_hid + n_hid - t) % n_hid) * rows
-        for s in range(1, n_dp):
-            side_ref[pl.ds(pl.multiple_of(s * slots + spot, 16), rows), :] = part[s - 1]
+    side_ref[slots:, :] = part_ref[...]
     step = units // chunks
     copies = []
     for which, out in ((0, up_ref), (1, down_ref)):
@@ -216,10 +210,9 @@
         compiler_params=ROOM,
         name="load",
     )(send, gates, w_up, w_down)
-    share = slots // n_hid
     parts = pl.pallas_call(
         cut_kernel,
-        out_shape=[jax.ShapeDtypeStruct((share, 2 * cols), bf16)] * (n_dp - 1),
+        out_shape=[jax.ShapeDtypeStruct((slots, 2 * cols), bf16)] * (n_dp - 1),
         in_specs=[ANY, VMEM],
         out_specs=[VMEM] * (n_dp - 1),
         compiler_params=ROOM,
@@ -230,16 +223,15 @@
     factors = pl.pallas_call(
         factor_kernel,
         out_shape=jax.ShapeDtypeStruct((slots, 2 * units), bf16),
-        in_specs=[ANY] + [VMEM] * 4,
+        in_specs=[VMEM] * 4,
         out_specs=VMEM,
         compiler_params=ROOM,
         cost_estimate=pl.CostEstimate(
             flops=4 * slots * w_up.size, bytes_accessed=4 * w_up.size, transcendentals=slots * units
         ),
         name="factor",
-    )(parts[0], gate_held, rows, upper, lower)
-    parts = jnp.stack(parts)
-    parts = [hop(parts, "hidden", t) for t in range(n_hid)]
+    )(gate_held, rows, upper, lower)
+    parts = jnp.concatenate(parts, axis=0)
 
     gathered = jnp.concatenate([hop(factors, "dp", s) for s in range(n_dp)], axis=0)
 
@@ -254,6 +246,15 @@
         ),
         name="piece",
     )(factors, upper)
+    piece = pl.pallas_call(
+        tie_kernel,
+        out_shape=jax.ShapeDtypeStruct(piece.shape, piece.dtype),
+        in_specs=[ANY] * 2,
+        out_specs=ANY,
+        input_output_aliases={0: 0},
+        compiler_params=ROOM,
+        name="tie",
+    )(piece, parts)
     returned = lax.all_to_all(piece, ("expert", "hidden"), 0, 0)
     grad_rows = lax.dot_general(
         spread,
@@ -264,9 +265,9 @@
 
     chunks = max(1, units // 256)
     grads = pl.pallas_call(
-        functools.partial(weight_kernel, chunks, (n_dp, n_hid)),
+        functools.partial(weight_kernel, chunks),
         out_shape=[jax.ShapeDtypeStruct((1, cols, units), jnp.float32)] * 2,
-        in_specs=[VMEM] * (n_hid + 2),
+        in_specs=[VMEM] * 3,
         out_specs=[HBM] * 2,
         scratch_shapes=[
             pltpu.VMEM((n_dp * slots, 2 * cols), bf16),
@@ -278,7 +279,7 @@
             flops=4 * n_dp * slots * cols * units, bytes_accessed=64 * cols * units, transcendentals=0
         ),
         name="weight",
-    )(rows, *parts, gathered)
+    )(rows, parts, gathered)
     return (grad_rows[None], *grads)
 
 

time: 41.5 us -> 45.2 us (1.089)
  waiting for transfers between devices: 7.59 us -> 12.6 us
  starting transfers between devices: 17.8 us -> 16.4 us
    ppermute x10 -> x9, waiting for transfers between devices: 7.59 us -> 10.2 us  [hop(): return lax.ppermute(x, axis, [(i, (i + step) % n) for i in range(n)])]
    all_to_all x1, waiting for transfers between devices: 0.01 us -> 2.45 us  [local(): returned = lax.all_to_all(piece, ('expert', 'hidden'), 0, 0)]
    ppermute x10 -> x9, starting transfers between devices: 13.8 us -> 13 us  [hop(): return lax.ppermute(x, axis, [(i, (i + step) % n) for i in range(n)])]
    all_to_all x1, starting transfers between devices: 3.94 us -> 3.4 us  [local(): returned = lax.all_to_all(piece, ('expert', 'hidden'), 0, 0)]
    pallas_call x2 -> x3, Pallas kernels: 3.19 us -> 3.18 us  [the longest x1 3.14 us: local(): pl.pallas_call(functools.partial(weight_kernel, chunks), out_shape=[jax.S...]
  transfers between devices with their start and end apart: 11 -> 10, of which waited for: 4 -> 3; matrix products, arithmetic and copies ran while one was open for 0% -> 0% of each run, Pallas kernels for 31% -> 28%
where the time goes in v10:
time: 45.2 us; the launch traced here: 45 us
  starting transfers between devices  16.4 us (36%)
  Pallas kernels  14.2 us (31%)
  waiting for transfers between devices  12.6 us (28%)
  matrix products  0.91 us (2%)
  between operations  0.76 us (2%)
    ppermute x9, starting transfers between devices, hop(): return lax.ppermute(x, axis, [(i, (i + step) % n) for i in range(n)])  13 us
    ppermute x9, waiting for transfers between devices, hop(): return lax.ppermute(x, axis, [(i, (i + step) % n) for i in range(n)])  10.2 us
    pallas_call x1, Pallas kernels, local(): pl.pallas_call(load_kernel, out_shape=[jax.ShapeDtypeStruct(x.shape, x.dt...  4.64 us
    all_to_all x1, starting transfers between devices, local(): returned = lax.all_to_all(piece, ('expert', 'hidden'), 0, 0)  3.4 us
    pallas_call x1, Pallas kernels, local(): pl.pallas_call(functools.partial(weight_kernel, chunks), out_shape=[jax.S...  3.14 us
    pallas_call x1, Pallas kernels, local(): pl.pallas_call(functools.partial(piece_kernel, n_hid), out_shape=jax.Shap...  2.63 us
    all_to_all x1, waiting for transfers between devices, local(): returned = lax.all_to_all(piece, ('expert', 'hidden'), 0, 0)  2.45 us
    pallas_call x1, Pallas kernels, local(): pl.pallas_call(factor_kernel, out_shape=jax.ShapeDtypeStruct((slots, 2 *...  2.29 us
  transfers between devices with their start and end apart: 10, of which 3 were waited for; matrix products, arithmetic and copies ran while one was open for 0% of the time, Pallas kernels for 28%

profile of v10, /device:TPU:0, one launch (start us, length us, event | category | flops | bytes accessed | tf_op | source)
XLA Modules:
  0.0 45.0 jit_solution(6446615705594351856)
XLA Ops:
  0.6 1.4 %pick.1 = (bf16[32,6144]{1,0:T(8,128)(2,1)S(1)}, bf16[64,64]{1,0:T(8,128)(2,1)S(1)}) custom-call(s32[1,1,4,8]{3,2,1,0:T(4,128)} %picks_hbm.1, bf16[1,64,3072]{2,1,0:T(8,128)(2,1)} %tokens_hbm.1, bf16[1,64,3072]{2,1,0:T(8,128)(2,1)} %upstream_hbm.1), custom_call_target="tpu_custom_call" | custom-call | tf_op jit(solution)/shard_map/pick/pallas_call | solution.py:180
  2.1 2.5 %collective-permute-start.2 = (bf16[8,6144]{1,0:T(8,128)(2,1)S(1)}, bf16[8,6144]{1,0:T(8,128)(2,1)S(1)}, u32[]{:S(2)}, u32[]{:S(2)}) collective-permute-start(bf16[8,6144]{1,0:T(8,128)(2,1)S(1)} %get-tuple-element.24), channel_id=1, source_target_pairs={{0,6},{2,0},{4,2},{6,4},{1,7},{3,1},{5,3},{7,5},{8,14},{10,8},{12,... | collective-permute-start | bytes 294920 | tf_op jit(solution)/shard_map/ppermute | solution.py:28
  4.6 0.6 %collective-permute-start.1 = (bf16[8,6144]{1,0:T(8,128)(2,1)S(1)}, bf16[8,6144]{1,0:T(8,128)(2,1)S(1)}, u32[]{:S(2)}, u32[]{:S(2)}) collective-permute-start(bf16[8,6144]{1,0:T(8,128)(2,1)S(1)} %get-tuple-element.25), channel_id=1, source_target_pairs={{0,4},{2,6},{4,0},{6,2},{1,5},{3,7},{5,1},{7,3},{8,12},{10,14},{12... | collective-permute-start | bytes 294920 | tf_op jit(solution)/shard_map/ppermute | solution.py:28
  5.2 0.2 collective-permute-start
  5.4 4.6 %load.1 = (f32[1,1,4,8]{3,2,1,0:T(4,128)S(1)}, bf16[1,3072,1024]{2,1,0:T(8,128)(2,1)S(1)}, bf16[1,3072,1024]{2,1,0:T(8,128)(2,1)S(1)}) custom-call(bf16[32,6144]{1,0:T(8,128)(2,1)S(1)} %get-tuple-element.14.after_ref, f32[1,1,4,8]{3,2,1,0:T(4,128)} %gates_hbm.1, bf16[1,3072,1024]{2,1,0:T(8,128)(2,1)} %upper_hbm.1, bf16[1,3072,1024]{2,1,0:T(8,128)(2,1)} %lower_hbm.1), custom_call_target="tpu_custom_call" | custom-call | bytes 25165824 | tf_op jit(solution)/shard_map/load/pallas_call | solution.py:201
  10.0 0.0 collective-permute-done.2
  10.0 0.7 %collective-permute-done.1 = bf16[8,6144]{1,0:T(8,128)(2,1)S(1)} collective-permute-done((bf16[8,6144]{1,0:T(8,128)(2,1)S(1)}, bf16[8,6144]{1,0:T(8,128)(2,1)S(1)}, u32[]{:S(2)}, u32[]{:S(2)}) %collective-permute-start.1) | collective-permute-done | bytes 98336 | tf_op jit(solution)/shard_map/ppermute | solution.py:28
  10.7 0.0 collective-permute-done
  10.8 1.8 %collective-permute-start.3 = (bf16[32,1536]{1,0:T(8,128)(2,1)S(1)}, bf16[32,1536]{1,0:T(8,128)(2,1)S(1)}, u32[]{:S(2)}, u32[]{:S(2)}) collective-permute-start(bf16[32,1536]{1,0:T(8,128)(2,1)S(1)} %get-tuple-element.18), channel_id=1, source_target_pairs={{0,8},{8,16},{16,24},{24,0},{1,9},{9,17},{17,25},{25,1},{2,10},{10... | collective-permute-start | bytes 294920 | tf_op jit(solution)/shard_map/ppermute | solution.py:28
  12.6 2.3 %factor.1.factor_ref = bf16[32,2048]{1,0:T(8,128)(2,1)S(1)} custom-call(f32[1,1,4,8]{3,2,1,0:T(4,128)S(1)} %get-tuple-element.15.gates_ref.after_ref, bf16[32,6144]{1,0:T(8,128)(2,1)S(1)} %pad_maximum_fusion.1.rows_ref.own_ref, bf16[1,3072,1024]{2,1,0:T(8,128)(2,1)S(1)} %get-tuple-element.16.upper_ref, bf16[1,3072,1024]{2,1,0:T(8,128)(2,1)S(1)} %get-tuple-element.17.lower_ref), custom_call_target="tpu_custom_call" | custom-call | flops 402653184 | bytes 12582912 | tf_op jit(solution)/shard_map/factor/pallas_call | solution.py:223
  14.9 2.1 %collective-permute-start.8 = (bf16[32,2048]{1,0:T(8,128)(2,1)S(1)}, bf16[32,2048]{1,0:T(8,128)(2,1)S(1)}, u32[]{:S(2)}, u32[]{:S(2)}) collective-permute-start(bf16[32,2048]{1,0:T(8,128)(2,1)S(1)} %factor.1.factor_ref), channel_id=1, source_target_pairs={{0,24},{8,0},{16,8},{24,16},{1,25},{9,1},{17,9},{25,17},{2,26},{10... | collective-permute-start | bytes 393224 | tf_op jit(solution)/shard_map/ppermute | solution.py:28
  17.0 1.0 %collective-permute-start.7 = (bf16[32,2048]{1,0:T(8,128)(2,1)S(1)}, bf16[32,2048]{1,0:T(8,128)(2,1)S(1)}, u32[]{:S(2)}, u32[]{:S(2)}) collective-permute-start(bf16[32,2048]{1,0:T(8,128)(2,1)S(1)} %factor.1.factor_ref), channel_id=1, source_target_pairs={{0,16},{8,24},{16,0},{24,8},{1,17},{9,25},{17,1},{25,9},{2,18},{10... | collective-permute-start | bytes 393224 | tf_op jit(solution)/shard_map/ppermute | solution.py:28
  18.0 1.6 %collective-permute-start.6 = (bf16[32,2048]{1,0:T(8,128)(2,1)S(1)}, bf16[32,2048]{1,0:T(8,128)(2,1)S(1)}, u32[]{:S(2)}, u32[]{:S(2)}) collective-permute-start(bf16[32,2048]{1,0:T(8,128)(2,1)S(1)} %factor.1.factor_ref), channel_id=1, source_target_pairs={{0,8},{8,16},{16,24},{24,0},{1,9},{9,17},{17,25},{25,1},{2,10},{10... | collective-permute-start | bytes 393224 | tf_op jit(solution)/shard_map/ppermute | solution.py:28
  19.6 0.4 collective-permute-start.4
  19.9 2.6 %piece.1.refs_0_ = bf16[8,8,1536]{2,1,0:T(8,128)(2,1)} custom-call(bf16[32,2048]{1,0:T(8,128)(2,1)S(1)} %factor.1.factor_ref, bf16[1,3072,1024]{2,1,0:T(8,128)(2,1)S(1)} %get-tuple-element.16.upper_ref), custom_call_target="tpu_custom_call" | custom-call | flops 201326592 | bytes 6291456 | tf_op jit(solution)/shard_map/piece/pallas_call | solution.py:238
  22.6 0.0 collective-permute-done.3
  22.6 2.9 %collective-permute-start.5 = (bf16[32,1536]{1,0:T(8,128)(2,1)S(1)}, bf16[32,1536]{1,0:T(8,128)(2,1)S(1)}, u32[]{:S(2)}, u32[]{:S(2)}) collective-permute-start(bf16[32,1536]{1,0:T(8,128)(2,1)S(1)} %get-tuple-element.20), channel_id=1, source_target_pairs={{0,24},{8,0},{16,8},{24,16},{1,25},{9,1},{17,9},{25,17},{2,26},{10... | collective-permute-start | bytes 294920 | tf_op jit(solution)/shard_map/ppermute | solution.py:28
  25.5 9.5 %collective-permute-done.4 = bf16[32,1536]{1,0:T(8,128)(2,1)S(1)} collective-permute-done((bf16[32,1536]{1,0:T(8,128)(2,1)S(1)}, bf16[32,1536]{1,0:T(8,128)(2,1)S(1)}, u32[]{:S(2)}, u32[]{:S(2)}) %collective-permute-start.4) | collective-permute-done | bytes 98336 | tf_op jit(solution)/shard_map/ppermute | solution.py:28
  35.0 0.0 collective-permute-done.5
  35.0 3.4 %all-to-all-start = ((bf16[8,8,1536]{2,1,0:T(8,128)(2,1)}), bf16[8,8,1536]{2,1,0:T(8,128)(2,1)S(1)}, u32[]{:S(2)}, u32[]{:S(2)}) async-start(bf16[8,8,1536]{2,1,0:T(8,128)(2,1)} %tie.1), calls=%async_computation | async-start | bytes 393216 | tf_op jit(solution)/shard_map/all_to_all | solution.py:258
  38.4 0.0 collective-permute-done.8
  38.4 0.0 collective-permute-done.7
  38.4 0.0 collective-permute-done.6
  38.5 3.1 %weight.1 = (f32[1,768,1024]{2,1,0:T(8,128)}, f32[1,768,1024]{2,1,0:T(8,128)}) custom-call(bf16[32,6144]{1,0:T(8,128)(2,1)S(1)} %pad_maximum_fusion.1.rows_ref.own_ref, bf16[96,1536]{1,0:T(8,128)(2,1)S(1)} %constant_dynamic-update-slice_fusion.refs_1_.part_ref, bf16[128,2048]{1,0:T(8,128)(2,1)S(1)} %pad_maximum_fusion.factor_ref), custom_call_target="tpu_custom_call" | custom-call | flops 402653184 | bytes 50331648 | tf_op jit(solution)/shard_map/weight/pallas_call | solution.py:267
  41.7 2.4 %all-to-all-done = bf16[8,8,1536]{2,1,0:T(8,128)(2,1)S(1)} async-done(((bf16[8,8,1536]{2,1,0:T(8,128)(2,1)}), bf16[8,8,1536]{2,1,0:T(8,128)(2,1)S(1)}, u32[]{:S(2)}, u32[]{:S(2)}) %all-to-all-start) | async-done | bytes 196640 | tf_op jit(solution)/shard_map/all_to_all | solution.py:258
  44.1 0.9 %fusion = bf16[1,64,1536]{2,1,0:T(8,128)(2,1)} fusion(bf16[64,64]{1,0:T(8,128)(2,1)S(1)} %get-tuple-element.13, bf16[8,8,1536]{2,1,0:T(8,128)(2,1)S(1)} %all-to-all-done), kind=kOutput, calls=%fused_computation.1 | convolution fusion | flops 12681216 | bytes 401408 | tf_op jit(solution)/shard_map/dot_general | solution.py:259
  (8 shorter events, 0.2 us)
Async XLA Ops:
  2.1 7.9 %collective-permute-start.2 = (bf16[8,6144]{1,0:T(8,128)(2,1)S(1)}, bf16[8,6144]{1,0:T(8,128)(2,1)S(1)}, u32[]{:S(2)}, u32[]{:S(2)}) collective-permute-start(bf16[8,6144]{1,0:T(8,128)(2,1)S(1)} %get-tuple-element.24), channel_id=1, source_target_pairs={{0,6},{2,0},{4,2},{6,4},{1,7},{3,1},{5,3},{7,5},{8,14},{10,8},{12,... | collective-permute-start | bytes 294920 | tf_op jit(solution)/shard_map/ppermute | solution.py:28
  4.6 6.1 %collective-permute-start.1 = (bf16[8,6144]{1,0:T(8,128)(2,1)S(1)}, bf16[8,6144]{1,0:T(8,128)(2,1)S(1)}, u32[]{:S(2)}, u32[]{:S(2)}) collective-permute-start(bf16[8,6144]{1,0:T(8,128)(2,1)S(1)} %get-tuple-element.25), channel_id=1, source_target_pairs={{0,4},{2,6},{4,0},{6,2},{1,5},{3,7},{5,1},{7,3},{8,12},{10,14},{12... | collective-permute-start | bytes 294920 | tf_op jit(solution)/shard_map/ppermute | solution.py:28
  5.2 5.5 %collective-permute-start = (bf16[8,6144]{1,0:T(8,128)(2,1)S(1)}, bf16[8,6144]{1,0:T(8,128)(2,1)S(1)}, u32[]{:S(2)}, u32[]{:S(2)}) collective-permute-start(bf16[8,6144]{1,0:T(8,128)(2,1)S(1)} %get-tuple-element.26), channel_id=1, source_target_pairs={{0,2},{2,4},{4,6},{6,0},{1,3},{3,5},{5,7},{7,1},{8,10},{10,12},{12... | collective-permute-start | bytes 294920 | tf_op jit(solution)/shard_map/ppermute | solution.py:28
  10.8 11.8 %collective-permute-start.3 = (bf16[32,1536]{1,0:T(8,128)(2,1)S(1)}, bf16[32,1536]{1,0:T(8,128)(2,1)S(1)}, u32[]{:S(2)}, u32[]{:S(2)}) collective-permute-start(bf16[32,1536]{1,0:T(8,128)(2,1)S(1)} %get-tuple-element.18), channel_id=1, source_target_pairs={{0,8},{8,16},{16,24},{24,0},{1,9},{9,17},{17,25},{25,1},{2,10},{10... | collective-permute-start | bytes 294920 | tf_op jit(solution)/shard_map/ppermute | solution.py:28
  14.9 23.5 %collective-permute-start.8 = (bf16[32,2048]{1,0:T(8,128)(2,1)S(1)}, bf16[32,2048]{1,0:T(8,128)(2,1)S(1)}, u32[]{:S(2)}, u32[]{:S(2)}) collective-permute-start(bf16[32,2048]{1,0:T(8,128)(2,1)S(1)} %factor.1.factor_ref), channel_id=1, source_target_pairs={{0,24},{8,0},{16,8},{24,16},{1,25},{9,1},{17,9},{25,17},{2,26},{10... | collective-permute-start | bytes 393224 | tf_op jit(solution)/shard_map/ppermute | solution.py:28
  17.0 21.4 %collective-permute-start.7 = (bf16[32,2048]{1,0:T(8,128)(2,1)S(1)}, bf16[32,2048]{1,0:T(8,128)(2,1)S(1)}, u32[]{:S(2)}, u32[]{:S(2)}) collective-permute-start(bf16[32,2048]{1,0:T(8,128)(2,1)S(1)} %factor.1.factor_ref), channel_id=1, source_target_pairs={{0,16},{8,24},{16,0},{24,8},{1,17},{9,25},{17,1},{25,9},{2,18},{10... | collective-permute-start | bytes 393224 | tf_op jit(solution)/shard_map/ppermute | solution.py:28
  18.0 20.5 %collective-permute-start.6 = (bf16[32,2048]{1,0:T(8,128)(2,1)S(1)}, bf16[32,2048]{1,0:T(8,128)(2,1)S(1)}, u32[]{:S(2)}, u32[]{:S(2)}) collective-permute-start(bf16[32,2048]{1,0:T(8,128)(2,1)S(1)} %factor.1.factor_ref), channel_id=1, source_target_pairs={{0,8},{8,16},{16,24},{24,0},{1,9},{9,17},{17,25},{25,1},{2,10},{10... | collective-permute-start | bytes 393224 | tf_op jit(solution)/shard_map/ppermute | solution.py:28
  19.6 15.4 %collective-permute-start.4 = (bf16[32,1536]{1,0:T(8,128)(2,1)S(1)}, bf16[32,1536]{1,0:T(8,128)(2,1)S(1)}, u32[]{:S(2)}, u32[]{:S(2)}) collective-permute-start(bf16[32,1536]{1,0:T(8,128)(2,1)S(1)} %get-tuple-element.19), channel_id=1, source_target_pairs={{0,16},{8,24},{16,0},{24,8},{1,17},{9,25},{17,1},{25,9},{2,18},{10... | collective-permute-start | bytes 294920 | tf_op jit(solution)/shard_map/ppermute | solution.py:28
  22.6 12.4 %collective-permute-start.5 = (bf16[32,1536]{1,0:T(8,128)(2,1)S(1)}, bf16[32,1536]{1,0:T(8,128)(2,1)S(1)}, u32[]{:S(2)}, u32[]{:S(2)}) collective-permute-start(bf16[32,1536]{1,0:T(8,128)(2,1)S(1)} %get-tuple-element.20), channel_id=1, source_target_pairs={{0,24},{8,0},{16,8},{24,16},{1,25},{9,1},{17,9},{25,17},{2,26},{10... | collective-permute-start | bytes 294920 | tf_op jit(solution)/shard_map/ppermute | solution.py:28
  35.0 9.1 %all-to-all-start = ((bf16[8,8,1536]{2,1,0:T(8,128)(2,1)}), bf16[8,8,1536]{2,1,0:T(8,128)(2,1)S(1)}, u32[]{:S(2)}, u32[]{:S(2)}) async-start(bf16[8,8,1536]{2,1,0:T(8,128)(2,1)} %tie.1), calls=%async_computation | async-start | bytes 393216 | tf_op jit(solution)/shard_map/all_to_all | solution.py:258

commit v11 on v9

--- a/solution.py
+++ b/solution.py
@@ -23,9 +23,8 @@
 
 def hop(x, axis, step):
     n = lax.axis_size(axis)
-    if step % n == 0:
-        return x
-    return lax.ppermute(x, axis, [(i, (i + step) % n) for i in range(n)])
+    assert n & (n - 1) == 0
+    return lax.ppermute(x, axis, [(i, i ^ step) for i in range(n)]) if step else x
 
 
 def column(ref, order):
@@ -58,7 +57,7 @@
         spots = lax.broadcasted_iota(jnp.int32, (wanted.shape[0], tok_dev), 1)
         return jnp.where(wanted == spots, 1.0, 0.0).astype(jnp.bfloat16)
 
-    selector = one_hot([(me + s) % n_exp for s in range(n_exp)])
+    selector = one_hot([me ^ s for s in range(n_exp)])
     spread_ref[...] = one_hot([e for e in range(n_exp) for _ in range(n_hid)])
     for at, copy, source in ((0, copies[1], tokens_ref), (width, copies[2], upstream_ref)):
         copy.wait()
@@ -75,7 +74,7 @@
     my_dp = lax.axis_index("dp")
     spot = pl.ds(pl.multiple_of(lax.axis_index("hidden") * share, 16), share)
     for s, out_ref in enumerate(out_refs):
-        at = ((my_dp + s + 1) % n_dp) * cols
+        at = (my_dp ^ (s + 1)) * cols
         for half in range(2):
             out_ref[:, half * cols : (half + 1) * cols] = rows_ref[
                 spot, pl.ds(pl.multiple_of(half * width + at, 128), cols)
@@ -99,7 +98,7 @@
     n_exp = gates_ref.shape[2]
     width, units = upper_ref.shape[1:]
     me = lax.axis_index("expert")
-    gate = column(gates_ref, [(me + n_exp - s) % n_exp for s in range(n_exp)])
+    gate = column(gates_ref, [me ^ s for s in range(n_exp)])
     pre = jnp.dot(rows_ref[:, :width], upper_ref[0], preferred_element_type=jnp.float32)
     back = jnp.dot(rows_ref[:, width:], lower_ref[0], preferred_element_type=jnp.float32)
     value, slope = gelu_pair(pre)
@@ -116,7 +115,7 @@
         factor_ref[:, :units], upper_ref[0], (((1,), (1,)), ((), ())), preferred_element_type=jnp.float32
     )
     for s in range(n_exp):
-        owner = ((me + n_exp - s) % n_exp) * n_hid
+        owner = (me ^ s) * n_hid
         for h in range(n_hid):
             out_ref[owner + h] = piece[
                 s * n_pick : (s + 1) * n_pick, h * part : (h + 1) * part
@@ -149,7 +148,7 @@
             :, pl.ds(pl.multiple_of(half * width + start, 128), cols)
         ]
     for t, part in enumerate(part_refs):
-        spot = ((my_hid + n_hid - t) % n_hid) * rows
+        spot = (my_hid ^ t) * rows
         for s in range(1, n_dp):
             side_ref[pl.ds(pl.multiple_of(s * slots + spot, 16), rows), :] = part[s - 1]
     step = units // chunks

time: 39.7 us -> 39.8 us (level)
    all_to_all x1, waiting for transfers between devices: 0.01 us -> 0.85 us  [local(): returned = lax.all_to_all(piece, ('expert', 'hidden'), 0, 0)]
    ppermute x10, waiting for transfers between devices: 6.13 us -> 5.3 us  [hop(): lax.ppermute(x, axis, [(i, i ^ step) for i in range(n)])]
  transfers between devices with their start and end apart: 11 -> 11, of which waited for: 4 -> 5; matrix products, arithmetic and copies ran while one was open for 0% -> 0% of each run, Pallas kernels for 32% -> 32%
where the time goes in v11:
time: 39.8 us; the launch traced here: 39.6 us
  starting transfers between devices  17.5 us (44%)
  Pallas kernels  14.2 us (36%)
  waiting for transfers between devices  6.15 us (15%)
  matrix products  0.91 us (2%)
  between operations  0.73 us (2%)
    ppermute x10, starting transfers between devices, hop(): lax.ppermute(x, axis, [(i, i ^ step) for i in range(n)])  14.1 us
    ppermute x10, waiting for transfers between devices, hop(): lax.ppermute(x, axis, [(i, i ^ step) for i in range(n)])  5.3 us
    pallas_call x1, Pallas kernels, local(): pl.pallas_call(load_kernel, out_shape=[jax.ShapeDtypeStruct(x.shape, x.dt...  4.64 us
    all_to_all x1, starting transfers between devices, local(): returned = lax.all_to_all(piece, ('expert', 'hidden'), 0, 0)  3.39 us
    pallas_call x1, Pallas kernels, local(): pl.pallas_call(functools.partial(weight_kernel, chunks, (n_dp, n_hid)), o...  3.18 us
    pallas_call x1, Pallas kernels, local(): pl.pallas_call(functools.partial(piece_kernel, n_hid), out_shape=jax.Shap...  2.63 us
    pallas_call x1, Pallas kernels, local(): pl.pallas_call(factor_kernel, out_shape=jax.ShapeDtypeStruct((slots, 2 *...  2.29 us
    pallas_call x1, Pallas kernels, local(): pl.pallas_call(functools.partial(pick_kernel, n_hid), out_shape=[jax.Shap...  1.42 us
  transfers between devices with their start and end apart: 11, of which 5 were waited for; matrix products, arithmetic and copies ran while one was open for 0% of the time, Pallas kernels for 32%

profile of v11, /device:TPU:0, one launch (start us, length us, event | category | flops | bytes accessed | tf_op | source)
XLA Modules:
  0.0 39.6 jit_solution(13452129883623699156)
XLA Ops:
  0.6 1.4 %pick.1 = (bf16[32,6144]{1,0:T(8,128)(2,1)S(1)}, bf16[64,64]{1,0:T(8,128)(2,1)S(1)}) custom-call(s32[1,1,4,8]{3,2,1,0:T(4,128)} %picks_hbm.1, bf16[1,64,3072]{2,1,0:T(8,128)(2,1)} %tokens_hbm.1, bf16[1,64,3072]{2,1,0:T(8,128)(2,1)} %upstream_hbm.1), custom_call_target="tpu_custom_call" | custom-call | tf_op jit(solution)/shard_map/pick/pallas_call | solution.py:195
  2.1 2.5 %collective-permute-start.2 = (bf16[8,6144]{1,0:T(8,128)(2,1)S(1)}, bf16[8,6144]{1,0:T(8,128)(2,1)S(1)}, u32[]{:S(2)}, u32[]{:S(2)}) collective-permute-start(bf16[8,6144]{1,0:T(8,128)(2,1)S(1)} %get-tuple-element.24), channel_id=1, source_target_pairs={{0,6},{2,4},{4,2},{6,0},{1,7},{3,5},{5,3},{7,1},{8,14},{10,12},{12... | collective-permute-start | bytes 294920 | tf_op jit(solution)/shard_map/ppermute | solution.py:27
  4.6 0.6 %collective-permute-start.1 = (bf16[8,6144]{1,0:T(8,128)(2,1)S(1)}, bf16[8,6144]{1,0:T(8,128)(2,1)S(1)}, u32[]{:S(2)}, u32[]{:S(2)}) collective-permute-start(bf16[8,6144]{1,0:T(8,128)(2,1)S(1)} %get-tuple-element.25), channel_id=1, source_target_pairs={{0,4},{2,6},{4,0},{6,2},{1,5},{3,7},{5,1},{7,3},{8,12},{10,14},{12... | collective-permute-start | bytes 294920 | tf_op jit(solution)/shard_map/ppermute | solution.py:27
  5.2 0.0 collective-permute-start
  5.3 4.6 %load.1 = (f32[1,1,4,8]{3,2,1,0:T(4,128)S(1)}, bf16[1,3072,1024]{2,1,0:T(8,128)(2,1)S(1)}, bf16[1,3072,1024]{2,1,0:T(8,128)(2,1)S(1)}) custom-call(bf16[32,6144]{1,0:T(8,128)(2,1)S(1)} %get-tuple-element.14.after_ref, f32[1,1,4,8]{3,2,1,0:T(4,128)} %gates_hbm.1, bf16[1,3072,1024]{2,1,0:T(8,128)(2,1)} %upper_hbm.1, bf16[1,3072,1024]{2,1,0:T(8,128)(2,1)} %lower_hbm.1), custom_call_target="tpu_custom_call" | custom-call | bytes 25165824 | tf_op jit(solution)/shard_map/load/pallas_call | solution.py:216
  9.9 0.0 collective-permute-done.2
  9.9 0.1 collective-permute-done.1
  10.0 0.0 collective-permute-done
  10.1 2.4 %collective-permute-start.3 = (bf16[16,1536]{1,0:T(8,128)(2,1)S(1)}, bf16[16,1536]{1,0:T(8,128)(2,1)S(1)}, u32[]{:S(2)}, u32[]{:S(2)}) collective-permute-start(bf16[16,1536]{1,0:T(8,128)(2,1)S(1)} %get-tuple-element.16), channel_id=1, source_target_pairs={{0,8},{8,0},{16,24},{24,16},{1,9},{9,1},{17,25},{25,17},{2,10},{10... | collective-permute-start | bytes 147464 | tf_op jit(solution)/shard_map/ppermute | solution.py:27
  12.5 2.6 %collective-permute-start.4 = (bf16[16,1536]{1,0:T(8,128)(2,1)S(1)}, bf16[16,1536]{1,0:T(8,128)(2,1)S(1)}, u32[]{:S(2)}, u32[]{:S(2)}) collective-permute-start(bf16[16,1536]{1,0:T(8,128)(2,1)S(1)} %get-tuple-element.19), channel_id=1, source_target_pairs={{0,16},{8,24},{16,0},{24,8},{1,17},{9,25},{17,1},{25,9},{2,18},{10... | collective-permute-start | bytes 147464 | tf_op jit(solution)/shard_map/ppermute | solution.py:27
  15.1 0.0 collective-permute-start.5
  15.1 0.0 collective-permute-done.3.after_ref.refs_0_
  15.1 2.3 %factor.1.factor_ref.after_ref = bf16[32,2048]{1,0:T(8,128)(2,1)S(1)} custom-call(bf16[16,1536]{1,0:T(8,128)(2,1)S(1)} %collective-permute-done.3.after_ref.refs_0_, f32[1,1,4,8]{3,2,1,0:T(4,128)S(1)} %get-tuple-element.15.after_ref.gates_ref, bf16[32,6144]{1,0:T(8,128)(2,1)S(1)} %pad_maximum_fusion.1.rows_ref.own_ref, ...), custom_call_target="tpu_custom_call" | custom-call | flops 402653184 | bytes 12582912 | tf_op jit(solution)/shard_map/factor/pallas_call | solution.py:239
  17.4 1.1 %collective-permute-done.4.refs_1_ = bf16[16,1536]{1,0:T(8,128)(2,1)S(1)} collective-permute-done((bf16[16,1536]{1,0:T(8,128)(2,1)S(1)}, bf16[16,1536]{1,0:T(8,128)(2,1)S(1)}, u32[]{:S(2)}, u32[]{:S(2)}) %collective-permute-start.4) | collective-permute-done | bytes 49184 | tf_op jit(solution)/shard_map/ppermute | solution.py:27
  18.5 2.5 %collective-permute-done.5.refs_2_ = bf16[16,1536]{1,0:T(8,128)(2,1)S(1)} collective-permute-done((bf16[16,1536]{1,0:T(8,128)(2,1)S(1)}, bf16[16,1536]{1,0:T(8,128)(2,1)S(1)}, u32[]{:S(2)}, u32[]{:S(2)}) %collective-permute-start.5) | collective-permute-done | bytes 49184 | tf_op jit(solution)/shard_map/ppermute | solution.py:27
  21.0 1.6 %collective-permute-start.6 = (bf16[3,16,1536]{2,1,0:T(8,128)(2,1)S(1)}, bf16[3,16,1536]{2,1,0:T(8,128)(2,1)S(1)}, u32[]{:S(2)}, u32[]{:S(2)}) collective-permute-start(bf16[3,16,1536]{2,1,0:T(8,128)(2,1)S(1)} %stack.1.refs_0_), channel_id=1, source_target_pairs={{0,1},{1,0},{2,3},{3,2},{4,5},{5,4},{6,7},{7,6},{8,9},{9,8},{10,11... | collective-permute-start | bytes 442376 | tf_op jit(solution)/shard_map/ppermute | solution.py:27
  22.6 0.9 %collective-permute-start.9 = (bf16[32,2048]{1,0:T(8,128)(2,1)S(1)}, bf16[32,2048]{1,0:T(8,128)(2,1)S(1)}, u32[]{:S(2)}, u32[]{:S(2)}) collective-permute-start(bf16[32,2048]{1,0:T(8,128)(2,1)S(1)} %factor.1.factor_ref.after_ref), channel_id=1, source_target_pairs={{0,24},{8,16},{16,8},{24,0},{1,25},{9,17},{17,9},{25,1},{2,26},{10... | collective-permute-start | bytes 393224 | tf_op jit(solution)/shard_map/ppermute | solution.py:27
  23.5 0.0 collective-permute-start.8
  23.5 3.4 %collective-permute-start.7 = (bf16[32,2048]{1,0:T(8,128)(2,1)S(1)}, bf16[32,2048]{1,0:T(8,128)(2,1)S(1)}, u32[]{:S(2)}, u32[]{:S(2)}) collective-permute-start(bf16[32,2048]{1,0:T(8,128)(2,1)S(1)} %factor.1.factor_ref.after_ref), channel_id=1, source_target_pairs={{0,8},{8,0},{16,24},{24,16},{1,9},{9,1},{17,25},{25,17},{2,10},{10... | collective-permute-start | bytes 393224 | tf_op jit(solution)/shard_map/ppermute | solution.py:27
  27.0 2.6 %piece.1.refs_0_ = bf16[8,8,1536]{2,1,0:T(8,128)(2,1)} custom-call(bf16[32,2048]{1,0:T(8,128)(2,1)S(1)} %factor.1.factor_ref.after_ref, bf16[1,3072,1024]{2,1,0:T(8,128)(2,1)S(1)} %get-tuple-element.17.upper_ref), custom_call_target="tpu_custom_call" | custom-call | flops 201326592 | bytes 6291456 | tf_op jit(solution)/shard_map/piece/pallas_call | solution.py:262
  29.6 0.0 collective-permute-done.6.refs_1_
  29.6 3.4 %all-to-all-start = ((bf16[8,8,1536]{2,1,0:T(8,128)(2,1)}), bf16[8,8,1536]{2,1,0:T(8,128)(2,1)S(1)}, u32[]{:S(2)}, u32[]{:S(2)}) async-start(bf16[8,8,1536]{2,1,0:T(8,128)(2,1)} %tie.1), calls=%async_computation | async-start | bytes 393216 | tf_op jit(solution)/shard_map/all_to_all | solution.py:282
  33.0 0.0 collective-permute-done.9
  33.0 1.6 %collective-permute-done.8 = bf16[32,2048]{1,0:T(8,128)(2,1)S(1)} collective-permute-done((bf16[32,2048]{1,0:T(8,128)(2,1)S(1)}, bf16[32,2048]{1,0:T(8,128)(2,1)S(1)}, u32[]{:S(2)}, u32[]{:S(2)}) %collective-permute-start.8) | collective-permute-done | bytes 131104 | tf_op jit(solution)/shard_map/ppermute | solution.py:27
  34.6 0.0 collective-permute-done.7
  34.6 3.2 %weight.1 = (f32[1,768,1024]{2,1,0:T(8,128)}, f32[1,768,1024]{2,1,0:T(8,128)}) custom-call(bf16[32,6144]{1,0:T(8,128)(2,1)S(1)} %pad_maximum_fusion.1.rows_ref.own_ref, bf16[3,16,1536]{2,1,0:T(8,128)(2,1)S(1)} %stack.1.refs_0_, bf16[3,16,1536]{2,1,0:T(8,128)(2,1)S(1)} %collective-permute-done.6.refs_1_, bf16[128,2048]{1,0:T(8,128)(2,1)S(1)} %pad_maximum_fusion.refs_2_), custom_call_target="tpu_custom_call" | custom-call | flops 402653184 | bytes 50331648 | tf_op jit(solution)/shard_map/weight/pallas_call | solution.py:291
  37.8 0.8 %all-to-all-done = bf16[8,8,1536]{2,1,0:T(8,128)(2,1)S(1)} async-done(((bf16[8,8,1536]{2,1,0:T(8,128)(2,1)}), bf16[8,8,1536]{2,1,0:T(8,128)(2,1)S(1)}, u32[]{:S(2)}, u32[]{:S(2)}) %all-to-all-start) | async-done | bytes 196640 | tf_op jit(solution)/shard_map/all_to_all | solution.py:282
  38.7 0.9 %fusion = bf16[1,64,1536]{2,1,0:T(8,128)(2,1)} fusion(bf16[64,64]{1,0:T(8,128)(2,1)S(1)} %get-tuple-element.13, bf16[8,8,1536]{2,1,0:T(8,128)(2,1)S(1)} %all-to-all-done), kind=kOutput, calls=%fused_computation.1 | convolution fusion | flops 12681216 | bytes 401408 | tf_op jit(solution)/shard_map/dot_general | solution.py:283
  (6 shorter events, 0.1 us)
Async XLA Ops:
  2.1 7.8 %collective-permute-start.2 = (bf16[8,6144]{1,0:T(8,128)(2,1)S(1)}, bf16[8,6144]{1,0:T(8,128)(2,1)S(1)}, u32[]{:S(2)}, u32[]{:S(2)}) collective-permute-start(bf16[8,6144]{1,0:T(8,128)(2,1)S(1)} %get-tuple-element.24), channel_id=1, source_target_pairs={{0,6},{2,4},{4,2},{6,0},{1,7},{3,5},{5,3},{7,1},{8,14},{10,12},{12... | collective-permute-start | bytes 294920 | tf_op jit(solution)/shard_map/ppermute | solution.py:27
  4.6 5.5 %collective-permute-start.1 = (bf16[8,6144]{1,0:T(8,128)(2,1)S(1)}, bf16[8,6144]{1,0:T(8,128)(2,1)S(1)}, u32[]{:S(2)}, u32[]{:S(2)}) collective-permute-start(bf16[8,6144]{1,0:T(8,128)(2,1)S(1)} %get-tuple-element.25), channel_id=1, source_target_pairs={{0,4},{2,6},{4,0},{6,2},{1,5},{3,7},{5,1},{7,3},{8,12},{10,14},{12... | collective-permute-start | bytes 294920 | tf_op jit(solution)/shard_map/ppermute | solution.py:27
  5.2 4.8 %collective-permute-start = (bf16[8,6144]{1,0:T(8,128)(2,1)S(1)}, bf16[8,6144]{1,0:T(8,128)(2,1)S(1)}, u32[]{:S(2)}, u32[]{:S(2)}) collective-permute-start(bf16[8,6144]{1,0:T(8,128)(2,1)S(1)} %get-tuple-element.26), channel_id=1, source_target_pairs={{0,2},{2,0},{4,6},{6,4},{1,3},{3,1},{5,7},{7,5},{8,10},{10,8},{12,... | collective-permute-start | bytes 294920 | tf_op jit(solution)/shard_map/ppermute | solution.py:27
  10.1 5.0 %collective-permute-start.3 = (bf16[16,1536]{1,0:T(8,128)(2,1)S(1)}, bf16[16,1536]{1,0:T(8,128)(2,1)S(1)}, u32[]{:S(2)}, u32[]{:S(2)}) collective-permute-start(bf16[16,1536]{1,0:T(8,128)(2,1)S(1)} %get-tuple-element.16), channel_id=1, source_target_pairs={{0,8},{8,0},{16,24},{24,16},{1,9},{9,1},{17,25},{25,17},{2,10},{10... | collective-permute-start | bytes 147464 | tf_op jit(solution)/shard_map/ppermute | solution.py:27
  12.5 6.0 %collective-permute-start.4 = (bf16[16,1536]{1,0:T(8,128)(2,1)S(1)}, bf16[16,1536]{1,0:T(8,128)(2,1)S(1)}, u32[]{:S(2)}, u32[]{:S(2)}) collective-permute-start(bf16[16,1536]{1,0:T(8,128)(2,1)S(1)} %get-tuple-element.19), channel_id=1, source_target_pairs={{0,16},{8,24},{16,0},{24,8},{1,17},{9,25},{17,1},{25,9},{2,18},{10... | collective-permute-start | bytes 147464 | tf_op jit(solution)/shard_map/ppermute | solution.py:27
  15.1 5.9 %collective-permute-start.5 = (bf16[16,1536]{1,0:T(8,128)(2,1)S(1)}, bf16[16,1536]{1,0:T(8,128)(2,1)S(1)}, u32[]{:S(2)}, u32[]{:S(2)}) collective-permute-start(bf16[16,1536]{1,0:T(8,128)(2,1)S(1)} %get-tuple-element.20), channel_id=1, source_target_pairs={{0,24},{8,16},{16,8},{24,0},{1,25},{9,17},{17,9},{25,1},{2,26},{10... | collective-permute-start | bytes 147464 | tf_op jit(solution)/shard_map/ppermute | solution.py:27
  21.0 8.6 %collective-permute-start.6 = (bf16[3,16,1536]{2,1,0:T(8,128)(2,1)S(1)}, bf16[3,16,1536]{2,1,0:T(8,128)(2,1)S(1)}, u32[]{:S(2)}, u32[]{:S(2)}) collective-permute-start(bf16[3,16,1536]{2,1,0:T(8,128)(2,1)S(1)} %stack.1.refs_0_), channel_id=1, source_target_pairs={{0,1},{1,0},{2,3},{3,2},{4,5},{5,4},{6,7},{7,6},{8,9},{9,8},{10,11... | collective-permute-start | bytes 442376 | tf_op jit(solution)/shard_map/ppermute | solution.py:27
  22.6 10.4 %collective-permute-start.9 = (bf16[32,2048]{1,0:T(8,128)(2,1)S(1)}, bf16[32,2048]{1,0:T(8,128)(2,1)S(1)}, u32[]{:S(2)}, u32[]{:S(2)}) collective-permute-start(bf16[32,2048]{1,0:T(8,128)(2,1)S(1)} %factor.1.factor_ref.after_ref), channel_id=1, source_target_pairs={{0,24},{8,16},{16,8},{24,0},{1,25},{9,17},{17,9},{25,1},{2,26},{10... | collective-permute-start | bytes 393224 | tf_op jit(solution)/shard_map/ppermute | solution.py:27
  23.5 11.1 %collective-permute-start.8 = (bf16[32,2048]{1,0:T(8,128)(2,1)S(1)}, bf16[32,2048]{1,0:T(8,128)(2,1)S(1)}, u32[]{:S(2)}, u32[]{:S(2)}) collective-permute-start(bf16[32,2048]{1,0:T(8,128)(2,1)S(1)} %factor.1.factor_ref.after_ref), channel_id=1, source_target_pairs={{0,16},{8,24},{16,0},{24,8},{1,17},{9,25},{17,1},{25,9},{2,18},{10... | collective-permute-start | bytes 393224 | tf_op jit(solution)/shard_map/ppermute | solution.py:27
  23.5 11.1 %collective-permute-start.7 = (bf16[32,2048]{1,0:T(8,128)(2,1)S(1)}, bf16[32,2048]{1,0:T(8,128)(2,1)S(1)}, u32[]{:S(2)}, u32[]{:S(2)}) collective-permute-start(bf16[32,2048]{1,0:T(8,128)(2,1)S(1)} %factor.1.factor_ref.after_ref), channel_id=1, source_target_pairs={{0,8},{8,0},{16,24},{24,16},{1,9},{9,1},{17,25},{25,17},{2,10},{10... | collective-permute-start | bytes 393224 | tf_op jit(solution)/shard_map/ppermute | solution.py:27
  29.6 9.1 %all-to-all-start = ((bf16[8,8,1536]{2,1,0:T(8,128)(2,1)}), bf16[8,8,1536]{2,1,0:T(8,128)(2,1)S(1)}, u32[]{:S(2)}, u32[]{:S(2)}) async-start(bf16[8,8,1536]{2,1,0:T(8,128)(2,1)} %tie.1), calls=%async_computation | async-start | bytes 393216 | tf_op jit(solution)/shard_map/all_to_all | solution.py:282

commit v12 on v11

--- a/solution.py
+++ b/solution.py
@@ -128,14 +128,9 @@
         out_ref[s] = part[...]
 
 
-def tie_kernel(*refs):
-    pass
-
-
 def weight_kernel(chunks, shape, own_ref, *refs):
     n_dp, n_hid = shape
-    part_refs, refs = refs[:n_hid], refs[n_hid:]
-    factor_ref, up_ref, down_ref, side_ref, held, sems = refs
+    part_ref, factor_ref, up_ref, down_ref, side_ref, held, sems = refs
     units = factor_ref.shape[1] // 2
     cols = side_ref.shape[1] // 2
     width = own_ref.shape[1] // 2
@@ -147,10 +142,12 @@
         side_ref[:slots, half * cols : (half + 1) * cols] = own_ref[
             :, pl.ds(pl.multiple_of(half * width + start, 128), cols)
         ]
-    for t, part in enumerate(part_refs):
+    for t in range(n_hid):
         spot = (my_hid ^ t) * rows
         for s in range(1, n_dp):
-            side_ref[pl.ds(pl.multiple_of(s * slots + spot, 16), rows), :] = part[s - 1]
+            side_ref[pl.ds(pl.multiple_of(s * slots + spot, 16), rows), :] = part_ref[
+                s - 1, t * rows : (t + 1) * rows
+            ]
     step = units // chunks
     copies = []
     for which, out in ((0, up_ref), (1, down_ref)):
@@ -255,7 +252,7 @@
         compiler_params=ROOM,
         name="stack",
     )(factors, *parts)
-    parts = [hop(parts, "hidden", t) for t in range(n_hid)]
+    parts = jnp.concatenate([hop(parts, "hidden", t) for t in range(n_hid)], axis=1)
 
     gathered = jnp.concatenate([hop(factors, "dp", s) for s in range(n_dp)], axis=0)
 
@@ -270,15 +267,6 @@
         ),
         name="piece",
     )(factors, upper)
-    piece = pl.pallas_call(
-        tie_kernel,
-        out_shape=jax.ShapeDtypeStruct(piece.shape, piece.dtype),
-        in_specs=[ANY] * n_hid,
-        out_specs=ANY,
-        input_output_aliases={0: 0},
-        compiler_params=ROOM,
-        name="tie",
-    )(piece, *parts[1:])
     returned = lax.all_to_all(piece, ("expert", "hidden"), 0, 0)
     grad_rows = lax.dot_general(
         spread,
@@ -291,7 +279,7 @@
     grads = pl.pallas_call(
         functools.partial(weight_kernel, chunks, (n_dp, n_hid)),
         out_shape=[jax.ShapeDtypeStruct((1, cols, units), jnp.float32)] * 2,
-        in_specs=[VMEM] * (n_hid + 2),
+        in_specs=[VMEM] * 3,
         out_specs=[HBM] * 2,
         scratch_shapes=[
             pltpu.VMEM((n_dp * slots, 2 * cols), bf16),
@@ -303,7 +291,7 @@
             flops=4 * n_dp * slots * cols * units, bytes_accessed=64 * cols * units, transcendentals=0
         ),
         name="weight",
-    )(rows, *parts, gathered)
+    )(rows, parts, gathered)
     return (grad_rows[None], *grads)
 
 

time: 39.8 us -> 44.6 us (1.12)
  waiting for transfers between devices: 6.15 us -> 9.07 us
  starting transfers between devices: 17.5 us -> 19.4 us
    ppermute x10, waiting for transfers between devices: 5.3 us -> 9.06 us  [hop(): lax.ppermute(x, axis, [(i, i ^ step) for i in range(n)])]
    ppermute x10, starting transfers between devices: 14.1 us -> 15.6 us  [hop(): lax.ppermute(x, axis, [(i, i ^ step) for i in range(n)])]
    all_to_all x1, waiting for transfers between devices: 0.85 us -> 0.01 us  [local(): returned = lax.all_to_all(piece, ('expert', 'hidden'), 0, 0)]
  transfers between devices with their start and end apart: 11 -> 11, of which waited for: 5 -> 4; matrix products, arithmetic and copies ran while one was open for 0% -> 0% of each run, Pallas kernels for 32% -> 24%
where the time goes in v12:
time: 44.6 us; the launch traced here: 44.4 us
  starting transfers between devices  19.4 us (43%)
  Pallas kernels  14.2 us (32%)
  waiting for transfers between devices  9.07 us (20%)
  matrix products  0.91 us (2%)
  between operations  0.73 us (2%)
    ppermute x10, starting transfers between devices, hop(): lax.ppermute(x, axis, [(i, i ^ step) for i in range(n)])  15.6 us
    ppermute x10, waiting for transfers between devices, hop(): lax.ppermute(x, axis, [(i, i ^ step) for i in range(n)])  9.06 us
    pallas_call x1, Pallas kernels, local(): pl.pallas_call(load_kernel, out_shape=[jax.ShapeDtypeStruct(x.shape, x.dt...  4.64 us
    all_to_all x1, starting transfers between devices, local(): returned = lax.all_to_all(piece, ('expert', 'hidden'), 0, 0)  3.72 us
    pallas_call x1, Pallas kernels, local(): pl.pallas_call(functools.partial(weight_kernel, chunks, (n_dp, n_hid)), o...  3.18 us
    pallas_call x1, Pallas kernels, local(): pl.pallas_call(functools.partial(piece_kernel, n_hid), out_shape=jax.Shap...  2.63 us
    pallas_call x1, Pallas kernels, local(): pl.pallas_call(factor_kernel, out_shape=jax.ShapeDtypeStruct((slots, 2 *...  2.29 us
    pallas_call x1, Pallas kernels, local(): pl.pallas_call(functools.partial(pick_kernel, n_hid), out_shape=[jax.Shap...  1.42 us
  transfers between devices with their start and end apart: 11, of which 4 were waited for; matrix products, arithmetic and copies ran while one was open for 0% of the time, Pallas kernels for 24%

profile of v12, /device:TPU:0, one launch (start us, length us, event | category | flops | bytes accessed | tf_op | source)
XLA Modules:
  0.0 44.4 jit_solution(4524250363058430654)
XLA Ops:
  0.6 1.4 %pick.1 = (bf16[32,6144]{1,0:T(8,128)(2,1)S(1)}, bf16[64,64]{1,0:T(8,128)(2,1)S(1)}) custom-call(s32[1,1,4,8]{3,2,1,0:T(4,128)} %picks_hbm.1, bf16[1,64,3072]{2,1,0:T(8,128)(2,1)} %tokens_hbm.1, bf16[1,64,3072]{2,1,0:T(8,128)(2,1)} %upstream_hbm.1), custom_call_target="tpu_custom_call" | custom-call | tf_op jit(solution)/shard_map/pick/pallas_call | solution.py:192
  2.1 2.5 %collective-permute-start.2 = (bf16[8,6144]{1,0:T(8,128)(2,1)S(1)}, bf16[8,6144]{1,0:T(8,128)(2,1)S(1)}, u32[]{:S(2)}, u32[]{:S(2)}) collective-permute-start(bf16[8,6144]{1,0:T(8,128)(2,1)S(1)} %get-tuple-element.24), channel_id=1, source_target_pairs={{0,6},{2,4},{4,2},{6,0},{1,7},{3,5},{5,3},{7,1},{8,14},{10,12},{12... | collective-permute-start | bytes 294920 | tf_op jit(solution)/shard_map/ppermute | solution.py:27
  4.6 0.6 %collective-permute-start.1 = (bf16[8,6144]{1,0:T(8,128)(2,1)S(1)}, bf16[8,6144]{1,0:T(8,128)(2,1)S(1)}, u32[]{:S(2)}, u32[]{:S(2)}) collective-permute-start(bf16[8,6144]{1,0:T(8,128)(2,1)S(1)} %get-tuple-element.25), channel_id=1, source_target_pairs={{0,4},{2,6},{4,0},{6,2},{1,5},{3,7},{5,1},{7,3},{8,12},{10,14},{12... | collective-permute-start | bytes 294920 | tf_op jit(solution)/shard_map/ppermute | solution.py:27
  5.2 0.0 collective-permute-start
  5.3 4.6 %load.1 = (f32[1,1,4,8]{3,2,1,0:T(4,128)S(1)}, bf16[1,3072,1024]{2,1,0:T(8,128)(2,1)S(1)}, bf16[1,3072,1024]{2,1,0:T(8,128)(2,1)S(1)}) custom-call(bf16[32,6144]{1,0:T(8,128)(2,1)S(1)} %get-tuple-element.14.after_ref, f32[1,1,4,8]{3,2,1,0:T(4,128)} %gates_hbm.1, bf16[1,3072,1024]{2,1,0:T(8,128)(2,1)} %upper_hbm.1, bf16[1,3072,1024]{2,1,0:T(8,128)(2,1)} %lower_hbm.1), custom_call_target="tpu_custom_call" | custom-call | bytes 25165824 | tf_op jit(solution)/shard_map/load/pallas_call | solution.py:213
  9.9 0.0 collective-permute-done.2
  9.9 0.1 collective-permute-done.1
  10.0 0.0 collective-permute-done
  10.1 2.4 %collective-permute-start.3 = (bf16[16,1536]{1,0:T(8,128)(2,1)S(1)}, bf16[16,1536]{1,0:T(8,128)(2,1)S(1)}, u32[]{:S(2)}, u32[]{:S(2)}) collective-permute-start(bf16[16,1536]{1,0:T(8,128)(2,1)S(1)} %get-tuple-element.16), channel_id=1, source_target_pairs={{0,8},{8,0},{16,24},{24,16},{1,9},{9,1},{17,25},{25,17},{2,10},{10... | collective-permute-start | bytes 147464 | tf_op jit(solution)/shard_map/ppermute | solution.py:27
  12.5 2.1 %collective-permute-done.3.after_ref.refs_0_ = bf16[16,1536]{1,0:T(8,128)(2,1)S(1)} collective-permute-done((bf16[16,1536]{1,0:T(8,128)(2,1)S(1)}, bf16[16,1536]{1,0:T(8,128)(2,1)S(1)}, u32[]{:S(2)}, u32[]{:S(2)}) %collective-permute-start.3) | collective-permute-done | bytes 49184 | tf_op jit(solution)/shard_map/ppermute | solution.py:27
  14.6 2.3 %factor.1.factor_ref.after_ref = bf16[32,2048]{1,0:T(8,128)(2,1)S(1)} custom-call(bf16[16,1536]{1,0:T(8,128)(2,1)S(1)} %collective-permute-done.3.after_ref.refs_0_, f32[1,1,4,8]{3,2,1,0:T(4,128)S(1)} %get-tuple-element.15.after_ref.gates_ref, bf16[32,6144]{1,0:T(8,128)(2,1)S(1)} %pad_maximum_fusion.1.rows_ref.own_ref, ...), custom_call_target="tpu_custom_call" | custom-call | flops 402653184 | bytes 12582912 | tf_op jit(solution)/shard_map/factor/pallas_call | solution.py:236
  16.9 4.1 %collective-permute-start.9 = (bf16[32,2048]{1,0:T(8,128)(2,1)S(1)}, bf16[32,2048]{1,0:T(8,128)(2,1)S(1)}, u32[]{:S(2)}, u32[]{:S(2)}) collective-permute-start(bf16[32,2048]{1,0:T(8,128)(2,1)S(1)} %factor.1.factor_ref.after_ref), channel_id=1, source_target_pairs={{0,24},{8,16},{16,8},{24,0},{1,25},{9,17},{17,9},{25,1},{2,26},{10... | collective-permute-start | bytes 393224 | tf_op jit(solution)/shard_map/ppermute | solution.py:27
  21.0 0.0 collective-permute-start.8
  21.0 0.6 %collective-permute-start.7 = (bf16[32,2048]{1,0:T(8,128)(2,1)S(1)}, bf16[32,2048]{1,0:T(8,128)(2,1)S(1)}, u32[]{:S(2)}, u32[]{:S(2)}) collective-permute-start(bf16[32,2048]{1,0:T(8,128)(2,1)S(1)} %factor.1.factor_ref.after_ref), channel_id=1, source_target_pairs={{0,8},{8,0},{16,24},{24,16},{1,9},{9,1},{17,25},{25,17},{2,10},{10... | collective-permute-start | bytes 393224 | tf_op jit(solution)/shard_map/ppermute | solution.py:27
  21.6 2.3 %collective-permute-start.4 = (bf16[16,1536]{1,0:T(8,128)(2,1)S(1)}, bf16[16,1536]{1,0:T(8,128)(2,1)S(1)}, u32[]{:S(2)}, u32[]{:S(2)}) collective-permute-start(bf16[16,1536]{1,0:T(8,128)(2,1)S(1)} %get-tuple-element.19), channel_id=1, source_target_pairs={{0,16},{8,24},{16,0},{24,8},{1,17},{9,25},{17,1},{25,9},{2,18},{10... | collective-permute-start | bytes 147464 | tf_op jit(solution)/shard_map/ppermute | solution.py:27
  23.9 1.5 %collective-permute-start.5 = (bf16[16,1536]{1,0:T(8,128)(2,1)S(1)}, bf16[16,1536]{1,0:T(8,128)(2,1)S(1)}, u32[]{:S(2)}, u32[]{:S(2)}) collective-permute-start(bf16[16,1536]{1,0:T(8,128)(2,1)S(1)} %get-tuple-element.20), channel_id=1, source_target_pairs={{0,24},{8,16},{16,8},{24,0},{1,25},{9,17},{17,9},{25,1},{2,26},{10... | collective-permute-start | bytes 147464 | tf_op jit(solution)/shard_map/ppermute | solution.py:27
  25.4 2.6 %piece.1 = bf16[8,8,1536]{2,1,0:T(8,128)(2,1)} custom-call(bf16[32,2048]{1,0:T(8,128)(2,1)S(1)} %factor.1.factor_ref.after_ref, bf16[1,3072,1024]{2,1,0:T(8,128)(2,1)S(1)} %get-tuple-element.17.upper_ref), custom_call_target="tpu_custom_call" | custom-call | flops 201326592 | bytes 6291456 | tf_op jit(solution)/shard_map/piece/pallas_call | solution.py:259
  28.0 3.7 %all-to-all-start = ((bf16[8,8,1536]{2,1,0:T(8,128)(2,1)}), bf16[8,8,1536]{2,1,0:T(8,128)(2,1)S(1)}, u32[]{:S(2)}, u32[]{:S(2)}) async-start(bf16[8,8,1536]{2,1,0:T(8,128)(2,1)} %piece.1), calls=%async_computation | async-start | bytes 393216 | tf_op jit(solution)/shard_map/all_to_all | solution.py:270
  31.7 3.1 %collective-permute-done.4.refs_1_ = bf16[16,1536]{1,0:T(8,128)(2,1)S(1)} collective-permute-done((bf16[16,1536]{1,0:T(8,128)(2,1)S(1)}, bf16[16,1536]{1,0:T(8,128)(2,1)S(1)}, u32[]{:S(2)}, u32[]{:S(2)}) %collective-permute-start.4) | collective-permute-done | bytes 49184 | tf_op jit(solution)/shard_map/ppermute | solution.py:27
  34.8 0.0 collective-permute-done.5.refs_2_
  34.8 1.6 %collective-permute-start.6 = (bf16[3,16,1536]{2,1,0:T(8,128)(2,1)S(1)}, bf16[3,16,1536]{2,1,0:T(8,128)(2,1)S(1)}, u32[]{:S(2)}, u32[]{:S(2)}) collective-permute-start(bf16[3,16,1536]{2,1,0:T(8,128)(2,1)S(1)} %stack.1), channel_id=1, source_target_pairs={{0,1},{1,0},{2,3},{3,2},{4,5},{5,4},{6,7},{7,6},{8,9},{9,8},{10,11... | collective-permute-start | bytes 442376 | tf_op jit(solution)/shard_map/ppermute | solution.py:27
  36.4 0.0 collective-permute-done.9
  36.4 0.0 collective-permute-done.8
  36.4 0.0 collective-permute-done.7
  36.4 3.8 %collective-permute-done.6 = bf16[3,16,1536]{2,1,0:T(8,128)(2,1)S(1)} collective-permute-done((bf16[3,16,1536]{2,1,0:T(8,128)(2,1)S(1)}, bf16[3,16,1536]{2,1,0:T(8,128)(2,1)S(1)}, u32[]{:S(2)}, u32[]{:S(2)}) %collective-permute-start.6) | collective-permute-done | bytes 147488 | tf_op jit(solution)/shard_map/ppermute | solution.py:27
  40.3 3.2 %weight.1 = (f32[1,768,1024]{2,1,0:T(8,128)}, f32[1,768,1024]{2,1,0:T(8,128)}) custom-call(bf16[32,6144]{1,0:T(8,128)(2,1)S(1)} %pad_maximum_fusion.1.rows_ref.own_ref, bf16[3,32,1536]{2,1,0:T(8,128)(2,1)S(1)} %pad_maximum_fusion.2.refs_0_, bf16[128,2048]{1,0:T(8,128)(2,1)S(1)} %pad_maximum_fusion.refs_1_), custom_call_target="tpu_custom_call" | custom-call | flops 402653184 | bytes 50331648 | tf_op jit(solution)/shard_map/weight/pallas_call | solution.py:279
  43.4 0.0 all-to-all-done
  43.5 0.9 %fusion = bf16[1,64,1536]{2,1,0:T(8,128)(2,1)} fusion(bf16[64,64]{1,0:T(8,128)(2,1)S(1)} %get-tuple-element.13, bf16[8,8,1536]{2,1,0:T(8,128)(2,1)S(1)} %all-to-all-done), kind=kOutput, calls=%fused_computation.1 | convolution fusion | flops 12681216 | bytes 401408 | tf_op jit(solution)/shard_map/dot_general | solution.py:271
  (6 shorter events, 0.1 us)
Async XLA Ops:
  2.1 7.8 %collective-permute-start.2 = (bf16[8,6144]{1,0:T(8,128)(2,1)S(1)}, bf16[8,6144]{1,0:T(8,128)(2,1)S(1)}, u32[]{:S(2)}, u32[]{:S(2)}) collective-permute-start(bf16[8,6144]{1,0:T(8,128)(2,1)S(1)} %get-tuple-element.24), channel_id=1, source_target_pairs={{0,6},{2,4},{4,2},{6,0},{1,7},{3,5},{5,3},{7,1},{8,14},{10,12},{12... | collective-permute-start | bytes 294920 | tf_op jit(solution)/shard_map/ppermute | solution.py:27
  4.6 5.5 %collective-permute-start.1 = (bf16[8,6144]{1,0:T(8,128)(2,1)S(1)}, bf16[8,6144]{1,0:T(8,128)(2,1)S(1)}, u32[]{:S(2)}, u32[]{:S(2)}) collective-permute-start(bf16[8,6144]{1,0:T(8,128)(2,1)S(1)} %get-tuple-element.25), channel_id=1, source_target_pairs={{0,4},{2,6},{4,0},{6,2},{1,5},{3,7},{5,1},{7,3},{8,12},{10,14},{12... | collective-permute-start | bytes 294920 | tf_op jit(solution)/shard_map/ppermute | solution.py:27
  5.2 4.8 %collective-permute-start = (bf16[8,6144]{1,0:T(8,128)(2,1)S(1)}, bf16[8,6144]{1,0:T(8,128)(2,1)S(1)}, u32[]{:S(2)}, u32[]{:S(2)}) collective-permute-start(bf16[8,6144]{1,0:T(8,128)(2,1)S(1)} %get-tuple-element.26), channel_id=1, source_target_pairs={{0,2},{2,0},{4,6},{6,4},{1,3},{3,1},{5,7},{7,5},{8,10},{10,8},{12,... | collective-permute-start | bytes 294920 | tf_op jit(solution)/shard_map/ppermute | solution.py:27
  10.1 4.5 %collective-permute-start.3 = (bf16[16,1536]{1,0:T(8,128)(2,1)S(1)}, bf16[16,1536]{1,0:T(8,128)(2,1)S(1)}, u32[]{:S(2)}, u32[]{:S(2)}) collective-permute-start(bf16[16,1536]{1,0:T(8,128)(2,1)S(1)} %get-tuple-element.16), channel_id=1, source_target_pairs={{0,8},{8,0},{16,24},{24,16},{1,9},{9,1},{17,25},{25,17},{2,10},{10... | collective-permute-start | bytes 147464 | tf_op jit(solution)/shard_map/ppermute | solution.py:27
  16.9 19.5 %collective-permute-start.9 = (bf16[32,2048]{1,0:T(8,128)(2,1)S(1)}, bf16[32,2048]{1,0:T(8,128)(2,1)S(1)}, u32[]{:S(2)}, u32[]{:S(2)}) collective-permute-start(bf16[32,2048]{1,0:T(8,128)(2,1)S(1)} %factor.1.factor_ref.after_ref), channel_id=1, source_target_pairs={{0,24},{8,16},{16,8},{24,0},{1,25},{9,17},{17,9},{25,1},{2,26},{10... | collective-permute-start | bytes 393224 | tf_op jit(solution)/shard_map/ppermute | solution.py:27
  21.0 15.4 %collective-permute-start.8 = (bf16[32,2048]{1,0:T(8,128)(2,1)S(1)}, bf16[32,2048]{1,0:T(8,128)(2,1)S(1)}, u32[]{:S(2)}, u32[]{:S(2)}) collective-permute-start(bf16[32,2048]{1,0:T(8,128)(2,1)S(1)} %factor.1.factor_ref.after_ref), channel_id=1, source_target_pairs={{0,16},{8,24},{16,0},{24,8},{1,17},{9,25},{17,1},{25,9},{2,18},{10... | collective-permute-start | bytes 393224 | tf_op jit(solution)/shard_map/ppermute | solution.py:27
  21.0 15.4 %collective-permute-start.7 = (bf16[32,2048]{1,0:T(8,128)(2,1)S(1)}, bf16[32,2048]{1,0:T(8,128)(2,1)S(1)}, u32[]{:S(2)}, u32[]{:S(2)}) collective-permute-start(bf16[32,2048]{1,0:T(8,128)(2,1)S(1)} %factor.1.factor_ref.after_ref), channel_id=1, source_target_pairs={{0,8},{8,0},{16,24},{24,16},{1,9},{9,1},{17,25},{25,17},{2,10},{10... | collective-permute-start | bytes 393224 | tf_op jit(solution)/shard_map/ppermute | solution.py:27
  21.6 13.2 %collective-permute-start.4 = (bf16[16,1536]{1,0:T(8,128)(2,1)S(1)}, bf16[16,1536]{1,0:T(8,128)(2,1)S(1)}, u32[]{:S(2)}, u32[]{:S(2)}) collective-permute-start(bf16[16,1536]{1,0:T(8,128)(2,1)S(1)} %get-tuple-element.19), channel_id=1, source_target_pairs={{0,16},{8,24},{16,0},{24,8},{1,17},{9,25},{17,1},{25,9},{2,18},{10... | collective-permute-start | bytes 147464 | tf_op jit(solution)/shard_map/ppermute | solution.py:27
  23.9 10.9 %collective-permute-start.5 = (bf16[16,1536]{1,0:T(8,128)(2,1)S(1)}, bf16[16,1536]{1,0:T(8,128)(2,1)S(1)}, u32[]{:S(2)}, u32[]{:S(2)}) collective-permute-start(bf16[16,1536]{1,0:T(8,128)(2,1)S(1)} %get-tuple-element.20), channel_id=1, source_target_pairs={{0,24},{8,16},{16,8},{24,0},{1,25},{9,17},{17,9},{25,1},{2,26},{10... | collective-permute-start | bytes 147464 | tf_op jit(solution)/shard_map/ppermute | solution.py:27
  28.0 15.4 %all-to-all-start = ((bf16[8,8,1536]{2,1,0:T(8,128)(2,1)}), bf16[8,8,1536]{2,1,0:T(8,128)(2,1)S(1)}, u32[]{:S(2)}, u32[]{:S(2)}) async-start(bf16[8,8,1536]{2,1,0:T(8,128)(2,1)} %piece.1), calls=%async_computation | async-start | bytes 393216 | tf_op jit(solution)/shard_map/all_to_all | solution.py:270
  34.8 5.4 %collective-permute-start.6 = (bf16[3,16,1536]{2,1,0:T(8,128)(2,1)S(1)}, bf16[3,16,1536]{2,1,0:T(8,128)(2,1)S(1)}, u32[]{:S(2)}, u32[]{:S(2)}) collective-permute-start(bf16[3,16,1536]{2,1,0:T(8,128)(2,1)S(1)} %stack.1), channel_id=1, source_target_pairs={{0,1},{1,0},{2,3},{3,2},{4,5},{5,4},{6,7},{7,6},{8,9},{9,8},{10,11... | collective-permute-start | bytes 442376 | tf_op jit(solution)/shard_map/ppermute | solution.py:27

commit v13 on v11

--- a/solution.py
+++ b/solution.py
@@ -257,7 +257,11 @@
     )(factors, *parts)
     parts = [hop(parts, "hidden", t) for t in range(n_hid)]
 
-    gathered = jnp.concatenate([hop(factors, "dp", s) for s in range(n_dp)], axis=0)
+    gathered = [hop(factors, "dp", s) for s in range(n_dp)]
+    while len(gathered) > 1:
+        pairs = [jnp.concatenate(gathered[k : k + 2], axis=0) for k in range(0, len(gathered), 2)]
+        gathered = lax.optimization_barrier(pairs)
+    gathered = gathered[0]
 
     piece = pl.pallas_call(
         functools.partial(piece_kernel, n_hid),

time: 39.8 us -> 48 us (1.21)
  waiting for transfers between devices: 6.15 us -> 12.3 us
  starting transfers between devices: 17.5 us -> 19.4 us
    ppermute x10, waiting for transfers between devices: 5.3 us -> 9.81 us  [hop(): lax.ppermute(x, axis, [(i, i ^ step) for i in range(n)])]
    all_to_all x1, waiting for transfers between devices: 0.85 us -> 2.52 us  [local(): returned = lax.all_to_all(piece, ('expert', 'hidden'), 0, 0)]
    ppermute x10, starting transfers between devices: 14.1 us -> 15.6 us  [hop(): lax.ppermute(x, axis, [(i, i ^ step) for i in range(n)])]
  transfers between devices with their start and end apart: 11 -> 11, of which waited for: 5 -> 5; matrix products, arithmetic and copies ran while one was open for 0% -> 0% of each run, Pallas kernels for 32% -> 22%
where the time goes in v13:
time: 48 us; the launch traced here: 47.7 us
  starting transfers between devices  19.4 us (40%)
  Pallas kernels  14.2 us (30%)
  waiting for transfers between devices  12.3 us (26%)
  matrix products  0.91 us (2%)
  between operations  0.74 us (2%)
    ppermute x10, starting transfers between devices, hop(): lax.ppermute(x, axis, [(i, i ^ step) for i in range(n)])  15.6 us
    ppermute x10, waiting for transfers between devices, hop(): lax.ppermute(x, axis, [(i, i ^ step) for i in range(n)])  9.81 us
    pallas_call x1, Pallas kernels, local(): pl.pallas_call(load_kernel, out_shape=[jax.ShapeDtypeStruct(x.shape, x.dt...  4.64 us
    all_to_all x1, starting transfers between devices, local(): returned = lax.all_to_all(piece, ('expert', 'hidden'), 0, 0)  3.8 us
    pallas_call x1, Pallas kernels, local(): pl.pallas_call(functools.partial(weight_kernel, chunks, (n_dp, n_hid)), o...  3.18 us
    pallas_call x1, Pallas kernels, local(): pl.pallas_call(functools.partial(piece_kernel, n_hid), out_shape=jax.Shap...  2.63 us
    all_to_all x1, waiting for transfers between devices, local(): returned = lax.all_to_all(piece, ('expert', 'hidden'), 0, 0)  2.52 us
    pallas_call x1, Pallas kernels, local(): pl.pallas_call(factor_kernel, out_shape=jax.ShapeDtypeStruct((slots, 2 *...  2.29 us
  transfers between devices with their start and end apart: 11, of which 5 were waited for; matrix products, arithmetic and copies ran while one was open for 0% of the time, Pallas kernels for 22%

profile of v13, /device:TPU:0, one launch (start us, length us, event | category | flops | bytes accessed | tf_op | source)
XLA Modules:
  0.0 47.7 jit_solution(4286517261361341523)
XLA Ops:
  0.6 1.4 %pick.1 = (bf16[32,6144]{1,0:T(8,128)(2,1)S(1)}, bf16[64,64]{1,0:T(8,128)(2,1)S(1)}) custom-call(s32[1,1,4,8]{3,2,1,0:T(4,128)} %picks_hbm.1, bf16[1,64,3072]{2,1,0:T(8,128)(2,1)} %tokens_hbm.1, bf16[1,64,3072]{2,1,0:T(8,128)(2,1)} %upstream_hbm.1), custom_call_target="tpu_custom_call" | custom-call | tf_op jit(solution)/shard_map/pick/pallas_call | solution.py:195
  2.1 2.5 %collective-permute-start.2 = (bf16[8,6144]{1,0:T(8,128)(2,1)S(1)}, bf16[8,6144]{1,0:T(8,128)(2,1)S(1)}, u32[]{:S(2)}, u32[]{:S(2)}) collective-permute-start(bf16[8,6144]{1,0:T(8,128)(2,1)S(1)} %get-tuple-element.28), channel_id=1, source_target_pairs={{0,6},{2,4},{4,2},{6,0},{1,7},{3,5},{5,3},{7,1},{8,14},{10,12},{12... | collective-permute-start | bytes 294920 | tf_op jit(solution)/shard_map/ppermute | solution.py:27
  4.6 0.6 %collective-permute-start.1 = (bf16[8,6144]{1,0:T(8,128)(2,1)S(1)}, bf16[8,6144]{1,0:T(8,128)(2,1)S(1)}, u32[]{:S(2)}, u32[]{:S(2)}) collective-permute-start(bf16[8,6144]{1,0:T(8,128)(2,1)S(1)} %get-tuple-element.29), channel_id=1, source_target_pairs={{0,4},{2,6},{4,0},{6,2},{1,5},{3,7},{5,1},{7,3},{8,12},{10,14},{12... | collective-permute-start | bytes 294920 | tf_op jit(solution)/shard_map/ppermute | solution.py:27
  5.2 0.0 collective-permute-start
  5.3 4.6 %load.1 = (f32[1,1,4,8]{3,2,1,0:T(4,128)S(1)}, bf16[1,3072,1024]{2,1,0:T(8,128)(2,1)S(1)}, bf16[1,3072,1024]{2,1,0:T(8,128)(2,1)S(1)}) custom-call(bf16[32,6144]{1,0:T(8,128)(2,1)S(1)} %get-tuple-element.16.after_ref, f32[1,1,4,8]{3,2,1,0:T(4,128)} %gates_hbm.1, bf16[1,3072,1024]{2,1,0:T(8,128)(2,1)} %upper_hbm.1, bf16[1,3072,1024]{2,1,0:T(8,128)(2,1)} %lower_hbm.1), custom_call_target="tpu_custom_call" | custom-call | bytes 25165824 | tf_op jit(solution)/shard_map/load/pallas_call | solution.py:216
  9.9 0.0 collective-permute-done.2
  9.9 0.1 collective-permute-done.1
  10.0 0.0 collective-permute-done
  10.1 2.4 %collective-permute-start.3 = (bf16[16,1536]{1,0:T(8,128)(2,1)S(1)}, bf16[16,1536]{1,0:T(8,128)(2,1)S(1)}, u32[]{:S(2)}, u32[]{:S(2)}) collective-permute-start(bf16[16,1536]{1,0:T(8,128)(2,1)S(1)} %get-tuple-element.18), channel_id=1, source_target_pairs={{0,8},{8,0},{16,24},{24,16},{1,9},{9,1},{17,25},{25,17},{2,10},{10... | collective-permute-start | bytes 147464 | tf_op jit(solution)/shard_map/ppermute | solution.py:27
  12.5 2.1 %collective-permute-done.3.after_ref.refs_0_ = bf16[16,1536]{1,0:T(8,128)(2,1)S(1)} collective-permute-done((bf16[16,1536]{1,0:T(8,128)(2,1)S(1)}, bf16[16,1536]{1,0:T(8,128)(2,1)S(1)}, u32[]{:S(2)}, u32[]{:S(2)}) %collective-permute-start.3) | collective-permute-done | bytes 49184 | tf_op jit(solution)/shard_map/ppermute | solution.py:27
  14.6 2.3 %factor.1.factor_ref.after_ref = bf16[32,2048]{1,0:T(8,128)(2,1)S(1)} custom-call(bf16[16,1536]{1,0:T(8,128)(2,1)S(1)} %collective-permute-done.3.after_ref.refs_0_, f32[1,1,4,8]{3,2,1,0:T(4,128)S(1)} %get-tuple-element.17.after_ref.gates_ref, bf16[32,6144]{1,0:T(8,128)(2,1)S(1)} %pad_maximum_fusion.1.rows_ref.own_ref, ...), custom_call_target="tpu_custom_call" | custom-call | flops 402653184 | bytes 12582912 | tf_op jit(solution)/shard_map/factor/pallas_call | solution.py:239
  16.9 2.1 %collective-permute-start.7 = (bf16[32,2048]{1,0:T(8,128)(2,1)S(1)}, bf16[32,2048]{1,0:T(8,128)(2,1)S(1)}, u32[]{:S(2)}, u32[]{:S(2)}) collective-permute-start(bf16[32,2048]{1,0:T(8,128)(2,1)S(1)} %factor.1.factor_ref.after_ref), channel_id=1, source_target_pairs={{0,8},{8,0},{16,24},{24,16},{1,9},{9,1},{17,25},{25,17},{2,10},{10... | collective-permute-start | bytes 393224 | tf_op jit(solution)/shard_map/ppermute | solution.py:27
  19.0 2.6 %collective-permute-start.4 = (bf16[16,1536]{1,0:T(8,128)(2,1)S(1)}, bf16[16,1536]{1,0:T(8,128)(2,1)S(1)}, u32[]{:S(2)}, u32[]{:S(2)}) collective-permute-start(bf16[16,1536]{1,0:T(8,128)(2,1)S(1)} %get-tuple-element.21), channel_id=1, source_target_pairs={{0,16},{8,24},{16,0},{24,8},{1,17},{9,25},{17,1},{25,9},{2,18},{10... | collective-permute-start | bytes 147464 | tf_op jit(solution)/shard_map/ppermute | solution.py:27
  21.6 0.0 collective-permute-start.5
  21.6 3.8 %collective-permute-start.9 = (bf16[32,2048]{1,0:T(8,128)(2,1)S(1)}, bf16[32,2048]{1,0:T(8,128)(2,1)S(1)}, u32[]{:S(2)}, u32[]{:S(2)}) collective-permute-start(bf16[32,2048]{1,0:T(8,128)(2,1)S(1)} %factor.1.factor_ref.after_ref), channel_id=1, source_target_pairs={{0,24},{8,16},{16,8},{24,0},{1,25},{9,17},{17,9},{25,1},{2,26},{10... | collective-permute-start | bytes 393224 | tf_op jit(solution)/shard_map/ppermute | solution.py:27
  25.4 0.0 collective-permute-start.8
  25.4 0.0 collective-permute-done.4.refs_1_
  25.4 2.7 %collective-permute-done.5.refs_2_ = bf16[16,1536]{1,0:T(8,128)(2,1)S(1)} collective-permute-done((bf16[16,1536]{1,0:T(8,128)(2,1)S(1)}, bf16[16,1536]{1,0:T(8,128)(2,1)S(1)}, u32[]{:S(2)}, u32[]{:S(2)}) %collective-permute-start.5) | collective-permute-done | bytes 49184 | tf_op jit(solution)/shard_map/ppermute | solution.py:27
  28.1 1.6 %collective-permute-start.6 = (bf16[3,16,1536]{2,1,0:T(8,128)(2,1)S(1)}, bf16[3,16,1536]{2,1,0:T(8,128)(2,1)S(1)}, u32[]{:S(2)}, u32[]{:S(2)}) collective-permute-start(bf16[3,16,1536]{2,1,0:T(8,128)(2,1)S(1)} %stack.1.refs_0_), channel_id=1, source_target_pairs={{0,1},{1,0},{2,3},{3,2},{4,5},{5,4},{6,7},{7,6},{8,9},{9,8},{10,11... | collective-permute-start | bytes 442376 | tf_op jit(solution)/shard_map/ppermute | solution.py:27
  29.7 2.6 %piece.1.refs_0_ = bf16[8,8,1536]{2,1,0:T(8,128)(2,1)} custom-call(bf16[32,2048]{1,0:T(8,128)(2,1)S(1)} %factor.1.factor_ref.after_ref, bf16[1,3072,1024]{2,1,0:T(8,128)(2,1)S(1)} %get-tuple-element.19.upper_ref), custom_call_target="tpu_custom_call" | custom-call | flops 201326592 | bytes 6291456 | tf_op jit(solution)/shard_map/piece/pallas_call | solution.py:266
  32.3 0.0 collective-permute-done.7
  32.3 0.0 collective-permute-done.9
  32.3 4.9 %collective-permute-done.8 = bf16[32,2048]{1,0:T(8,128)(2,1)S(1)} collective-permute-done((bf16[32,2048]{1,0:T(8,128)(2,1)S(1)}, bf16[32,2048]{1,0:T(8,128)(2,1)S(1)}, u32[]{:S(2)}, u32[]{:S(2)}) %collective-permute-start.8) | collective-permute-done | bytes 131104 | tf_op jit(solution)/shard_map/ppermute | solution.py:27
  37.3 0.0 collective-permute-done.6.refs_1_
  37.3 3.8 %all-to-all-start = ((bf16[8,8,1536]{2,1,0:T(8,128)(2,1)}), bf16[8,8,1536]{2,1,0:T(8,128)(2,1)S(1)}, u32[]{:S(2)}, u32[]{:S(2)}) async-start(bf16[8,8,1536]{2,1,0:T(8,128)(2,1)} %tie.1), calls=%async_computation | async-start | bytes 393216 | tf_op jit(solution)/shard_map/all_to_all | solution.py:286
  41.1 3.2 %weight.1 = (f32[1,768,1024]{2,1,0:T(8,128)}, f32[1,768,1024]{2,1,0:T(8,128)}) custom-call(bf16[32,6144]{1,0:T(8,128)(2,1)S(1)} %pad_maximum_fusion.1.rows_ref.own_ref, bf16[3,16,1536]{2,1,0:T(8,128)(2,1)S(1)} %stack.1.refs_0_, bf16[3,16,1536]{2,1,0:T(8,128)(2,1)S(1)} %collective-permute-done.6.refs_1_, bf16[128,2048]{1,0:T(8,128)(2,1)S(1)} %pad_maximum_fusion.refs_2_), custom_call_target="tpu_custom_call" | custom-call | flops 402653184 | bytes 50331648 | tf_op jit(solution)/shard_map/weight/pallas_call | solution.py:295
  44.3 2.5 %all-to-all-done = bf16[8,8,1536]{2,1,0:T(8,128)(2,1)S(1)} async-done(((bf16[8,8,1536]{2,1,0:T(8,128)(2,1)}), bf16[8,8,1536]{2,1,0:T(8,128)(2,1)S(1)}, u32[]{:S(2)}, u32[]{:S(2)}) %all-to-all-start) | async-done | bytes 196640 | tf_op jit(solution)/shard_map/all_to_all | solution.py:286
  46.8 0.9 %fusion = bf16[1,64,1536]{2,1,0:T(8,128)(2,1)} fusion(bf16[64,64]{1,0:T(8,128)(2,1)S(1)} %get-tuple-element.15, bf16[8,8,1536]{2,1,0:T(8,128)(2,1)S(1)} %all-to-all-done), kind=kOutput, calls=%fused_computation.1 | convolution fusion | flops 12681216 | bytes 401408 | tf_op jit(solution)/shard_map/dot_general | solution.py:287
  (8 shorter events, 0.2 us)
Async XLA Ops:
  2.1 7.8 %collective-permute-start.2 = (bf16[8,6144]{1,0:T(8,128)(2,1)S(1)}, bf16[8,6144]{1,0:T(8,128)(2,1)S(1)}, u32[]{:S(2)}, u32[]{:S(2)}) collective-permute-start(bf16[8,6144]{1,0:T(8,128)(2,1)S(1)} %get-tuple-element.28), channel_id=1, source_target_pairs={{0,6},{2,4},{4,2},{6,0},{1,7},{3,5},{5,3},{7,1},{8,14},{10,12},{12... | collective-permute-start | bytes 294920 | tf_op jit(solution)/shard_map/ppermute | solution.py:27
  4.6 5.5 %collective-permute-start.1 = (bf16[8,6144]{1,0:T(8,128)(2,1)S(1)}, bf16[8,6144]{1,0:T(8,128)(2,1)S(1)}, u32[]{:S(2)}, u32[]{:S(2)}) collective-permute-start(bf16[8,6144]{1,0:T(8,128)(2,1)S(1)} %get-tuple-element.29), channel_id=1, source_target_pairs={{0,4},{2,6},{4,0},{6,2},{1,5},{3,7},{5,1},{7,3},{8,12},{10,14},{12... | collective-permute-start | bytes 294920 | tf_op jit(solution)/shard_map/ppermute | solution.py:27
  5.2 4.8 %collective-permute-start = (bf16[8,6144]{1,0:T(8,128)(2,1)S(1)}, bf16[8,6144]{1,0:T(8,128)(2,1)S(1)}, u32[]{:S(2)}, u32[]{:S(2)}) collective-permute-start(bf16[8,6144]{1,0:T(8,128)(2,1)S(1)} %get-tuple-element.30), channel_id=1, source_target_pairs={{0,2},{2,0},{4,6},{6,4},{1,3},{3,1},{5,7},{7,5},{8,10},{10,8},{12,... | collective-permute-start | bytes 294920 | tf_op jit(solution)/shard_map/ppermute | solution.py:27
  10.1 4.5 %collective-permute-start.3 = (bf16[16,1536]{1,0:T(8,128)(2,1)S(1)}, bf16[16,1536]{1,0:T(8,128)(2,1)S(1)}, u32[]{:S(2)}, u32[]{:S(2)}) collective-permute-start(bf16[16,1536]{1,0:T(8,128)(2,1)S(1)} %get-tuple-element.18), channel_id=1, source_target_pairs={{0,8},{8,0},{16,24},{24,16},{1,9},{9,1},{17,25},{25,17},{2,10},{10... | collective-permute-start | bytes 147464 | tf_op jit(solution)/shard_map/ppermute | solution.py:27
  16.9 15.4 %collective-permute-start.7 = (bf16[32,2048]{1,0:T(8,128)(2,1)S(1)}, bf16[32,2048]{1,0:T(8,128)(2,1)S(1)}, u32[]{:S(2)}, u32[]{:S(2)}) collective-permute-start(bf16[32,2048]{1,0:T(8,128)(2,1)S(1)} %factor.1.factor_ref.after_ref), channel_id=1, source_target_pairs={{0,8},{8,0},{16,24},{24,16},{1,9},{9,1},{17,25},{25,17},{2,10},{10... | collective-permute-start | bytes 393224 | tf_op jit(solution)/shard_map/ppermute | solution.py:27
  19.0 6.4 %collective-permute-start.4 = (bf16[16,1536]{1,0:T(8,128)(2,1)S(1)}, bf16[16,1536]{1,0:T(8,128)(2,1)S(1)}, u32[]{:S(2)}, u32[]{:S(2)}) collective-permute-start(bf16[16,1536]{1,0:T(8,128)(2,1)S(1)} %get-tuple-element.21), channel_id=1, source_target_pairs={{0,16},{8,24},{16,0},{24,8},{1,17},{9,25},{17,1},{25,9},{2,18},{10... | collective-permute-start | bytes 147464 | tf_op jit(solution)/shard_map/ppermute | solution.py:27
  21.6 6.5 %collective-permute-start.5 = (bf16[16,1536]{1,0:T(8,128)(2,1)S(1)}, bf16[16,1536]{1,0:T(8,128)(2,1)S(1)}, u32[]{:S(2)}, u32[]{:S(2)}) collective-permute-start(bf16[16,1536]{1,0:T(8,128)(2,1)S(1)} %get-tuple-element.22), channel_id=1, source_target_pairs={{0,24},{8,16},{16,8},{24,0},{1,25},{9,17},{17,9},{25,1},{2,26},{10... | collective-permute-start | bytes 147464 | tf_op jit(solution)/shard_map/ppermute | solution.py:27
  21.6 10.8 %collective-permute-start.9 = (bf16[32,2048]{1,0:T(8,128)(2,1)S(1)}, bf16[32,2048]{1,0:T(8,128)(2,1)S(1)}, u32[]{:S(2)}, u32[]{:S(2)}) collective-permute-start(bf16[32,2048]{1,0:T(8,128)(2,1)S(1)} %factor.1.factor_ref.after_ref), channel_id=1, source_target_pairs={{0,24},{8,16},{16,8},{24,0},{1,25},{9,17},{17,9},{25,1},{2,26},{10... | collective-permute-start | bytes 393224 | tf_op jit(solution)/shard_map/ppermute | solution.py:27
  25.4 11.8 %collective-permute-start.8 = (bf16[32,2048]{1,0:T(8,128)(2,1)S(1)}, bf16[32,2048]{1,0:T(8,128)(2,1)S(1)}, u32[]{:S(2)}, u32[]{:S(2)}) collective-permute-start(bf16[32,2048]{1,0:T(8,128)(2,1)S(1)} %factor.1.factor_ref.after_ref), channel_id=1, source_target_pairs={{0,16},{8,24},{16,0},{24,8},{1,17},{9,25},{17,1},{25,9},{2,18},{10... | collective-permute-start | bytes 393224 | tf_op jit(solution)/shard_map/ppermute | solution.py:27
  28.1 9.1 %collective-permute-start.6 = (bf16[3,16,1536]{2,1,0:T(8,128)(2,1)S(1)}, bf16[3,16,1536]{2,1,0:T(8,128)(2,1)S(1)}, u32[]{:S(2)}, u32[]{:S(2)}) collective-permute-start(bf16[3,16,1536]{2,1,0:T(8,128)(2,1)S(1)} %stack.1.refs_0_), channel_id=1, source_target_pairs={{0,1},{1,0},{2,3},{3,2},{4,5},{5,4},{6,7},{7,6},{8,9},{9,8},{10,11... | collective-permute-start | bytes 442376 | tf_op jit(solution)/shard_map/ppermute | solution.py:27
  37.3 9.6 %all-to-all-start = ((bf16[8,8,1536]{2,1,0:T(8,128)(2,1)}), bf16[8,8,1536]{2,1,0:T(8,128)(2,1)S(1)}, u32[]{:S(2)}, u32[]{:S(2)}) async-start(bf16[8,8,1536]{2,1,0:T(8,128)(2,1)} %tie.1), calls=%async_computation | async-start | bytes 393216 | tf_op jit(solution)/shard_map/all_to_all | solution.py:286

commit v14 on v11

--- a/solution.py
+++ b/solution.py
@@ -234,7 +234,7 @@
         compiler_params=ROOM,
         name="cut",
     )(gate_held, rows)
-    parts = [hop(x, "dp", s + 1) for s, x in enumerate(parts)]
+    parts = [hop(parts[s], "dp", s + 1) for s in reversed(range(n_dp - 1))][::-1]
 
     factors = pl.pallas_call(
         factor_kernel,
@@ -246,7 +246,7 @@
             flops=4 * slots * w_up.size, bytes_accessed=4 * w_up.size, transcendentals=slots * units
         ),
         name="factor",
-    )(parts[0], gate_held, rows, upper, lower)
+    )(parts[-1], gate_held, rows, upper, lower)
     parts = pl.pallas_call(
         stack_kernel,
         out_shape=jax.ShapeDtypeStruct((n_dp - 1, share, 2 * cols), bf16),

time: 39.8 us -> 38.9 us (0.977)
  waiting for transfers between devices: 6.15 us -> 5.13 us
    all_to_all x1, waiting for transfers between devices: 0.85 us -> 0.01 us  [local(): returned = lax.all_to_all(piece, ('expert', 'hidden'), 0, 0)]
  transfers between devices with their start and end apart: 11 -> 11, of which waited for: 5 -> 4; matrix products, arithmetic and copies ran while one was open for 0% -> 0% of each run, Pallas kernels for 32% -> 33%
where the time goes in v14:
time: 38.9 us; the launch traced here: 38.7 us
  starting transfers between devices  17.6 us (45%)
  Pallas kernels  14.2 us (37%)
  waiting for transfers between devices  5.13 us (13%)
  matrix products  0.91 us (2%)
  between operations  0.74 us (2%)
    ppermute x10, starting transfers between devices, hop(): lax.ppermute(x, axis, [(i, i ^ step) for i in range(n)])  14.2 us
    ppermute x10, waiting for transfers between devices, hop(): lax.ppermute(x, axis, [(i, i ^ step) for i in range(n)])  5.13 us
    pallas_call x1, Pallas kernels, local(): pl.pallas_call(load_kernel, out_shape=[jax.ShapeDtypeStruct(x.shape, x.dt...  4.64 us
    all_to_all x1, starting transfers between devices, local(): returned = lax.all_to_all(piece, ('expert', 'hidden'), 0, 0)  3.39 us
    pallas_call x1, Pallas kernels, local(): pl.pallas_call(functools.partial(weight_kernel, chunks, (n_dp, n_hid)), o...  3.18 us
    pallas_call x1, Pallas kernels, local(): pl.pallas_call(functools.partial(piece_kernel, n_hid), out_shape=jax.Shap...  2.63 us
    pallas_call x1, Pallas kernels, local(): pl.pallas_call(factor_kernel, out_shape=jax.ShapeDtypeStruct((slots, 2 *...  2.29 us
    pallas_call x1, Pallas kernels, local(): pl.pallas_call(functools.partial(pick_kernel, n_hid), out_shape=[jax.Shap...  1.42 us
  transfers between devices with their start and end apart: 11, of which 4 were waited for; matrix products, arithmetic and copies ran while one was open for 0% of the time, Pallas kernels for 33%

profile of v14, /device:TPU:0, one launch (start us, length us, event | category | flops | bytes accessed | tf_op | source)
XLA Modules:
  0.0 38.7 jit_solution(10130849771926735414)
XLA Ops:
  0.6 1.4 %pick.1 = (bf16[32,6144]{1,0:T(8,128)(2,1)S(1)}, bf16[64,64]{1,0:T(8,128)(2,1)S(1)}) custom-call(s32[1,1,4,8]{3,2,1,0:T(4,128)} %picks_hbm.1, bf16[1,64,3072]{2,1,0:T(8,128)(2,1)} %tokens_hbm.1, bf16[1,64,3072]{2,1,0:T(8,128)(2,1)} %upstream_hbm.1), custom_call_target="tpu_custom_call" | custom-call | tf_op jit(solution)/shard_map/pick/pallas_call | solution.py:195
  2.1 2.5 %collective-permute-start.2 = (bf16[8,6144]{1,0:T(8,128)(2,1)S(1)}, bf16[8,6144]{1,0:T(8,128)(2,1)S(1)}, u32[]{:S(2)}, u32[]{:S(2)}) collective-permute-start(bf16[8,6144]{1,0:T(8,128)(2,1)S(1)} %get-tuple-element.24), channel_id=1, source_target_pairs={{0,6},{2,4},{4,2},{6,0},{1,7},{3,5},{5,3},{7,1},{8,14},{10,12},{12... | collective-permute-start | bytes 294920 | tf_op jit(solution)/shard_map/ppermute | solution.py:27
  4.6 0.6 %collective-permute-start.1 = (bf16[8,6144]{1,0:T(8,128)(2,1)S(1)}, bf16[8,6144]{1,0:T(8,128)(2,1)S(1)}, u32[]{:S(2)}, u32[]{:S(2)}) collective-permute-start(bf16[8,6144]{1,0:T(8,128)(2,1)S(1)} %get-tuple-element.25), channel_id=1, source_target_pairs={{0,4},{2,6},{4,0},{6,2},{1,5},{3,7},{5,1},{7,3},{8,12},{10,14},{12... | collective-permute-start | bytes 294920 | tf_op jit(solution)/shard_map/ppermute | solution.py:27
  5.2 0.0 collective-permute-start
  5.3 4.6 %load.1 = (f32[1,1,4,8]{3,2,1,0:T(4,128)S(1)}, bf16[1,3072,1024]{2,1,0:T(8,128)(2,1)S(1)}, bf16[1,3072,1024]{2,1,0:T(8,128)(2,1)S(1)}) custom-call(bf16[32,6144]{1,0:T(8,128)(2,1)S(1)} %get-tuple-element.14.after_ref, f32[1,1,4,8]{3,2,1,0:T(4,128)} %gates_hbm.1, bf16[1,3072,1024]{2,1,0:T(8,128)(2,1)} %upper_hbm.1, bf16[1,3072,1024]{2,1,0:T(8,128)(2,1)} %lower_hbm.1), custom_call_target="tpu_custom_call" | custom-call | bytes 25165824 | tf_op jit(solution)/shard_map/load/pallas_call | solution.py:216
  9.9 0.0 collective-permute-done.2
  9.9 0.1 collective-permute-done.1
  10.0 0.0 collective-permute-done
  10.1 4.4 %collective-permute-start.3 = (bf16[16,1536]{1,0:T(8,128)(2,1)S(1)}, bf16[16,1536]{1,0:T(8,128)(2,1)S(1)}, u32[]{:S(2)}, u32[]{:S(2)}) collective-permute-start(bf16[16,1536]{1,0:T(8,128)(2,1)S(1)} %get-tuple-element.16), channel_id=1, source_target_pairs={{0,24},{8,16},{16,8},{24,0},{1,25},{9,17},{17,9},{25,1},{2,26},{10... | collective-permute-start | bytes 147464 | tf_op jit(solution)/shard_map/ppermute | solution.py:27
  14.6 0.0 collective-permute-start.4
  14.6 0.6 %collective-permute-start.5 = (bf16[16,1536]{1,0:T(8,128)(2,1)S(1)}, bf16[16,1536]{1,0:T(8,128)(2,1)S(1)}, u32[]{:S(2)}, u32[]{:S(2)}) collective-permute-start(bf16[16,1536]{1,0:T(8,128)(2,1)S(1)} %get-tuple-element.20), channel_id=1, source_target_pairs={{0,16},{8,24},{16,0},{24,8},{1,17},{9,25},{17,1},{25,9},{2,18},{10... | collective-permute-start | bytes 147464 | tf_op jit(solution)/shard_map/ppermute | solution.py:27
  15.2 1.9 %collective-permute-done.3.after_ref.refs_2_ = bf16[16,1536]{1,0:T(8,128)(2,1)S(1)} collective-permute-done((bf16[16,1536]{1,0:T(8,128)(2,1)S(1)}, bf16[16,1536]{1,0:T(8,128)(2,1)S(1)}, u32[]{:S(2)}, u32[]{:S(2)}) %collective-permute-start.3) | collective-permute-done | bytes 49184 | tf_op jit(solution)/shard_map/ppermute | solution.py:27
  17.1 2.3 %factor.1.factor_ref.after_ref = bf16[32,2048]{1,0:T(8,128)(2,1)S(1)} custom-call(bf16[16,1536]{1,0:T(8,128)(2,1)S(1)} %collective-permute-done.3.after_ref.refs_2_, f32[1,1,4,8]{3,2,1,0:T(4,128)S(1)} %get-tuple-element.15.after_ref.gates_ref, bf16[32,6144]{1,0:T(8,128)(2,1)S(1)} %pad_maximum_fusion.1.rows_ref.own_ref, ...), custom_call_target="tpu_custom_call" | custom-call | flops 402653184 | bytes 12582912 | tf_op jit(solution)/shard_map/factor/pallas_call | solution.py:239
  19.4 0.0 collective-permute-done.4.refs_0_
  19.4 0.6 %collective-permute-done.5.refs_1_ = bf16[16,1536]{1,0:T(8,128)(2,1)S(1)} collective-permute-done((bf16[16,1536]{1,0:T(8,128)(2,1)S(1)}, bf16[16,1536]{1,0:T(8,128)(2,1)S(1)}, u32[]{:S(2)}, u32[]{:S(2)}) %collective-permute-start.5) | collective-permute-done | bytes 49184 | tf_op jit(solution)/shard_map/ppermute | solution.py:27
  20.1 1.6 %collective-permute-start.6 = (bf16[3,16,1536]{2,1,0:T(8,128)(2,1)S(1)}, bf16[3,16,1536]{2,1,0:T(8,128)(2,1)S(1)}, u32[]{:S(2)}, u32[]{:S(2)}) collective-permute-start(bf16[3,16,1536]{2,1,0:T(8,128)(2,1)S(1)} %stack.1.refs_0_), channel_id=1, source_target_pairs={{0,1},{1,0},{2,3},{3,2},{4,5},{5,4},{6,7},{7,6},{8,9},{9,8},{10,11... | collective-permute-start | bytes 442376 | tf_op jit(solution)/shard_map/ppermute | solution.py:27
  21.6 3.2 %collective-permute-start.9 = (bf16[32,2048]{1,0:T(8,128)(2,1)S(1)}, bf16[32,2048]{1,0:T(8,128)(2,1)S(1)}, u32[]{:S(2)}, u32[]{:S(2)}) collective-permute-start(bf16[32,2048]{1,0:T(8,128)(2,1)S(1)} %factor.1.factor_ref.after_ref), channel_id=1, source_target_pairs={{0,24},{8,16},{16,8},{24,0},{1,25},{9,17},{17,9},{25,1},{2,26},{10... | collective-permute-start | bytes 393224 | tf_op jit(solution)/shard_map/ppermute | solution.py:27
  24.8 0.0 collective-permute-start.8
  24.8 1.2 %collective-permute-start.7 = (bf16[32,2048]{1,0:T(8,128)(2,1)S(1)}, bf16[32,2048]{1,0:T(8,128)(2,1)S(1)}, u32[]{:S(2)}, u32[]{:S(2)}) collective-permute-start(bf16[32,2048]{1,0:T(8,128)(2,1)S(1)} %factor.1.factor_ref.after_ref), channel_id=1, source_target_pairs={{0,8},{8,0},{16,24},{24,16},{1,9},{9,1},{17,25},{25,17},{2,10},{10... | collective-permute-start | bytes 393224 | tf_op jit(solution)/shard_map/ppermute | solution.py:27
  26.0 2.6 %piece.1.refs_0_ = bf16[8,8,1536]{2,1,0:T(8,128)(2,1)} custom-call(bf16[32,2048]{1,0:T(8,128)(2,1)S(1)} %factor.1.factor_ref.after_ref, bf16[1,3072,1024]{2,1,0:T(8,128)(2,1)S(1)} %get-tuple-element.17.upper_ref), custom_call_target="tpu_custom_call" | custom-call | flops 201326592 | bytes 6291456 | tf_op jit(solution)/shard_map/piece/pallas_call | solution.py:262
  28.6 0.0 collective-permute-done.6.refs_1_
  28.6 3.4 %all-to-all-start = ((bf16[8,8,1536]{2,1,0:T(8,128)(2,1)}), bf16[8,8,1536]{2,1,0:T(8,128)(2,1)S(1)}, u32[]{:S(2)}, u32[]{:S(2)}) async-start(bf16[8,8,1536]{2,1,0:T(8,128)(2,1)} %tie.1), calls=%async_computation | async-start | bytes 393216 | tf_op jit(solution)/shard_map/all_to_all | solution.py:282
  32.0 0.0 collective-permute-done.9
  32.0 2.5 %collective-permute-done.8 = bf16[32,2048]{1,0:T(8,128)(2,1)S(1)} collective-permute-done((bf16[32,2048]{1,0:T(8,128)(2,1)S(1)}, bf16[32,2048]{1,0:T(8,128)(2,1)S(1)}, u32[]{:S(2)}, u32[]{:S(2)}) %collective-permute-start.8) | collective-permute-done | bytes 131104 | tf_op jit(solution)/shard_map/ppermute | solution.py:27
  34.5 0.0 collective-permute-done.7
  34.6 3.2 %weight.1 = (f32[1,768,1024]{2,1,0:T(8,128)}, f32[1,768,1024]{2,1,0:T(8,128)}) custom-call(bf16[32,6144]{1,0:T(8,128)(2,1)S(1)} %pad_maximum_fusion.1.rows_ref.own_ref, bf16[3,16,1536]{2,1,0:T(8,128)(2,1)S(1)} %stack.1.refs_0_, bf16[3,16,1536]{2,1,0:T(8,128)(2,1)S(1)} %collective-permute-done.6.refs_1_, bf16[128,2048]{1,0:T(8,128)(2,1)S(1)} %pad_maximum_fusion.refs_2_), custom_call_target="tpu_custom_call" | custom-call | flops 402653184 | bytes 50331648 | tf_op jit(solution)/shard_map/weight/pallas_call | solution.py:291
  37.7 0.0 all-to-all-done
  37.8 0.9 %fusion = bf16[1,64,1536]{2,1,0:T(8,128)(2,1)} fusion(bf16[64,64]{1,0:T(8,128)(2,1)S(1)} %get-tuple-element.13, bf16[8,8,1536]{2,1,0:T(8,128)(2,1)S(1)} %all-to-all-done), kind=kOutput, calls=%fused_computation.1 | convolution fusion | flops 12681216 | bytes 401408 | tf_op jit(solution)/shard_map/dot_general | solution.py:283
  (6 shorter events, 0.1 us)
Async XLA Ops:
  2.1 7.8 %collective-permute-start.2 = (bf16[8,6144]{1,0:T(8,128)(2,1)S(1)}, bf16[8,6144]{1,0:T(8,128)(2,1)S(1)}, u32[]{:S(2)}, u32[]{:S(2)}) collective-permute-start(bf16[8,6144]{1,0:T(8,128)(2,1)S(1)} %get-tuple-element.24), channel_id=1, source_target_pairs={{0,6},{2,4},{4,2},{6,0},{1,7},{3,5},{5,3},{7,1},{8,14},{10,12},{12... | collective-permute-start | bytes 294920 | tf_op jit(solution)/shard_map/ppermute | solution.py:27
  4.6 5.5 %collective-permute-start.1 = (bf16[8,6144]{1,0:T(8,128)(2,1)S(1)}, bf16[8,6144]{1,0:T(8,128)(2,1)S(1)}, u32[]{:S(2)}, u32[]{:S(2)}) collective-permute-start(bf16[8,6144]{1,0:T(8,128)(2,1)S(1)} %get-tuple-element.25), channel_id=1, source_target_pairs={{0,4},{2,6},{4,0},{6,2},{1,5},{3,7},{5,1},{7,3},{8,12},{10,14},{12... | collective-permute-start | bytes 294920 | tf_op jit(solution)/shard_map/ppermute | solution.py:27
  5.2 4.8 %collective-permute-start = (bf16[8,6144]{1,0:T(8,128)(2,1)S(1)}, bf16[8,6144]{1,0:T(8,128)(2,1)S(1)}, u32[]{:S(2)}, u32[]{:S(2)}) collective-permute-start(bf16[8,6144]{1,0:T(8,128)(2,1)S(1)} %get-tuple-element.26), channel_id=1, source_target_pairs={{0,2},{2,0},{4,6},{6,4},{1,3},{3,1},{5,7},{7,5},{8,10},{10,8},{12,... | collective-permute-start | bytes 294920 | tf_op jit(solution)/shard_map/ppermute | solution.py:27
  10.1 7.0 %collective-permute-start.3 = (bf16[16,1536]{1,0:T(8,128)(2,1)S(1)}, bf16[16,1536]{1,0:T(8,128)(2,1)S(1)}, u32[]{:S(2)}, u32[]{:S(2)}) collective-permute-start(bf16[16,1536]{1,0:T(8,128)(2,1)S(1)} %get-tuple-element.16), channel_id=1, source_target_pairs={{0,24},{8,16},{16,8},{24,0},{1,25},{9,17},{17,9},{25,1},{2,26},{10... | collective-permute-start | bytes 147464 | tf_op jit(solution)/shard_map/ppermute | solution.py:27
  14.6 4.9 %collective-permute-start.4 = (bf16[16,1536]{1,0:T(8,128)(2,1)S(1)}, bf16[16,1536]{1,0:T(8,128)(2,1)S(1)}, u32[]{:S(2)}, u32[]{:S(2)}) collective-permute-start(bf16[16,1536]{1,0:T(8,128)(2,1)S(1)} %get-tuple-element.19), channel_id=1, source_target_pairs={{0,8},{8,0},{16,24},{24,16},{1,9},{9,1},{17,25},{25,17},{2,10},{10... | collective-permute-start | bytes 147464 | tf_op jit(solution)/shard_map/ppermute | solution.py:27
  14.6 5.5 %collective-permute-start.5 = (bf16[16,1536]{1,0:T(8,128)(2,1)S(1)}, bf16[16,1536]{1,0:T(8,128)(2,1)S(1)}, u32[]{:S(2)}, u32[]{:S(2)}) collective-permute-start(bf16[16,1536]{1,0:T(8,128)(2,1)S(1)} %get-tuple-element.20), channel_id=1, source_target_pairs={{0,16},{8,24},{16,0},{24,8},{1,17},{9,25},{17,1},{25,9},{2,18},{10... | collective-permute-start | bytes 147464 | tf_op jit(solution)/shard_map/ppermute | solution.py:27
  20.1 8.6 %collective-permute-start.6 = (bf16[3,16,1536]{2,1,0:T(8,128)(2,1)S(1)}, bf16[3,16,1536]{2,1,0:T(8,128)(2,1)S(1)}, u32[]{:S(2)}, u32[]{:S(2)}) collective-permute-start(bf16[3,16,1536]{2,1,0:T(8,128)(2,1)S(1)} %stack.1.refs_0_), channel_id=1, source_target_pairs={{0,1},{1,0},{2,3},{3,2},{4,5},{5,4},{6,7},{7,6},{8,9},{9,8},{10,11... | collective-permute-start | bytes 442376 | tf_op jit(solution)/shard_map/ppermute | solution.py:27
  21.6 10.4 %collective-permute-start.9 = (bf16[32,2048]{1,0:T(8,128)(2,1)S(1)}, bf16[32,2048]{1,0:T(8,128)(2,1)S(1)}, u32[]{:S(2)}, u32[]{:S(2)}) collective-permute-start(bf16[32,2048]{1,0:T(8,128)(2,1)S(1)} %factor.1.factor_ref.after_ref), channel_id=1, source_target_pairs={{0,24},{8,16},{16,8},{24,0},{1,25},{9,17},{17,9},{25,1},{2,26},{10... | collective-permute-start | bytes 393224 | tf_op jit(solution)/shard_map/ppermute | solution.py:27
  24.8 9.7 %collective-permute-start.8 = (bf16[32,2048]{1,0:T(8,128)(2,1)S(1)}, bf16[32,2048]{1,0:T(8,128)(2,1)S(1)}, u32[]{:S(2)}, u32[]{:S(2)}) collective-permute-start(bf16[32,2048]{1,0:T(8,128)(2,1)S(1)} %factor.1.factor_ref.after_ref), channel_id=1, source_target_pairs={{0,16},{8,24},{16,0},{24,8},{1,17},{9,25},{17,1},{25,9},{2,18},{10... | collective-permute-start | bytes 393224 | tf_op jit(solution)/shard_map/ppermute | solution.py:27
  24.8 9.7 %collective-permute-start.7 = (bf16[32,2048]{1,0:T(8,128)(2,1)S(1)}, bf16[32,2048]{1,0:T(8,128)(2,1)S(1)}, u32[]{:S(2)}, u32[]{:S(2)}) collective-permute-start(bf16[32,2048]{1,0:T(8,128)(2,1)S(1)} %factor.1.factor_ref.after_ref), channel_id=1, source_target_pairs={{0,8},{8,0},{16,24},{24,16},{1,9},{9,1},{17,25},{25,17},{2,10},{10... | collective-permute-start | bytes 393224 | tf_op jit(solution)/shard_map/ppermute | solution.py:27
  28.6 9.1 %all-to-all-start = ((bf16[8,8,1536]{2,1,0:T(8,128)(2,1)}), bf16[8,8,1536]{2,1,0:T(8,128)(2,1)S(1)}, u32[]{:S(2)}, u32[]{:S(2)}) async-start(bf16[8,8,1536]{2,1,0:T(8,128)(2,1)} %tie.1), calls=%async_computation | async-start | bytes 393216 | tf_op jit(solution)/shard_map/all_to_all | solution.py:282

commit v15 on v14

--- a/solution.py
+++ b/solution.py
@@ -122,19 +122,13 @@
             ].astype(jnp.bfloat16)
 
 
-def stack_kernel(after_ref, *refs):
-    *part_refs, out_ref = refs
-    for s, part in enumerate(part_refs):
-        out_ref[s] = part[...]
-
-
 def tie_kernel(*refs):
     pass
 
 
 def weight_kernel(chunks, shape, own_ref, *refs):
     n_dp, n_hid = shape
-    part_refs, refs = refs[:n_hid], refs[n_hid:]
+    part_refs, refs = refs[: 2 * n_hid], refs[2 * n_hid :]
     factor_ref, up_ref, down_ref, side_ref, held, sems = refs
     units = factor_ref.shape[1] // 2
     cols = side_ref.shape[1] // 2
@@ -147,10 +141,13 @@
         side_ref[:slots, half * cols : (half + 1) * cols] = own_ref[
             :, pl.ds(pl.multiple_of(half * width + start, 128), cols)
         ]
-    for t, part in enumerate(part_refs):
-        spot = (my_hid ^ t) * rows
+    for k, part in enumerate(part_refs):
+        spot = (my_hid ^ (k // 2)) * rows
+        half = k % 2
         for s in range(1, n_dp):
-            side_ref[pl.ds(pl.multiple_of(s * slots + spot, 16), rows), :] = part[s - 1]
+            side_ref[
+                pl.ds(pl.multiple_of(s * slots + spot, 16), rows), half * cols : (half + 1) * cols
+            ] = part[s - 1]
     step = units // chunks
     copies = []
     for which, out in ((0, up_ref), (1, down_ref)):
@@ -247,15 +244,8 @@
         ),
         name="factor",
     )(parts[-1], gate_held, rows, upper, lower)
-    parts = pl.pallas_call(
-        stack_kernel,
-        out_shape=jax.ShapeDtypeStruct((n_dp - 1, share, 2 * cols), bf16),
-        in_specs=[ANY] + [VMEM] * (n_dp - 1),
-        out_specs=VMEM,
-        compiler_params=ROOM,
-        name="stack",
-    )(factors, *parts)
-    parts = [hop(parts, "hidden", t) for t in range(n_hid)]
+    parts = [jnp.stack([x[:, k * cols : (k + 1) * cols] for x in parts]) for k in range(2)]
+    others = [hop(x, "hidden", t) for t in range(1, n_hid) for x in parts]
 
     gathered = jnp.concatenate([hop(factors, "dp", s) for s in range(n_dp)], axis=0)
 
@@ -273,12 +263,12 @@
     piece = pl.pallas_call(
         tie_kernel,
         out_shape=jax.ShapeDtypeStruct(piece.shape, piece.dtype),
-        in_specs=[ANY] * n_hid,
+        in_specs=[ANY] * (2 * n_hid - 1),
         out_specs=ANY,
         input_output_aliases={0: 0},
         compiler_params=ROOM,
         name="tie",
-    )(piece, *parts[1:])
+    )(piece, *others)
     returned = lax.all_to_all(piece, ("expert", "hidden"), 0, 0)
     grad_rows = lax.dot_general(
         spread,
@@ -291,7 +281,7 @@
     grads = pl.pallas_call(
         functools.partial(weight_kernel, chunks, (n_dp, n_hid)),
         out_shape=[jax.ShapeDtypeStruct((1, cols, units), jnp.float32)] * 2,
-        in_specs=[VMEM] * (n_hid + 2),
+        in_specs=[VMEM] * (2 * n_hid + 2),
         out_specs=[HBM] * 2,
         scratch_shapes=[
             pltpu.VMEM((n_dp * slots, 2 * cols), bf16),
@@ -303,7 +293,7 @@
             flops=4 * n_dp * slots * cols * units, bytes_accessed=64 * cols * units, transcendentals=0
         ),
         name="weight",
-    )(rows, *parts, gathered)
+    )(rows, *parts, *others, gathered)
     return (grad_rows[None], *grads)
 
 

time: 38.9 us -> 40.2 us (1.033)
  starting transfers between devices: 17.6 us -> 18.3 us
  waiting for transfers between devices: 5.13 us -> 5.67 us
    all_to_all x1, waiting for transfers between devices: 0.01 us -> 2.41 us  [local(): returned = lax.all_to_all(piece, ('expert', 'hidden'), 0, 0)]
    ppermute x10 -> x11, waiting for transfers between devices: 5.13 us -> 3.26 us  [hop(): lax.ppermute(x, axis, [(i, i ^ step) for i in range(n)])]
    ppermute x10 -> x11, starting transfers between devices: 14.2 us -> 14.9 us  [hop(): lax.ppermute(x, axis, [(i, i ^ step) for i in range(n)])]
  transfers between devices with their start and end apart: 11 -> 12, of which waited for: 4 -> 4; matrix products, arithmetic and copies ran while one was open for 0% -> 0% of each run, Pallas kernels for 33% -> 32%
where the time goes in v15:
time: 40.2 us; the launch traced here: 40 us
  starting transfers between devices  18.3 us (46%)
  Pallas kernels  14.2 us (35%)
  waiting for transfers between devices  5.67 us (14%)
  matrix products  0.9 us (2%)
  between operations  0.77 us (2%)
    ppermute x11, starting transfers between devices, hop(): lax.ppermute(x, axis, [(i, i ^ step) for i in range(n)])  14.9 us
    pallas_call x1, Pallas kernels, local(): pl.pallas_call(load_kernel, out_shape=[jax.ShapeDtypeStruct(x.shape, x.dt...  4.64 us
    all_to_all x1, starting transfers between devices, local(): returned = lax.all_to_all(piece, ('expert', 'hidden'), 0, 0)  3.39 us
    ppermute x11, waiting for transfers between devices, hop(): lax.ppermute(x, axis, [(i, i ^ step) for i in range(n)])  3.26 us
    pallas_call x1, Pallas kernels, local(): pl.pallas_call(functools.partial(weight_kernel, chunks, (n_dp, n_hid)), o...  3.18 us
    pallas_call x1, Pallas kernels, local(): pl.pallas_call(functools.partial(piece_kernel, n_hid), out_shape=jax.Shap...  2.63 us
    all_to_all x1, waiting for transfers between devices, local(): returned = lax.all_to_all(piece, ('expert', 'hidden'), 0, 0)  2.41 us
    pallas_call x1, Pallas kernels, local(): pl.pallas_call(factor_kernel, out_shape=jax.ShapeDtypeStruct((slots, 2 *...  2.29 us
  transfers between devices with their start and end apart: 12, of which 4 were waited for; matrix products, arithmetic and copies ran while one was open for 0% of the time, Pallas kernels for 32%

profile of v15, /device:TPU:0, one launch (start us, length us, event | category | flops | bytes accessed | tf_op | source)
XLA Modules:
  0.0 40.0 jit_solution(6629337793955764749)
XLA Ops:
  0.6 1.4 %pick.1 = (bf16[32,6144]{1,0:T(8,128)(2,1)S(1)}, bf16[64,64]{1,0:T(8,128)(2,1)S(1)}) custom-call(s32[1,1,4,8]{3,2,1,0:T(4,128)} %picks_hbm.1, bf16[1,64,3072]{2,1,0:T(8,128)(2,1)} %tokens_hbm.1, bf16[1,64,3072]{2,1,0:T(8,128)(2,1)} %upstream_hbm.1), custom_call_target="tpu_custom_call" | custom-call | tf_op jit(solution)/shard_map/pick/pallas_call | solution.py:192
  2.1 2.5 %collective-permute-start.2 = (bf16[8,6144]{1,0:T(8,128)(2,1)S(1)}, bf16[8,6144]{1,0:T(8,128)(2,1)S(1)}, u32[]{:S(2)}, u32[]{:S(2)}) collective-permute-start(bf16[8,6144]{1,0:T(8,128)(2,1)S(1)} %get-tuple-element.24), channel_id=1, source_target_pairs={{0,6},{2,4},{4,2},{6,0},{1,7},{3,5},{5,3},{7,1},{8,14},{10,12},{12... | collective-permute-start | bytes 294920 | tf_op jit(solution)/shard_map/ppermute | solution.py:27
  4.6 0.6 %collective-permute-start.1 = (bf16[8,6144]{1,0:T(8,128)(2,1)S(1)}, bf16[8,6144]{1,0:T(8,128)(2,1)S(1)}, u32[]{:S(2)}, u32[]{:S(2)}) collective-permute-start(bf16[8,6144]{1,0:T(8,128)(2,1)S(1)} %get-tuple-element.25), channel_id=1, source_target_pairs={{0,4},{2,6},{4,0},{6,2},{1,5},{3,7},{5,1},{7,3},{8,12},{10,14},{12... | collective-permute-start | bytes 294920 | tf_op jit(solution)/shard_map/ppermute | solution.py:27
  5.2 0.0 collective-permute-start
  5.3 4.6 %load.1 = (f32[1,1,4,8]{3,2,1,0:T(4,128)S(1)}, bf16[1,3072,1024]{2,1,0:T(8,128)(2,1)S(1)}, bf16[1,3072,1024]{2,1,0:T(8,128)(2,1)S(1)}) custom-call(bf16[32,6144]{1,0:T(8,128)(2,1)S(1)} %get-tuple-element.14.after_ref, f32[1,1,4,8]{3,2,1,0:T(4,128)} %gates_hbm.1, bf16[1,3072,1024]{2,1,0:T(8,128)(2,1)} %upper_hbm.1, bf16[1,3072,1024]{2,1,0:T(8,128)(2,1)} %lower_hbm.1), custom_call_target="tpu_custom_call" | custom-call | bytes 25165824 | tf_op jit(solution)/shard_map/load/pallas_call | solution.py:213
  9.9 0.0 collective-permute-done.2
  9.9 0.1 collective-permute-done.1
  10.0 0.0 collective-permute-done
  10.1 4.4 %collective-permute-start.3 = (bf16[16,1536]{1,0:T(8,128)(2,1)S(1)}, bf16[16,1536]{1,0:T(8,128)(2,1)S(1)}, u32[]{:S(2)}, u32[]{:S(2)}) collective-permute-start(bf16[16,1536]{1,0:T(8,128)(2,1)S(1)} %get-tuple-element.16), channel_id=1, source_target_pairs={{0,24},{8,16},{16,8},{24,0},{1,25},{9,17},{17,9},{25,1},{2,26},{10... | collective-permute-start | bytes 147464 | tf_op jit(solution)/shard_map/ppermute | solution.py:27
  14.5 0.0 collective-permute-start.4
  14.6 0.6 %collective-permute-start.5 = (bf16[16,1536]{1,0:T(8,128)(2,1)S(1)}, bf16[16,1536]{1,0:T(8,128)(2,1)S(1)}, u32[]{:S(2)}, u32[]{:S(2)}) collective-permute-start(bf16[16,1536]{1,0:T(8,128)(2,1)S(1)} %get-tuple-element.20), channel_id=1, source_target_pairs={{0,16},{8,24},{16,0},{24,8},{1,17},{9,25},{17,1},{25,9},{2,18},{10... | collective-permute-start | bytes 147464 | tf_op jit(solution)/shard_map/ppermute | solution.py:27
  15.2 1.9 %collective-permute-done.3.after_ref = bf16[16,1536]{1,0:T(8,128)(2,1)S(1)} collective-permute-done((bf16[16,1536]{1,0:T(8,128)(2,1)S(1)}, bf16[16,1536]{1,0:T(8,128)(2,1)S(1)}, u32[]{:S(2)}, u32[]{:S(2)}) %collective-permute-start.3) | collective-permute-done | bytes 49184 | tf_op jit(solution)/shard_map/ppermute | solution.py:27
  17.1 2.3 %factor.1.factor_ref = bf16[32,2048]{1,0:T(8,128)(2,1)S(1)} custom-call(bf16[16,1536]{1,0:T(8,128)(2,1)S(1)} %collective-permute-done.3.after_ref, f32[1,1,4,8]{3,2,1,0:T(4,128)S(1)} %get-tuple-element.15.after_ref.gates_ref, bf16[32,6144]{1,0:T(8,128)(2,1)S(1)} %pad_maximum_fusion.1.rows_ref.own_ref, ...), custom_call_target="tpu_custom_call" | custom-call | flops 402653184 | bytes 12582912 | tf_op jit(solution)/shard_map/factor/pallas_call | solution.py:236
  19.4 3.9 %collective-permute-start.10 = (bf16[32,2048]{1,0:T(8,128)(2,1)S(1)}, bf16[32,2048]{1,0:T(8,128)(2,1)S(1)}, u32[]{:S(2)}, u32[]{:S(2)}) collective-permute-start(bf16[32,2048]{1,0:T(8,128)(2,1)S(1)} %factor.1.factor_ref), channel_id=1, source_target_pairs={{0,24},{8,16},{16,8},{24,0},{1,25},{9,17},{17,9},{25,1},{2,26},{10... | collective-permute-start | bytes 393224 | tf_op jit(solution)/shard_map/ppermute | solution.py:27
  23.3 0.0 collective-permute-start.9
  23.3 0.6 %collective-permute-start.8 = (bf16[32,2048]{1,0:T(8,128)(2,1)S(1)}, bf16[32,2048]{1,0:T(8,128)(2,1)S(1)}, u32[]{:S(2)}, u32[]{:S(2)}) collective-permute-start(bf16[32,2048]{1,0:T(8,128)(2,1)S(1)} %factor.1.factor_ref), channel_id=1, source_target_pairs={{0,8},{8,0},{16,24},{24,16},{1,9},{9,1},{17,25},{25,17},{2,10},{10... | collective-permute-start | bytes 393224 | tf_op jit(solution)/shard_map/ppermute | solution.py:27
  24.0 0.0 collective-permute-done.4
  24.0 0.0 collective-permute-done.5
  24.0 1.6 %collective-permute-start.6 = (bf16[3,16,768]{2,1,0:T(8,128)(2,1)S(1)}, bf16[3,16,768]{2,1,0:T(8,128)(2,1)S(1)}, u32[]{:S(2)}, u32[]{:S(2)}) collective-permute-start(bf16[3,16,768]{2,1,0:T(8,128)(2,1)S(1)} %pad_maximum_fusion.2.refs_0_), channel_id=1, source_target_pairs={{0,1},{1,0},{2,3},{3,2},{4,5},{5,4},{6,7},{7,6},{8,9},{9,8},{10,11... | collective-permute-start | bytes 221192 | tf_op jit(solution)/shard_map/ppermute | solution.py:27
  25.6 0.6 %collective-permute-start.7 = (bf16[3,16,768]{2,1,0:T(8,128)(2,1)S(1)}, bf16[3,16,768]{2,1,0:T(8,128)(2,1)S(1)}, u32[]{:S(2)}, u32[]{:S(2)}) collective-permute-start(bf16[3,16,768]{2,1,0:T(8,128)(2,1)S(1)} %pad_maximum_fusion.3.refs_1_), channel_id=1, source_target_pairs={{0,1},{1,0},{2,3},{3,2},{4,5},{5,4},{6,7},{7,6},{8,9},{9,8},{10,11... | collective-permute-start | bytes 221192 | tf_op jit(solution)/shard_map/ppermute | solution.py:27
  26.2 2.6 %piece.1.refs_0_ = bf16[8,8,1536]{2,1,0:T(8,128)(2,1)} custom-call(bf16[32,2048]{1,0:T(8,128)(2,1)S(1)} %factor.1.factor_ref, bf16[1,3072,1024]{2,1,0:T(8,128)(2,1)S(1)} %get-tuple-element.17.upper_ref), custom_call_target="tpu_custom_call" | custom-call | flops 201326592 | bytes 6291456 | tf_op jit(solution)/shard_map/piece/pallas_call | solution.py:252
  28.8 0.0 collective-permute-done.6.refs_1_.refs_2_
  28.8 1.2 %collective-permute-done.7.refs_2_.refs_3_ = bf16[3,16,768]{2,1,0:T(8,128)(2,1)S(1)} collective-permute-done((bf16[3,16,768]{2,1,0:T(8,128)(2,1)S(1)}, bf16[3,16,768]{2,1,0:T(8,128)(2,1)S(1)}, u32[]{:S(2)}, u32[]{:S(2)}) %collective-permute-start.7) | collective-permute-done | bytes 73760 | tf_op jit(solution)/shard_map/ppermute | solution.py:27
  30.0 3.4 %all-to-all-start = ((bf16[8,8,1536]{2,1,0:T(8,128)(2,1)}), bf16[8,8,1536]{2,1,0:T(8,128)(2,1)S(1)}, u32[]{:S(2)}, u32[]{:S(2)}) async-start(bf16[8,8,1536]{2,1,0:T(8,128)(2,1)} %tie.1), calls=%async_computation | async-start | bytes 393216 | tf_op jit(solution)/shard_map/all_to_all | solution.py:272
  33.4 0.0 collective-permute-done.10
  33.4 0.0 collective-permute-done.9
  33.4 0.0 collective-permute-done.8
  33.5 3.2 %weight.1 = (f32[1,768,1024]{2,1,0:T(8,128)}, f32[1,768,1024]{2,1,0:T(8,128)}) custom-call(bf16[32,6144]{1,0:T(8,128)(2,1)S(1)} %pad_maximum_fusion.1.rows_ref.own_ref, bf16[3,16,768]{2,1,0:T(8,128)(2,1)S(1)} %pad_maximum_fusion.2.refs_0_, bf16[3,16,768]{2,1,0:T(8,128)(2,1)S(1)} %pad_maximum_fusion.3.refs_1_, ...), custom_call_target="tpu_custom_call" | custom-call | flops 402653184 | bytes 50331648 | tf_op jit(solution)/shard_map/weight/pallas_call | solution.py:281
  36.7 2.4 %all-to-all-done = bf16[8,8,1536]{2,1,0:T(8,128)(2,1)S(1)} async-done(((bf16[8,8,1536]{2,1,0:T(8,128)(2,1)}), bf16[8,8,1536]{2,1,0:T(8,128)(2,1)S(1)}, u32[]{:S(2)}, u32[]{:S(2)}) %all-to-all-start) | async-done | bytes 196640 | tf_op jit(solution)/shard_map/all_to_all | solution.py:272
  39.1 0.9 %fusion = bf16[1,64,1536]{2,1,0:T(8,128)(2,1)} fusion(bf16[64,64]{1,0:T(8,128)(2,1)S(1)} %get-tuple-element.13, bf16[8,8,1536]{2,1,0:T(8,128)(2,1)S(1)} %all-to-all-done), kind=kOutput, calls=%fused_computation.1 | convolution fusion | flops 12681216 | bytes 401408 | tf_op jit(solution)/shard_map/dot_general | solution.py:273
  (10 shorter events, 0.2 us)
Async XLA Ops:
  2.1 7.8 %collective-permute-start.2 = (bf16[8,6144]{1,0:T(8,128)(2,1)S(1)}, bf16[8,6144]{1,0:T(8,128)(2,1)S(1)}, u32[]{:S(2)}, u32[]{:S(2)}) collective-permute-start(bf16[8,6144]{1,0:T(8,128)(2,1)S(1)} %get-tuple-element.24), channel_id=1, source_target_pairs={{0,6},{2,4},{4,2},{6,0},{1,7},{3,5},{5,3},{7,1},{8,14},{10,12},{12... | collective-permute-start | bytes 294920 | tf_op jit(solution)/shard_map/ppermute | solution.py:27
  4.6 5.5 %collective-permute-start.1 = (bf16[8,6144]{1,0:T(8,128)(2,1)S(1)}, bf16[8,6144]{1,0:T(8,128)(2,1)S(1)}, u32[]{:S(2)}, u32[]{:S(2)}) collective-permute-start(bf16[8,6144]{1,0:T(8,128)(2,1)S(1)} %get-tuple-element.25), channel_id=1, source_target_pairs={{0,4},{2,6},{4,0},{6,2},{1,5},{3,7},{5,1},{7,3},{8,12},{10,14},{12... | collective-permute-start | bytes 294920 | tf_op jit(solution)/shard_map/ppermute | solution.py:27
  5.2 4.8 %collective-permute-start = (bf16[8,6144]{1,0:T(8,128)(2,1)S(1)}, bf16[8,6144]{1,0:T(8,128)(2,1)S(1)}, u32[]{:S(2)}, u32[]{:S(2)}) collective-permute-start(bf16[8,6144]{1,0:T(8,128)(2,1)S(1)} %get-tuple-element.26), channel_id=1, source_target_pairs={{0,2},{2,0},{4,6},{6,4},{1,3},{3,1},{5,7},{7,5},{8,10},{10,8},{12,... | collective-permute-start | bytes 294920 | tf_op jit(solution)/shard_map/ppermute | solution.py:27
  10.1 7.0 %collective-permute-start.3 = (bf16[16,1536]{1,0:T(8,128)(2,1)S(1)}, bf16[16,1536]{1,0:T(8,128)(2,1)S(1)}, u32[]{:S(2)}, u32[]{:S(2)}) collective-permute-start(bf16[16,1536]{1,0:T(8,128)(2,1)S(1)} %get-tuple-element.16), channel_id=1, source_target_pairs={{0,24},{8,16},{16,8},{24,0},{1,25},{9,17},{17,9},{25,1},{2,26},{10... | collective-permute-start | bytes 147464 | tf_op jit(solution)/shard_map/ppermute | solution.py:27
  14.5 9.4 %collective-permute-start.4 = (bf16[16,1536]{1,0:T(8,128)(2,1)S(1)}, bf16[16,1536]{1,0:T(8,128)(2,1)S(1)}, u32[]{:S(2)}, u32[]{:S(2)}) collective-permute-start(bf16[16,1536]{1,0:T(8,128)(2,1)S(1)} %get-tuple-element.19), channel_id=1, source_target_pairs={{0,8},{8,0},{16,24},{24,16},{1,9},{9,1},{17,25},{25,17},{2,10},{10... | collective-permute-start | bytes 147464 | tf_op jit(solution)/shard_map/ppermute | solution.py:27
  14.6 9.4 %collective-permute-start.5 = (bf16[16,1536]{1,0:T(8,128)(2,1)S(1)}, bf16[16,1536]{1,0:T(8,128)(2,1)S(1)}, u32[]{:S(2)}, u32[]{:S(2)}) collective-permute-start(bf16[16,1536]{1,0:T(8,128)(2,1)S(1)} %get-tuple-element.20), channel_id=1, source_target_pairs={{0,16},{8,24},{16,0},{24,8},{1,17},{9,25},{17,1},{25,9},{2,18},{10... | collective-permute-start | bytes 147464 | tf_op jit(solution)/shard_map/ppermute | solution.py:27
  19.4 14.0 %collective-permute-start.10 = (bf16[32,2048]{1,0:T(8,128)(2,1)S(1)}, bf16[32,2048]{1,0:T(8,128)(2,1)S(1)}, u32[]{:S(2)}, u32[]{:S(2)}) collective-permute-start(bf16[32,2048]{1,0:T(8,128)(2,1)S(1)} %factor.1.factor_ref), channel_id=1, source_target_pairs={{0,24},{8,16},{16,8},{24,0},{1,25},{9,17},{17,9},{25,1},{2,26},{10... | collective-permute-start | bytes 393224 | tf_op jit(solution)/shard_map/ppermute | solution.py:27
  23.3 10.1 %collective-permute-start.9 = (bf16[32,2048]{1,0:T(8,128)(2,1)S(1)}, bf16[32,2048]{1,0:T(8,128)(2,1)S(1)}, u32[]{:S(2)}, u32[]{:S(2)}) collective-permute-start(bf16[32,2048]{1,0:T(8,128)(2,1)S(1)} %factor.1.factor_ref), channel_id=1, source_target_pairs={{0,16},{8,24},{16,0},{24,8},{1,17},{9,25},{17,1},{25,9},{2,18},{10... | collective-permute-start | bytes 393224 | tf_op jit(solution)/shard_map/ppermute | solution.py:27
  23.3 10.1 %collective-permute-start.8 = (bf16[32,2048]{1,0:T(8,128)(2,1)S(1)}, bf16[32,2048]{1,0:T(8,128)(2,1)S(1)}, u32[]{:S(2)}, u32[]{:S(2)}) collective-permute-start(bf16[32,2048]{1,0:T(8,128)(2,1)S(1)} %factor.1.factor_ref), channel_id=1, source_target_pairs={{0,8},{8,0},{16,24},{24,16},{1,9},{9,1},{17,25},{25,17},{2,10},{10... | collective-permute-start | bytes 393224 | tf_op jit(solution)/shard_map/ppermute | solution.py:27
  24.0 4.8 %collective-permute-start.6 = (bf16[3,16,768]{2,1,0:T(8,128)(2,1)S(1)}, bf16[3,16,768]{2,1,0:T(8,128)(2,1)S(1)}, u32[]{:S(2)}, u32[]{:S(2)}) collective-permute-start(bf16[3,16,768]{2,1,0:T(8,128)(2,1)S(1)} %pad_maximum_fusion.2.refs_0_), channel_id=1, source_target_pairs={{0,1},{1,0},{2,3},{3,2},{4,5},{5,4},{6,7},{7,6},{8,9},{9,8},{10,11... | collective-permute-start | bytes 221192 | tf_op jit(solution)/shard_map/ppermute | solution.py:27
  25.6 4.4 %collective-permute-start.7 = (bf16[3,16,768]{2,1,0:T(8,128)(2,1)S(1)}, bf16[3,16,768]{2,1,0:T(8,128)(2,1)S(1)}, u32[]{:S(2)}, u32[]{:S(2)}) collective-permute-start(bf16[3,16,768]{2,1,0:T(8,128)(2,1)S(1)} %pad_maximum_fusion.3.refs_1_), channel_id=1, source_target_pairs={{0,1},{1,0},{2,3},{3,2},{4,5},{5,4},{6,7},{7,6},{8,9},{9,8},{10,11... | collective-permute-start | bytes 221192 | tf_op jit(solution)/shard_map/ppermute | solution.py:27
  30.0 9.1 %all-to-all-start = ((bf16[8,8,1536]{2,1,0:T(8,128)(2,1)}), bf16[8,8,1536]{2,1,0:T(8,128)(2,1)S(1)}, u32[]{:S(2)}, u32[]{:S(2)}) async-start(bf16[8,8,1536]{2,1,0:T(8,128)(2,1)} %tie.1), calls=%async_computation | async-start | bytes 393216 | tf_op jit(solution)/shard_map/all_to_all | solution.py:272

commit v16 on v14

--- a/solution.py
+++ b/solution.py
@@ -151,24 +151,34 @@
         spot = (my_hid ^ t) * rows
         for s in range(1, n_dp):
             side_ref[pl.ds(pl.multiple_of(s * slots + spot, 16), rows), :] = part[s - 1]
-    step = units // chunks
+    step = cols // chunks
     copies = []
     for which, out in ((0, up_ref), (1, down_ref)):
         for c in range(chunks):
             spot = pl.ds(c * step, step)
-            held[which, :, spot] = lax.dot_general(
-                side_ref[:, which * cols : (which + 1) * cols],
-                factor_ref[:, pl.ds(which * units + c * step, step)],
+            held[which, spot, :] = lax.dot_general(
+                side_ref[:, pl.ds(which * cols + c * step, step)],
+                factor_ref[:, which * units : (which + 1) * units],
                 (((0,), (0,)), ((), ())),
                 preferred_element_type=jnp.float32,
             )
             copy = pltpu.make_async_copy(
-                held.at[which, :, spot], out.at[0, :, spot], sems.at[which, c]
+                held.at[which, spot, :], out.at[0, spot, :], sems.at[which, c]
             )
             copy.start()
             copies.append(copy)
     for copy in copies:
         copy.wait()
+
+
+def return_kernel(spread_ref, came_ref, out_ref):
+    came = jnp.concatenate([came_ref[k].astype(jnp.float32) for k in range(came_ref.shape[0])], axis=0)
+    out_ref[0] = lax.dot_general(
+        spread_ref[...],
+        came.astype(jnp.bfloat16),
+        (((0,), (0,)), ((), ())),
+        preferred_element_type=jnp.float32,
+    ).astype(jnp.bfloat16)
 
 
 VMEM = pl.BlockSpec(memory_space=pltpu.VMEM)
@@ -280,14 +290,16 @@
         name="tie",
     )(piece, *parts[1:])
     returned = lax.all_to_all(piece, ("expert", "hidden"), 0, 0)
-    grad_rows = lax.dot_general(
-        spread,
-        returned.reshape(slots * n_hid, part),
-        (((0,), (0,)), ((), ())),
-        preferred_element_type=jnp.float32,
-    ).astype(bf16)
-
-    chunks = max(1, units // 256)
+    grad_in = pl.pallas_call(
+        return_kernel,
+        out_shape=jax.ShapeDtypeStruct((1, tok_dev, part), bf16),
+        in_specs=[VMEM] * 2,
+        out_specs=VMEM,
+        compiler_params=ROOM,
+        name="return",
+    )(spread, returned)
+
+    chunks = cols // 128
     grads = pl.pallas_call(
         functools.partial(weight_kernel, chunks, (n_dp, n_hid)),
         out_shape=[jax.ShapeDtypeStruct((1, cols, units), jnp.float32)] * 2,
@@ -304,7 +316,7 @@
         ),
         name="weight",
     )(rows, *parts, gathered)
-    return (grad_rows[None], *grads)
+    return (grad_in, *grads)
 
 
 def solution(mesh):

time: 38.9 us -> 38.9 us (level)
  matrix products: 0.91 us -> 0 us
  Pallas kernels: 14.2 us -> 15 us
    dot_general x1 -> x0, matrix products: 0.91 us -> none  [local(): lax.dot_general(spread, returned.reshape(slots * n_hid, part), (((0,), (0...]
    pallas_call x0 -> x1, Pallas kernels: none -> 0.9 us  [local(): pl.pallas_call(return_kernel, out_shape=jax.ShapeDtypeStruct((1, tok_dev,...]
  transfers between devices with their start and end apart: 11 -> 11, of which waited for: 4 -> 5; matrix products, arithmetic and copies ran while one was open for 0% -> 0% of each run, Pallas kernels for 33% -> 33%
where the time goes in v16:
time: 38.9 us; the launch traced here: 38.6 us
  starting transfers between devices  17.6 us (45%)
  Pallas kernels  15 us (39%)
  waiting for transfers between devices  5.24 us (13%)
  between operations  0.73 us (2%)
    ppermute x10, starting transfers between devices, hop(): lax.ppermute(x, axis, [(i, i ^ step) for i in range(n)])  14.2 us
    ppermute x10, waiting for transfers between devices, hop(): lax.ppermute(x, axis, [(i, i ^ step) for i in range(n)])  5.13 us
    pallas_call x1, Pallas kernels, local(): pl.pallas_call(load_kernel, out_shape=[jax.ShapeDtypeStruct(x.shape, x.dt...  4.64 us
    all_to_all x1, starting transfers between devices, local(): returned = lax.all_to_all(piece, ('expert', 'hidden'), 0, 0)  3.39 us
    pallas_call x1, Pallas kernels, local(): pl.pallas_call(functools.partial(weight_kernel, chunks, (n_dp, n_hid)), o...  3.04 us
    pallas_call x1, Pallas kernels, local(): pl.pallas_call(functools.partial(piece_kernel, n_hid), out_shape=jax.Shap...  2.63 us
    pallas_call x1, Pallas kernels, local(): pl.pallas_call(factor_kernel, out_shape=jax.ShapeDtypeStruct((slots, 2 *...  2.29 us
    pallas_call x1, Pallas kernels, local(): pl.pallas_call(functools.partial(pick_kernel, n_hid), out_shape=[jax.Shap...  1.42 us
  transfers between devices with their start and end apart: 11, of which 5 were waited for; matrix products, arithmetic and copies ran while one was open for 0% of the time, Pallas kernels for 33%

profile of v16, /device:TPU:0, one launch (start us, length us, event | category | flops | bytes accessed | tf_op | source)
XLA Modules:
  0.0 38.6 jit_solution(10018906136337913364)
XLA Ops:
  0.6 1.4 %pick.1 = (bf16[32,6144]{1,0:T(8,128)(2,1)S(1)}, bf16[64,64]{1,0:T(8,128)(2,1)S(1)}) custom-call(s32[1,1,4,8]{3,2,1,0:T(4,128)} %picks_hbm.1, bf16[1,64,3072]{2,1,0:T(8,128)(2,1)} %tokens_hbm.1, bf16[1,64,3072]{2,1,0:T(8,128)(2,1)} %upstream_hbm.1), custom_call_target="tpu_custom_call" | custom-call | tf_op jit(solution)/shard_map/pick/pallas_call | solution.py:205
  2.1 2.5 %collective-permute-start.2 = (bf16[8,6144]{1,0:T(8,128)(2,1)S(1)}, bf16[8,6144]{1,0:T(8,128)(2,1)S(1)}, u32[]{:S(2)}, u32[]{:S(2)}) collective-permute-start(bf16[8,6144]{1,0:T(8,128)(2,1)S(1)} %get-tuple-element.24), channel_id=1, source_target_pairs={{0,6},{2,4},{4,2},{6,0},{1,7},{3,5},{5,3},{7,1},{8,14},{10,12},{12... | collective-permute-start | bytes 294920 | tf_op jit(solution)/shard_map/ppermute | solution.py:27
  4.6 0.6 %collective-permute-start.1 = (bf16[8,6144]{1,0:T(8,128)(2,1)S(1)}, bf16[8,6144]{1,0:T(8,128)(2,1)S(1)}, u32[]{:S(2)}, u32[]{:S(2)}) collective-permute-start(bf16[8,6144]{1,0:T(8,128)(2,1)S(1)} %get-tuple-element.25), channel_id=1, source_target_pairs={{0,4},{2,6},{4,0},{6,2},{1,5},{3,7},{5,1},{7,3},{8,12},{10,14},{12... | collective-permute-start | bytes 294920 | tf_op jit(solution)/shard_map/ppermute | solution.py:27
  5.2 0.0 collective-permute-start
  5.3 4.6 %load.1 = (f32[1,1,4,8]{3,2,1,0:T(4,128)S(1)}, bf16[1,3072,1024]{2,1,0:T(8,128)(2,1)S(1)}, bf16[1,3072,1024]{2,1,0:T(8,128)(2,1)S(1)}) custom-call(bf16[32,6144]{1,0:T(8,128)(2,1)S(1)} %get-tuple-element.14.after_ref, f32[1,1,4,8]{3,2,1,0:T(4,128)} %gates_hbm.1, bf16[1,3072,1024]{2,1,0:T(8,128)(2,1)} %upper_hbm.1, bf16[1,3072,1024]{2,1,0:T(8,128)(2,1)} %lower_hbm.1), custom_call_target="tpu_custom_call" | custom-call | bytes 25165824 | tf_op jit(solution)/shard_map/load/pallas_call | solution.py:226
  9.9 0.0 collective-permute-done.2
  9.9 0.1 collective-permute-done.1
  10.0 0.0 collective-permute-done
  10.1 4.4 %collective-permute-start.3 = (bf16[16,1536]{1,0:T(8,128)(2,1)S(1)}, bf16[16,1536]{1,0:T(8,128)(2,1)S(1)}, u32[]{:S(2)}, u32[]{:S(2)}) collective-permute-start(bf16[16,1536]{1,0:T(8,128)(2,1)S(1)} %get-tuple-element.16), channel_id=1, source_target_pairs={{0,24},{8,16},{16,8},{24,0},{1,25},{9,17},{17,9},{25,1},{2,26},{10... | collective-permute-start | bytes 147464 | tf_op jit(solution)/shard_map/ppermute | solution.py:27
  14.6 0.0 collective-permute-start.4
  14.6 0.6 %collective-permute-start.5 = (bf16[16,1536]{1,0:T(8,128)(2,1)S(1)}, bf16[16,1536]{1,0:T(8,128)(2,1)S(1)}, u32[]{:S(2)}, u32[]{:S(2)}) collective-permute-start(bf16[16,1536]{1,0:T(8,128)(2,1)S(1)} %get-tuple-element.20), channel_id=1, source_target_pairs={{0,16},{8,24},{16,0},{24,8},{1,17},{9,25},{17,1},{25,9},{2,18},{10... | collective-permute-start | bytes 147464 | tf_op jit(solution)/shard_map/ppermute | solution.py:27
  15.2 1.9 %collective-permute-done.3.after_ref.refs_2_ = bf16[16,1536]{1,0:T(8,128)(2,1)S(1)} collective-permute-done((bf16[16,1536]{1,0:T(8,128)(2,1)S(1)}, bf16[16,1536]{1,0:T(8,128)(2,1)S(1)}, u32[]{:S(2)}, u32[]{:S(2)}) %collective-permute-start.3) | collective-permute-done | bytes 49184 | tf_op jit(solution)/shard_map/ppermute | solution.py:27
  17.1 2.3 %factor.1.factor_ref.after_ref = bf16[32,2048]{1,0:T(8,128)(2,1)S(1)} custom-call(bf16[16,1536]{1,0:T(8,128)(2,1)S(1)} %collective-permute-done.3.after_ref.refs_2_, f32[1,1,4,8]{3,2,1,0:T(4,128)S(1)} %get-tuple-element.15.after_ref.gates_ref, bf16[32,6144]{1,0:T(8,128)(2,1)S(1)} %pad_maximum_fusion.1.rows_ref.own_ref, ...), custom_call_target="tpu_custom_call" | custom-call | flops 402653184 | bytes 12582912 | tf_op jit(solution)/shard_map/factor/pallas_call | solution.py:249
  19.4 0.0 collective-permute-done.4.refs_0_
  19.4 0.6 %collective-permute-done.5.refs_1_ = bf16[16,1536]{1,0:T(8,128)(2,1)S(1)} collective-permute-done((bf16[16,1536]{1,0:T(8,128)(2,1)S(1)}, bf16[16,1536]{1,0:T(8,128)(2,1)S(1)}, u32[]{:S(2)}, u32[]{:S(2)}) %collective-permute-start.5) | collective-permute-done | bytes 49184 | tf_op jit(solution)/shard_map/ppermute | solution.py:27
  20.1 1.6 %collective-permute-start.6 = (bf16[3,16,1536]{2,1,0:T(8,128)(2,1)S(1)}, bf16[3,16,1536]{2,1,0:T(8,128)(2,1)S(1)}, u32[]{:S(2)}, u32[]{:S(2)}) collective-permute-start(bf16[3,16,1536]{2,1,0:T(8,128)(2,1)S(1)} %stack.1.refs_0_), channel_id=1, source_target_pairs={{0,1},{1,0},{2,3},{3,2},{4,5},{5,4},{6,7},{7,6},{8,9},{9,8},{10,11... | collective-permute-start | bytes 442376 | tf_op jit(solution)/shard_map/ppermute | solution.py:27
  21.6 3.2 %collective-permute-start.9 = (bf16[32,2048]{1,0:T(8,128)(2,1)S(1)}, bf16[32,2048]{1,0:T(8,128)(2,1)S(1)}, u32[]{:S(2)}, u32[]{:S(2)}) collective-permute-start(bf16[32,2048]{1,0:T(8,128)(2,1)S(1)} %factor.1.factor_ref.after_ref), channel_id=1, source_target_pairs={{0,24},{8,16},{16,8},{24,0},{1,25},{9,17},{17,9},{25,1},{2,26},{10... | collective-permute-start | bytes 393224 | tf_op jit(solution)/shard_map/ppermute | solution.py:27
  24.8 0.0 collective-permute-start.8
  24.8 1.2 %collective-permute-start.7 = (bf16[32,2048]{1,0:T(8,128)(2,1)S(1)}, bf16[32,2048]{1,0:T(8,128)(2,1)S(1)}, u32[]{:S(2)}, u32[]{:S(2)}) collective-permute-start(bf16[32,2048]{1,0:T(8,128)(2,1)S(1)} %factor.1.factor_ref.after_ref), channel_id=1, source_target_pairs={{0,8},{8,0},{16,24},{24,16},{1,9},{9,1},{17,25},{25,17},{2,10},{10... | collective-permute-start | bytes 393224 | tf_op jit(solution)/shard_map/ppermute | solution.py:27
  26.0 2.6 %piece.1.refs_0_ = bf16[8,8,1536]{2,1,0:T(8,128)(2,1)} custom-call(bf16[32,2048]{1,0:T(8,128)(2,1)S(1)} %factor.1.factor_ref.after_ref, bf16[1,3072,1024]{2,1,0:T(8,128)(2,1)S(1)} %get-tuple-element.17.upper_ref), custom_call_target="tpu_custom_call" | custom-call | flops 201326592 | bytes 6291456 | tf_op jit(solution)/shard_map/piece/pallas_call | solution.py:272
  28.6 0.0 collective-permute-done.6.refs_1_
  28.6 3.4 %all-to-all-start = ((bf16[8,8,1536]{2,1,0:T(8,128)(2,1)}), bf16[8,8,1536]{2,1,0:T(8,128)(2,1)S(1)}, u32[]{:S(2)}, u32[]{:S(2)}) async-start(bf16[8,8,1536]{2,1,0:T(8,128)(2,1)} %tie.1), calls=%async_computation | async-start | bytes 393216 | tf_op jit(solution)/shard_map/all_to_all | solution.py:292
  32.0 0.0 collective-permute-done.9
  32.0 2.5 %collective-permute-done.8 = bf16[32,2048]{1,0:T(8,128)(2,1)S(1)} collective-permute-done((bf16[32,2048]{1,0:T(8,128)(2,1)S(1)}, bf16[32,2048]{1,0:T(8,128)(2,1)S(1)}, u32[]{:S(2)}, u32[]{:S(2)}) %collective-permute-start.8) | collective-permute-done | bytes 131104 | tf_op jit(solution)/shard_map/ppermute | solution.py:27
  34.5 0.0 collective-permute-done.7
  34.6 3.0 %weight.1 = (f32[1,768,1024]{2,1,0:T(8,128)}, f32[1,768,1024]{2,1,0:T(8,128)}) custom-call(bf16[32,6144]{1,0:T(8,128)(2,1)S(1)} %pad_maximum_fusion.1.rows_ref.own_ref, bf16[3,16,1536]{2,1,0:T(8,128)(2,1)S(1)} %stack.1.refs_0_, bf16[3,16,1536]{2,1,0:T(8,128)(2,1)S(1)} %collective-permute-done.6.refs_1_, bf16[128,2048]{1,0:T(8,128)(2,1)S(1)} %pad_maximum_fusion.refs_2_), custom_call_target="tpu_custom_call" | custom-call | flops 402653184 | bytes 50331648 | tf_op jit(solution)/shard_map/weight/pallas_call | solution.py:303
  37.6 0.1 all-to-all-done.came_ref
  37.7 0.9 %return.1 = bf16[1,64,1536]{2,1,0:T(8,128)(2,1)} custom-call(bf16[64,64]{1,0:T(8,128)(2,1)S(1)} %get-tuple-element.13.spread_ref, bf16[8,8,1536]{2,1,0:T(8,128)(2,1)S(1)} %all-to-all-done.came_ref), custom_call_target="tpu_custom_call" | custom-call | tf_op jit(solution)/shard_map/return/pallas_call | solution.py:293
  (6 shorter events, 0.1 us)
Async XLA Ops:
  2.1 7.8 %collective-permute-start.2 = (bf16[8,6144]{1,0:T(8,128)(2,1)S(1)}, bf16[8,6144]{1,0:T(8,128)(2,1)S(1)}, u32[]{:S(2)}, u32[]{:S(2)}) collective-permute-start(bf16[8,6144]{1,0:T(8,128)(2,1)S(1)} %get-tuple-element.24), channel_id=1, source_target_pairs={{0,6},{2,4},{4,2},{6,0},{1,7},{3,5},{5,3},{7,1},{8,14},{10,12},{12... | collective-permute-start | bytes 294920 | tf_op jit(solution)/shard_map/ppermute | solution.py:27
  4.6 5.5 %collective-permute-start.1 = (bf16[8,6144]{1,0:T(8,128)(2,1)S(1)}, bf16[8,6144]{1,0:T(8,128)(2,1)S(1)}, u32[]{:S(2)}, u32[]{:S(2)}) collective-permute-start(bf16[8,6144]{1,0:T(8,128)(2,1)S(1)} %get-tuple-element.25), channel_id=1, source_target_pairs={{0,4},{2,6},{4,0},{6,2},{1,5},{3,7},{5,1},{7,3},{8,12},{10,14},{12... | collective-permute-start | bytes 294920 | tf_op jit(solution)/shard_map/ppermute | solution.py:27
  5.2 4.8 %collective-permute-start = (bf16[8,6144]{1,0:T(8,128)(2,1)S(1)}, bf16[8,6144]{1,0:T(8,128)(2,1)S(1)}, u32[]{:S(2)}, u32[]{:S(2)}) collective-permute-start(bf16[8,6144]{1,0:T(8,128)(2,1)S(1)} %get-tuple-element.26), channel_id=1, source_target_pairs={{0,2},{2,0},{4,6},{6,4},{1,3},{3,1},{5,7},{7,5},{8,10},{10,8},{12,... | collective-permute-start | bytes 294920 | tf_op jit(solution)/shard_map/ppermute | solution.py:27
  10.1 7.0 %collective-permute-start.3 = (bf16[16,1536]{1,0:T(8,128)(2,1)S(1)}, bf16[16,1536]{1,0:T(8,128)(2,1)S(1)}, u32[]{:S(2)}, u32[]{:S(2)}) collective-permute-start(bf16[16,1536]{1,0:T(8,128)(2,1)S(1)} %get-tuple-element.16), channel_id=1, source_target_pairs={{0,24},{8,16},{16,8},{24,0},{1,25},{9,17},{17,9},{25,1},{2,26},{10... | collective-permute-start | bytes 147464 | tf_op jit(solution)/shard_map/ppermute | solution.py:27
  14.6 4.9 %collective-permute-start.4 = (bf16[16,1536]{1,0:T(8,128)(2,1)S(1)}, bf16[16,1536]{1,0:T(8,128)(2,1)S(1)}, u32[]{:S(2)}, u32[]{:S(2)}) collective-permute-start(bf16[16,1536]{1,0:T(8,128)(2,1)S(1)} %get-tuple-element.19), channel_id=1, source_target_pairs={{0,8},{8,0},{16,24},{24,16},{1,9},{9,1},{17,25},{25,17},{2,10},{10... | collective-permute-start | bytes 147464 | tf_op jit(solution)/shard_map/ppermute | solution.py:27
  14.6 5.5 %collective-permute-start.5 = (bf16[16,1536]{1,0:T(8,128)(2,1)S(1)}, bf16[16,1536]{1,0:T(8,128)(2,1)S(1)}, u32[]{:S(2)}, u32[]{:S(2)}) collective-permute-start(bf16[16,1536]{1,0:T(8,128)(2,1)S(1)} %get-tuple-element.20), channel_id=1, source_target_pairs={{0,16},{8,24},{16,0},{24,8},{1,17},{9,25},{17,1},{25,9},{2,18},{10... | collective-permute-start | bytes 147464 | tf_op jit(solution)/shard_map/ppermute | solution.py:27
  20.1 8.6 %collective-permute-start.6 = (bf16[3,16,1536]{2,1,0:T(8,128)(2,1)S(1)}, bf16[3,16,1536]{2,1,0:T(8,128)(2,1)S(1)}, u32[]{:S(2)}, u32[]{:S(2)}) collective-permute-start(bf16[3,16,1536]{2,1,0:T(8,128)(2,1)S(1)} %stack.1.refs_0_), channel_id=1, source_target_pairs={{0,1},{1,0},{2,3},{3,2},{4,5},{5,4},{6,7},{7,6},{8,9},{9,8},{10,11... | collective-permute-start | bytes 442376 | tf_op jit(solution)/shard_map/ppermute | solution.py:27
  21.6 10.4 %collective-permute-start.9 = (bf16[32,2048]{1,0:T(8,128)(2,1)S(1)}, bf16[32,2048]{1,0:T(8,128)(2,1)S(1)}, u32[]{:S(2)}, u32[]{:S(2)}) collective-permute-start(bf16[32,2048]{1,0:T(8,128)(2,1)S(1)} %factor.1.factor_ref.after_ref), channel_id=1, source_target_pairs={{0,24},{8,16},{16,8},{24,0},{1,25},{9,17},{17,9},{25,1},{2,26},{10... | collective-permute-start | bytes 393224 | tf_op jit(solution)/shard_map/ppermute | solution.py:27
  24.8 9.7 %collective-permute-start.8 = (bf16[32,2048]{1,0:T(8,128)(2,1)S(1)}, bf16[32,2048]{1,0:T(8,128)(2,1)S(1)}, u32[]{:S(2)}, u32[]{:S(2)}) collective-permute-start(bf16[32,2048]{1,0:T(8,128)(2,1)S(1)} %factor.1.factor_ref.after_ref), channel_id=1, source_target_pairs={{0,16},{8,24},{16,0},{24,8},{1,17},{9,25},{17,1},{25,9},{2,18},{10... | collective-permute-start | bytes 393224 | tf_op jit(solution)/shard_map/ppermute | solution.py:27
  24.8 9.7 %collective-permute-start.7 = (bf16[32,2048]{1,0:T(8,128)(2,1)S(1)}, bf16[32,2048]{1,0:T(8,128)(2,1)S(1)}, u32[]{:S(2)}, u32[]{:S(2)}) collective-permute-start(bf16[32,2048]{1,0:T(8,128)(2,1)S(1)} %factor.1.factor_ref.after_ref), channel_id=1, source_target_pairs={{0,8},{8,0},{16,24},{24,16},{1,9},{9,1},{17,25},{25,17},{2,10},{10... | collective-permute-start | bytes 393224 | tf_op jit(solution)/shard_map/ppermute | solution.py:27
  28.6 9.1 %all-to-all-start = ((bf16[8,8,1536]{2,1,0:T(8,128)(2,1)}), bf16[8,8,1536]{2,1,0:T(8,128)(2,1)S(1)}, u32[]{:S(2)}, u32[]{:S(2)}) async-start(bf16[8,8,1536]{2,1,0:T(8,128)(2,1)} %tie.1), calls=%async_computation | async-start | bytes 393216 | tf_op jit(solution)/shard_map/all_to_all | solution.py:292

commit v17 on v16

--- a/solution.py
+++ b/solution.py
@@ -94,7 +94,7 @@
         copy.wait()
 
 
-def factor_kernel(after_ref, gates_ref, rows_ref, upper_ref, lower_ref, out_ref):
+def factor_kernel(gates_ref, rows_ref, upper_ref, lower_ref, out_ref):
     n_exp = gates_ref.shape[2]
     width, units = upper_ref.shape[1:]
     me = lax.axis_index("expert")
@@ -249,14 +249,14 @@
     factors = pl.pallas_call(
         factor_kernel,
         out_shape=jax.ShapeDtypeStruct((slots, 2 * units), bf16),
-        in_specs=[ANY] + [VMEM] * 4,
+        in_specs=[VMEM] * 4,
         out_specs=VMEM,
         compiler_params=ROOM,
         cost_estimate=pl.CostEstimate(
             flops=4 * slots * w_up.size, bytes_accessed=4 * w_up.size, transcendentals=slots * units
         ),
         name="factor",
-    )(parts[-1], gate_held, rows, upper, lower)
+    )(gate_held, rows, upper, lower)
     parts = pl.pallas_call(
         stack_kernel,
         out_shape=jax.ShapeDtypeStruct((n_dp - 1, share, 2 * cols), bf16),

time: 38.9 us -> 39.8 us (1.023)
  waiting for transfers between devices: 5.24 us -> 6.28 us
    all_to_all x1, waiting for transfers between devices: 0.1 us -> 0.98 us  [local(): returned = lax.all_to_all(piece, ('expert', 'hidden'), 0, 0)]
  transfers between devices with their start and end apart: 11 -> 11, of which waited for: 5 -> 5; matrix products, arithmetic and copies ran while one was open for 0% -> 0% of each run, Pallas kernels for 33% -> 32%
where the time goes in v17:
time: 39.8 us; the launch traced here: 39.6 us
  starting transfers between devices  17.5 us (44%)
  Pallas kernels  15 us (38%)
  waiting for transfers between devices  6.28 us (16%)
  between operations  0.74 us (2%)
    ppermute x10, starting transfers between devices, hop(): lax.ppermute(x, axis, [(i, i ^ step) for i in range(n)])  14.1 us
    ppermute x10, waiting for transfers between devices, hop(): lax.ppermute(x, axis, [(i, i ^ step) for i in range(n)])  5.29 us
    pallas_call x1, Pallas kernels, local(): pl.pallas_call(load_kernel, out_shape=[jax.ShapeDtypeStruct(x.shape, x.dt...  4.64 us
    all_to_all x1, starting transfers between devices, local(): returned = lax.all_to_all(piece, ('expert', 'hidden'), 0, 0)  3.39 us
    pallas_call x1, Pallas kernels, local(): pl.pallas_call(functools.partial(weight_kernel, chunks, (n_dp, n_hid)), o...  3.04 us
    pallas_call x1, Pallas kernels, local(): pl.pallas_call(functools.partial(piece_kernel, n_hid), out_shape=jax.Shap...  2.63 us
    pallas_call x1, Pallas kernels, local(): pl.pallas_call(factor_kernel, out_shape=jax.ShapeDtypeStruct((slots, 2 *...  2.29 us
    pallas_call x1, Pallas kernels, local(): pl.pallas_call(functools.partial(pick_kernel, n_hid), out_shape=[jax.Shap...  1.42 us
  transfers between devices with their start and end apart: 11, of which 5 were waited for; matrix products, arithmetic and copies ran while one was open for 0% of the time, Pallas kernels for 32%

profile of v17, /device:TPU:0, one launch (start us, length us, event | category | flops | bytes accessed | tf_op | source)
XLA Modules:
  0.0 39.6 jit_solution(14464127257587379857)
XLA Ops:
  0.6 1.4 %pick.1 = (bf16[32,6144]{1,0:T(8,128)(2,1)S(1)}, bf16[64,64]{1,0:T(8,128)(2,1)S(1)}) custom-call(s32[1,1,4,8]{3,2,1,0:T(4,128)} %picks_hbm.1, bf16[1,64,3072]{2,1,0:T(8,128)(2,1)} %tokens_hbm.1, bf16[1,64,3072]{2,1,0:T(8,128)(2,1)} %upstream_hbm.1), custom_call_target="tpu_custom_call" | custom-call | tf_op jit(solution)/shard_map/pick/pallas_call | solution.py:205
  2.1 2.5 %collective-permute-start.2 = (bf16[8,6144]{1,0:T(8,128)(2,1)S(1)}, bf16[8,6144]{1,0:T(8,128)(2,1)S(1)}, u32[]{:S(2)}, u32[]{:S(2)}) collective-permute-start(bf16[8,6144]{1,0:T(8,128)(2,1)S(1)} %get-tuple-element.24), channel_id=1, source_target_pairs={{0,6},{2,4},{4,2},{6,0},{1,7},{3,5},{5,3},{7,1},{8,14},{10,12},{12... | collective-permute-start | bytes 294920 | tf_op jit(solution)/shard_map/ppermute | solution.py:27
  4.6 0.6 %collective-permute-start.1 = (bf16[8,6144]{1,0:T(8,128)(2,1)S(1)}, bf16[8,6144]{1,0:T(8,128)(2,1)S(1)}, u32[]{:S(2)}, u32[]{:S(2)}) collective-permute-start(bf16[8,6144]{1,0:T(8,128)(2,1)S(1)} %get-tuple-element.25), channel_id=1, source_target_pairs={{0,4},{2,6},{4,0},{6,2},{1,5},{3,7},{5,1},{7,3},{8,12},{10,14},{12... | collective-permute-start | bytes 294920 | tf_op jit(solution)/shard_map/ppermute | solution.py:27
  5.2 0.0 collective-permute-start
  5.3 4.6 %load.1 = (f32[1,1,4,8]{3,2,1,0:T(4,128)S(1)}, bf16[1,3072,1024]{2,1,0:T(8,128)(2,1)S(1)}, bf16[1,3072,1024]{2,1,0:T(8,128)(2,1)S(1)}) custom-call(bf16[32,6144]{1,0:T(8,128)(2,1)S(1)} %get-tuple-element.14.after_ref, f32[1,1,4,8]{3,2,1,0:T(4,128)} %gates_hbm.1, bf16[1,3072,1024]{2,1,0:T(8,128)(2,1)} %upper_hbm.1, bf16[1,3072,1024]{2,1,0:T(8,128)(2,1)} %lower_hbm.1), custom_call_target="tpu_custom_call" | custom-call | bytes 25165824 | tf_op jit(solution)/shard_map/load/pallas_call | solution.py:226
  9.9 0.0 collective-permute-done.2
  9.9 0.1 collective-permute-done.1
  10.0 0.0 collective-permute-done
  10.1 2.4 %collective-permute-start.3 = (bf16[16,1536]{1,0:T(8,128)(2,1)S(1)}, bf16[16,1536]{1,0:T(8,128)(2,1)S(1)}, u32[]{:S(2)}, u32[]{:S(2)}) collective-permute-start(bf16[16,1536]{1,0:T(8,128)(2,1)S(1)} %get-tuple-element.18), channel_id=1, source_target_pairs={{0,8},{8,0},{16,24},{24,16},{1,9},{9,1},{17,25},{25,17},{2,10},{10... | collective-permute-start | bytes 147464 | tf_op jit(solution)/shard_map/ppermute | solution.py:27
  12.5 2.6 %collective-permute-start.4 = (bf16[16,1536]{1,0:T(8,128)(2,1)S(1)}, bf16[16,1536]{1,0:T(8,128)(2,1)S(1)}, u32[]{:S(2)}, u32[]{:S(2)}) collective-permute-start(bf16[16,1536]{1,0:T(8,128)(2,1)S(1)} %get-tuple-element.19), channel_id=1, source_target_pairs={{0,16},{8,24},{16,0},{24,8},{1,17},{9,25},{17,1},{25,9},{2,18},{10... | collective-permute-start | bytes 147464 | tf_op jit(solution)/shard_map/ppermute | solution.py:27
  15.1 0.0 collective-permute-start.5
  15.1 2.3 %factor.1.factor_ref.after_ref = bf16[32,2048]{1,0:T(8,128)(2,1)S(1)} custom-call(f32[1,1,4,8]{3,2,1,0:T(4,128)S(1)} %get-tuple-element.15.gates_ref.after_ref, bf16[32,6144]{1,0:T(8,128)(2,1)S(1)} %pad_maximum_fusion.1.rows_ref.own_ref, bf16[1,3072,1024]{2,1,0:T(8,128)(2,1)S(1)} %get-tuple-element.16.upper_ref, ...), custom_call_target="tpu_custom_call" | custom-call | flops 402653184 | bytes 12582912 | tf_op jit(solution)/shard_map/factor/pallas_call | solution.py:249
  17.4 0.0 collective-permute-done.3.refs_0_
  17.4 1.1 %collective-permute-done.4.refs_1_ = bf16[16,1536]{1,0:T(8,128)(2,1)S(1)} collective-permute-done((bf16[16,1536]{1,0:T(8,128)(2,1)S(1)}, bf16[16,1536]{1,0:T(8,128)(2,1)S(1)}, u32[]{:S(2)}, u32[]{:S(2)}) %collective-permute-start.4) | collective-permute-done | bytes 49184 | tf_op jit(solution)/shard_map/ppermute | solution.py:27
  18.5 2.5 %collective-permute-done.5.refs_2_ = bf16[16,1536]{1,0:T(8,128)(2,1)S(1)} collective-permute-done((bf16[16,1536]{1,0:T(8,128)(2,1)S(1)}, bf16[16,1536]{1,0:T(8,128)(2,1)S(1)}, u32[]{:S(2)}, u32[]{:S(2)}) %collective-permute-start.5) | collective-permute-done | bytes 49184 | tf_op jit(solution)/shard_map/ppermute | solution.py:27
  21.0 1.6 %collective-permute-start.6 = (bf16[3,16,1536]{2,1,0:T(8,128)(2,1)S(1)}, bf16[3,16,1536]{2,1,0:T(8,128)(2,1)S(1)}, u32[]{:S(2)}, u32[]{:S(2)}) collective-permute-start(bf16[3,16,1536]{2,1,0:T(8,128)(2,1)S(1)} %stack.1.refs_0_), channel_id=1, source_target_pairs={{0,1},{1,0},{2,3},{3,2},{4,5},{5,4},{6,7},{7,6},{8,9},{9,8},{10,11... | collective-permute-start | bytes 442376 | tf_op jit(solution)/shard_map/ppermute | solution.py:27
  22.6 0.9 %collective-permute-start.9 = (bf16[32,2048]{1,0:T(8,128)(2,1)S(1)}, bf16[32,2048]{1,0:T(8,128)(2,1)S(1)}, u32[]{:S(2)}, u32[]{:S(2)}) collective-permute-start(bf16[32,2048]{1,0:T(8,128)(2,1)S(1)} %factor.1.factor_ref.after_ref), channel_id=1, source_target_pairs={{0,24},{8,16},{16,8},{24,0},{1,25},{9,17},{17,9},{25,1},{2,26},{10... | collective-permute-start | bytes 393224 | tf_op jit(solution)/shard_map/ppermute | solution.py:27
  23.5 0.0 collective-permute-start.8
  23.5 3.4 %collective-permute-start.7 = (bf16[32,2048]{1,0:T(8,128)(2,1)S(1)}, bf16[32,2048]{1,0:T(8,128)(2,1)S(1)}, u32[]{:S(2)}, u32[]{:S(2)}) collective-permute-start(bf16[32,2048]{1,0:T(8,128)(2,1)S(1)} %factor.1.factor_ref.after_ref), channel_id=1, source_target_pairs={{0,8},{8,0},{16,24},{24,16},{1,9},{9,1},{17,25},{25,17},{2,10},{10... | collective-permute-start | bytes 393224 | tf_op jit(solution)/shard_map/ppermute | solution.py:27
  27.0 2.6 %piece.1.refs_0_ = bf16[8,8,1536]{2,1,0:T(8,128)(2,1)} custom-call(bf16[32,2048]{1,0:T(8,128)(2,1)S(1)} %factor.1.factor_ref.after_ref, bf16[1,3072,1024]{2,1,0:T(8,128)(2,1)S(1)} %get-tuple-element.16.upper_ref), custom_call_target="tpu_custom_call" | custom-call | flops 201326592 | bytes 6291456 | tf_op jit(solution)/shard_map/piece/pallas_call | solution.py:272
  29.6 0.0 collective-permute-done.6.refs_1_
  29.6 3.4 %all-to-all-start = ((bf16[8,8,1536]{2,1,0:T(8,128)(2,1)}), bf16[8,8,1536]{2,1,0:T(8,128)(2,1)S(1)}, u32[]{:S(2)}, u32[]{:S(2)}) async-start(bf16[8,8,1536]{2,1,0:T(8,128)(2,1)} %tie.1), calls=%async_computation | async-start | bytes 393216 | tf_op jit(solution)/shard_map/all_to_all | solution.py:292
  33.0 0.0 collective-permute-done.9
  33.0 1.6 %collective-permute-done.8 = bf16[32,2048]{1,0:T(8,128)(2,1)S(1)} collective-permute-done((bf16[32,2048]{1,0:T(8,128)(2,1)S(1)}, bf16[32,2048]{1,0:T(8,128)(2,1)S(1)}, u32[]{:S(2)}, u32[]{:S(2)}) %collective-permute-start.8) | collective-permute-done | bytes 131104 | tf_op jit(solution)/shard_map/ppermute | solution.py:27
  34.6 0.0 collective-permute-done.7
  34.6 3.0 %weight.1 = (f32[1,768,1024]{2,1,0:T(8,128)}, f32[1,768,1024]{2,1,0:T(8,128)}) custom-call(bf16[32,6144]{1,0:T(8,128)(2,1)S(1)} %pad_maximum_fusion.1.rows_ref.own_ref, bf16[3,16,1536]{2,1,0:T(8,128)(2,1)S(1)} %stack.1.refs_0_, bf16[3,16,1536]{2,1,0:T(8,128)(2,1)S(1)} %collective-permute-done.6.refs_1_, bf16[128,2048]{1,0:T(8,128)(2,1)S(1)} %pad_maximum_fusion.refs_2_), custom_call_target="tpu_custom_call" | custom-call | flops 402653184 | bytes 50331648 | tf_op jit(solution)/shard_map/weight/pallas_call | solution.py:303
  37.7 1.0 %all-to-all-done.came_ref = bf16[8,8,1536]{2,1,0:T(8,128)(2,1)S(1)} async-done(((bf16[8,8,1536]{2,1,0:T(8,128)(2,1)}), bf16[8,8,1536]{2,1,0:T(8,128)(2,1)S(1)}, u32[]{:S(2)}, u32[]{:S(2)}) %all-to-all-start) | async-done | bytes 196640 | tf_op jit(solution)/shard_map/all_to_all | solution.py:292
  38.7 0.9 %return.1 = bf16[1,64,1536]{2,1,0:T(8,128)(2,1)} custom-call(bf16[64,64]{1,0:T(8,128)(2,1)S(1)} %get-tuple-element.13.spread_ref, bf16[8,8,1536]{2,1,0:T(8,128)(2,1)S(1)} %all-to-all-done.came_ref), custom_call_target="tpu_custom_call" | custom-call | tf_op jit(solution)/shard_map/return/pallas_call | solution.py:293
  (6 shorter events, 0.1 us)
Async XLA Ops:
  2.1 7.8 %collective-permute-start.2 = (bf16[8,6144]{1,0:T(8,128)(2,1)S(1)}, bf16[8,6144]{1,0:T(8,128)(2,1)S(1)}, u32[]{:S(2)}, u32[]{:S(2)}) collective-permute-start(bf16[8,6144]{1,0:T(8,128)(2,1)S(1)} %get-tuple-element.24), channel_id=1, source_target_pairs={{0,6},{2,4},{4,2},{6,0},{1,7},{3,5},{5,3},{7,1},{8,14},{10,12},{12... | collective-permute-start | bytes 294920 | tf_op jit(solution)/shard_map/ppermute | solution.py:27
  4.6 5.5 %collective-permute-start.1 = (bf16[8,6144]{1,0:T(8,128)(2,1)S(1)}, bf16[8,6144]{1,0:T(8,128)(2,1)S(1)}, u32[]{:S(2)}, u32[]{:S(2)}) collective-permute-start(bf16[8,6144]{1,0:T(8,128)(2,1)S(1)} %get-tuple-element.25), channel_id=1, source_target_pairs={{0,4},{2,6},{4,0},{6,2},{1,5},{3,7},{5,1},{7,3},{8,12},{10,14},{12... | collective-permute-start | bytes 294920 | tf_op jit(solution)/shard_map/ppermute | solution.py:27
  5.2 4.8 %collective-permute-start = (bf16[8,6144]{1,0:T(8,128)(2,1)S(1)}, bf16[8,6144]{1,0:T(8,128)(2,1)S(1)}, u32[]{:S(2)}, u32[]{:S(2)}) collective-permute-start(bf16[8,6144]{1,0:T(8,128)(2,1)S(1)} %get-tuple-element.26), channel_id=1, source_target_pairs={{0,2},{2,0},{4,6},{6,4},{1,3},{3,1},{5,7},{7,5},{8,10},{10,8},{12,... | collective-permute-start | bytes 294920 | tf_op jit(solution)/shard_map/ppermute | solution.py:27
  10.1 7.3 %collective-permute-start.3 = (bf16[16,1536]{1,0:T(8,128)(2,1)S(1)}, bf16[16,1536]{1,0:T(8,128)(2,1)S(1)}, u32[]{:S(2)}, u32[]{:S(2)}) collective-permute-start(bf16[16,1536]{1,0:T(8,128)(2,1)S(1)} %get-tuple-element.18), channel_id=1, source_target_pairs={{0,8},{8,0},{16,24},{24,16},{1,9},{9,1},{17,25},{25,17},{2,10},{10... | collective-permute-start | bytes 147464 | tf_op jit(solution)/shard_map/ppermute | solution.py:27
  12.5 6.0 %collective-permute-start.4 = (bf16[16,1536]{1,0:T(8,128)(2,1)S(1)}, bf16[16,1536]{1,0:T(8,128)(2,1)S(1)}, u32[]{:S(2)}, u32[]{:S(2)}) collective-permute-start(bf16[16,1536]{1,0:T(8,128)(2,1)S(1)} %get-tuple-element.19), channel_id=1, source_target_pairs={{0,16},{8,24},{16,0},{24,8},{1,17},{9,25},{17,1},{25,9},{2,18},{10... | collective-permute-start | bytes 147464 | tf_op jit(solution)/shard_map/ppermute | solution.py:27
  15.1 5.9 %collective-permute-start.5 = (bf16[16,1536]{1,0:T(8,128)(2,1)S(1)}, bf16[16,1536]{1,0:T(8,128)(2,1)S(1)}, u32[]{:S(2)}, u32[]{:S(2)}) collective-permute-start(bf16[16,1536]{1,0:T(8,128)(2,1)S(1)} %get-tuple-element.20), channel_id=1, source_target_pairs={{0,24},{8,16},{16,8},{24,0},{1,25},{9,17},{17,9},{25,1},{2,26},{10... | collective-permute-start | bytes 147464 | tf_op jit(solution)/shard_map/ppermute | solution.py:27
  21.0 8.6 %collective-permute-start.6 = (bf16[3,16,1536]{2,1,0:T(8,128)(2,1)S(1)}, bf16[3,16,1536]{2,1,0:T(8,128)(2,1)S(1)}, u32[]{:S(2)}, u32[]{:S(2)}) collective-permute-start(bf16[3,16,1536]{2,1,0:T(8,128)(2,1)S(1)} %stack.1.refs_0_), channel_id=1, source_target_pairs={{0,1},{1,0},{2,3},{3,2},{4,5},{5,4},{6,7},{7,6},{8,9},{9,8},{10,11... | collective-permute-start | bytes 442376 | tf_op jit(solution)/shard_map/ppermute | solution.py:27
  22.6 10.4 %collective-permute-start.9 = (bf16[32,2048]{1,0:T(8,128)(2,1)S(1)}, bf16[32,2048]{1,0:T(8,128)(2,1)S(1)}, u32[]{:S(2)}, u32[]{:S(2)}) collective-permute-start(bf16[32,2048]{1,0:T(8,128)(2,1)S(1)} %factor.1.factor_ref.after_ref), channel_id=1, source_target_pairs={{0,24},{8,16},{16,8},{24,0},{1,25},{9,17},{17,9},{25,1},{2,26},{10... | collective-permute-start | bytes 393224 | tf_op jit(solution)/shard_map/ppermute | solution.py:27
  23.5 11.1 %collective-permute-start.8 = (bf16[32,2048]{1,0:T(8,128)(2,1)S(1)}, bf16[32,2048]{1,0:T(8,128)(2,1)S(1)}, u32[]{:S(2)}, u32[]{:S(2)}) collective-permute-start(bf16[32,2048]{1,0:T(8,128)(2,1)S(1)} %factor.1.factor_ref.after_ref), channel_id=1, source_target_pairs={{0,16},{8,24},{16,0},{24,8},{1,17},{9,25},{17,1},{25,9},{2,18},{10... | collective-permute-start | bytes 393224 | tf_op jit(solution)/shard_map/ppermute | solution.py:27
  23.5 11.1 %collective-permute-start.7 = (bf16[32,2048]{1,0:T(8,128)(2,1)S(1)}, bf16[32,2048]{1,0:T(8,128)(2,1)S(1)}, u32[]{:S(2)}, u32[]{:S(2)}) collective-permute-start(bf16[32,2048]{1,0:T(8,128)(2,1)S(1)} %factor.1.factor_ref.after_ref), channel_id=1, source_target_pairs={{0,8},{8,0},{16,24},{24,16},{1,9},{9,1},{17,25},{25,17},{2,10},{10... | collective-permute-start | bytes 393224 | tf_op jit(solution)/shard_map/ppermute | solution.py:27
  29.6 9.1 %all-to-all-start = ((bf16[8,8,1536]{2,1,0:T(8,128)(2,1)}), bf16[8,8,1536]{2,1,0:T(8,128)(2,1)S(1)}, u32[]{:S(2)}, u32[]{:S(2)}) async-start(bf16[8,8,1536]{2,1,0:T(8,128)(2,1)} %tie.1), calls=%async_computation | async-start | bytes 393216 | tf_op jit(solution)/shard_map/all_to_all | solution.py:292

commit v18 on v17

--- a/solution.py
+++ b/solution.py
@@ -125,7 +125,7 @@
 def stack_kernel(after_ref, *refs):
     *part_refs, out_ref = refs
     for s, part in enumerate(part_refs):
-        out_ref[s] = part[...]
+        out_ref[len(part_refs) - 1 - s] = part[...]
 
 
 def tie_kernel(*refs):
@@ -264,7 +264,7 @@
         out_specs=VMEM,
         compiler_params=ROOM,
         name="stack",
-    )(factors, *parts)
+    )(factors, *parts[::-1])
     parts = [hop(parts, "hidden", t) for t in range(n_hid)]
 
     gathered = jnp.concatenate([hop(factors, "dp", s) for s in range(n_dp)], axis=0)

time: 39.8 us -> 38.5 us (0.967)
  waiting for transfers between devices: 6.28 us -> 4.84 us
    all_to_all x1, waiting for transfers between devices: 0.98 us -> 0.01 us  [local(): returned = lax.all_to_all(piece, ('expert', 'hidden'), 0, 0)]
    ppermute x10, waiting for transfers between devices: 5.29 us -> 4.84 us  [hop(): lax.ppermute(x, axis, [(i, i ^ step) for i in range(n)])]
  transfers between devices with their start and end apart: 11 -> 11, of which waited for: 5 -> 3; matrix products, arithmetic and copies ran while one was open for 0% -> 0% of each run, Pallas kernels for 32% -> 33%
where the time goes in v18:
time: 38.5 us; the launch traced here: 38.2 us
  starting transfers between devices  17.6 us (46%)
  Pallas kernels  15 us (39%)
  waiting for transfers between devices  4.84 us (13%)
  between operations  0.74 us (2%)
    ppermute x10, starting transfers between devices, hop(): lax.ppermute(x, axis, [(i, i ^ step) for i in range(n)])  14.2 us
    ppermute x10, waiting for transfers between devices, hop(): lax.ppermute(x, axis, [(i, i ^ step) for i in range(n)])  4.84 us
    pallas_call x1, Pallas kernels, local(): pl.pallas_call(load_kernel, out_shape=[jax.ShapeDtypeStruct(x.shape, x.dt...  4.64 us
    all_to_all x1, starting transfers between devices, local(): returned = lax.all_to_all(piece, ('expert', 'hidden'), 0, 0)  3.39 us
    pallas_call x1, Pallas kernels, local(): pl.pallas_call(functools.partial(weight_kernel, chunks, (n_dp, n_hid)), o...  3.04 us
    pallas_call x1, Pallas kernels, local(): pl.pallas_call(functools.partial(piece_kernel, n_hid), out_shape=jax.Shap...  2.63 us
    pallas_call x1, Pallas kernels, local(): pl.pallas_call(factor_kernel, out_shape=jax.ShapeDtypeStruct((slots, 2 *...  2.29 us
    pallas_call x1, Pallas kernels, local(): pl.pallas_call(functools.partial(pick_kernel, n_hid), out_shape=[jax.Shap...  1.42 us
  transfers between devices with their start and end apart: 11, of which 3 were waited for; matrix products, arithmetic and copies ran while one was open for 0% of the time, Pallas kernels for 33%

profile of v18, /device:TPU:0, one launch (start us, length us, event | category | flops | bytes accessed | tf_op | source)
XLA Modules:
  0.0 38.2 jit_solution(10720163159587555016)
XLA Ops:
  0.6 1.4 %pick.1 = (bf16[32,6144]{1,0:T(8,128)(2,1)S(1)}, bf16[64,64]{1,0:T(8,128)(2,1)S(1)}) custom-call(s32[1,1,4,8]{3,2,1,0:T(4,128)} %picks_hbm.1, bf16[1,64,3072]{2,1,0:T(8,128)(2,1)} %tokens_hbm.1, bf16[1,64,3072]{2,1,0:T(8,128)(2,1)} %upstream_hbm.1), custom_call_target="tpu_custom_call" | custom-call | tf_op jit(solution)/shard_map/pick/pallas_call | solution.py:205
  2.1 2.5 %collective-permute-start.2 = (bf16[8,6144]{1,0:T(8,128)(2,1)S(1)}, bf16[8,6144]{1,0:T(8,128)(2,1)S(1)}, u32[]{:S(2)}, u32[]{:S(2)}) collective-permute-start(bf16[8,6144]{1,0:T(8,128)(2,1)S(1)} %get-tuple-element.24), channel_id=1, source_target_pairs={{0,6},{2,4},{4,2},{6,0},{1,7},{3,5},{5,3},{7,1},{8,14},{10,12},{12... | collective-permute-start | bytes 294920 | tf_op jit(solution)/shard_map/ppermute | solution.py:27
  4.6 0.6 %collective-permute-start.1 = (bf16[8,6144]{1,0:T(8,128)(2,1)S(1)}, bf16[8,6144]{1,0:T(8,128)(2,1)S(1)}, u32[]{:S(2)}, u32[]{:S(2)}) collective-permute-start(bf16[8,6144]{1,0:T(8,128)(2,1)S(1)} %get-tuple-element.25), channel_id=1, source_target_pairs={{0,4},{2,6},{4,0},{6,2},{1,5},{3,7},{5,1},{7,3},{8,12},{10,14},{12... | collective-permute-start | bytes 294920 | tf_op jit(solution)/shard_map/ppermute | solution.py:27
  5.2 0.0 collective-permute-start
  5.3 4.6 %load.1 = (f32[1,1,4,8]{3,2,1,0:T(4,128)S(1)}, bf16[1,3072,1024]{2,1,0:T(8,128)(2,1)S(1)}, bf16[1,3072,1024]{2,1,0:T(8,128)(2,1)S(1)}) custom-call(bf16[32,6144]{1,0:T(8,128)(2,1)S(1)} %get-tuple-element.14.after_ref, f32[1,1,4,8]{3,2,1,0:T(4,128)} %gates_hbm.1, bf16[1,3072,1024]{2,1,0:T(8,128)(2,1)} %upper_hbm.1, bf16[1,3072,1024]{2,1,0:T(8,128)(2,1)} %lower_hbm.1), custom_call_target="tpu_custom_call" | custom-call | bytes 25165824 | tf_op jit(solution)/shard_map/load/pallas_call | solution.py:226
  9.9 0.0 collective-permute-done.2
  9.9 0.1 collective-permute-done.1
  10.0 0.0 collective-permute-done
  10.1 4.4 %collective-permute-start.3 = (bf16[16,1536]{1,0:T(8,128)(2,1)S(1)}, bf16[16,1536]{1,0:T(8,128)(2,1)S(1)}, u32[]{:S(2)}, u32[]{:S(2)}) collective-permute-start(bf16[16,1536]{1,0:T(8,128)(2,1)S(1)} %get-tuple-element.18), channel_id=1, source_target_pairs={{0,24},{8,16},{16,8},{24,0},{1,25},{9,17},{17,9},{25,1},{2,26},{10... | collective-permute-start | bytes 147464 | tf_op jit(solution)/shard_map/ppermute | solution.py:27
  14.5 0.0 collective-permute-start.4
  14.6 0.6 %collective-permute-start.5 = (bf16[16,1536]{1,0:T(8,128)(2,1)S(1)}, bf16[16,1536]{1,0:T(8,128)(2,1)S(1)}, u32[]{:S(2)}, u32[]{:S(2)}) collective-permute-start(bf16[16,1536]{1,0:T(8,128)(2,1)S(1)} %get-tuple-element.20), channel_id=1, source_target_pairs={{0,8},{8,0},{16,24},{24,16},{1,9},{9,1},{17,25},{25,17},{2,10},{10... | collective-permute-start | bytes 147464 | tf_op jit(solution)/shard_map/ppermute | solution.py:27
  15.2 2.3 %factor.1.factor_ref.after_ref = bf16[32,2048]{1,0:T(8,128)(2,1)S(1)} custom-call(f32[1,1,4,8]{3,2,1,0:T(4,128)S(1)} %get-tuple-element.15.gates_ref.after_ref, bf16[32,6144]{1,0:T(8,128)(2,1)S(1)} %pad_maximum_fusion.1.rows_ref.own_ref, bf16[1,3072,1024]{2,1,0:T(8,128)(2,1)S(1)} %get-tuple-element.16.upper_ref, ...), custom_call_target="tpu_custom_call" | custom-call | flops 402653184 | bytes 12582912 | tf_op jit(solution)/shard_map/factor/pallas_call | solution.py:249
  17.5 0.0 collective-permute-done.3.refs_0_
  17.5 2.0 %collective-permute-done.4.refs_1_ = bf16[16,1536]{1,0:T(8,128)(2,1)S(1)} collective-permute-done((bf16[16,1536]{1,0:T(8,128)(2,1)S(1)}, bf16[16,1536]{1,0:T(8,128)(2,1)S(1)}, u32[]{:S(2)}, u32[]{:S(2)}) %collective-permute-start.4) | collective-permute-done | bytes 49184 | tf_op jit(solution)/shard_map/ppermute | solution.py:27
  19.5 0.0 collective-permute-done.5.refs_2_
  19.6 1.6 %collective-permute-start.6 = (bf16[3,16,1536]{2,1,0:T(8,128)(2,1)S(1)}, bf16[3,16,1536]{2,1,0:T(8,128)(2,1)S(1)}, u32[]{:S(2)}, u32[]{:S(2)}) collective-permute-start(bf16[3,16,1536]{2,1,0:T(8,128)(2,1)S(1)} %stack.1.refs_0_), channel_id=1, source_target_pairs={{0,1},{1,0},{2,3},{3,2},{4,5},{5,4},{6,7},{7,6},{8,9},{9,8},{10,11... | collective-permute-start | bytes 442376 | tf_op jit(solution)/shard_map/ppermute | solution.py:27
  21.1 2.1 %collective-permute-start.9 = (bf16[32,2048]{1,0:T(8,128)(2,1)S(1)}, bf16[32,2048]{1,0:T(8,128)(2,1)S(1)}, u32[]{:S(2)}, u32[]{:S(2)}) collective-permute-start(bf16[32,2048]{1,0:T(8,128)(2,1)S(1)} %factor.1.factor_ref.after_ref), channel_id=1, source_target_pairs={{0,24},{8,16},{16,8},{24,0},{1,25},{9,17},{17,9},{25,1},{2,26},{10... | collective-permute-start | bytes 393224 | tf_op jit(solution)/shard_map/ppermute | solution.py:27
  23.3 0.1 collective-permute-start.8
  23.4 2.1 %collective-permute-start.7 = (bf16[32,2048]{1,0:T(8,128)(2,1)S(1)}, bf16[32,2048]{1,0:T(8,128)(2,1)S(1)}, u32[]{:S(2)}, u32[]{:S(2)}) collective-permute-start(bf16[32,2048]{1,0:T(8,128)(2,1)S(1)} %factor.1.factor_ref.after_ref), channel_id=1, source_target_pairs={{0,8},{8,0},{16,24},{24,16},{1,9},{9,1},{17,25},{25,17},{2,10},{10... | collective-permute-start | bytes 393224 | tf_op jit(solution)/shard_map/ppermute | solution.py:27
  25.5 2.6 %piece.1.refs_0_ = bf16[8,8,1536]{2,1,0:T(8,128)(2,1)} custom-call(bf16[32,2048]{1,0:T(8,128)(2,1)S(1)} %factor.1.factor_ref.after_ref, bf16[1,3072,1024]{2,1,0:T(8,128)(2,1)S(1)} %get-tuple-element.16.upper_ref), custom_call_target="tpu_custom_call" | custom-call | flops 201326592 | bytes 6291456 | tf_op jit(solution)/shard_map/piece/pallas_call | solution.py:272
  28.1 0.0 collective-permute-done.6.refs_1_
  28.1 3.4 %all-to-all-start = ((bf16[8,8,1536]{2,1,0:T(8,128)(2,1)}), bf16[8,8,1536]{2,1,0:T(8,128)(2,1)S(1)}, u32[]{:S(2)}, u32[]{:S(2)}) async-start(bf16[8,8,1536]{2,1,0:T(8,128)(2,1)} %tie.1), calls=%async_computation | async-start | bytes 393216 | tf_op jit(solution)/shard_map/all_to_all | solution.py:292
  31.5 0.0 collective-permute-done.9
  31.5 2.7 %collective-permute-done.8 = bf16[32,2048]{1,0:T(8,128)(2,1)S(1)} collective-permute-done((bf16[32,2048]{1,0:T(8,128)(2,1)S(1)}, bf16[32,2048]{1,0:T(8,128)(2,1)S(1)}, u32[]{:S(2)}, u32[]{:S(2)}) %collective-permute-start.8) | collective-permute-done | bytes 131104 | tf_op jit(solution)/shard_map/ppermute | solution.py:27
  34.2 0.0 collective-permute-done.7
  34.3 3.0 %weight.1 = (f32[1,768,1024]{2,1,0:T(8,128)}, f32[1,768,1024]{2,1,0:T(8,128)}) custom-call(bf16[32,6144]{1,0:T(8,128)(2,1)S(1)} %pad_maximum_fusion.1.rows_ref.own_ref, bf16[3,16,1536]{2,1,0:T(8,128)(2,1)S(1)} %stack.1.refs_0_, bf16[3,16,1536]{2,1,0:T(8,128)(2,1)S(1)} %collective-permute-done.6.refs_1_, bf16[128,2048]{1,0:T(8,128)(2,1)S(1)} %pad_maximum_fusion.refs_2_), custom_call_target="tpu_custom_call" | custom-call | flops 402653184 | bytes 50331648 | tf_op jit(solution)/shard_map/weight/pallas_call | solution.py:303
  37.3 0.0 all-to-all-done.came_ref
  37.3 0.9 %return.1 = bf16[1,64,1536]{2,1,0:T(8,128)(2,1)} custom-call(bf16[64,64]{1,0:T(8,128)(2,1)S(1)} %get-tuple-element.13.spread_ref, bf16[8,8,1536]{2,1,0:T(8,128)(2,1)S(1)} %all-to-all-done.came_ref), custom_call_target="tpu_custom_call" | custom-call | tf_op jit(solution)/shard_map/return/pallas_call | solution.py:293
  (6 shorter events, 0.1 us)
Async XLA Ops:
  2.1 7.8 %collective-permute-start.2 = (bf16[8,6144]{1,0:T(8,128)(2,1)S(1)}, bf16[8,6144]{1,0:T(8,128)(2,1)S(1)}, u32[]{:S(2)}, u32[]{:S(2)}) collective-permute-start(bf16[8,6144]{1,0:T(8,128)(2,1)S(1)} %get-tuple-element.24), channel_id=1, source_target_pairs={{0,6},{2,4},{4,2},{6,0},{1,7},{3,5},{5,3},{7,1},{8,14},{10,12},{12... | collective-permute-start | bytes 294920 | tf_op jit(solution)/shard_map/ppermute | solution.py:27
  4.6 5.5 %collective-permute-start.1 = (bf16[8,6144]{1,0:T(8,128)(2,1)S(1)}, bf16[8,6144]{1,0:T(8,128)(2,1)S(1)}, u32[]{:S(2)}, u32[]{:S(2)}) collective-permute-start(bf16[8,6144]{1,0:T(8,128)(2,1)S(1)} %get-tuple-element.25), channel_id=1, source_target_pairs={{0,4},{2,6},{4,0},{6,2},{1,5},{3,7},{5,1},{7,3},{8,12},{10,14},{12... | collective-permute-start | bytes 294920 | tf_op jit(solution)/shard_map/ppermute | solution.py:27
  5.2 4.8 %collective-permute-start = (bf16[8,6144]{1,0:T(8,128)(2,1)S(1)}, bf16[8,6144]{1,0:T(8,128)(2,1)S(1)}, u32[]{:S(2)}, u32[]{:S(2)}) collective-permute-start(bf16[8,6144]{1,0:T(8,128)(2,1)S(1)} %get-tuple-element.26), channel_id=1, source_target_pairs={{0,2},{2,0},{4,6},{6,4},{1,3},{3,1},{5,7},{7,5},{8,10},{10,8},{12,... | collective-permute-start | bytes 294920 | tf_op jit(solution)/shard_map/ppermute | solution.py:27
  10.1 7.4 %collective-permute-start.3 = (bf16[16,1536]{1,0:T(8,128)(2,1)S(1)}, bf16[16,1536]{1,0:T(8,128)(2,1)S(1)}, u32[]{:S(2)}, u32[]{:S(2)}) collective-permute-start(bf16[16,1536]{1,0:T(8,128)(2,1)S(1)} %get-tuple-element.18), channel_id=1, source_target_pairs={{0,24},{8,16},{16,8},{24,0},{1,25},{9,17},{17,9},{25,1},{2,26},{10... | collective-permute-start | bytes 147464 | tf_op jit(solution)/shard_map/ppermute | solution.py:27
  14.5 5.0 %collective-permute-start.4 = (bf16[16,1536]{1,0:T(8,128)(2,1)S(1)}, bf16[16,1536]{1,0:T(8,128)(2,1)S(1)}, u32[]{:S(2)}, u32[]{:S(2)}) collective-permute-start(bf16[16,1536]{1,0:T(8,128)(2,1)S(1)} %get-tuple-element.19), channel_id=1, source_target_pairs={{0,16},{8,24},{16,0},{24,8},{1,17},{9,25},{17,1},{25,9},{2,18},{10... | collective-permute-start | bytes 147464 | tf_op jit(solution)/shard_map/ppermute | solution.py:27
  14.6 5.0 %collective-permute-start.5 = (bf16[16,1536]{1,0:T(8,128)(2,1)S(1)}, bf16[16,1536]{1,0:T(8,128)(2,1)S(1)}, u32[]{:S(2)}, u32[]{:S(2)}) collective-permute-start(bf16[16,1536]{1,0:T(8,128)(2,1)S(1)} %get-tuple-element.20), channel_id=1, source_target_pairs={{0,8},{8,0},{16,24},{24,16},{1,9},{9,1},{17,25},{25,17},{2,10},{10... | collective-permute-start | bytes 147464 | tf_op jit(solution)/shard_map/ppermute | solution.py:27
  19.6 8.6 %collective-permute-start.6 = (bf16[3,16,1536]{2,1,0:T(8,128)(2,1)S(1)}, bf16[3,16,1536]{2,1,0:T(8,128)(2,1)S(1)}, u32[]{:S(2)}, u32[]{:S(2)}) collective-permute-start(bf16[3,16,1536]{2,1,0:T(8,128)(2,1)S(1)} %stack.1.refs_0_), channel_id=1, source_target_pairs={{0,1},{1,0},{2,3},{3,2},{4,5},{5,4},{6,7},{7,6},{8,9},{9,8},{10,11... | collective-permute-start | bytes 442376 | tf_op jit(solution)/shard_map/ppermute | solution.py:27
  21.1 10.4 %collective-permute-start.9 = (bf16[32,2048]{1,0:T(8,128)(2,1)S(1)}, bf16[32,2048]{1,0:T(8,128)(2,1)S(1)}, u32[]{:S(2)}, u32[]{:S(2)}) collective-permute-start(bf16[32,2048]{1,0:T(8,128)(2,1)S(1)} %factor.1.factor_ref.after_ref), channel_id=1, source_target_pairs={{0,24},{8,16},{16,8},{24,0},{1,25},{9,17},{17,9},{25,1},{2,26},{10... | collective-permute-start | bytes 393224 | tf_op jit(solution)/shard_map/ppermute | solution.py:27
  23.3 10.9 %collective-permute-start.8 = (bf16[32,2048]{1,0:T(8,128)(2,1)S(1)}, bf16[32,2048]{1,0:T(8,128)(2,1)S(1)}, u32[]{:S(2)}, u32[]{:S(2)}) collective-permute-start(bf16[32,2048]{1,0:T(8,128)(2,1)S(1)} %factor.1.factor_ref.after_ref), channel_id=1, source_target_pairs={{0,16},{8,24},{16,0},{24,8},{1,17},{9,25},{17,1},{25,9},{2,18},{10... | collective-permute-start | bytes 393224 | tf_op jit(solution)/shard_map/ppermute | solution.py:27
  23.4 10.8 %collective-permute-start.7 = (bf16[32,2048]{1,0:T(8,128)(2,1)S(1)}, bf16[32,2048]{1,0:T(8,128)(2,1)S(1)}, u32[]{:S(2)}, u32[]{:S(2)}) collective-permute-start(bf16[32,2048]{1,0:T(8,128)(2,1)S(1)} %factor.1.factor_ref.after_ref), channel_id=1, source_target_pairs={{0,8},{8,0},{16,24},{24,16},{1,9},{9,1},{17,25},{25,17},{2,10},{10... | collective-permute-start | bytes 393224 | tf_op jit(solution)/shard_map/ppermute | solution.py:27
  28.1 9.2 %all-to-all-start = ((bf16[8,8,1536]{2,1,0:T(8,128)(2,1)}), bf16[8,8,1536]{2,1,0:T(8,128)(2,1)S(1)}, u32[]{:S(2)}, u32[]{:S(2)}) async-start(bf16[8,8,1536]{2,1,0:T(8,128)(2,1)} %tie.1), calls=%async_computation | async-start | bytes 393216 | tf_op jit(solution)/shard_map/all_to_all | solution.py:292
